TPU v7x, 32 devices: a whole 2x2x4 slice. The times are simulated.
32 devices in a mesh: seq: 8 (over z, core), clip: 4 (over y, x).
Axes of the slice: x: 2, y: 2, z: 4, core: 2. Of those that a mesh axis runs over, the one named last changes fastest.
Arguments:
- tokens: bfloat16 [8, 8, 256, 1024], P('clip', 'seq'), may hold values from -6 to 6
- cotangent: bfloat16 [8, 8, 256, 1024], P('clip', 'seq'), may hold values from -6 to 6
- context_count: int32 [8], P('clip'), may hold values from 1 to 7
- noise_level: int32 [8, 8], P('clip', 'seq'), may hold values from 0 to 1023
- frame_time: int32 [8, 8], P('clip', 'seq'), may hold values from 0 to 21, as said below
- level_table: bfloat16 [1024, 1024], replicated, may hold values from -6 to 6
- mod_weight: bfloat16 [1024, 6144], replicated, may hold values from -0.1875 to 0.1875
- mod_bias: bfloat16 [6144], replicated, may hold values from -3 to 3
- qkv_weight: bfloat16 [1024, 3072], replicated, may hold values from -0.1875 to 0.1875
- qkv_bias: bfloat16 [3072], replicated, may hold values from -3 to 3
- proj_weight: bfloat16 [1024, 1024], replicated, may hold values from -3 to 3
- proj_bias: bfloat16 [1024], replicated, may hold values from -3 to 3
- up_weight: bfloat16 [1024, 4096], replicated, may hold values from -0.1875 to 0.1875
- up_bias: bfloat16 [4096], replicated, may hold values from -3 to 3
- down_weight: bfloat16 [4096, 1024], replicated, may hold values from -0.09375 to 0.09375
- down_bias: bfloat16 [1024], replicated, may hold values from -3 to 3
Outputs:
- layer_out: bfloat16 [8, 8, 256, 1024], P('clip', 'seq')
- tokens_grad: float32 [8, 8, 256, 1024], P('clip', 'seq')
- table_grad: float32 [1024, 1024], P('seq')
- mod_wgrad: float32 [1024, 6144], P('seq')
- mod_bgrad: float32 [6144], P('seq')
- qkv_wgrad: float32 [1024, 3072], P('seq')
- qkv_bgrad: float32 [3072], P('seq')
- proj_wgrad: float32 [1024, 1024], P('seq')
- proj_bgrad: float32 [1024], P('seq')
- up_wgrad: float32 [1024, 4096], P('seq')
- up_bgrad: float32 [4096], P('seq')
- down_wgrad: float32 [4096, 1024], P('seq')
- down_bgrad: float32 [1024], P('seq')
Inputs may be any that keep to these rules, and one draw needn't show every extreme that they name: `frame_time`: within each clip the time stamps start at 0 and rise by 1 to 3 from one frame to the next; in every draw one clip rises by 3 at every frame.
All inputs are finite; a program needn't handle non-finite values.
Results may differ from a plain program's by a relative error of at most 0.017.
Values may be sent and summed in bfloat16 or wider, within the bound.
No kernel may reach another device: no remote copies, remote signals or barrier semaphores. Data moves between devices by JAX's collectives and lax.ppermute only.
A program may use at most 320 MiB of HBM per device.

v0:
```python
import jax
import jax.numpy as jnp
from jax import lax
from jax.sharding import PartitionSpec as P

HEADS = 16


EPS = 1e-06
HIGHEST_PRECISION = lax.Precision.HIGHEST
MASKED = -1e30


def silu_act(values_in):
    return values_in * jax.nn.sigmoid(values_in)


def gelu_act(values_in):
    return (
        0.5
        * values_in
        * (
            1.0
            + jnp.tanh(
                0.7978845608028654 * (values_in + 0.044715 * values_in * values_in * values_in)
            )
        )
    )


def modulate(values_in, shift_part, scale_part):
    center = jnp.mean(values_in, axis=-1, keepdims=True)
    offset = values_in - center
    spread = jnp.mean(offset * offset, axis=-1, keepdims=True)
    return offset * lax.rsqrt(spread + EPS) * (1.0 + scale_part) + shift_part


def rotary_tables(stamps, patch_count, head_size):
    quarter = head_size // 4
    freqs = 10000.0 ** (-jnp.arange(quarter).astype(jnp.float32) / quarter)
    temporal = stamps.astype(jnp.float32)[:, None, None] * freqs[None, None, :]
    spatial = jnp.arange(patch_count).astype(jnp.float32)[None, :, None] * freqs[None, None, :]
    shape_full = (stamps.shape[0], patch_count, quarter)
    angles = jnp.concatenate(
        [jnp.broadcast_to(temporal, shape_full), jnp.broadcast_to(spatial, shape_full)], axis=-1
    )
    cosine = jnp.cos(angles)
    sine = jnp.sin(angles)
    return (jnp.concatenate([cosine, cosine], axis=-1), jnp.concatenate([sine, sine], axis=-1))


def rotate(tensor, cosine, sine):
    half_size = tensor.shape[-1] // 2
    turned = jnp.concatenate([-tensor[..., half_size:], tensor[..., :half_size]], axis=-1)
    return tensor * cosine[..., None, :] + turned * sine[..., None, :]


def contract_rows(left, right):
    return lax.dot_general(
        left, right, (((0,), (0,)), ((), ())), preferred_element_type=jnp.float32
    )


def through_weight(grad_rows, weight):
    return lax.dot_general(
        grad_rows, weight, (((1,), (1,)), ((), ())), preferred_element_type=jnp.float32
    )


def column_sums(grad_rows):
    return jnp.sum(grad_rows.astype(jnp.float32), axis=0)


def on_device(
    tokens,
    cotangent,
    context_count,
    noise_level,
    frame_time,
    level_table,
    mod_weight,
    mod_bias,
    qkv_weight,
    qkv_bias,
    proj_weight,
    proj_bias,
    up_weight,
    up_bias,
    down_weight,
    down_bias,
):
    frame_total = lax.axis_size("seq")
    frame_index = lax.axis_index("seq")
    clip_count, _, patch_count, model_width = tokens.shape
    head_size = model_width // HEADS
    score_scale = head_size ** (-0.5)
    row_count = clip_count * patch_count
    head_shape = (clip_count, patch_count, HEADS, head_size)
    token_shape = (clip_count, patch_count, model_width)
    inputs = tokens.reshape(token_shape).astype(jnp.float32)
    levels_used = jnp.where(frame_index < context_count, 0, noise_level[:, 0])
    onehot = (
        levels_used[:, None] == jnp.arange(level_table.shape[0], dtype=jnp.int32)[None, :]
    ).astype(jnp.float32)
    condition = jnp.dot(
        onehot.astype(jnp.bfloat16), level_table, preferred_element_type=jnp.float32
    )
    activated, silu_pull = jax.vjp(silu_act, condition)
    condition_low = activated.astype(jnp.bfloat16)
    modulation = jnp.dot(
        condition_low, mod_weight, preferred_element_type=jnp.float32
    ) + mod_bias.astype(jnp.float32)
    shift_one, scale_one, gate_one, shift_two, scale_two, gate_two = jnp.split(
        modulation[:, None, :], 6, axis=-1
    )
    normed, norm_one_pull = jax.vjp(modulate, inputs, shift_one, scale_one)
    normed_low = normed.astype(jnp.bfloat16).reshape(row_count, model_width)
    projected = jnp.dot(
        normed_low, qkv_weight, preferred_element_type=jnp.float32
    ) + qkv_bias.astype(jnp.float32)
    projected = projected.reshape(clip_count, patch_count, 3, HEADS, head_size)
    cosine, sine = rotary_tables(frame_time[:, 0], patch_count, head_size)

    def rotate_here(tensor):
        return rotate(tensor, cosine, sine)

    queries = rotate_here(projected[:, :, 0]).astype(jnp.bfloat16)
    rotated_keys, rotate_pull = jax.vjp(rotate_here, projected[:, :, 1])
    own_pair = jnp.stack(
        [
            rotated_keys.astype(jnp.bfloat16).reshape(token_shape),
            projected[:, :, 2].astype(jnp.bfloat16).reshape(token_shape),
        ],
        axis=0,
    )[None]
    gathered = lax.all_gather(own_pair, "seq", axis=0, tiled=True)
    key_limit = jnp.maximum(frame_index, context_count - 1)

    def frame_scores(key_pair, position):
        key_block = key_pair[0].reshape(head_shape)
        scores = (
            jnp.einsum("cqhd,ckhd->chqk", queries, key_block, preferred_element_type=jnp.float32)
            * score_scale
        )
        visible = (position <= key_limit)[:, None, None, None]
        return (scores, visible)

    def max_step(carry, position):
        running_max, running_sum = carry
        scores, visible = frame_scores(gathered[position], position)
        scores = jnp.where(visible, scores, MASKED)
        new_max = jnp.maximum(running_max, jnp.max(scores, axis=-1))
        running_sum = running_sum * jnp.exp(running_max - new_max) + jnp.sum(
            jnp.exp(scores - new_max[..., None]), axis=-1
        )
        return ((new_max, running_sum), None)

    stat_shape = (clip_count, HEADS, patch_count)
    positions = jnp.arange(frame_total, dtype=jnp.int32)
    (running_max, running_sum), _ = lax.scan(
        max_step,
        (jnp.full(stat_shape, MASKED, jnp.float32), jnp.zeros(stat_shape, jnp.float32)),
        positions,
    )
    log_total = running_max + jnp.log(running_sum)

    def value_step(carry, position):
        rounded_part, residue_part = carry
        key_pair = gathered[position]
        scores, visible = frame_scores(key_pair, position)
        probabilities = jnp.where(visible, jnp.exp(scores - log_total[..., None]), 0.0)
        weights_low = probabilities.astype(jnp.bfloat16)
        weights_rest = (probabilities - weights_low.astype(jnp.float32)).astype(jnp.bfloat16)
        value_block = key_pair[1].reshape(head_shape)
        rounded_part = rounded_part + jnp.einsum(
            "chqk,ckhd->cqhd", weights_low, value_block, preferred_element_type=jnp.float32
        )
        residue_part = residue_part + jnp.einsum(
            "chqk,ckhd->cqhd", weights_rest, value_block, preferred_element_type=jnp.float32
        )
        return ((rounded_part, residue_part), None)

    zero_heads = jnp.zeros(head_shape, jnp.float32)
    (attended, residue), _ = lax.scan(value_step, (zero_heads, zero_heads), positions)
    attended_full = attended + residue
    attended_low = attended.astype(jnp.bfloat16).reshape(row_count, model_width)
    branch_one = (
        jnp.dot(attended_low, proj_weight, preferred_element_type=jnp.float32)
        + proj_bias.astype(jnp.float32)
    ).reshape(token_shape)
    middle = inputs + gate_one * branch_one
    normed_two, norm_two_pull = jax.vjp(modulate, middle, shift_two, scale_two)
    normed_two_low = normed_two.astype(jnp.bfloat16).reshape(row_count, model_width)
    hidden = jnp.dot(
        normed_two_low, up_weight, preferred_element_type=jnp.float32
    ) + up_bias.astype(jnp.float32)
    active, gelu_pull = jax.vjp(gelu_act, hidden)
    active_low = active.astype(jnp.bfloat16)
    branch_two = (
        jnp.dot(active_low, down_weight, preferred_element_type=jnp.float32)
        + down_bias.astype(jnp.float32)
    ).reshape(token_shape)
    result = middle + gate_two * branch_two
    layer_out = result.astype(jnp.bfloat16).reshape(clip_count, 1, patch_count, model_width)
    grad_out = cotangent.reshape(token_shape).astype(jnp.float32)
    grad_gate_two = jnp.sum(grad_out * branch_two, axis=1)
    grad_branch_two = (grad_out * gate_two).astype(jnp.bfloat16).reshape(row_count, model_width)
    down_wgrad = contract_rows(active_low, grad_branch_two)
    down_bgrad = column_sums(grad_branch_two)
    (grad_hidden,) = gelu_pull(through_weight(grad_branch_two, down_weight))
    grad_hidden = grad_hidden.astype(jnp.bfloat16)
    up_wgrad = contract_rows(normed_two_low, grad_hidden)
    up_bgrad = column_sums(grad_hidden)
    grad_normed_two = through_weight(grad_hidden, up_weight).reshape(token_shape)
    grad_middle, grad_shift_two, grad_scale_two = norm_two_pull(grad_normed_two)
    grad_middle = grad_middle + grad_out
    grad_gate_one = jnp.sum(grad_middle * branch_one, axis=1)
    grad_branch_one = (grad_middle * gate_one).astype(jnp.bfloat16).reshape(row_count, model_width)
    proj_wgrad = contract_rows(attended_low, grad_branch_one)
    proj_bgrad = column_sums(grad_branch_one)
    grad_attended = (
        through_weight(grad_branch_one, proj_weight).astype(jnp.bfloat16).reshape(head_shape)
    )
    row_delta = jnp.swapaxes(
        jnp.sum(grad_attended.astype(jnp.float32) * attended_full, axis=-1), 1, 2
    )

    def score_grads(key_pair, position):
        key_block = key_pair[0].reshape(head_shape)
        value_block = key_pair[1].reshape(head_shape)
        scores, visible = frame_scores(key_pair, position)
        probabilities = jnp.where(visible, jnp.exp(scores - log_total[..., None]), 0.0)
        grad_weights = jnp.einsum(
            "cqhd,ckhd->chqk", grad_attended, value_block, preferred_element_type=jnp.float32
        )
        grad_scores = (probabilities * (grad_weights - row_delta[..., None])).astype(jnp.bfloat16)
        return (key_block, probabilities, grad_scores)

    def grad_step(grad_queries, position):
        key_block, probabilities, grad_scores = score_grads(gathered[position], position)
        grad_queries = (
            grad_queries
            + jnp.einsum(
                "chqk,ckhd->cqhd", grad_scores, key_block, preferred_element_type=jnp.float32
            )
            * score_scale
        )
        grad_keys = (
            jnp.einsum("chqk,cqhd->ckhd", grad_scores, queries, preferred_element_type=jnp.float32)
            * score_scale
        )
        grad_values = jnp.einsum(
            "chqk,cqhd->ckhd",
            probabilities.astype(jnp.bfloat16),
            grad_attended,
            preferred_element_type=jnp.float32,
        )
        pair_term = jnp.stack(
            [grad_keys.reshape(token_shape), grad_values.reshape(token_shape)], axis=0
        )
        return (grad_queries, pair_term)

    grad_queries, pair_terms = lax.scan(grad_step, zero_heads, positions)
    owned = lax.psum_scatter(pair_terms, "seq", scatter_dimension=0, tiled=True)
    key_grad_sum = owned[0, 0].reshape(head_shape)
    value_grad_sum = owned[0, 1].reshape(head_shape)
    (grad_query_raw,) = rotate_pull(grad_queries)
    (grad_key_raw,) = rotate_pull(key_grad_sum)
    grad_projected = jnp.stack([grad_query_raw, grad_key_raw, value_grad_sum], axis=2)
    grad_projected = grad_projected.reshape(row_count, 3 * model_width).astype(jnp.bfloat16)
    qkv_wgrad = contract_rows(normed_low, grad_projected)
    qkv_bgrad = column_sums(grad_projected)
    grad_normed = through_weight(grad_projected, qkv_weight).reshape(token_shape)
    grad_inputs, grad_shift_one, grad_scale_one = norm_one_pull(grad_normed)
    tokens_grad = (grad_inputs + grad_middle).reshape(clip_count, 1, patch_count, model_width)
    grad_modulation = jnp.concatenate(
        [
            grad_shift_one[:, 0],
            grad_scale_one[:, 0],
            grad_gate_one,
            grad_shift_two[:, 0],
            grad_scale_two[:, 0],
            grad_gate_two,
        ],
        axis=-1,
    ).astype(jnp.bfloat16)
    mod_wgrad = contract_rows(condition_low, grad_modulation)
    mod_bgrad = column_sums(grad_modulation)
    (grad_condition,) = silu_pull(through_weight(grad_modulation, mod_weight))
    table_grad = lax.dot_general(
        onehot,
        grad_condition,
        (((0,), (0,)), ((), ())),
        precision=HIGHEST_PRECISION,
        preferred_element_type=jnp.float32,
    )
    (
        table_grad,
        mod_wgrad,
        mod_bgrad,
        qkv_wgrad,
        qkv_bgrad,
        proj_wgrad,
        proj_bgrad,
        up_wgrad,
        up_bgrad,
        down_wgrad,
        down_bgrad,
    ) = (
        lax.psum_scatter(
            table_grad.astype(jnp.bfloat16), "seq", scatter_dimension=0, tiled=True
        ).astype(jnp.float32),
        lax.psum_scatter(
            mod_wgrad.astype(jnp.bfloat16), "seq", scatter_dimension=0, tiled=True
        ).astype(jnp.float32),
        lax.psum_scatter(
            mod_bgrad.astype(jnp.bfloat16), "seq", scatter_dimension=0, tiled=True
        ).astype(jnp.float32),
        lax.psum_scatter(
            qkv_wgrad.astype(jnp.bfloat16), "seq", scatter_dimension=0, tiled=True
        ).astype(jnp.float32),
        lax.psum_scatter(
            qkv_bgrad.astype(jnp.bfloat16), "seq", scatter_dimension=0, tiled=True
        ).astype(jnp.float32),
        lax.psum_scatter(
            proj_wgrad.astype(jnp.bfloat16), "seq", scatter_dimension=0, tiled=True
        ).astype(jnp.float32),
        lax.psum_scatter(
            proj_bgrad.astype(jnp.bfloat16), "seq", scatter_dimension=0, tiled=True
        ).astype(jnp.float32),
        lax.psum_scatter(
            up_wgrad.astype(jnp.bfloat16), "seq", scatter_dimension=0, tiled=True
        ).astype(jnp.float32),
        lax.psum_scatter(
            up_bgrad.astype(jnp.bfloat16), "seq", scatter_dimension=0, tiled=True
        ).astype(jnp.float32),
        lax.psum_scatter(
            down_wgrad.astype(jnp.bfloat16), "seq", scatter_dimension=0, tiled=True
        ).astype(jnp.float32),
        lax.psum_scatter(
            down_bgrad.astype(jnp.bfloat16), "seq", scatter_dimension=0, tiled=True
        ).astype(jnp.float32),
    )
    (
        table_grad,
        mod_wgrad,
        mod_bgrad,
        qkv_wgrad,
        qkv_bgrad,
        proj_wgrad,
        proj_bgrad,
        up_wgrad,
        up_bgrad,
        down_wgrad,
        down_bgrad,
    ) = (
        lax.psum(table_grad.astype(jnp.bfloat16), "clip").astype(jnp.float32),
        lax.psum(mod_wgrad.astype(jnp.bfloat16), "clip").astype(jnp.float32),
        lax.psum(mod_bgrad.astype(jnp.bfloat16), "clip").astype(jnp.float32),
        lax.psum(qkv_wgrad.astype(jnp.bfloat16), "clip").astype(jnp.float32),
        lax.psum(qkv_bgrad.astype(jnp.bfloat16), "clip").astype(jnp.float32),
        lax.psum(proj_wgrad.astype(jnp.bfloat16), "clip").astype(jnp.float32),
        lax.psum(proj_bgrad.astype(jnp.bfloat16), "clip").astype(jnp.float32),
        lax.psum(up_wgrad.astype(jnp.bfloat16), "clip").astype(jnp.float32),
        lax.psum(up_bgrad.astype(jnp.bfloat16), "clip").astype(jnp.float32),
        lax.psum(down_wgrad.astype(jnp.bfloat16), "clip").astype(jnp.float32),
        lax.psum(down_bgrad.astype(jnp.bfloat16), "clip").astype(jnp.float32),
    )
    return (
        layer_out,
        tokens_grad,
        table_grad,
        mod_wgrad,
        mod_bgrad,
        qkv_wgrad,
        qkv_bgrad,
        proj_wgrad,
        proj_bgrad,
        up_wgrad,
        up_bgrad,
        down_wgrad,
        down_bgrad,
    )


def solution(mesh):
    placed = (
        P("clip", "seq", None, None),
        P("clip", "seq", None, None),
        P("clip"),
        P("clip", "seq"),
        P("clip", "seq"),
        P(),
        P(),
        P(),
        P(),
        P(),
        P(),
        P(),
        P(),
        P(),
        P(),
        P(),
    )
    return jax.shard_map(
        on_device,
        mesh=mesh,
        in_specs=placed,
        out_specs=(
            P("clip", "seq", None, None),
            P("clip", "seq", None, None),
            P("seq", None),
            P("seq", None),
            P("seq"),
            P("seq", None),
            P("seq"),
            P("seq", None),
            P("seq"),
            P("seq", None),
            P("seq"),
            P("seq", None),
            P("seq"),
        ),
        check_vma=False,
    )
```

profile of v0, /device:TPU:0, one launch (start us, length us, event | category | flops | bytes accessed | tf_op | source)
XLA Modules:
  0.0 1516.4 jit_solution(602897740887113050)
XLA Ops:
  12.2 6.6 fusion.33
  19.5 5.7 convolution_add_fusion.1
  25.3 6.6 copy.129
  31.8 8.3 reshape.441
  40.1 2.5 slice.79
  42.6 4.6 slice_bitcast_fusion
  51.7 4.6 fusion.46
  59.2 3.9 copy.134
  65.2 151.9 %all-gather.3.cloned.1.call-done = bf16[16,2,256,1024]{3,2,1,0:T(8,128)(2,1)} async-done(((bf16[2,2,256,1024]{3,2,1,0:T(8,128)(2,1)}), bf16[16,2,256,1024]{3,2,1,0:T(8,128)(2,1)}) %all-gather.3.cloned.1.call-update) | async-done | bytes 16777232 | tf_op jit(solution)/shard_map/all_gather | solution.py:136
  217.1 22.1 %copy.137 = bf16[8,2,2,256,1024]{3,4,2,1,0:T(8,128)(2,1)} copy(bf16[8,2,2,256,1024]{4,3,2,1,0:T(8,128)(2,1)} %bitcast.418) | data formatting | bytes 33554432
  239.2 66.9 %while.39 = (s32[]{:T(128)}, f32[2,16,256]{2,1,0:T(8,128)S(1)}, f32[2,16,256]{2,1,0:T(8,128)S(1)}, s32[8]{0:T(128)S(1)}, s32[2]{0:T(128)S(1)}, /*index=5*/bf16[8...) while((s32[]{:T(128)}, f32[2,16,256]{2,1,0:T(8,128)S(1)}, ...), condition=%wide.region_5.6_spmd.clone, body=%wide.region_2.5_spmd.clone.sunk | while | flops 283156480 | bytes 21397692 | solution.py:160
  306.1 111.5 %while.40 = (s32[]{:T(128)}, f32[2,256,16,64]{1,3,2,0:T(8,128)}, f32[2,256,16,64]{1,3,2,0:T(8,128)}, s32[8]{0:T(128)S(1)}, bf16[8,2,2,256,1024]{3,4,2,1,0:T(8,12...) while((s32[]{:T(128)}, f32[2,256,16,64]{1,3,2,0:T(8,128)}, ...), condition=%wide.region_7.8_spmd.clone, body=%wide.region_6.7_spmd.clone.sunk | while | flops 830472192 | bytes 58786068 | solution.py:184
  312.6 2.3 bitcast_add_fusion.10
  314.9 3.0 bitcast_add_fusion.9
  324.4 2.3 bitcast_add_fusion.10
  326.8 5.4 bitcast_add_fusion.9
  338.6 2.3 bitcast_add_fusion.10
  341.0 5.4 bitcast_add_fusion.9
  355.2 5.4 bitcast_add_fusion.9
  369.4 5.4 bitcast_add_fusion.9
  383.6 5.4 bitcast_add_fusion.9
  397.8 5.4 bitcast_add_fusion.9
  412.0 5.4 bitcast_add_fusion.9
  426.0 6.8 fusion.100
  432.8 15.5 %fusion.90 = (bf16[4096]{0:T(1024)(128)(2,1)}, bf16[512,4096]{1,0:T(8,128)(2,1)}) fusion(f32[512,4096]{1,0:T(8,128)} %fusion.100, f32[4096]{0:T(1024)S(1)} %convert_element_type.296, bf16[512,1024]{1,0:T(8,128)(2,1)S(1)} %get-tuple-element.543, bf16[4096,1024]{1,0:T(8,128)(2,1)S(1)} %bitcast.422), kind=kOutput, calls=%fused_computation.204 | convolution fusion | flops 4349489152 | bytes 22044672 | tf_op jit(solution)/shard_map/dot_general | solution.py:65
  448.3 8.4 fusion.101
  463.3 2.9 reshape.462
  466.3 2.5 copy.146
  468.8 3.2 multiply_reduce_fusion.1
  472.1 124.6 %while.41 = (s32[]{:T(128)}, f32[2,256,16,64]{1,3,2,0:T(8,128)S(1)}, f32[8,2,2,256,1024]{3,4,2,1,0:T(8,128)}, s32[8]{0:T(128)S(1)}, bf16[8,2,2,256,1024]{3,4,2,1...) while((s32[]{:T(128)}, ...), condition=%wide.region_14.15_spmd.clone, body=%wide.region_13.14_spmd.clone.sunk | while | flops 1366294528 | bytes 70353160 | solution.py:263
  480.1 3.0 multiply_convert_fusion.8
  495.6 3.0 multiply_convert_fusion.8
  511.2 3.0 multiply_convert_fusion.8
  526.8 3.0 multiply_convert_fusion.8
  542.4 3.0 multiply_convert_fusion.8
  557.9 3.0 multiply_convert_fusion.8
  573.5 3.0 multiply_convert_fusion.8
  578.8 2.3 fusion.188
  589.1 3.0 multiply_convert_fusion.8
  597.9 3.8 convolution_convert_fusion.4
  603.0 9.4 convolution_convert_fusion.2
  613.6 13.3 convolution_convert_fusion.1
  627.6 293.0 %reduce-scatter.8.cloned.1.call-done = f32[1,2,2,256,1024]{3,4,2,1,0:T(8,128)} async-done(((f32[8,2,2,256,1024]{3,4,2,1,0:T(8,128)}), f32[1,2,2,256,1024]{3,4,2,1,0:T(8,128)}) %reduce-scatter.8.cloned.1.call-update) | async-done | bytes 4194320 | tf_op jit(solution)/shard_map/reduce_scatter | solution.py:264
  925.6 2.9 copy_multiply_fusion.1
  930.3 3.2 add_bitcast_fusion.2
  933.6 24.1 %fusion.94 = (bf16[3,16,64]{2,1,0:T(8,128)(2,1)S(1)}, bf16[2,256,3,16,64]{1,0,4,3,2:T(2,128)(2,1)S(1)}) fusion(bf16[2,256,1,16,64]{1,0,4,3,2:T(2,128)(2,1)S(1)} %bitcast.430, bf16[2,256,1,16,64]{1,0,4,3,2:T(2,128)(2,1)S(1)} %get-tuple-element.516, bf16[2,256,1,16,64]{1,0,4,3,2:T(2,128)(2,1)S(1)} %get-tuple-element.515), kind=kLoop, calls=%fused_computation.206 | loop fusion | flops 4715520 | bytes 6297600 | tf_op jit(solution)/shard_map/reduce_sum | solution.py:71
  957.9 7.1 fusion.62
  965.1 14.7 fusion.50
  980.0 3.3 fusion.102
  983.3 3.3 convolution_convert_fusion.5
  986.7 2.6 copy.171
  990.3 2.9 fusion.60
  993.1 5.6 convolution_convert_fusion.3
  998.8 6.4 convolution_convert_fusion
  1005.3 42.4 %reduce-scatter.18.cloned.1.call-done = bf16[128,4096]{1,0:T(8,128)(2,1)} async-done(((bf16[1024,4096]{1,0:T(8,128)(2,1)}), bf16[128,4096]{1,0:T(8,128)(2,1)}) %reduce-scatter.18.cloned.1.call-update) | async-done | bytes 1048592 | tf_op jit(solution)/shard_map/reduce_scatter | solution.py:331
  1047.7 90.2 %reduce-scatter.20.cloned.1.call-done = bf16[512,1024]{1,0:T(8,128)(2,1)} async-done(((bf16[4096,1024]{1,0:T(8,128)(2,1)}), bf16[512,1024]{1,0:T(8,128)(2,1)}) %reduce-scatter.20.cloned.1.call-update) | async-done | bytes 1048592 | tf_op jit(solution)/shard_map/reduce_scatter | solution.py:337
  1137.9 36.4 %reduce-scatter.10.cloned.1.call-done = bf16[128,1024]{1,0:T(8,128)(2,1)} async-done(((bf16[1024,1024]{1,0:T(8,128)(2,1)}), bf16[128,1024]{1,0:T(8,128)(2,1)}) %reduce-scatter.10.cloned.1.call-update) | async-done | bytes 262160 | tf_op jit(solution)/shard_map/reduce_scatter | solution.py:310
  1174.4 70.9 %reduce-scatter.14.cloned.1.call-done = bf16[128,3072]{1,0:T(8,128)(2,1)} async-done(((bf16[1024,3072]{1,0:T(8,128)(2,1)}), bf16[128,3072]{1,0:T(8,128)(2,1)}) %reduce-scatter.14.cloned.1.call-update) | async-done | bytes 786448 | tf_op jit(solution)/shard_map/reduce_scatter | solution.py:319
  1245.2 130.0 %reduce-scatter.12.cloned.1.call-done = bf16[128,6144]{1,0:T(8,128)(2,1)} async-done(((bf16[1024,6144]{1,0:T(8,128)(2,1)}), bf16[128,6144]{1,0:T(8,128)(2,1)}) %reduce-scatter.12.cloned.1.call-update) | async-done | bytes 1572880 | tf_op jit(solution)/shard_map/reduce_scatter | solution.py:313
  1380.7 26.1 %all-reduce.9 = (bf16[6144]{0:T(1024)(128)(2,1)S(1)}, bf16[3072]{0:T(1024)(128)(2,1)S(1)}, bf16[1024]{0:T(1024)(128)(2,1)S(1)}, bf16[4096]{0:T(1024)(128)(2,1)S(1)}, bf16[1024]{0:T(1024)(128)(2,1)S(1)}) all-reduce(bf16[6144]{0:T(1024)(128)(2,1)S(1)} %reduce_sum.240, ...), channel_id=6, replica_groups=mesh['seq'=8,'clip'=4] {'seq'}, use_global_device_ids=true, to_apply=%region_29.30.clone | all-reduce | flops 15360 | bytes 61440
  1407.2 10.0 all-reduce.10
  1419.9 3.6 fusion.67
  1423.5 74.5 %all-reduce.14.cloned.1.call-done = (bf16[128,1024]{1,0:T(8,128)(2,1)}, bf16[128,6144]{1,0:T(8,128)(2,1)}, bf16[128,3072]{1,0:T(8,128)(2,1)}, bf16[128,1024]{1,0...) async-done(((bf16[128,1024]{1,0:T(8,128)(2,1)}, bf16[128,6144]{1,0:T(8,128)(2,1)}, bf16[128,3072]{1,0:T(8,128)(2,1)}, bf16[128,1024]{1,0:T(8,128)(2,1)}, ...) | async-done | bytes 4980752 | tf_op jit(solution)/shard_map/psum | solution.py:357
  1501.7 2.4 convert_element_type.320
  (486 shorter events, 238.2 us)
Async XLA Ops:
  7.2 413.5 %copy-start = (bf16[1024,1024]{1,0:T(8,128)(2,1)S(1)}, bf16[1024,1024]{1,0:T(8,128)(2,1)}, u32[]{:S(2)}) copy-start(bf16[1024,1024]{1,0:T(8,128)(2,1)} %param.32) | copy-start | bytes 6291460
  7.2 4.0 copy-start.61
  7.2 4.0 copy-start.57
  7.2 4.0 copy-start.67
  7.2 4.0 copy-start.66
  7.2 209.8 %all-gather.3.cloned.1.call-start = ((), (), s32[]{:S(2)}) async-start(), calls=%async_computation.14 | async-start | bytes 18874368 | tf_op jit(solution)/shard_map/all_gather | solution.py:136
  7.3 4.5 copy-start.23
  11.8 7.8 slice-start.8
  12.2 6.6 copy-start.40
  12.2 6.7 copy-start.4
  12.2 7.3 slice-start.9
  18.8 404.9 %copy-start.44 = (f32[2,1024]{1,0:T(2,128)}, f32[2,1024]{1,0:T(2,128)S(1)}, u32[]{:S(2)}) copy-start(f32[2,1024]{1,0:T(2,128)S(1)} %get-tuple-element.523) | copy-start | bytes 24580
  18.8 438.7 %copy-start.38 = (f32[2,1024]{1,0:T(2,128)}, f32[2,1024]{1,0:T(2,128)S(1)}, u32[]{:S(2)}) copy-start(f32[2,1024]{1,0:T(2,128)S(1)} %get-tuple-element.525) | copy-start | bytes 24580
  18.8 440.2 %copy-start.36 = (f32[2,1024]{1,0:T(2,128)}, f32[2,1024]{1,0:T(2,128)S(1)}, u32[]{:S(2)}) copy-start(f32[2,1024]{1,0:T(2,128)S(1)} %get-tuple-element.528) | copy-start | bytes 24580
  42.6 4.6 copy-start.68
  48.5 7.9 copy-start.21
  63.1 857.5 %reduce-scatter.8.cloned.1.call-start = ((), (), s32[]{:S(2)}) async-start(), calls=%async_computation.7 | async-start | bytes 37748736 | tf_op jit(solution)/shard_map/reduce_scatter | solution.py:264
  326.8 5.4 copy-start.25
  341.0 5.4 copy-start.25
  355.2 5.4 copy-start.25
  369.4 5.4 copy-start.25
  383.6 5.4 copy-start.25
  397.8 5.4 copy-start.25
  412.0 5.4 copy-start.25
  420.7 4.9 slice-start.6
  422.0 35.6 %copy-start.2 = (f32[512,1024]{1,0:T(8,128)}, f32[512,1024]{1,0:T(8,128)S(1)}, u32[]{:S(2)}) copy-start(f32[512,1024]{1,0:T(8,128)S(1)} %convolution_add_fusion.2) | copy-start | bytes 6291460
  422.6 34.2 %copy-start.48 = (f32[2,256]{1,0:T(2,128)}, f32[2,256]{1,0:T(2,128)S(1)}, u32[]{:S(2)}) copy-start(f32[2,256]{1,0:T(2,128)S(1)} %get-tuple-element.534) | copy-start | bytes 6148
  422.7 3.4 slice-start.7
  424.6 8.2 slice-start.3
  425.5 7.3 copy-start.34
  425.5 7.3 copy-start.32
  426.0 6.8 slice-start.4
  468.8 3.3 copy-start.7
  596.7 408.7 %reduce-scatter.16.cloned.1.call-start = ((), (), s32[]{:S(2)}) async-start(), calls=%async_computation.11 | async-start | bytes 2359296 | tf_op jit(solution)/shard_map/reduce_scatter | solution.py:325
  601.7 446.0 %reduce-scatter.18.cloned.1.call-start = ((), (), s32[]{:S(2)}) async-start(), calls=%async_computation.12 | async-start | bytes 9437184 | tf_op jit(solution)/shard_map/reduce_scatter | solution.py:331
  612.4 525.6 %reduce-scatter.20.cloned.1.call-start = ((), (), s32[]{:S(2)}) async-start(), calls=%async_computation.13 | async-start | bytes 9437184 | tf_op jit(solution)/shard_map/reduce_scatter | solution.py:337
  626.9 547.5 %reduce-scatter.10.cloned.1.call-start = ((), (), s32[]{:S(2)}) async-start(), calls=%async_computation.8 | async-start | bytes 2359296 | tf_op jit(solution)/shard_map/reduce_scatter | solution.py:310
  933.6 24.2 %copy-start.6 = (bf16[2,1,256,1024]{3,2,1,0:T(8,128)(2,1)S(1)}, bf16[2,1,256,1024]{3,2,1,0:T(8,128)(2,1)}, u32[]{:S(2)}) copy-start(bf16[2,1,256,1024]{3,2,1,0:T(8,128)(2,1)} %param.22) | copy-start | bytes 3145732
  933.6 24.2 %copy-start.43 = (f32[2,1024]{1,0:T(2,128)S(1)}, f32[2,1024]{1,0:T(2,128)}, u32[]{:S(2)}) copy-start(f32[2,1024]{1,0:T(2,128)} %copy-done.42) | copy-start | bytes 24580
  933.6 24.2 %copy-start.51 = (f32[2,256]{1,0:T(2,128)S(1)}, f32[2,256]{1,0:T(2,128)}, u32[]{:S(2)}) copy-start(f32[2,256]{1,0:T(2,128)} %copy-done.50) | copy-start | bytes 6148
  957.8 7.2 copy-start.14
  957.8 7.2 copy-start.53
  957.8 7.2 copy-start.3
  957.8 7.2 copy-start.9
  957.8 7.2 copy-start.12
  957.8 7.2 copy-start.37
  957.8 7.2 copy-start.39
  957.9 7.2 copy-start.49
  957.9 7.2 copy-start.56
  957.9 22.0 %slice-start = ((s8[12582912]{0:T(1024)(128)(4,1)}), s8[4194304]{0:T(1024)(128)(4,1)S(1)}, s32[]{:S(2)}) async-start(s8[12582912]{0:T(1024)(128)(4,1)} %bitcast.411), calls=%async_computation.16 | async-start | bytes 8388608
  957.9 22.0 %slice-start.1 = ((s8[12582912]{0:T(1024)(128)(4,1)}), s8[4194304]{0:T(1024)(128)(4,1)S(1)}, s32[]{:S(2)}) async-start(s8[12582912]{0:T(1024)(128)(4,1)} %bitcast.411), calls=%async_computation.17 | async-start | bytes 8388608
  965.0 14.8 copy-start.15
  965.1 14.8 slice-start.2
  979.9 3.4 copy-start.41
  979.9 3.4 copy-start.63
  986.6 258.6 %reduce-scatter.14.cloned.1.call-start = ((), (), s32[]{:S(2)}) async-start(), calls=%async_computation.10 | async-start | bytes 7077888 | tf_op jit(solution)/shard_map/reduce_scatter | solution.py:319
  986.7 3.6 copy-start.16
  986.7 3.6 copy-start.47
  998.7 376.5 %reduce-scatter.12.cloned.1.call-start = ((), (), s32[]{:S(2)}) async-start(), calls=%async_computation.9 | async-start | bytes 14155776 | tf_op jit(solution)/shard_map/reduce_scatter | solution.py:313
  1005.3 492.8 %all-reduce.14.cloned.1.call-start = ((), (), s32[]{:S(2)}) async-start(), calls=%async_computation.15 | async-start | bytes 9961472 | tf_op jit(solution)/shard_map/psum | solution.py:357
  1375.2 3.8 copy-start.45
  1375.2 5.5 copy-start.58
  1375.2 5.5 copy-start.60
  1498.0 6.1 copy-start.31
  (46 other events, 66.5 us)
Sparse Core Ops, SparseCore 0:
  63.2 153.7 all-gather.2
  596.8 323.7 reduce-scatter.7
  923.0 34.1 reduce-scatter.15
  959.4 88.2 reduce-scatter.17
  1050.0 87.9 reduce-scatter.19
  1140.2 34.1 reduce-scatter.9
  1176.8 68.4 reduce-scatter.13
  1247.6 127.5 reduce-scatter.11
  1380.4 117.5 all-reduce.13
where the time goes:
time: 1520 us
  waiting for transfers between devices  889 us (58%)
  matrix products  266 us (18%)
  local copies, waits for them, and re-layouts  130 us (9%)
  other arithmetic  128 us (8%)
  loops' own time  48.1 us (3%)
  blocking collectives  36.1 us (2%)
  between operations  18 us (1%)
    reduce_scatter x1, waiting for transfers between devices, on_device(): owned = lax.psum_scatter(pair_terms, 'seq', scatter_dimension=0, tiled=True)  293 us
    all_gather x1, waiting for transfers between devices, on_device(): gathered = lax.all_gather(own_pair, 'seq', axis=0, tiled=True)  152 us
    reduce_scatter x1, waiting for transfers between devices, on_device(): lax.psum_scatter(mod_wgrad.astype(jnp.bfloat16), 'seq', scatter_dimension...  130 us
    reduce_scatter x1, waiting for transfers between devices, on_device(): lax.psum_scatter(down_wgrad.astype(jnp.bfloat16), 'seq', scatter_dimensio...  90.2 us
    psum x1, waiting for transfers between devices, on_device(): lax.psum(table_grad.astype(jnp.bfloat16), 'clip').astype(jnp.float32)  74.5 us
    reduce_scatter x1, waiting for transfers between devices, on_device(): lax.psum_scatter(qkv_wgrad.astype(jnp.bfloat16), 'seq', scatter_dimension...  70.9 us
    reduce_scatter x1, waiting for transfers between devices, on_device(): lax.psum_scatter(up_wgrad.astype(jnp.bfloat16), 'seq', scatter_dimension=...  42.4 us
    unnamed x175, local copies, waits for them, and re-layouts  41.2 us
  transfers between devices with their start and end apart: 9, of which 8 were waited for; matrix products, arithmetic and copies ran while one was open for 8% of the time, Pallas kernels for 0%

commit v1 on v0

v1 whole, which is shorter than its diff:
```python
import functools

import jax
import jax.numpy as jnp
from jax import lax
from jax.experimental import pallas as pl
from jax.experimental.pallas import tpu as pltpu
from jax.sharding import PartitionSpec as P

HEADS = 16
EPS = 1e-06
HIGHEST_PRECISION = lax.Precision.HIGHEST
F32 = jnp.float32
BF16 = jnp.bfloat16
ANY = pl.BlockSpec(memory_space=pl.ANY)
VMEM = pl.BlockSpec(memory_space=pltpu.VMEM)
SMEM = pl.BlockSpec(memory_space=pltpu.SMEM)
LANES = 128
BLOCK = 256
FF_BLOCK = 512
GELU_A = 0.7978845608028654
GELU_B = 0.044715


def shaped(shape, dtype):
    return jax.ShapeDtypeStruct(shape, dtype)


def params(mib):
    return pltpu.CompilerParams(vmem_limit_bytes=mib << 20)


def cost(flops, moved, transcendentals=0):
    return pl.CostEstimate(
        flops=int(flops), bytes_accessed=int(moved), transcendentals=int(transcendentals)
    )


def dot_nn(left, right):
    return lax.dot_general(left, right, (((1,), (0,)), ((), ())), preferred_element_type=F32)


def dot_nt(left, right):
    return lax.dot_general(left, right, (((1,), (1,)), ((), ())), preferred_element_type=F32)


def dot_tn(left, right):
    return lax.dot_general(left, right, (((0,), (0,)), ((), ())), preferred_element_type=F32)


def split_heads(values, pairs, head):
    if pairs == 1:
        return [values]
    lane = lax.broadcasted_iota(jnp.int32, values.shape, 1)
    return [jnp.where(lane // head == h, values, jnp.zeros_like(values)) for h in range(pairs)]


def swap_halves(values, head):
    half = head // 2
    lane = lax.broadcasted_iota(jnp.int32, values.shape, 1)
    ahead = pltpu.roll(values, values.shape[1] - half, 1)
    behind = pltpu.roll(values, half, 1)
    return jnp.where(lax.rem(lane, head) < half, ahead, behind)


def turn(values, cosine, signed_sine, head, back):
    parts = []
    for at in range(0, values.shape[1], LANES):
        piece = values[:, at : at + LANES]
        other = swap_halves(piece, head) * signed_sine
        parts.append(piece * cosine - other if back else piece * cosine + other)
    return jnp.concatenate(parts, axis=1)


def norm_parts(values):
    center = jnp.mean(values, axis=-1, keepdims=True)
    offset = values - center
    spread = jnp.mean(offset * offset, axis=-1, keepdims=True)
    inverse = lax.rsqrt(spread + EPS)
    return offset * inverse, inverse


def norm_pull(grad, hat, inverse, scale_row):
    grad_shift = jnp.sum(grad, axis=0, keepdims=True)
    grad_scale = jnp.sum(grad * hat, axis=0, keepdims=True)
    inner = grad * (1.0 + scale_row)
    mean_one = jnp.mean(inner, axis=-1, keepdims=True)
    mean_two = jnp.mean(inner * hat, axis=-1, keepdims=True)
    return inverse * (inner - mean_one - hat * mean_two), grad_shift, grad_scale


def store_by_parity(own_ref, other_ref, where, parity, block_index, value):
    own = parity == block_index % 2

    @pl.when(own)
    def _():
        own_ref[:, where] = value

    @pl.when(jnp.logical_not(own))
    def _():
        other_ref[:, where] = value


def qkv_kernel(slots, head, meta, tokens, mod, cosine, sine, *refs):
    weights, biases = refs[:3], refs[3:6]
    outs, own, other, normed, held = refs[6 : 6 + slots], refs[-4], refs[-3], refs[-2], refs[-1]
    step = pl.program_id(0)
    me = meta[0]
    rows, width = tokens.shape
    lanes = width // slots

    @pl.when(step == 0)
    def _():
        hat, _ = norm_parts(tokens[...].astype(F32))
        low = (hat * (1.0 + mod[1:2]) + mod[0:1]).astype(BF16)
        normed[...] = low
        chunk = width // slots
        for block in range(slots):
            store_by_parity(
                own, other, slice(block // 2 * chunk, (block // 2 + 1) * chunk), me % 2, block,
                low[:, block * chunk : (block + 1) * chunk],
            )

    for kind in range(3):
        value = dot_nn(normed[...], weights[kind][...]) + biases[kind][...].astype(F32)
        if kind < 2:
            value = turn(value, cosine[...], sine[...], head, False)
        value = value.astype(BF16)
        if kind == 0:
            value = value * jnp.asarray(head**-0.5, BF16)
        for part in range(BLOCK // lanes):
            target = (step * (BLOCK // lanes) + part) ^ me
            held[target, kind] = value[:, part * lanes : (part + 1) * lanes]

    @pl.when(step == pl.num_programs(0) - 1)
    def _():
        for slot in range(slots):
            outs[slot][...] = held[slot]


def qkv_call(meta, tokens, mod, cosine, sine, weight, bias, slots, head):
    rows, width = tokens.shape
    lanes = width // slots
    steps = width // BLOCK
    whole = lambda shape: pl.BlockSpec(shape, lambda t: (0,) * len(shape))
    weight_specs = [
        pl.BlockSpec((width, BLOCK), lambda t, k=k: (0, k * steps + t)) for k in range(3)
    ]
    bias_specs = [pl.BlockSpec((1, BLOCK), lambda t, k=k: (0, k * steps + t)) for k in range(3)]
    half = width // 2
    return pl.pallas_call(
        functools.partial(qkv_kernel, slots, head),
        grid=(steps,),
        out_shape=[shaped((3, rows, lanes), BF16)] * slots + [shaped((rows, half), BF16)] * 2,
        in_specs=[SMEM, whole(tokens.shape), whole(mod.shape), whole(cosine.shape), whole(sine.shape)]
        + weight_specs
        + bias_specs,
        out_specs=[whole((3, rows, lanes))] * slots + [whole((rows, half))] * 2,
        scratch_shapes=[pltpu.VMEM((rows, width), BF16), pltpu.VMEM((slots, 3, rows, lanes), BF16)],
        compiler_params=params(32),
        cost_estimate=cost(6 * rows * width * width, 6 * width * width + 14 * rows * width),
        name="norm_qkv",
    )(meta, tokens, mod, cosine, sine, weight, weight, weight, bias, bias, bias)


def attend_kernel(slots, head, meta, *refs):
    parts, outs = refs[:slots], refs[slots : 2 * slots]
    exact, logs, held, scores, values, sems = refs[2 * slots :]
    copies = [pltpu.make_async_copy(parts[k], held.at[k], sems.at[k]) for k in range(slots)]
    for copy in copies:
        copy.start()
    for copy in copies:
        copy.wait()
    me, context = meta[0], meta[1]
    rows, width = held.shape[2], held.shape[3]
    pairs = width // head

    def prepare(frame, _):
        split = split_heads(held[frame ^ me, 2], pairs, head)
        ones = split_heads(jnp.ones((rows, width), BF16), pairs, head)
        for h in range(pairs):
            values[frame, h] = jnp.concatenate([split[h], ones[h]], axis=1)
        return 0

    lax.fori_loop(0, slots, prepare, 0)

    def attend(slot, count):
        queries = split_heads(held[slot, 0], pairs, head)
        total, tops = None, []
        for h in range(pairs):
            peak = None
            for frame in range(count):
                score = dot_nt(queries[h], held[frame ^ me, 1])
                scores[frame, h * rows : (h + 1) * rows] = score
                for at in range(0, rows, LANES):
                    piece = score[:, at : at + LANES]
                    peak = piece if peak is None else jnp.maximum(peak, piece)
            top = jnp.max(peak, axis=1, keepdims=True)
            tops.append(top)
            for frame in range(count):
                power = jnp.exp(scores[frame, h * rows : (h + 1) * rows] - top).astype(BF16)
                term = dot_nn(power, values[frame, h])
                total = term if total is None else total + term
        weight_sum = total[:, width:]
        result = total[:, :width] / weight_sum
        exact[slot] = result
        top = jnp.broadcast_to(tops[0], (rows, width))
        if pairs > 1:
            lane = lax.broadcasted_iota(jnp.int32, (rows, width), 1)
            for h in range(1, pairs):
                top = jnp.where(lane // head >= h, tops[h], top)
        turned = (top + jnp.log(weight_sum)).T
        logs[slot] = jnp.concatenate(
            [turned[h * head : h * head + 1] for h in range(pairs)], axis=1
        )

    def one_frame(frame, _):
        count = jnp.maximum(frame, context - 1) + 1
        for known in range(1, slots + 1):

            @pl.when(count == known)
            def _():
                attend(frame ^ me, known)

        return 0

    lax.fori_loop(0, slots, one_frame, 0)
    for slot in range(slots):
        outs[slot][...] = exact[slot].astype(BF16)


def attend_call(meta, parts, head):
    slots = len(parts)
    _, rows, width = parts[0].shape
    pairs = width // head
    work = slots * slots * rows * rows
    return pl.pallas_call(
        functools.partial(attend_kernel, slots, head),
        out_shape=[shaped((rows, width), BF16)] * slots
        + [shaped((slots, rows, width), F32), shaped((slots, 1, pairs * rows), F32)],
        in_specs=[SMEM] + [ANY] * slots,
        out_specs=[VMEM] * (slots + 2),
        scratch_shapes=[
            pltpu.VMEM((slots, 3, rows, width), BF16),
            pltpu.VMEM((slots, pairs * rows, rows), F32),
            pltpu.VMEM((slots, pairs, rows, 2 * width), BF16),
            pltpu.SemaphoreType.DMA((slots,)),
        ],
        compiler_params=params(40),
        cost_estimate=cost(work * 16 * width, slots * rows * width * 12, work * pairs),
        name="attend",
    )(meta, *parts)


def attend_grad_kernel(slots, head, meta, *refs):
    parts, grads = refs[:slots], refs[slots : 2 * slots]
    exact, logs = refs[2 * slots], refs[2 * slots + 1]
    outs = refs[2 * slots + 2 : 3 * slots + 2]
    held, grad, query_rows, grad_rows, delta, grad_q, grad_k, grad_v, sems, more = refs[
        3 * slots + 2 :
    ]
    copies = [pltpu.make_async_copy(parts[k], held.at[k], sems.at[k]) for k in range(slots)]
    copies += [pltpu.make_async_copy(grads[k], grad.at[k], more.at[k]) for k in range(slots)]
    for copy in copies:
        copy.start()
    for copy in copies:
        copy.wait()
    me, context = meta[0], meta[1]
    rows, width = held.shape[2], held.shape[3]
    pairs = width // head

    def prepare(slot, _):
        query_rows[slot] = jnp.concatenate(split_heads(held[slot, 0], pairs, head), axis=0)
        grad_rows[slot] = jnp.concatenate(split_heads(grad[slot], pairs, head), axis=0)
        product = (grad[slot].astype(F32) * exact[slot]).T
        delta[slot] = jnp.concatenate(
            [
                jnp.sum(product[h * head : (h + 1) * head], axis=0, keepdims=True)
                for h in range(pairs)
            ],
            axis=1,
        )
        grad_q[slot] = jnp.zeros((rows, width), F32)
        return 0

    lax.fori_loop(0, slots, prepare, 0)

    def key_frame(frame, _):
        place = frame ^ me
        keys, values = held[place, 1], held[place, 2]
        head_keys = split_heads(keys, pairs, head)
        grad_k[...] = jnp.zeros_like(grad_k)
        grad_v[...] = jnp.zeros_like(grad_v)

        def query_frame(query, _):
            slot = query ^ me
            score = dot_nt(keys, query_rows[slot])
            grad_weight = dot_nt(values, grad_rows[slot])
            weight = jnp.exp(score - logs[slot])
            grad_score = (weight * (grad_weight - delta[slot])).astype(BF16)
            grad_v[...] += dot_nn(weight.astype(BF16), grad_rows[slot])
            grad_k[...] += dot_nn(grad_score, query_rows[slot])
            total = grad_q[slot]
            for h in range(pairs):
                total = total + dot_tn(grad_score[:, h * rows : (h + 1) * rows], head_keys[h])
            grad_q[slot] = total
            return 0

        lax.fori_loop(jnp.where(frame < context, 0, frame), slots, query_frame, 0)
        held[place, 1] = grad_k[...].astype(BF16)
        held[place, 2] = grad_v[...].astype(BF16)
        return 0

    lax.fori_loop(0, slots, key_frame, 0)
    for slot in range(slots):
        outs[slot][0] = (grad_q[slot] * head**-0.5).astype(BF16)
        outs[slot][1] = held[slot, 1]
        outs[slot][2] = held[slot, 2]


def attend_grad_call(meta, parts, grads, exact, logs, head):
    slots = len(parts)
    _, rows, width = parts[0].shape
    pairs = width // head
    work = slots * slots * rows * rows
    return pl.pallas_call(
        functools.partial(attend_grad_kernel, slots, head),
        out_shape=[shaped((3, rows, width), BF16)] * slots,
        in_specs=[SMEM] + [ANY] * (2 * slots) + [VMEM, VMEM],
        out_specs=[VMEM] * slots,
        scratch_shapes=[
            pltpu.VMEM((slots, 3, rows, width), BF16),
            pltpu.VMEM((slots, rows, width), BF16),
            pltpu.VMEM((slots, pairs * rows, width), BF16),
            pltpu.VMEM((slots, pairs * rows, width), BF16),
            pltpu.VMEM((slots, 1, pairs * rows), F32),
            pltpu.VMEM((slots, rows, width), F32),
            pltpu.VMEM((rows, width), F32),
            pltpu.VMEM((rows, width), F32),
            pltpu.SemaphoreType.DMA((slots,)),
            pltpu.SemaphoreType.DMA((slots,)),
        ],
        compiler_params=params(40),
        cost_estimate=cost(work * 40 * width, slots * rows * width * 20, work * pairs),
        name="attend_grad",
    )(meta, *parts, *grads, exact, logs)


def forward_back_kernel(slots, meta, tokens, cotangent, mod, proj_b, up_b, down_b, *refs):
    parts, (proj_hbm, up_hbm, down_hbm) = refs[:slots], refs[slots : slots + 3]
    (
        layer_out, grad_middle_out, row_grads, up_bgrad,
        att_own, att_other, gone_low,
        n2_own, n2_other, hid_low,
        act_own, act_other, gtwo_low,
    ) = refs[slots + 3 : slots + 16]
    grads_out = refs[slots + 16 : 2 * slots + 16]
    held, proj, up, down, slope, active, sems = refs[2 * slots + 16 :]
    copies = [pltpu.make_async_copy(parts[k], held.at[k], sems.at[k]) for k in range(slots)]
    proj_copy = pltpu.make_async_copy(proj_hbm, proj, sems.at[slots])
    up_copy = pltpu.make_async_copy(up_hbm, up, sems.at[slots + 1])
    down_copy = pltpu.make_async_copy(down_hbm, down, sems.at[slots + 2])
    for copy in copies:
        copy.start()
    proj_copy.start()
    up_copy.start()
    down_copy.start()
    me = meta[0]
    parity = me % 2
    rows, width = tokens.shape
    lanes = width // slots
    hidden_width = up.shape[1]
    gate_one, shift_two, scale_two, gate_two = (mod[k : k + 1] for k in (2, 3, 4, 5))
    for copy in copies:
        copy.wait()
    attended = jnp.concatenate([held[k ^ me] for k in range(slots)], axis=1)
    for block in range(slots):
        store_by_parity(
            att_own, att_other, slice(block // 2 * lanes, (block // 2 + 1) * lanes), parity, block,
            held[block ^ me],
        )
    proj_copy.wait()
    branch_one = dot_nn(attended, proj[...]) + proj_b[...].astype(F32)
    middle = tokens[...].astype(F32) + gate_one * branch_one
    hat_two, inverse_two = norm_parts(middle)
    low_two = (hat_two * (1.0 + scale_two) + shift_two).astype(BF16)
    for block in range(slots):
        store_by_parity(
            n2_own, n2_other, slice(block // 2 * lanes, (block // 2 + 1) * lanes), parity, block,
            low_two[:, block * lanes : (block + 1) * lanes],
        )
    up_copy.wait()
    chunk = hidden_width // slots
    for block in range(hidden_width // FF_BLOCK):
        at = slice(block * FF_BLOCK, (block + 1) * FF_BLOCK)
        hidden = dot_nn(low_two, up[:, at]) + up_b[:, at].astype(F32)
        square = hidden * hidden
        bent = jnp.tanh(GELU_A * (hidden + GELU_B * square * hidden))
        half = 0.5 * (1.0 + bent)
        low = (hidden * half).astype(BF16)
        slope[:, at] = half + (0.5 * GELU_A) * hidden * (1.0 - bent * bent) * (
            1.0 + (3.0 * GELU_B) * square
        )
        active[:, at] = low
        for piece in range(FF_BLOCK // chunk):
            index = block * (FF_BLOCK // chunk) + piece
            store_by_parity(
                act_own, act_other, slice(index // 2 * chunk, (index // 2 + 1) * chunk), parity,
                index, low[:, piece * chunk : (piece + 1) * chunk],
            )
    down_copy.wait()
    branch_two = dot_nn(active[...], down[...]) + down_b[...].astype(F32)
    layer_out[...] = (middle + gate_two * branch_two).astype(BF16)
    grad_out = cotangent[...].astype(F32)
    low_grad_two = (grad_out * gate_two).astype(BF16)
    gtwo_low[...] = low_grad_two
    row_grads[3:4] = jnp.sum(grad_out * branch_two, axis=0, keepdims=True)
    row_grads[4:5] = jnp.sum(low_grad_two.astype(F32), axis=0, keepdims=True)
    grad_normed = None
    for block in range(hidden_width // FF_BLOCK):
        at = slice(block * FF_BLOCK, (block + 1) * FF_BLOCK)
        low = (dot_nt(low_grad_two, down[at, :]) * slope[:, at]).astype(BF16)
        hid_low[:, at] = low
        up_bgrad[:, at] = jnp.sum(low.astype(F32), axis=0, keepdims=True)
        term = dot_nt(low, up[:, at])
        grad_normed = term if grad_normed is None else grad_normed + term
    grad_middle, grad_shift, grad_scale = norm_pull(grad_normed, hat_two, inverse_two, scale_two)
    grad_middle = grad_middle + grad_out
    grad_middle_out[...] = grad_middle
    low_grad_one = (grad_middle * gate_one).astype(BF16)
    gone_low[...] = low_grad_one
    row_grads[0:1] = jnp.sum(grad_middle * branch_one, axis=0, keepdims=True)
    row_grads[1:2] = grad_shift
    row_grads[2:3] = grad_scale
    row_grads[5:6] = jnp.sum(low_grad_one.astype(F32), axis=0, keepdims=True)
    row_grads[6:8] = jnp.zeros((2, width), F32)
    grad_attended = dot_nt(low_grad_one, proj[...]).astype(BF16)
    for block in range(slots):
        held[block ^ me] = grad_attended[:, block * lanes : (block + 1) * lanes]
    for slot in range(slots):
        grads_out[slot][...] = held[slot]


def forward_back_call(
    meta, tokens, cotangent, mod, proj_b, up_b, down_b, parts, proj, up, down
):
    slots = len(parts)
    rows, width = tokens.shape
    lanes = width // slots
    hidden = up.shape[1]
    half, half_hidden = width // 2, hidden // 2
    out_shape = [
        shaped((rows, width), BF16),
        shaped((rows, width), F32),
        shaped((8, width), F32),
        shaped((1, hidden), F32),
        shaped((rows, half), BF16),
        shaped((rows, half), BF16),
        shaped((rows, width), BF16),
        shaped((rows, half), BF16),
        shaped((rows, half), BF16),
        shaped((rows, hidden), BF16),
        shaped((rows, half_hidden), BF16),
        shaped((rows, half_hidden), BF16),
        shaped((rows, width), BF16),
    ] + [shaped((rows, lanes), BF16)] * slots
    return pl.pallas_call(
        functools.partial(forward_back_kernel, slots),
        out_shape=out_shape,
        in_specs=[SMEM] + [VMEM] * 6 + [ANY] * (slots + 3),
        out_specs=[VMEM] * len(out_shape),
        scratch_shapes=[
            pltpu.VMEM((slots, rows, lanes), BF16),
            pltpu.VMEM(proj.shape, BF16),
            pltpu.VMEM(up.shape, BF16),
            pltpu.VMEM(down.shape, BF16),
            pltpu.VMEM((rows, hidden), F32),
            pltpu.VMEM((rows, hidden), BF16),
            pltpu.SemaphoreType.DMA((slots + 3,)),
        ],
        compiler_params=params(56),
        cost_estimate=cost(
            4 * rows * width * (width + 2 * hidden),
            4 * width * (width + 2 * hidden),
            rows * hidden,
        ),
        name="feed_forward",
    )(meta, tokens, cotangent, mod, proj_b, up_b, down_b, *parts, proj, up, down)


def qkv_grad_kernel(slots, head, meta, tokens, mod, cosine, sine, grad_middle, *refs):
    parts, weights = refs[:slots], refs[slots : slots + 3]
    tokens_grad, row_grads, outs = refs[slots + 3], refs[slots + 4], refs[slots + 5 : slots + 8]
    bias_grads = refs[slots + 8 : slots + 11]
    held, total, sems = refs[slots + 11 :]
    step = pl.program_id(0)
    me = meta[0]
    rows, width = tokens.shape
    lanes = width // slots

    @pl.when(step == 0)
    def _():
        copies = [pltpu.make_async_copy(parts[k], held.at[k], sems.at[k]) for k in range(slots)]
        for copy in copies:
            copy.start()
        for copy in copies:
            copy.wait()
        total[...] = jnp.zeros_like(total)

    term = None
    for kind in range(3):
        pieces = [
            held[(step * (BLOCK // lanes) + part) ^ me, kind] for part in range(BLOCK // lanes)
        ]
        low = jnp.concatenate(pieces, axis=1)
        if kind < 2:
            low = turn(low.astype(F32), cosine[...], sine[...], head, True).astype(BF16)
        outs[kind][...] = low
        bias_grads[kind][...] = jnp.sum(low.astype(F32), axis=0, keepdims=True)
        product = dot_nt(low, weights[kind][...])
        term = product if term is None else term + product
    total[...] += term

    @pl.when(step == pl.num_programs(0) - 1)
    def _():
        hat, inverse = norm_parts(tokens[...].astype(F32))
        grad, grad_shift, grad_scale = norm_pull(total[...], hat, inverse, mod[1:2])
        tokens_grad[...] = grad + grad_middle[...]
        row_grads[0:1] = grad_shift
        row_grads[1:2] = grad_scale
        row_grads[2:8] = jnp.zeros((6, width), F32)


def qkv_grad_call(meta, tokens, mod, cosine, sine, grad_middle, parts, weight, head):
    slots = len(parts)
    rows, width = tokens.shape
    lanes = width // slots
    steps = width // BLOCK
    whole = lambda shape: pl.BlockSpec(shape, lambda t: (0,) * len(shape))
    weight_specs = [
        pl.BlockSpec((width, BLOCK), lambda t, k=k: (0, k * steps + t)) for k in range(3)
    ]
    column = lambda height: pl.BlockSpec((height, BLOCK), lambda t: (0, t))
    return pl.pallas_call(
        functools.partial(qkv_grad_kernel, slots, head),
        grid=(steps,),
        out_shape=[shaped((rows, width), F32), shaped((8, width), F32)]
        + [shaped((rows, width), BF16)] * 3
        + [shaped((1, width), F32)] * 3,
        in_specs=[SMEM]
        + [whole(a.shape) for a in (tokens, mod, cosine, sine, grad_middle)]
        + [ANY] * slots
        + weight_specs,
        out_specs=[whole((rows, width)), whole((8, width))] + [column(rows)] * 3 + [column(1)] * 3,
        scratch_shapes=[
            pltpu.VMEM((slots, 3, rows, lanes), BF16),
            pltpu.VMEM((rows, width), F32),
            pltpu.SemaphoreType.DMA((slots,)),
        ],
        compiler_params=params(32),
        cost_estimate=cost(6 * rows * width * width, 6 * width * width + 20 * rows * width),
        name="qkv_grad",
    )(meta, tokens, mod, cosine, sine, grad_middle, *parts, weight, weight, weight)


def weight_grad_kernel(jobs, pieces, zs, meta, *refs):
    count = sum(job[0] + job[1] for job in jobs)
    outs = refs[count : count + pieces]
    held, sems = refs[-2:]
    step = pl.program_id(0) * pl.num_programs(1) + pl.program_id(1)
    last = pl.num_programs(0) * pl.num_programs(1) - 1
    slot = step % 2
    tile_rows, cols = held.shape[1] * held.shape[2], held.shape[3]

    def drain(which):
        pltpu.make_async_copy(held.at[which], held.at[which], sems.at[which]).wait()

    @pl.when(step >= 2)
    def _():
        drain(slot)

    at = 0
    index = 0
    for rows_n, cols_n, tall, repeats, first in jobs:
        lefts = refs[at : at + rows_n]
        rights = refs[at + rows_n : at + rows_n + cols_n]
        at += rows_n + cols_n
        for repeat in range(repeats):

            @pl.when(pl.program_id(1) == index)
            def _():
                total = None
                for left, right in zip(lefts, rights):
                    picked = left[:, repeat * tile_rows : (repeat + 1) * tile_rows] if tall else left[...]
                    term = dot_tn(picked, right[...])
                    total = term if total is None else total + term
                value = total.astype(BF16)
                height = tile_rows // zs
                held[slot] = value.reshape(held.shape[1:])
                for k in range(pieces):

                    @pl.when(pl.program_id(0) == k)
                    def _():
                        if tall:
                            for z in range(zs):
                                place = repeat * zs + z
                                inner = first + place % repeats * height
                                pltpu.make_async_copy(
                                    held.at[slot, z],
                                    outs[k].at[place // repeats, pl.ds(inner, height)],
                                    sems.at[slot],
                                ).start()
                        else:
                            pltpu.make_async_copy(
                                held.at[slot],
                                outs[k].at[:, pl.ds(first + repeat * height, height)],
                                sems.at[slot],
                            ).start()

            index += 1

    @pl.when(step == last)
    def _():
        drain(1 - slot)
        drain(slot)


def weight_grad_call(meta, products, pieces, zs, name):
    jobs, specs, arrays = [], [], []
    first = 0
    width = products[0][0][0].shape[1]
    cols = 2 * width // pieces
    height = width // zs
    flops = 0
    steps = sum(
        (p[0][0].shape[1] // width) if p[2] else (p[1][0].shape[1] // (2 * width)) for p in products
    )
    index = 0
    for lefts, rights, tall in products:
        repeats = lefts[0].shape[1] // width if tall else rights[0].shape[1] // (2 * width)
        jobs.append((len(lefts), len(rights), tall, repeats, first))
        first += height * repeats
        for left in lefts:
            arrays.append(left)
            specs.append(pl.BlockSpec(left.shape, lambda e, t, m: (0, 0)))
            flops += 2 * left.shape[0] * left.shape[1] * rights[0].shape[1]
        for right in rights:
            arrays.append(right)
            start = index

            def place(e, t, m, start=start, repeats=repeats, tall=tall):
                block = 0 if tall else jnp.clip(t - start, 0, repeats - 1)
                return (0, block * pieces + (e ^ m[2]))

            specs.append(pl.BlockSpec((right.shape[0], cols), place))
        index += repeats
    out = shaped((zs, first, cols), BF16)
    return pl.pallas_call(
        functools.partial(weight_grad_kernel, tuple(jobs), pieces, zs),
        out_shape=[out] * pieces,
        grid_spec=pltpu.PrefetchScalarGridSpec(
            num_scalar_prefetch=1,
            grid=(pieces, steps),
            in_specs=specs,
            out_specs=[ANY] * pieces,
            scratch_shapes=[
                pltpu.VMEM((2, zs, height, cols), BF16),
                pltpu.SemaphoreType.DMA((2,)),
            ],
        ),
        compiler_params=params(48),
        cost_estimate=cost(flops, sum(a.size * 2 for a in arrays) + pieces * zs * first * cols * 2),
        name=name,
    )(meta, *arrays)


def unpack_kernel(jobs, pieces, meta, *refs):
    parts, outs = refs[:pieces], refs[pieces:]
    clip = meta[2]
    cols = parts[0].shape[1]
    for e in range(pieces):
        first = 0
        for out, (height, repeats, tall) in zip(outs, jobs):
            for repeat in range(repeats):
                base = 0 if tall else repeat * cols * pieces
                target = pl.ds(pl.multiple_of(base + (clip ^ e) * cols, cols), cols)
                value = parts[e][first : first + height].astype(F32)
                if tall:
                    out[repeat * height : (repeat + 1) * height, target] = value
                else:
                    out[:, target] = value
                first += height


def unpack_call(meta, parts, jobs, outs, name):
    return pl.pallas_call(
        functools.partial(unpack_kernel, jobs, len(parts)),
        out_shape=outs,
        in_specs=[SMEM] + [VMEM] * len(parts),
        out_specs=[VMEM] * len(outs),
        compiler_params=params(32),
        cost_estimate=cost(0, sum(o.size * 4 for o in outs)),
        name=name,
    )(meta, *parts)


def exchange(array, axis, size, distance):
    return lax.ppermute(array, axis, [(k, k ^ distance) for k in range(size)])


def spread(slots_out, axis, size):
    return [slots_out[0]] + [exchange(slots_out[d], axis, size, d) for d in range(1, size)]


def sum_shares(shares, clip_size, seq_size, me):
    zs = seq_size // 2
    arrived = spread(shares, "clip", clip_size)
    kept = []
    for k in range(zs):
        total = None
        for share in arrived:
            part = lax.dynamic_index_in_dim(share, (me // 2) ^ k, 0, keepdims=False).astype(F32)
            total = part if total is None else total + part
        kept.append(total.astype(BF16))
    landed = [kept[0]] + [exchange(kept[k], "seq", seq_size, 2 * k) for k in range(1, zs)]
    total = landed[0].astype(F32)
    for part in landed[1:]:
        total = total + part.astype(F32)
    return total.astype(BF16)


def gather_pieces(piece, clip_size):
    return [piece] + [exchange(piece, "clip", clip_size, d) for d in range(1, clip_size)]


def gather_all(rows, clip_size, seq_size):
    by_seq = jnp.stack([rows] + [exchange(rows, "seq", seq_size, d) for d in range(1, seq_size)])
    return jnp.concatenate(
        [by_seq] + [exchange(by_seq, "clip", clip_size, d) for d in range(1, clip_size)]
    )


def silu_act(values_in):
    return values_in * jax.nn.sigmoid(values_in)


def rotary_tables(stamps, patch_count, head):
    lane = jnp.arange(LANES, dtype=jnp.int32)
    quarter = head // 4
    pair = lane % (head // 2)
    freqs = 10000.0 ** (-(pair % quarter).astype(F32) / quarter)
    temporal = stamps.astype(F32)[:, None, None] * freqs[None, None, :]
    spatial = jnp.arange(patch_count).astype(F32)[None, :, None] * freqs[None, None, :]
    angles = jnp.where((pair < quarter)[None, None, :], temporal, spatial)
    sign = jnp.where(lane % head < head // 2, -1.0, 1.0).astype(F32)
    return jnp.cos(angles), jnp.sin(angles) * sign[None, None, :]


def on_device(
    tokens,
    cotangent,
    context_count,
    noise_level,
    frame_time,
    level_table,
    mod_weight,
    mod_bias,
    qkv_weight,
    qkv_bias,
    proj_weight,
    proj_bias,
    up_weight,
    up_bias,
    down_weight,
    down_bias,
):
    seq_size, clip_size = lax.axis_size("seq"), lax.axis_size("clip")
    me, mine = lax.axis_index("seq"), lax.axis_index("clip")
    clips, _, rows, width = tokens.shape
    head = width // HEADS
    hidden = up_weight.shape[1]
    zs = seq_size // 2
    me = me.astype(jnp.int32)
    mine = mine.astype(jnp.int32)
    metas = [jnp.stack([me, context_count[c], mine]) for c in range(clips)]
    levels_used = jnp.where(me < context_count, 0, noise_level[:, 0])
    condition = jnp.concatenate(
        [
            lax.dynamic_slice(level_table, (levels_used[c], jnp.int32(0)), (1, width))
            for c in range(clips)
        ]
    )
    condition_low = silu_act(condition.astype(F32)).astype(BF16)
    modulation = jnp.dot(
        condition_low, mod_weight, preferred_element_type=F32
    ) + mod_bias.astype(F32)
    mods = modulation.reshape(clips, 6, width)
    cosine, sine = rotary_tables(frame_time[:, 0], rows, head)

    level_rows = jnp.stack([levels_used // 32, levels_used % 32]).astype(BF16)
    level_rows = jnp.concatenate([level_rows, jnp.zeros((2, width - clips), BF16)], axis=1)
    early = jnp.concatenate(
        [condition, level_rows, jnp.zeros((16 - clips - 2, width), BF16)], axis=0
    )
    early = gather_all(early, clip_size, seq_size)

    qkv_bias_row = qkv_bias[None]
    sent, normed_own, normed_other = [], [], []
    for c in range(clips):
        out = qkv_call(
            metas[c], tokens[c, 0], mods[c], cosine[c], sine[c], qkv_weight, qkv_bias_row,
            seq_size, head,
        )
        sent.append(out[:seq_size])
        normed_own.append(out[seq_size])
        normed_other.append(out[seq_size + 1])
    parts = [spread(s, "seq", seq_size) for s in sent]
    attended, exact, logs = [], [], []
    for c in range(clips):
        out = attend_call(metas[c], parts[c], head)
        attended.append(spread(out[:seq_size], "seq", seq_size))
        exact.append(out[seq_size])
        logs.append(out[seq_size + 1])
    layer, middles, row_grads, up_bgrads, saved, grads = [], [], [], [], [], []
    for c in range(clips):
        out = forward_back_call(
            metas[c], tokens[c, 0], cotangent[c, 0], mods[c], proj_bias[None], up_bias[None],
            down_bias[None], attended[c], proj_weight, up_weight, down_weight,
        )
        layer.append(out[0])
        middles.append(out[1])
        row_grads.append(out[2])
        up_bgrads.append(out[3])
        saved.append(out[4:13])
        grads.append(spread(out[13:], "seq", seq_size))
    swap = lambda array: exchange(array, "seq", seq_size, 1)
    products = []
    for own, other, right, tall in ((3, 4, 5, False), (6, 7, 8, True), (0, 1, 2, False)):
        lefts, rights = [], []
        for c in range(clips):
            lefts += [saved[c][own], swap(saved[c][other])]
            rights += [saved[c][right], swap(saved[c][right])]
        products.append((lefts, rights, tall))
    shares = weight_grad_call(metas[0], products, clip_size, zs, "weight_grads")
    piece = sum_shares(shares, clip_size, seq_size, me)
    row = width // seq_size
    up_wgrad, down_wgrad, proj_wgrad = unpack_call(
        metas[0],
        gather_pieces(piece, clip_size),
        (
            (row, hidden // width, False),
            (row, hidden // width, True),
            (row, 1, False),
        ),
        [shaped((row, hidden), F32), shaped((hidden // seq_size, width), F32), shaped((row, width), F32)],
        "place_weight_grads",
    )

    returned = []
    for c in range(clips):
        out = attend_grad_call(metas[c], parts[c], grads[c], exact[c], logs[c], head)
        returned.append(spread(out, "seq", seq_size))
    tokens_grads, late_rows, grad_projected, qkv_bgrads = [], [], [], []
    for c in range(clips):
        out = qkv_grad_call(
            metas[c], tokens[c, 0], mods[c], cosine[c], sine[c], middles[c], returned[c],
            qkv_weight, head,
        )
        tokens_grads.append(out[0])
        late_rows.append(out[1])
        grad_projected.append(out[2:5])
        qkv_bgrads.append(jnp.concatenate(out[5:8], axis=0))
    lefts = []
    for c in range(clips):
        lefts += [normed_own[c], swap(normed_other[c])]
    products = []
    for kind in range(3):
        rights = []
        for c in range(clips):
            rights += [grad_projected[c][kind], swap(grad_projected[c][kind])]
        products.append((lefts, rights, False))
    shares = weight_grad_call(metas[0], products, clip_size, zs, "qkv_weight_grad")
    piece = sum_shares(shares, clip_size, seq_size, me)
    (qkv_wgrad,) = unpack_call(
        metas[0],
        gather_pieces(piece, clip_size),
        ((row, 3, False),),
        [shaped((row, 3 * width), F32)],
        "place_qkv_grad",
    )

    mod_rows = [
        jnp.concatenate([late_rows[c][0:2], row_grads[c][0:4]], axis=0) for c in range(clips)
    ]
    bias_rows = [
        sum(qkv_bgrads),
        sum(up_bgrads).reshape(hidden // width, width),
        sum(r[4:5] for r in row_grads),
        sum(r[5:6] for r in row_grads),
    ]
    late = jnp.concatenate(mod_rows + bias_rows, axis=0).astype(BF16)
    used = late.shape[0]
    late = jnp.concatenate([late, jnp.zeros((-used % 16, width), BF16)], axis=0)
    late = gather_all(late, clip_size, seq_size)
    devices = late.shape[0]
    grad_modulation = late[:, : 6 * clips].reshape(devices * clips, 6 * width)
    bias_sums = jnp.sum(late[:, 6 * clips : used].astype(F32), axis=0)
    all_condition = early[:, :clips].reshape(devices * clips, width).astype(F32)
    codes = early[:, clips : clips + 2, :clips].astype(jnp.int32)
    all_levels = (codes[:, 0] * 32 + codes[:, 1]).reshape(devices * clips)
    all_active, silu_pull = jax.vjp(silu_act, all_condition)
    my_active = lax.dynamic_slice_in_dim(all_active, me * row, row, axis=1).astype(BF16)
    mod_wgrad = lax.dot_general(
        my_active, grad_modulation, (((0,), (0,)), ((), ())), preferred_element_type=F32
    )
    (grad_condition,) = silu_pull(
        lax.dot_general(
            grad_modulation, mod_weight, (((1,), (1,)), ((), ())), preferred_element_type=F32
        )
    )
    table_row = level_table.shape[0] // seq_size
    onehot = (
        all_levels[:, None] == (me * table_row + jnp.arange(table_row, dtype=jnp.int32))[None, :]
    ).astype(F32)
    table_grad = lax.dot_general(
        onehot,
        grad_condition,
        (((0,), (0,)), ((), ())),
        precision=HIGHEST_PRECISION,
        preferred_element_type=F32,
    )
    mod_sums = jnp.sum(grad_modulation.astype(F32), axis=0)

    def own_part(vector):
        size = vector.shape[0] // seq_size
        return lax.dynamic_slice_in_dim(vector, me * size, size, axis=0)

    mod_bgrad = own_part(mod_sums)
    qkv_bgrad = own_part(bias_sums[:3].reshape(3 * width))
    up_bgrad = own_part(bias_sums[3 : 3 + hidden // width].reshape(hidden))
    down_bgrad = own_part(bias_sums[3 + hidden // width])
    proj_bgrad = own_part(bias_sums[4 + hidden // width])
    layer_out = jnp.stack(layer)[:, None]
    tokens_grad = jnp.stack(tokens_grads)[:, None]
    return (
        layer_out,
        tokens_grad,
        table_grad,
        mod_wgrad,
        mod_bgrad,
        qkv_wgrad,
        qkv_bgrad,
        proj_wgrad,
        proj_bgrad,
        up_wgrad,
        up_bgrad,
        down_wgrad,
        down_bgrad,
    )


def solution(mesh):
    placed = (
        P("clip", "seq", None, None),
        P("clip", "seq", None, None),
        P("clip"),
        P("clip", "seq"),
        P("clip", "seq"),
    ) + (P(),) * 11
    return jax.shard_map(
        on_device,
        mesh=mesh,
        in_specs=placed,
        out_specs=(
            P("clip", "seq", None, None),
            P("clip", "seq", None, None),
            P("seq", None),
            P("seq", None),
            P("seq"),
            P("seq", None),
            P("seq"),
            P("seq", None),
            P("seq"),
            P("seq", None),
            P("seq"),
            P("seq", None),
            P("seq"),
        ),
        check_vma=False,
    )
```

time: 1520 us -> 734 us (0.48)
  waiting for transfers between devices: 889 us -> 223 us
  matrix products: 266 us -> 18.5 us
  Pallas kernels: 0 us -> 216 us
  starting transfers between devices: 0.55 us -> 174 us
  other arithmetic: 128 us -> 22.9 us
  local copies, waits for them, and re-layouts: 130 us -> 64.7 us
  loops' own time: 48.1 us -> 0 us
  blocking collectives: 36.1 us -> 0 us
    reduce_scatter x7 -> x0, waiting for transfers between devices: 663 us -> none  [the longest x1 293 us: on_device(): owned = lax.psum_scatter(pair_terms, 'seq', scatter_dimension=0, tiled=True)]
    dot_general x88 -> x3, matrix products: 262 us -> 17.2 us  [the longest x1 8.64 us: on_device(): lax.dot_general(grad_modulation, mod_weight, (((1,), (1,)), ((), ())), pr...]
    ppermute x0 -> x114, waiting for transfers between devices: none -> 223 us  [exchange(): return lax.ppermute(array, axis, [(k, k ^ distance) for k in range(size)])]
    pallas_call x0 -> x14, Pallas kernels: none -> 216 us  [the longest x2 61.7 us: attend_grad_call(): pl.pallas_call(functools.partial(attend_grad_kernel, slots, head), out_sh...]
    ppermute x0 -> x114, starting transfers between devices: none -> 174 us  [exchange(): return lax.ppermute(array, axis, [(k, k ^ distance) for k in range(size)])]
    all_gather x1 -> x0, waiting for transfers between devices: 152 us -> none  [on_device(): gathered = lax.all_gather(own_pair, 'seq', axis=0, tiled=True)]
    psum x1 -> x0, waiting for transfers between devices: 74.5 us -> none  [on_device(): lax.psum(table_grad.astype(jnp.bfloat16), 'clip').astype(jnp.float32)]
    reduce_sum x19 -> x2, other arithmetic: 50.7 us -> 1.95 us  [the longest x1 1.81 us: on_device(): bias_sums = jnp.sum(late[:, 6 * clips:used].astype(F32), axis=0)]
  transfers between devices with their start and end apart: 9 -> 114, of which waited for: 8 -> 20; matrix products, arithmetic and copies ran while one was open for 8% -> 9% of each run, Pallas kernels for 0% -> 29%
where the time goes in v1:
time: 734 us; the launch traced here: 725 us
  waiting for transfers between devices  223 us (30%)
  Pallas kernels  216 us (29%)
  starting transfers between devices  174 us (24%)
  local copies, waits for them, and re-layouts  64.7 us (9%)
  other arithmetic  22.9 us (3%)
  matrix products  18.5 us (3%)
    ppermute x114, waiting for transfers between devices, exchange(): return lax.ppermute(array, axis, [(k, k ^ distance) for k in range(size)])  223 us
    ppermute x114, starting transfers between devices, exchange(): return lax.ppermute(array, axis, [(k, k ^ distance) for k in range(size)])  174 us
    pallas_call x2, Pallas kernels, attend_grad_call(): pl.pallas_call(functools.partial(attend_grad_kernel, slots, head), out_sh...  61.7 us
    pallas_call x2, Pallas kernels, weight_grad_call(): pl.pallas_call(functools.partial(weight_grad_kernel, tuple(jobs), pieces,...  46.4 us
    unnamed x249, local copies, waits for them, and re-layouts  45.7 us
    pallas_call x2, Pallas kernels, forward_back_call(): pl.pallas_call(functools.partial(forward_back_kernel, slots), out_shape=o...  45.6 us
    pallas_call x2, Pallas kernels, attend_call(): pl.pallas_call(functools.partial(attend_kernel, slots, head), out_shape=[...  31.5 us
  transfers between devices with their start and end apart: 114, of which 20 were waited for; matrix products, arithmetic and copies ran while one was open for 9% of the time, Pallas kernels for 29%

profile of v1, /device:TPU:0, one launch (start us, length us, event | category | flops | bytes accessed | tf_op | source)
XLA Modules:
  0.0 724.9 jit_solution(10099394594546068466)
XLA Ops:
  7.4 3.4 collective-permute-start.60
  18.9 6.3 convolution_add_fusion
  26.6 2.6 slice_bitcast_fusion.2
  29.2 2.8 copy-done
  32.0 5.7 norm_qkv.2
  38.5 5.6 norm_qkv.3
  56.0 2.6 collective-permute-start.3
  59.4 3.7 collective-permute-start.5
  63.1 5.2 collective-permute-done.2.refs_3_
  69.2 13.0 %collective-permute-start.15 = (bf16[3,256,128]{2,1,0:T(8,128)(2,1)}, bf16[3,256,128]{2,1,0:T(8,128)(2,1)S(1)}, u32[]{:S(2)}, u32[]{:S(2)}) collective-permute-start(bf16[3,256,128]{2,1,0:T(8,128)(2,1)} %copy-done.54), channel_id=1, source_target_pairs={{0,8},{4,12},{8,0},{12,4},{16,24},{20,28},{24,16},{28,20},{1,9},{5... | collective-permute-start | bytes 589832 | tf_op jit(solution)/shard_map/ppermute | solution.py:708
  82.8 2.3 collective-permute-done.4.refs_5_
  85.8 6.7 collective-permute-start.17
  92.5 7.8 %collective-permute-start.18 = (bf16[3,256,128]{2,1,0:T(8,128)(2,1)}, bf16[3,256,128]{2,1,0:T(8,128)(2,1)S(1)}, u32[]{:S(2)}, u32[]{:S(2)}) collective-permute-start(bf16[3,256,128]{2,1,0:T(8,128)(2,1)} %copy-done.51), channel_id=1, source_target_pairs={{0,20},{4,16},{8,28},{12,24},{16,4},{20,0},{24,12},{28,8},{1,21},{... | collective-permute-start | bytes 589832 | tf_op jit(solution)/shard_map/ppermute | solution.py:708
  100.4 3.5 collective-permute-start.20
  103.8 13.8 %attend.2 = (bf16[256,128]{1,0:T(8,128)(2,1)S(1)}, bf16[256,128]{1,0:T(8,128)(2,1)S(1)}, bf16[256,128]{1,0:T(8,128)(2,1)S(1)}, bf16[256,128]{1,0:T(8,128)(2,1)S(...) custom-call(s32[3]{0:T(128)S(1)} %add_add_fusion.meta, ...), custom_call_target="tpu_custom_call" | custom-call | flops 8589934592 | bytes 3145728 | tf_op jit(solution)/shard_map/attend/pallas_call | solution.py:237
  120.0 2.8 collective-permute-start.62
  123.2 1.9 collective-permute-start.8
  125.1 17.7 %attend.3 = (bf16[256,128]{1,0:T(8,128)(2,1)S(1)}, bf16[256,128]{1,0:T(8,128)(2,1)S(1)}, bf16[256,128]{1,0:T(8,128)(2,1)S(1)}, bf16[256,128]{1,0:T(8,128)(2,1)S(...) custom-call(s32[3]{0:T(128)S(1)} %add_add_fusion.1.meta, ...), custom_call_target="tpu_custom_call" | custom-call | flops 8589934592 | bytes 3145728 | tf_op jit(solution)/shard_map/attend/pallas_call | solution.py:237
  143.9 5.0 collective-permute-start.22
  149.6 3.2 collective-permute-start.24
  152.9 2.0 collective-permute-start.26
  156.8 2.8 collective-permute-start.10
  159.7 3.4 collective-permute-done.25.refs_5_
  164.7 1.9 collective-permute-start.13
  166.6 23.0 %feed_forward.3 = (bf16[256,1024]{1,0:T(8,128)(2,1)}, f32[256,1024]{1,0:T(8,128)}, f32[8,1024]{1,0:T(8,128)}, f32[1,4096]{1,0:T(1,128)}, bf16[256,512]{1,0:T(8,1...) custom-call(s32[3]{0:T(128)} %copy-done.14, ...), custom_call_target="tpu_custom_call" | custom-call | flops 9663676416 | bytes 37748736 | tf_op jit(solution)/shard_map/feed_forward/pallas_call | solution.py:467
  192.0 5.9 collective-permute-start.43
  198.1 22.6 %feed_forward.2 = (bf16[256,1024]{1,0:T(8,128)(2,1)}, f32[256,1024]{1,0:T(8,128)}, f32[8,1024]{1,0:T(8,128)}, f32[1,4096]{1,0:T(1,128)}, bf16[256,512]{1,0:T(8,1...) custom-call(s32[3]{0:T(128)} %copy-done.12, ...), custom_call_target="tpu_custom_call" | custom-call | flops 9663676416 | bytes 37748736 | tf_op jit(solution)/shard_map/feed_forward/pallas_call | solution.py:467
  228.2 2.4 collective-permute-start.48
  232.7 2.0 collective-permute-start.30
  235.4 3.8 collective-permute-start.31
  239.8 2.1 collective-permute-start.33
  253.3 36.7 %attend_grad.3 = (bf16[3,256,128]{2,1,0:T(8,128)(2,1)S(1)}, bf16[3,256,128]{2,1,0:T(8,128)(2,1)S(1)}, bf16[3,256,128]{2,1,0:T(8,128)(2,1)S(1)}, bf16[3,256,128]{...) custom-call(s32[3]{0:T(128)S(1)} %copy-done.15, ...), custom_call_target="tpu_custom_call" | custom-call | flops 21474836480 | bytes 5242880 | tf_op jit(solution)/shard_map/attend_grad/pallas_call | solution.py:326
  293.5 25.0 %attend_grad.2 = (bf16[3,256,128]{2,1,0:T(8,128)(2,1)S(1)}, bf16[3,256,128]{2,1,0:T(8,128)(2,1)S(1)}, bf16[3,256,128]{2,1,0:T(8,128)(2,1)S(1)}, bf16[3,256,128]{...) custom-call(s32[3]{0:T(128)S(1)} %copy-done.13, ...), custom_call_target="tpu_custom_call" | custom-call | flops 21474836480 | bytes 5242880 | tf_op jit(solution)/shard_map/attend_grad/pallas_call | solution.py:326
  320.3 2.1 collective-permute-start.54
  326.1 13.3 %collective-permute-done.53.refs_5_ = bf16[3,256,128]{2,1,0:T(8,128)(2,1)S(1)} collective-permute-done((bf16[3,256,128]{2,1,0:T(8,128)(2,1)S(1)}, bf16[3,256,128]{2,1,0:T(8,128)(2,1)S(1)}, u32[]{:S(2)}, u32[]{:S(2)}) %collective-permute-start.53) | collective-permute-done | bytes 196640 | tf_op jit(solution)/shard_map/ppermute | solution.py:708
  339.4 5.0 collective-permute-start.38
  344.5 8.1 %collective-permute-start.39 = (bf16[3,256,128]{2,1,0:T(8,128)(2,1)S(1)}, bf16[3,256,128]{2,1,0:T(8,128)(2,1)S(1)}, u32[]{:S(2)}, u32[]{:S(2)}) collective-permute-start(bf16[3,256,128]{2,1,0:T(8,128)(2,1)S(1)} %get-tuple-element.188), channel_id=1, source_target_pairs={{0,20},{4,16},{8,28},{12,24},{16,4},{20,0},{24,12},{28,8},{1,21},{... | collective-permute-start | bytes 589832 | tf_op jit(solution)/shard_map/ppermute | solution.py:708
  352.6 2.1 collective-permute-start.40
  357.0 7.3 %qkv_grad.3 = (f32[256,1024]{1,0:T(8,128)S(1)}, f32[8,1024]{1,0:T(8,128)S(1)}, bf16[256,1024]{1,0:T(8,128)(2,1)S(1)}, bf16[256,1024]{1,0:T(8,128)(2,1)S(1)}, bf1...) custom-call(s32[3]{0:T(128)S(1)} %copy-done.15, ...), custom_call_target="tpu_custom_call" | custom-call | flops 1610612736 | bytes 11534336 | tf_op jit(solution)/shard_map/qkv_grad/pallas_call | solution.py:544
  364.3 7.1 collective-permute-start.65
  373.9 7.3 %qkv_grad.2 = (f32[256,1024]{1,0:T(8,128)S(1)}, f32[8,1024]{1,0:T(8,128)S(1)}, bf16[256,1024]{1,0:T(8,128)(2,1)S(1)}, bf16[256,1024]{1,0:T(8,128)(2,1)S(1)}, bf1...) custom-call(s32[3]{0:T(128)S(1)} %copy-done.13, ...), custom_call_target="tpu_custom_call" | custom-call | flops 1610612736 | bytes 11534336 | tf_op jit(solution)/shard_map/qkv_grad/pallas_call | solution.py:544
  386.1 7.9 %collective-permute-start.70 = (bf16[32,1024]{1,0:T(8,128)(2,1)}, bf16[32,1024]{1,0:T(8,128)(2,1)}, u32[]{:S(2)}, u32[]{:S(2)}) collective-permute-start(bf16[32,1024]{1,0:T(8,128)(2,1)} %concatenate.38), channel_id=1, source_target_pairs={{0,20},{4,16},{8,28},{12,24},{16,4},{20,0},{24,12},{28,8},{1,21},{... | collective-permute-start | bytes 196616 | tf_op jit(solution)/shard_map/ppermute | solution.py:708
  396.6 4.1 collective-permute-done.70
  400.7 1.9 collective-permute-done.69
  410.3 1.9 reshape.245
  412.2 2.6 collective-permute-done.72
  423.5 3.5 collective-permute-start.73
  432.0 34.5 %weight_grads.1 = (bf16[4,1152,256]{2,1,0:T(8,128)(2,1)}, bf16[4,1152,256]{2,1,0:T(8,128)(2,1)}, bf16[4,1152,256]{2,1,0:T(8,128)(2,1)}, bf16[4,1152,256]{2,1,0:T(8,128)(2,1)}) custom-call(s32[3]{0:T(128)S(1)} %copy-done.13, bf16[256,512]{1,0:T(8,128)(2,1)S(1)} %copy-done.70, bf16[256,512]{1,0:T(8,128)(2,1)} %collective-permute-done.93.refs_1_, ...), custom_call_target="tpu_custom_call" | custom-call | flops 9663676416 | bytes 28311552 | tf_op jit(solution)/shard_map/weight_grads/pallas_call | solution.py:658
  467.3 4.3 collective-permute-start.106
  472.6 2.0 collective-permute-start.74
  477.4 11.9 %qkv_weight_grad.1 = (bf16[4,384,256]{2,1,0:T(8,128)(2,1)}, bf16[4,384,256]{2,1,0:T(8,128)(2,1)}, bf16[4,384,256]{2,1,0:T(8,128)(2,1)}, bf16[4,384,256]{2,1,0:T(8,128)(2,1)}) custom-call(s32[3]{0:T(128)S(1)} %copy-done.13, bf16[256,512]{1,0:T(8,128)(2,1)S(1)} %copy-done.32, bf16[256,512]{1,0:T(8,128)(2,1)S(1)} %copy-done.36, ...), custom_call_target="tpu_custom_call" | custom-call | flops 3221225472 | bytes 12582912 | tf_op jit(solution)/shard_map/qkv_weight_grad/pallas_call | solution.py:658
  489.3 106.8 %collective-permute-done.74 = bf16[8,32,1024]{2,1,0:T(8,128)(2,1)S(1)} collective-permute-done((bf16[8,32,1024]{2,1,0:T(8,128)(2,1)S(1)}, bf16[8,32,1024]{2,1,0:T(8,128)(2,1)S(1)}, u32[]{:S(2)}, u32[]{:S(2)}) %collective-permute-start.74) | collective-permute-done | bytes 524320 | tf_op jit(solution)/shard_map/ppermute | solution.py:708
  605.6 8.6 %fusion.57 = f32[64,1024]{1,0:T(8,128)S(1)} fusion(bf16[64,6144]{1,0:T(8,128)(2,1)S(1)} %reshape.242, bf16[1024,6144]{1,0:T(8,128)(2,1)} %param.22), kind=kOutput, calls=%fused_computation.165 | convolution fusion | flops 805306368 | bytes 13631488 | tf_op jit(solution)/shard_map/dot_general | solution.py:917
  614.8 3.5 fusion.4
  621.9 2.3 fusion.24
  624.1 7.9 %collective-permute-done.85 = bf16[4,384,256]{2,1,0:T(8,128)(2,1)} collective-permute-done((bf16[4,384,256]{2,1,0:T(8,128)(2,1)}, bf16[4,384,256]{2,1,0:T(8,128)(2,1)}, u32[]{:S(2)}, u32[]{:S(2)}) %collective-permute-start.85) | collective-permute-done | bytes 786464 | tf_op jit(solution)/shard_map/ppermute | solution.py:708
  636.2 9.4 %collective-permute-done.108 = bf16[1152,256]{1,0:T(8,128)(2,1)S(1)} collective-permute-done((bf16[1152,256]{1,0:T(8,128)(2,1)S(1)}, bf16[1152,256]{1,0:T(8,128)(2,1)S(1)}, u32[]{:S(2)}, u32[]{:S(2)}) %collective-permute-start.108) | collective-permute-done | bytes 589856 | tf_op jit(solution)/shard_map/ppermute | solution.py:708
  646.9 35.5 %collective-permute-done.109 = bf16[1152,256]{1,0:T(8,128)(2,1)S(1)} collective-permute-done((bf16[1152,256]{1,0:T(8,128)(2,1)S(1)}, bf16[1152,256]{1,0:T(8,128)(2,1)S(1)}, u32[]{:S(2)}, u32[]{:S(2)}) %collective-permute-start.109) | collective-permute-done | bytes 589856 | tf_op jit(solution)/shard_map/ppermute | solution.py:708
  682.4 2.0 fusion.2.refs_0_
  684.4 2.5 collective-permute-start.113
  689.2 2.5 collective-permute-start.92
  693.0 21.3 %collective-permute-done.92.refs_3_ = bf16[384,256]{1,0:T(8,128)(2,1)S(1)} collective-permute-done((bf16[384,256]{1,0:T(8,128)(2,1)S(1)}, bf16[384,256]{1,0:T(8,128)(2,1)S(1)}, u32[]{:S(2)}, u32[]{:S(2)}) %collective-permute-start.92) | collective-permute-done | bytes 196640 | tf_op jit(solution)/shard_map/ppermute | solution.py:708
  716.6 3.3 collective-permute-done.90.refs_1_
  721.7 3.0 place_weight_grads.1
  (502 shorter events, 134.2 us)
Async XLA Ops:
  7.4 51.8 %collective-permute-start.60 = (bf16[16,1024]{1,0:T(8,128)(2,1)}, bf16[16,1024]{1,0:T(8,128)(2,1)S(1)}, u32[]{:S(2)}, u32[]{:S(2)}) collective-permute-start(bf16[16,1024]{1,0:T(8,128)(2,1)} %maximum_maximum_fusion), channel_id=1, source_target_pairs={{0,20},{4,16},{8,28},{12,24},{16,4},{20,0},{24,12},{28,8},{1,21},{... | collective-permute-start | bytes 98312 | tf_op jit(solution)/shard_map/ppermute | solution.py:708
  10.8 45.2 %collective-permute-start.59 = (bf16[16,1024]{1,0:T(8,128)(2,1)}, bf16[16,1024]{1,0:T(8,128)(2,1)S(1)}, u32[]{:S(2)}, u32[]{:S(2)}) collective-permute-start(bf16[16,1024]{1,0:T(8,128)(2,1)} %maximum_maximum_fusion), channel_id=1, source_target_pairs={{0,16},{4,20},{8,24},{12,28},{16,0},{20,4},{24,8},{28,12},{1,17},{... | collective-permute-start | bytes 98312 | tf_op jit(solution)/shard_map/ppermute | solution.py:708
  11.4 44.0 %collective-permute-start.58 = (bf16[16,1024]{1,0:T(8,128)(2,1)}, bf16[16,1024]{1,0:T(8,128)(2,1)S(1)}, u32[]{:S(2)}, u32[]{:S(2)}) collective-permute-start(bf16[16,1024]{1,0:T(8,128)(2,1)} %maximum_maximum_fusion), channel_id=1, source_target_pairs={{0,12},{4,8},{8,4},{12,0},{16,28},{20,24},{24,20},{28,16},{1,13},{... | collective-permute-start | bytes 98312 | tf_op jit(solution)/shard_map/ppermute | solution.py:708
  12.8 39.6 %collective-permute-start.57 = (bf16[16,1024]{1,0:T(8,128)(2,1)}, bf16[16,1024]{1,0:T(8,128)(2,1)}, u32[]{:S(2)}, u32[]{:S(2)}) collective-permute-start(bf16[16,1024]{1,0:T(8,128)(2,1)} %maximum_maximum_fusion), channel_id=1, source_target_pairs={{0,8},{4,12},{8,0},{12,4},{16,24},{20,28},{24,16},{28,20},{1,9},{5... | collective-permute-start | bytes 98312 | tf_op jit(solution)/shard_map/ppermute | solution.py:708
  13.2 37.5 %collective-permute-start.56 = (bf16[16,1024]{1,0:T(8,128)(2,1)}, bf16[16,1024]{1,0:T(8,128)(2,1)}, u32[]{:S(2)}, u32[]{:S(2)}) collective-permute-start(bf16[16,1024]{1,0:T(8,128)(2,1)} %maximum_maximum_fusion), channel_id=1, source_target_pairs={{0,4},{4,0},{8,12},{12,8},{16,20},{20,16},{24,28},{28,24},{1,5},{5... | collective-permute-start | bytes 98312 | tf_op jit(solution)/shard_map/ppermute | solution.py:708
  59.3 25.8 %collective-permute-start.4 = (bf16[3,256,128]{2,1,0:T(8,128)(2,1)}, bf16[3,256,128]{2,1,0:T(8,128)(2,1)S(1)}, u32[]{:S(2)}, u32[]{:S(2)}) collective-permute-start(bf16[3,256,128]{2,1,0:T(8,128)(2,1)} %get-tuple-element.143), channel_id=1, source_target_pairs={{0,20},{4,16},{8,28},{12,24},{16,4},{20,0},{24,12},{28,8},{1,21},{... | collective-permute-start | bytes 589832 | tf_op jit(solution)/shard_map/ppermute | solution.py:708
  59.4 26.4 %collective-permute-start.5 = (bf16[3,256,128]{2,1,0:T(8,128)(2,1)}, bf16[3,256,128]{2,1,0:T(8,128)(2,1)S(1)}, u32[]{:S(2)}, u32[]{:S(2)}) collective-permute-start(bf16[3,256,128]{2,1,0:T(8,128)(2,1)} %get-tuple-element.144), channel_id=1, source_target_pairs={{0,24},{4,28},{8,16},{12,20},{16,8},{20,12},{24,0},{28,4},{1,25},{... | collective-permute-start | bytes 589832 | tf_op jit(solution)/shard_map/ppermute | solution.py:708
  63.1 29.4 %collective-permute-start.6 = (bf16[3,256,128]{2,1,0:T(8,128)(2,1)}, bf16[3,256,128]{2,1,0:T(8,128)(2,1)S(1)}, u32[]{:S(2)}, u32[]{:S(2)}) collective-permute-start(bf16[3,256,128]{2,1,0:T(8,128)(2,1)} %get-tuple-element.145), channel_id=1, source_target_pairs={{0,28},{4,24},{8,20},{12,16},{16,12},{20,8},{24,4},{28,0},{1,29},{... | collective-permute-start | bytes 589832 | tf_op jit(solution)/shard_map/ppermute | solution.py:708
  68.3 32.1 %collective-permute-start.14 = (bf16[3,256,128]{2,1,0:T(8,128)(2,1)}, bf16[3,256,128]{2,1,0:T(8,128)(2,1)S(1)}, u32[]{:S(2)}, u32[]{:S(2)}) collective-permute-start(bf16[3,256,128]{2,1,0:T(8,128)(2,1)} %get-tuple-element.156), channel_id=1, source_target_pairs={{0,4},{4,0},{8,12},{12,8},{16,20},{20,16},{24,28},{28,24},{1,5},{5... | collective-permute-start | bytes 589832 | tf_op jit(solution)/shard_map/ppermute | solution.py:708
  69.2 31.2 %collective-permute-start.15 = (bf16[3,256,128]{2,1,0:T(8,128)(2,1)}, bf16[3,256,128]{2,1,0:T(8,128)(2,1)S(1)}, u32[]{:S(2)}, u32[]{:S(2)}) collective-permute-start(bf16[3,256,128]{2,1,0:T(8,128)(2,1)} %copy-done.54), channel_id=1, source_target_pairs={{0,8},{4,12},{8,0},{12,4},{16,24},{20,28},{24,16},{28,20},{1,9},{5... | collective-permute-start | bytes 589832 | tf_op jit(solution)/shard_map/ppermute | solution.py:708
  85.1 34.2 %collective-permute-start.16 = (bf16[3,256,128]{2,1,0:T(8,128)(2,1)}, bf16[3,256,128]{2,1,0:T(8,128)(2,1)S(1)}, u32[]{:S(2)}, u32[]{:S(2)}) collective-permute-start(bf16[3,256,128]{2,1,0:T(8,128)(2,1)} %copy-done.53), channel_id=1, source_target_pairs={{0,12},{4,8},{8,4},{12,0},{16,28},{20,24},{24,20},{28,16},{1,13},{... | collective-permute-start | bytes 589832 | tf_op jit(solution)/shard_map/ppermute | solution.py:708
  85.8 34.2 %collective-permute-start.17 = (bf16[3,256,128]{2,1,0:T(8,128)(2,1)}, bf16[3,256,128]{2,1,0:T(8,128)(2,1)S(1)}, u32[]{:S(2)}, u32[]{:S(2)}) collective-permute-start(bf16[3,256,128]{2,1,0:T(8,128)(2,1)} %copy-done.52), channel_id=1, source_target_pairs={{0,16},{4,20},{8,24},{12,28},{16,0},{20,4},{24,8},{28,12},{1,17},{... | collective-permute-start | bytes 589832 | tf_op jit(solution)/shard_map/ppermute | solution.py:708
  92.5 30.3 %collective-permute-start.18 = (bf16[3,256,128]{2,1,0:T(8,128)(2,1)}, bf16[3,256,128]{2,1,0:T(8,128)(2,1)S(1)}, u32[]{:S(2)}, u32[]{:S(2)}) collective-permute-start(bf16[3,256,128]{2,1,0:T(8,128)(2,1)} %copy-done.51), channel_id=1, source_target_pairs={{0,20},{4,16},{8,28},{12,24},{16,4},{20,0},{24,12},{28,8},{1,21},{... | collective-permute-start | bytes 589832 | tf_op jit(solution)/shard_map/ppermute | solution.py:708
  120.0 29.5 %collective-permute-start.62 = (bf16[16,1024]{1,0:T(8,128)(2,1)}, bf16[16,1024]{1,0:T(8,128)(2,1)S(1)}, u32[]{:S(2)}, u32[]{:S(2)}) collective-permute-start(bf16[16,1024]{1,0:T(8,128)(2,1)} %maximum_maximum_fusion), channel_id=1, source_target_pairs={{0,28},{4,24},{8,20},{12,16},{16,12},{20,8},{24,4},{28,0},{1,29},{... | collective-permute-start | bytes 98312 | tf_op jit(solution)/shard_map/ppermute | solution.py:708
  122.9 26.7 %collective-permute-start.7 = (bf16[256,128]{1,0:T(8,128)(2,1)S(1)}, bf16[256,128]{1,0:T(8,128)(2,1)S(1)}, u32[]{:S(2)}, u32[]{:S(2)}) collective-permute-start(bf16[256,128]{1,0:T(8,128)(2,1)S(1)} %get-tuple-element.147), channel_id=1, source_target_pairs={{0,4},{4,0},{8,12},{12,8},{16,20},{20,16},{24,28},{28,24},{1,5},{5... | collective-permute-start | bytes 196616 | tf_op jit(solution)/shard_map/ppermute | solution.py:708
  123.2 29.5 %collective-permute-start.8 = (bf16[256,128]{1,0:T(8,128)(2,1)S(1)}, bf16[256,128]{1,0:T(8,128)(2,1)S(1)}, u32[]{:S(2)}, u32[]{:S(2)}) collective-permute-start(bf16[256,128]{1,0:T(8,128)(2,1)S(1)} %get-tuple-element.148), channel_id=1, source_target_pairs={{0,8},{4,12},{8,0},{12,4},{16,24},{20,28},{24,16},{28,20},{1,9},{5... | collective-permute-start | bytes 196616 | tf_op jit(solution)/shard_map/ppermute | solution.py:708
  156.8 32.8 %collective-permute-start.9 = (bf16[256,128]{1,0:T(8,128)(2,1)S(1)}, bf16[256,128]{1,0:T(8,128)(2,1)S(1)}, u32[]{:S(2)}, u32[]{:S(2)}) collective-permute-start(bf16[256,128]{1,0:T(8,128)(2,1)S(1)} %get-tuple-element.149), channel_id=1, source_target_pairs={{0,12},{4,8},{8,4},{12,0},{16,28},{20,24},{24,20},{28,16},{1,13},{... | collective-permute-start | bytes 196616 | tf_op jit(solution)/shard_map/ppermute | solution.py:708
  156.8 33.4 %collective-permute-start.10 = (bf16[256,128]{1,0:T(8,128)(2,1)S(1)}, bf16[256,128]{1,0:T(8,128)(2,1)S(1)}, u32[]{:S(2)}, u32[]{:S(2)}) collective-permute-start(bf16[256,128]{1,0:T(8,128)(2,1)S(1)} %get-tuple-element.150), channel_id=1, source_target_pairs={{0,16},{4,20},{8,24},{12,28},{16,0},{20,4},{24,8},{28,12},{1,17},{... | collective-permute-start | bytes 196616 | tf_op jit(solution)/shard_map/ppermute | solution.py:708
  163.0 27.3 %collective-permute-start.11 = (bf16[256,128]{1,0:T(8,128)(2,1)S(1)}, bf16[256,128]{1,0:T(8,128)(2,1)S(1)}, u32[]{:S(2)}, u32[]{:S(2)}) collective-permute-start(bf16[256,128]{1,0:T(8,128)(2,1)S(1)} %get-tuple-element.151), channel_id=1, source_target_pairs={{0,20},{4,16},{8,28},{12,24},{16,4},{20,0},{24,12},{28,8},{1,21},{... | collective-permute-start | bytes 196616 | tf_op jit(solution)/shard_map/ppermute | solution.py:708
  163.1 28.8 %collective-permute-start.12 = (bf16[256,128]{1,0:T(8,128)(2,1)S(1)}, bf16[256,128]{1,0:T(8,128)(2,1)S(1)}, u32[]{:S(2)}, u32[]{:S(2)}) collective-permute-start(bf16[256,128]{1,0:T(8,128)(2,1)S(1)} %get-tuple-element.152), channel_id=1, source_target_pairs={{0,24},{4,28},{8,16},{12,20},{16,8},{20,12},{24,0},{28,4},{1,25},{... | collective-permute-start | bytes 196616 | tf_op jit(solution)/shard_map/ppermute | solution.py:708
  164.7 27.4 %collective-permute-start.13 = (bf16[256,128]{1,0:T(8,128)(2,1)S(1)}, bf16[256,128]{1,0:T(8,128)(2,1)S(1)}, u32[]{:S(2)}, u32[]{:S(2)}) collective-permute-start(bf16[256,128]{1,0:T(8,128)(2,1)S(1)} %get-tuple-element.153), channel_id=1, source_target_pairs={{0,28},{4,24},{8,20},{12,16},{16,12},{20,8},{24,4},{28,0},{1,29},{... | collective-permute-start | bytes 196616 | tf_op jit(solution)/shard_map/ppermute | solution.py:708
  189.7 31.0 %collective-permute-start.76 = (bf16[256,512]{1,0:T(8,128)(2,1)S(1)}, bf16[256,512]{1,0:T(8,128)(2,1)S(1)}, u32[]{:S(2)}, u32[]{:S(2)}) collective-permute-start(bf16[256,512]{1,0:T(8,128)(2,1)S(1)} %get-tuple-element.225), channel_id=1, source_target_pairs={{0,4},{4,0},{8,12},{12,8},{16,20},{20,16},{24,28},{28,24},{1,5},{5... | collective-permute-start | bytes 786440 | tf_op jit(solution)/shard_map/ppermute | solution.py:708
  190.3 31.8 %collective-permute-start.77 = (bf16[256,512]{1,0:T(8,128)(2,1)S(1)}, bf16[256,512]{1,0:T(8,128)(2,1)S(1)}, u32[]{:S(2)}, u32[]{:S(2)}) collective-permute-start(bf16[256,512]{1,0:T(8,128)(2,1)S(1)} %get-tuple-element.227), channel_id=1, source_target_pairs={{0,4},{4,0},{8,12},{12,8},{16,20},{20,16},{24,28},{28,24},{1,5},{5... | collective-permute-start | bytes 786440 | tf_op jit(solution)/shard_map/ppermute | solution.py:708
  190.4 35.1 %collective-permute-start.64 = (bf16[8,16,1024]{2,1,0:T(8,128)(2,1)}, bf16[8,16,1024]{2,1,0:T(8,128)(2,1)S(1)}, u32[]{:S(2)}, u32[]{:S(2)}) collective-permute-start(bf16[8,16,1024]{2,1,0:T(8,128)(2,1)} %get-tuple-element.331), channel_id=1, source_target_pairs={{0,2},{1,3},{2,0},{3,1},{4,6},{5,7},{6,4},{7,5},{8,10},{9,11},{10,... | collective-permute-start | bytes 786440 | tf_op jit(solution)/shard_map/ppermute | solution.py:708
  191.9 34.8 %collective-permute-start.42 = (bf16[256,128]{1,0:T(8,128)(2,1)}, bf16[256,128]{1,0:T(8,128)(2,1)S(1)}, u32[]{:S(2)}, u32[]{:S(2)}) collective-permute-start(bf16[256,128]{1,0:T(8,128)(2,1)} %get-tuple-element.194), channel_id=1, source_target_pairs={{0,4},{4,0},{8,12},{12,8},{16,20},{20,16},{24,28},{28,24},{1,5},{5... | collective-permute-start | bytes 196616 | tf_op jit(solution)/shard_map/ppermute | solution.py:708
  192.0 36.2 %collective-permute-start.43 = (bf16[256,128]{1,0:T(8,128)(2,1)}, bf16[256,128]{1,0:T(8,128)(2,1)S(1)}, u32[]{:S(2)}, u32[]{:S(2)}) collective-permute-start(bf16[256,128]{1,0:T(8,128)(2,1)} %get-tuple-element.195), channel_id=1, source_target_pairs={{0,8},{4,12},{8,0},{12,4},{16,24},{20,28},{24,16},{28,20},{1,9},{5... | collective-permute-start | bytes 196616 | tf_op jit(solution)/shard_map/ppermute | solution.py:708
  232.7 57.3 %collective-permute-start.30 = (bf16[256,128]{1,0:T(8,128)(2,1)}, bf16[256,128]{1,0:T(8,128)(2,1)S(1)}, u32[]{:S(2)}, u32[]{:S(2)}) collective-permute-start(bf16[256,128]{1,0:T(8,128)(2,1)} %get-tuple-element.176), channel_id=1, source_target_pairs={{0,12},{4,8},{8,4},{12,0},{16,28},{20,24},{24,20},{28,16},{1,13},{... | collective-permute-start | bytes 196616 | tf_op jit(solution)/shard_map/ppermute | solution.py:708
  235.4 54.8 %collective-permute-start.31 = (bf16[256,128]{1,0:T(8,128)(2,1)}, bf16[256,128]{1,0:T(8,128)(2,1)S(1)}, u32[]{:S(2)}, u32[]{:S(2)}) collective-permute-start(bf16[256,128]{1,0:T(8,128)(2,1)} %get-tuple-element.177), channel_id=1, source_target_pairs={{0,16},{4,20},{8,24},{12,28},{16,0},{20,4},{24,8},{28,12},{1,17},{... | collective-permute-start | bytes 196616 | tf_op jit(solution)/shard_map/ppermute | solution.py:708
  239.8 50.9 %collective-permute-start.32 = (bf16[256,128]{1,0:T(8,128)(2,1)}, bf16[256,128]{1,0:T(8,128)(2,1)S(1)}, u32[]{:S(2)}, u32[]{:S(2)}) collective-permute-start(bf16[256,128]{1,0:T(8,128)(2,1)} %get-tuple-element.178), channel_id=1, source_target_pairs={{0,20},{4,16},{8,28},{12,24},{16,4},{20,0},{24,12},{28,8},{1,21},{... | collective-permute-start | bytes 196616 | tf_op jit(solution)/shard_map/ppermute | solution.py:708
  239.8 50.9 %collective-permute-start.33 = (bf16[256,128]{1,0:T(8,128)(2,1)}, bf16[256,128]{1,0:T(8,128)(2,1)S(1)}, u32[]{:S(2)}, u32[]{:S(2)}) collective-permute-start(bf16[256,128]{1,0:T(8,128)(2,1)} %get-tuple-element.179), channel_id=1, source_target_pairs={{0,24},{4,28},{8,16},{12,20},{16,8},{20,12},{24,0},{28,4},{1,25},{... | collective-permute-start | bytes 196616 | tf_op jit(solution)/shard_map/ppermute | solution.py:708
  241.9 50.3 %collective-permute-start.34 = (bf16[256,128]{1,0:T(8,128)(2,1)}, bf16[256,128]{1,0:T(8,128)(2,1)S(1)}, u32[]{:S(2)}, u32[]{:S(2)}) collective-permute-start(bf16[256,128]{1,0:T(8,128)(2,1)} %get-tuple-element.180), channel_id=1, source_target_pairs={{0,28},{4,24},{8,20},{12,16},{16,12},{20,8},{24,4},{28,0},{1,29},{... | collective-permute-start | bytes 196616 | tf_op jit(solution)/shard_map/ppermute | solution.py:708
  290.0 28.5 %collective-permute-start.63 = (bf16[8,16,1024]{2,1,0:T(8,128)(2,1)}, bf16[8,16,1024]{2,1,0:T(8,128)(2,1)S(1)}, u32[]{:S(2)}, u32[]{:S(2)}) collective-permute-start(bf16[8,16,1024]{2,1,0:T(8,128)(2,1)} %get-tuple-element.331), channel_id=1, source_target_pairs={{0,1},{1,0},{2,3},{3,2},{4,5},{5,4},{6,7},{7,6},{8,9},{9,8},{10,11... | collective-permute-start | bytes 786440 | tf_op jit(solution)/shard_map/ppermute | solution.py:708
  290.1 30.2 %collective-permute-start.49 = (bf16[3,256,128]{2,1,0:T(8,128)(2,1)S(1)}, bf16[3,256,128]{2,1,0:T(8,128)(2,1)S(1)}, u32[]{:S(2)}, u32[]{:S(2)}) collective-permute-start(bf16[3,256,128]{2,1,0:T(8,128)(2,1)S(1)} %get-tuple-element.204), channel_id=1, source_target_pairs={{0,4},{4,0},{8,12},{12,8},{16,20},{20,16},{24,28},{28,24},{1,5},{5... | collective-permute-start | bytes 589832 | tf_op jit(solution)/shard_map/ppermute | solution.py:708
  290.7 31.7 %collective-permute-start.50 = (bf16[3,256,128]{2,1,0:T(8,128)(2,1)S(1)}, bf16[3,256,128]{2,1,0:T(8,128)(2,1)S(1)}, u32[]{:S(2)}, u32[]{:S(2)}) collective-permute-start(bf16[3,256,128]{2,1,0:T(8,128)(2,1)S(1)} %get-tuple-element.205), channel_id=1, source_target_pairs={{0,8},{4,12},{8,0},{12,4},{16,24},{20,28},{24,16},{28,20},{1,9},{5... | collective-permute-start | bytes 589832 | tf_op jit(solution)/shard_map/ppermute | solution.py:708
  290.7 32.8 %collective-permute-start.51 = (bf16[3,256,128]{2,1,0:T(8,128)(2,1)S(1)}, bf16[3,256,128]{2,1,0:T(8,128)(2,1)S(1)}, u32[]{:S(2)}, u32[]{:S(2)}) collective-permute-start(bf16[3,256,128]{2,1,0:T(8,128)(2,1)S(1)} %get-tuple-element.206), channel_id=1, source_target_pairs={{0,12},{4,8},{8,4},{12,0},{16,28},{20,24},{24,20},{28,16},{1,13},{... | collective-permute-start | bytes 589832 | tf_op jit(solution)/shard_map/ppermute | solution.py:708
  292.1 32.1 %collective-permute-start.52 = (bf16[3,256,128]{2,1,0:T(8,128)(2,1)S(1)}, bf16[3,256,128]{2,1,0:T(8,128)(2,1)S(1)}, u32[]{:S(2)}, u32[]{:S(2)}) collective-permute-start(bf16[3,256,128]{2,1,0:T(8,128)(2,1)S(1)} %get-tuple-element.207), channel_id=1, source_target_pairs={{0,16},{4,20},{8,24},{12,28},{16,0},{20,4},{24,8},{28,12},{1,17},{... | collective-permute-start | bytes 589832 | tf_op jit(solution)/shard_map/ppermute | solution.py:708
  323.5 29.1 %collective-permute-start.35 = (bf16[3,256,128]{2,1,0:T(8,128)(2,1)S(1)}, bf16[3,256,128]{2,1,0:T(8,128)(2,1)S(1)}, u32[]{:S(2)}, u32[]{:S(2)}) collective-permute-start(bf16[3,256,128]{2,1,0:T(8,128)(2,1)S(1)} %get-tuple-element.184), channel_id=1, source_target_pairs={{0,4},{4,0},{8,12},{12,8},{16,20},{20,16},{24,28},{28,24},{1,5},{5... | collective-permute-start | bytes 589832 | tf_op jit(solution)/shard_map/ppermute | solution.py:708
  324.3 30.4 %collective-permute-start.36 = (bf16[3,256,128]{2,1,0:T(8,128)(2,1)S(1)}, bf16[3,256,128]{2,1,0:T(8,128)(2,1)S(1)}, u32[]{:S(2)}, u32[]{:S(2)}) collective-permute-start(bf16[3,256,128]{2,1,0:T(8,128)(2,1)S(1)} %get-tuple-element.185), channel_id=1, source_target_pairs={{0,8},{4,12},{8,0},{12,4},{16,24},{20,28},{24,16},{28,20},{1,9},{5... | collective-permute-start | bytes 589832 | tf_op jit(solution)/shard_map/ppermute | solution.py:708
  339.4 24.9 %collective-permute-start.37 = (bf16[3,256,128]{2,1,0:T(8,128)(2,1)S(1)}, bf16[3,256,128]{2,1,0:T(8,128)(2,1)S(1)}, u32[]{:S(2)}, u32[]{:S(2)}) collective-permute-start(bf16[3,256,128]{2,1,0:T(8,128)(2,1)S(1)} %get-tuple-element.186), channel_id=1, source_target_pairs={{0,12},{4,8},{8,4},{12,0},{16,28},{20,24},{24,20},{28,16},{1,13},{... | collective-permute-start | bytes 589832 | tf_op jit(solution)/shard_map/ppermute | solution.py:708
  339.4 32.0 %collective-permute-start.38 = (bf16[3,256,128]{2,1,0:T(8,128)(2,1)S(1)}, bf16[3,256,128]{2,1,0:T(8,128)(2,1)S(1)}, u32[]{:S(2)}, u32[]{:S(2)}) collective-permute-start(bf16[3,256,128]{2,1,0:T(8,128)(2,1)S(1)} %get-tuple-element.187), channel_id=1, source_target_pairs={{0,16},{4,20},{8,24},{12,28},{16,0},{20,4},{24,8},{28,12},{1,17},{... | collective-permute-start | bytes 589832 | tf_op jit(solution)/shard_map/ppermute | solution.py:708
  344.5 28.6 %collective-permute-start.39 = (bf16[3,256,128]{2,1,0:T(8,128)(2,1)S(1)}, bf16[3,256,128]{2,1,0:T(8,128)(2,1)S(1)}, u32[]{:S(2)}, u32[]{:S(2)}) collective-permute-start(bf16[3,256,128]{2,1,0:T(8,128)(2,1)S(1)} %get-tuple-element.188), channel_id=1, source_target_pairs={{0,20},{4,16},{8,28},{12,24},{16,4},{20,0},{24,12},{28,8},{1,21},{... | collective-permute-start | bytes 589832 | tf_op jit(solution)/shard_map/ppermute | solution.py:708
  396.1 27.3 %collective-permute-start.96 = (bf16[256,4096]{1,0:T(8,128)(2,1)}, bf16[256,4096]{1,0:T(8,128)(2,1)}, u32[]{:S(2)}, u32[]{:S(2)}) collective-permute-start(bf16[256,4096]{1,0:T(8,128)(2,1)} %get-tuple-element.243.refs_6_), channel_id=1, source_target_pairs={{0,4},{4,0},{8,12},{12,8},{16,20},{20,16},{24,28},{28,24},{1,5},{5... | collective-permute-start | bytes 6291464 | tf_op jit(solution)/shard_map/ppermute | solution.py:708
  396.6 27.0 %collective-permute-start.95 = (bf16[256,4096]{1,0:T(8,128)(2,1)}, bf16[256,4096]{1,0:T(8,128)(2,1)}, u32[]{:S(2)}, u32[]{:S(2)}) collective-permute-start(bf16[256,4096]{1,0:T(8,128)(2,1)} %get-tuple-element.242.refs_4_), channel_id=1, source_target_pairs={{0,4},{4,0},{8,12},{12,8},{16,20},{20,16},{24,28},{28,24},{1,5},{5... | collective-permute-start | bytes 6291464 | tf_op jit(solution)/shard_map/ppermute | solution.py:708
  422.5 44.1 %collective-permute-start.83 = (bf16[256,1024]{1,0:T(8,128)(2,1)}, bf16[256,1024]{1,0:T(8,128)(2,1)S(1)}, u32[]{:S(2)}, u32[]{:S(2)}) collective-permute-start(bf16[256,1024]{1,0:T(8,128)(2,1)} %copy-done.24), channel_id=1, source_target_pairs={{0,4},{4,0},{8,12},{12,8},{16,20},{20,16},{24,28},{28,24},{1,5},{5... | collective-permute-start | bytes 1572872 | tf_op jit(solution)/shard_map/ppermute | solution.py:708
  422.9 44.4 %collective-permute-start.78 = (bf16[256,1024]{1,0:T(8,128)(2,1)}, bf16[256,1024]{1,0:T(8,128)(2,1)S(1)}, u32[]{:S(2)}, u32[]{:S(2)}) collective-permute-start(bf16[256,1024]{1,0:T(8,128)(2,1)} %copy-done.25), channel_id=1, source_target_pairs={{0,4},{4,0},{8,12},{12,8},{16,20},{20,16},{24,28},{28,24},{1,5},{5... | collective-permute-start | bytes 1572872 | tf_op jit(solution)/shard_map/ppermute | solution.py:708
  423.0 48.6 %collective-permute-start.80 = (bf16[256,1024]{1,0:T(8,128)(2,1)}, bf16[256,1024]{1,0:T(8,128)(2,1)S(1)}, u32[]{:S(2)}, u32[]{:S(2)}) collective-permute-start(bf16[256,1024]{1,0:T(8,128)(2,1)} %copy-done.27), channel_id=1, source_target_pairs={{0,4},{4,0},{8,12},{12,8},{16,20},{20,16},{24,28},{28,24},{1,5},{5... | collective-permute-start | bytes 1572872 | tf_op jit(solution)/shard_map/ppermute | solution.py:708
  423.4 49.2 %collective-permute-start.82 = (bf16[256,1024]{1,0:T(8,128)(2,1)}, bf16[256,1024]{1,0:T(8,128)(2,1)S(1)}, u32[]{:S(2)}, u32[]{:S(2)}) collective-permute-start(bf16[256,1024]{1,0:T(8,128)(2,1)} %copy-done.29), channel_id=1, source_target_pairs={{0,4},{4,0},{8,12},{12,8},{16,20},{20,16},{24,28},{28,24},{1,5},{5... | collective-permute-start | bytes 1572872 | tf_op jit(solution)/shard_map/ppermute | solution.py:708
  423.5 52.6 %collective-permute-start.73 = (bf16[8,32,1024]{2,1,0:T(8,128)(2,1)S(1)}, bf16[8,32,1024]{2,1,0:T(8,128)(2,1)S(1)}, u32[]{:S(2)}, u32[]{:S(2)}) collective-permute-start(bf16[8,32,1024]{2,1,0:T(8,128)(2,1)S(1)} %get-tuple-element.313), channel_id=1, source_target_pairs={{0,1},{1,0},{2,3},{3,2},{4,5},{5,4},{6,7},{7,6},{8,9},{9,8},{10,11... | collective-permute-start | bytes 1572872 | tf_op jit(solution)/shard_map/ppermute | solution.py:708
  466.6 147.7 %collective-permute-start.105 = (bf16[4,1152,256]{2,1,0:T(8,128)(2,1)}, bf16[4,1152,256]{2,1,0:T(8,128)(2,1)}, u32[]{:S(2)}, u32[]{:S(2)}) collective-permute-start(bf16[4,1152,256]{2,1,0:T(8,128)(2,1)} %get-tuple-element.257), channel_id=1, source_target_pairs={{0,1},{1,0},{2,3},{3,2},{4,5},{5,4},{6,7},{7,6},{8,9},{9,8},{10,11... | collective-permute-start | bytes 7077896 | tf_op jit(solution)/shard_map/ppermute | solution.py:708
  467.3 147.5 %collective-permute-start.106 = (bf16[4,1152,256]{2,1,0:T(8,128)(2,1)}, bf16[4,1152,256]{2,1,0:T(8,128)(2,1)}, u32[]{:S(2)}, u32[]{:S(2)}) collective-permute-start(bf16[4,1152,256]{2,1,0:T(8,128)(2,1)} %get-tuple-element.258), channel_id=1, source_target_pairs={{0,2},{1,3},{2,0},{3,1},{4,6},{5,7},{6,4},{7,5},{8,10},{9,11},{10,... | collective-permute-start | bytes 7077896 | tf_op jit(solution)/shard_map/ppermute | solution.py:708
  471.6 143.2 %collective-permute-start.107 = (bf16[4,1152,256]{2,1,0:T(8,128)(2,1)}, bf16[4,1152,256]{2,1,0:T(8,128)(2,1)}, u32[]{:S(2)}, u32[]{:S(2)}) collective-permute-start(bf16[4,1152,256]{2,1,0:T(8,128)(2,1)} %get-tuple-element.259), channel_id=1, source_target_pairs={{0,3},{1,2},{2,1},{3,0},{4,7},{5,6},{6,5},{7,4},{8,11},{9,10},{10,... | collective-permute-start | bytes 7077896 | tf_op jit(solution)/shard_map/ppermute | solution.py:708
  472.6 123.5 %collective-permute-start.74 = (bf16[8,32,1024]{2,1,0:T(8,128)(2,1)S(1)}, bf16[8,32,1024]{2,1,0:T(8,128)(2,1)S(1)}, u32[]{:S(2)}, u32[]{:S(2)}) collective-permute-start(bf16[8,32,1024]{2,1,0:T(8,128)(2,1)S(1)} %get-tuple-element.313), channel_id=1, source_target_pairs={{0,2},{1,3},{2,0},{3,1},{4,6},{5,7},{6,4},{7,5},{8,10},{9,11},{10,... | collective-permute-start | bytes 1572872 | tf_op jit(solution)/shard_map/ppermute | solution.py:708
  476.2 121.3 %collective-permute-start.75 = (bf16[8,32,1024]{2,1,0:T(8,128)(2,1)S(1)}, bf16[8,32,1024]{2,1,0:T(8,128)(2,1)S(1)}, u32[]{:S(2)}, u32[]{:S(2)}) collective-permute-start(bf16[8,32,1024]{2,1,0:T(8,128)(2,1)S(1)} %get-tuple-element.313), channel_id=1, source_target_pairs={{0,3},{1,2},{2,1},{3,0},{4,7},{5,6},{6,5},{7,4},{8,11},{9,10},{10,... | collective-permute-start | bytes 1572872 | tf_op jit(solution)/shard_map/ppermute | solution.py:708
  597.5 34.6 %collective-permute-start.85 = (bf16[4,384,256]{2,1,0:T(8,128)(2,1)}, bf16[4,384,256]{2,1,0:T(8,128)(2,1)}, u32[]{:S(2)}, u32[]{:S(2)}) collective-permute-start(bf16[4,384,256]{2,1,0:T(8,128)(2,1)} %get-tuple-element.236), channel_id=1, source_target_pairs={{0,2},{1,3},{2,0},{3,1},{4,6},{5,7},{6,4},{7,5},{8,10},{9,11},{10,... | collective-permute-start | bytes 2359304 | tf_op jit(solution)/shard_map/ppermute | solution.py:708
  618.3 27.3 %collective-permute-start.108 = (bf16[1152,256]{1,0:T(8,128)(2,1)S(1)}, bf16[1152,256]{1,0:T(8,128)(2,1)S(1)}, u32[]{:S(2)}, u32[]{:S(2)}) collective-permute-start(bf16[1152,256]{1,0:T(8,128)(2,1)S(1)} %get-tuple-element.293), channel_id=1, source_target_pairs={{0,8},{4,12},{8,0},{12,4},{16,24},{20,28},{24,16},{28,20},{1,9},{5... | collective-permute-start | bytes 1769480 | tf_op jit(solution)/shard_map/ppermute | solution.py:708
  618.4 28.6 %collective-permute-start.110 = (bf16[1152,256]{1,0:T(8,128)(2,1)S(1)}, bf16[1152,256]{1,0:T(8,128)(2,1)S(1)}, u32[]{:S(2)}, u32[]{:S(2)}) collective-permute-start(bf16[1152,256]{1,0:T(8,128)(2,1)S(1)} %get-tuple-element.294), channel_id=1, source_target_pairs={{0,24},{4,28},{8,16},{12,20},{16,8},{20,12},{24,0},{28,4},{1,25},{... | collective-permute-start | bytes 1769480 | tf_op jit(solution)/shard_map/ppermute | solution.py:708
  620.0 62.4 %collective-permute-start.109 = (bf16[1152,256]{1,0:T(8,128)(2,1)S(1)}, bf16[1152,256]{1,0:T(8,128)(2,1)S(1)}, u32[]{:S(2)}, u32[]{:S(2)}) collective-permute-start(bf16[1152,256]{1,0:T(8,128)(2,1)S(1)} %get-tuple-element.295), channel_id=1, source_target_pairs={{0,16},{4,20},{8,24},{12,28},{16,0},{20,4},{24,8},{28,12},{1,17},{... | collective-permute-start | bytes 1769480 | tf_op jit(solution)/shard_map/ppermute | solution.py:708
  634.5 52.8 %collective-permute-start.87 = (bf16[384,256]{1,0:T(8,128)(2,1)S(1)}, bf16[384,256]{1,0:T(8,128)(2,1)S(1)}, u32[]{:S(2)}, u32[]{:S(2)}) collective-permute-start(bf16[384,256]{1,0:T(8,128)(2,1)S(1)} %get-tuple-element.296), channel_id=1, source_target_pairs={{0,8},{4,12},{8,0},{12,4},{16,24},{20,28},{24,16},{28,20},{1,9},{5... | collective-permute-start | bytes 589832 | tf_op jit(solution)/shard_map/ppermute | solution.py:708
  634.5 53.4 %collective-permute-start.89 = (bf16[384,256]{1,0:T(8,128)(2,1)S(1)}, bf16[384,256]{1,0:T(8,128)(2,1)S(1)}, u32[]{:S(2)}, u32[]{:S(2)}) collective-permute-start(bf16[384,256]{1,0:T(8,128)(2,1)S(1)} %get-tuple-element.297), channel_id=1, source_target_pairs={{0,24},{4,28},{8,16},{12,20},{16,8},{20,12},{24,0},{28,4},{1,25},{... | collective-permute-start | bytes 589832 | tf_op jit(solution)/shard_map/ppermute | solution.py:708
  645.6 42.4 %collective-permute-start.88 = (bf16[384,256]{1,0:T(8,128)(2,1)S(1)}, bf16[384,256]{1,0:T(8,128)(2,1)S(1)}, u32[]{:S(2)}, u32[]{:S(2)}) collective-permute-start(bf16[384,256]{1,0:T(8,128)(2,1)S(1)} %get-tuple-element.298), channel_id=1, source_target_pairs={{0,16},{4,20},{8,24},{12,28},{16,0},{20,4},{24,8},{28,12},{1,17},{... | collective-permute-start | bytes 589832 | tf_op jit(solution)/shard_map/ppermute | solution.py:708
  684.4 37.3 %collective-permute-start.113 = (bf16[1152,256]{1,0:T(8,128)(2,1)S(1)}, bf16[1152,256]{1,0:T(8,128)(2,1)S(1)}, u32[]{:S(2)}, u32[]{:S(2)}) collective-permute-start(bf16[1152,256]{1,0:T(8,128)(2,1)S(1)} %fusion.2.refs_0_), channel_id=1, source_target_pairs={{0,3},{1,2},{2,1},{3,0},{4,7},{5,6},{6,5},{7,4},{8,11},{9,10},{10,... | collective-permute-start | bytes 1769480 | tf_op jit(solution)/shard_map/ppermute | solution.py:708
  687.0 34.7 %collective-permute-start.112 = (bf16[1152,256]{1,0:T(8,128)(2,1)S(1)}, bf16[1152,256]{1,0:T(8,128)(2,1)S(1)}, u32[]{:S(2)}, u32[]{:S(2)}) collective-permute-start(bf16[1152,256]{1,0:T(8,128)(2,1)S(1)} %fusion.2.refs_0_), channel_id=1, source_target_pairs={{0,2},{1,3},{2,0},{3,1},{4,6},{5,7},{6,4},{7,5},{8,10},{9,11},{10,... | collective-permute-start | bytes 1769480 | tf_op jit(solution)/shard_map/ppermute | solution.py:708
  687.3 34.4 %collective-permute-start.111 = (bf16[1152,256]{1,0:T(8,128)(2,1)S(1)}, bf16[1152,256]{1,0:T(8,128)(2,1)S(1)}, u32[]{:S(2)}, u32[]{:S(2)}) collective-permute-start(bf16[1152,256]{1,0:T(8,128)(2,1)S(1)} %fusion.2.refs_0_), channel_id=1, source_target_pairs={{0,1},{1,0},{2,3},{3,2},{4,5},{5,4},{6,7},{7,6},{8,9},{9,8},{10,11... | collective-permute-start | bytes 1769480 | tf_op jit(solution)/shard_map/ppermute | solution.py:708
  689.2 25.1 %collective-permute-start.92 = (bf16[384,256]{1,0:T(8,128)(2,1)S(1)}, bf16[384,256]{1,0:T(8,128)(2,1)S(1)}, u32[]{:S(2)}, u32[]{:S(2)}) collective-permute-start(bf16[384,256]{1,0:T(8,128)(2,1)S(1)} %fusion.9.refs_0_), channel_id=1, source_target_pairs={{0,3},{1,2},{2,1},{3,0},{4,7},{5,6},{6,5},{7,4},{8,11},{9,10},{10,... | collective-permute-start | bytes 589832 | tf_op jit(solution)/shard_map/ppermute | solution.py:708
  (165 other events, 2161.4 us)

commit v2 on v1

v2 whole, which is shorter than its diff:
```python
import functools

import jax
import jax.numpy as jnp
from jax import lax
from jax.experimental import pallas as pl
from jax.experimental.pallas import tpu as pltpu
from jax.sharding import PartitionSpec as P

HEADS = 16
EPS = 1e-06
HIGHEST_PRECISION = lax.Precision.HIGHEST
F32 = jnp.float32
BF16 = jnp.bfloat16
ANY = pl.BlockSpec(memory_space=pl.ANY)
VMEM = pl.BlockSpec(memory_space=pltpu.VMEM)
SMEM = pl.BlockSpec(memory_space=pltpu.SMEM)
LANES = 128
BLOCK = 256
FF_BLOCK = 512
GELU_A = 0.7978845608028654
GELU_B = 0.044715


def shaped(shape, dtype):
    return jax.ShapeDtypeStruct(shape, dtype)


def params(mib):
    return pltpu.CompilerParams(vmem_limit_bytes=mib << 20)


def cost(flops, moved, transcendentals=0):
    return pl.CostEstimate(
        flops=int(flops), bytes_accessed=int(moved), transcendentals=int(transcendentals)
    )


def dot_nn(left, right):
    return lax.dot_general(left, right, (((1,), (0,)), ((), ())), preferred_element_type=F32)


def dot_nt(left, right):
    return lax.dot_general(left, right, (((1,), (1,)), ((), ())), preferred_element_type=F32)


def dot_tn(left, right):
    return lax.dot_general(left, right, (((0,), (0,)), ((), ())), preferred_element_type=F32)


def split_heads(values, pairs, head):
    if pairs == 1:
        return [values]
    lane = lax.broadcasted_iota(jnp.int32, values.shape, 1)
    return [jnp.where(lane // head == h, values, jnp.zeros_like(values)) for h in range(pairs)]


def swap_halves(values, head):
    half = head // 2
    lane = lax.broadcasted_iota(jnp.int32, values.shape, 1)
    ahead = pltpu.roll(values, values.shape[1] - half, 1)
    behind = pltpu.roll(values, half, 1)
    return jnp.where(lax.rem(lane, head) < half, ahead, behind)


def turn(values, cosine, signed_sine, head, back):
    parts = []
    for at in range(0, values.shape[1], LANES):
        piece = values[:, at : at + LANES]
        other = swap_halves(piece, head) * signed_sine
        parts.append(piece * cosine - other if back else piece * cosine + other)
    return jnp.concatenate(parts, axis=1)


def norm_parts(values):
    center = jnp.mean(values, axis=-1, keepdims=True)
    offset = values - center
    spread = jnp.mean(offset * offset, axis=-1, keepdims=True)
    inverse = lax.rsqrt(spread + EPS)
    return offset * inverse, inverse


def norm_pull(grad, hat, inverse, scale_row):
    grad_shift = jnp.sum(grad, axis=0, keepdims=True)
    grad_scale = jnp.sum(grad * hat, axis=0, keepdims=True)
    inner = grad * (1.0 + scale_row)
    mean_one = jnp.mean(inner, axis=-1, keepdims=True)
    mean_two = jnp.mean(inner * hat, axis=-1, keepdims=True)
    return inverse * (inner - mean_one - hat * mean_two), grad_shift, grad_scale


def store_by_parity(own_ref, other_ref, where, parity, block_index, value):
    own = parity == block_index % 2

    @pl.when(own)
    def _():
        own_ref[:, where] = value

    @pl.when(jnp.logical_not(own))
    def _():
        other_ref[:, where] = value


def half_columns(weight, groups, parity):
    rows, total = weight.shape
    view = weight.reshape(rows, 3, groups // 2, 2, total // (3 * groups))
    return lax.dynamic_index_in_dim(view, parity, 3, keepdims=False).reshape(rows, total // 2)


def half_specs(height, width, groups, aligned):
    specs = []
    for kind in range(3):
        for block in range(width // (2 * LANES)):
            if aligned:
                specs.append(
                    pl.BlockSpec(
                        (height, LANES), lambda t, m, k=kind, b=block: (0, k * groups + 2 * b + m[0] % 2)
                    )
                )
            else:
                specs.append(
                    pl.BlockSpec(
                        (height, LANES),
                        lambda t, m, k=kind, b=block: (0, k * (width // (2 * LANES)) + b),
                    )
                )
    return specs


def qkv_kernel(zs, head, clip, meta, tokens, other_tokens, mod, cosine, sine, *refs):
    blocks = tokens.shape[-1] // (2 * LANES)
    weights, biases = refs[: 3 * blocks], refs[3 * blocks : 6 * blocks]
    outs, normed_outs, (normed, held) = refs[6 * blocks : 6 * blocks + zs], refs[-4:-2], refs[-2:]
    rows, width = tokens.shape[-2:]
    lanes = width // (2 * zs)
    clips = mod.shape[0] // 2
    z = meta[0] // 2
    for role, source in enumerate((tokens, other_tokens)):
        row = role * clips + clip
        hat, _ = norm_parts(source[...].reshape(rows, width).astype(F32))
        low = (hat * (1.0 + mod[row, 1:2]) + mod[row, 0:1]).astype(BF16)
        normed[role * rows : (role + 1) * rows] = low
        normed_outs[role][...] = low
    for kind in range(3):
        pick = slice(kind * blocks, (kind + 1) * blocks)
        weight = jnp.concatenate([w[...] for w in weights[pick]], axis=1)
        bias = jnp.concatenate([b[...] for b in biases[pick]], axis=1).astype(F32)
        for role in range(2):
            row = role * clips + clip
            value = dot_nn(normed[role * rows : (role + 1) * rows], weight) + bias
            if kind < 2:
                value = turn(value, cosine[row], sine[row], head, False)
            value = value.astype(BF16)
            if kind == 0:
                value = value * jnp.asarray(head**-0.5, BF16)
            for group in range(zs):
                held[group ^ z, role, kind] = value[:, group * lanes : (group + 1) * lanes]
    for slot in range(zs):
        outs[slot][...] = held[slot]


def qkv_call(meta, clip, tokens, other_tokens, mod, cosine, sine, weight, bias, zs, head, aligned):
    rows, width = tokens.shape[-2:]
    lanes = width // (2 * zs)
    whole = lambda a: pl.BlockSpec(a.shape, lambda t, m: (0,) * a.ndim)
    blocks = width // (2 * LANES)
    flat = pl.BlockSpec((rows, width), lambda t, m: (0, 0))
    return pl.pallas_call(
        functools.partial(qkv_kernel, zs, head, clip),
        out_shape=[shaped((2, 3, rows, lanes), BF16)] * zs + [shaped((rows, width), BF16)] * 2,
        grid_spec=pltpu.PrefetchScalarGridSpec(
            num_scalar_prefetch=1,
            grid=(1,),
            in_specs=[
                pl.BlockSpec((1, 1, rows, width), lambda t, m: (clip, 0, 0, 0)),
                pl.BlockSpec((1, 1, rows, width), lambda t, m: (clip, 0, 0, 0)),
                whole(mod),
                whole(cosine),
                whole(sine),
            ]
            + half_specs(width, width, 2 * zs, aligned)
            + half_specs(1, width, 2 * zs, aligned),
            out_specs=[pl.BlockSpec((2, 3, rows, lanes), lambda t, m: (0, 0, 0, 0))] * zs
            + [flat, flat],
            scratch_shapes=[
                pltpu.VMEM((2 * rows, width), BF16),
                pltpu.VMEM((zs, 2, 3, rows, lanes), BF16),
            ],
        ),
        compiler_params=params(48),
        cost_estimate=cost(6 * rows * width * width, 3 * width * width + 16 * rows * width),
        name="norm_qkv",
    )(meta, tokens, other_tokens, mod, cosine, sine, *[weight] * (3 * blocks), *[bias] * (3 * blocks))


def attend_kernel(slots, head, meta, *refs):
    zs = slots // 2
    parts, outs = refs[:zs], refs[zs:slots]
    exact, logs, held, scores, values, sems = refs[slots:]
    copies = [
        pltpu.make_async_copy(parts[k], held.at[pl.ds(2 * k, 2)], sems.at[k]) for k in range(zs)
    ]
    for copy in copies:
        copy.start()
    for copy in copies:
        copy.wait()
    me, context = meta[0], meta[1]
    rows, width = held.shape[2], held.shape[3]
    pairs = width // head

    def prepare(frame, _):
        split = split_heads(held[frame ^ me, 2], pairs, head)
        ones = split_heads(jnp.ones((rows, width), BF16), pairs, head)
        for h in range(pairs):
            values[frame, h] = jnp.concatenate([split[h], ones[h]], axis=1)
        return 0

    lax.fori_loop(0, slots, prepare, 0)

    def attend(slot, count):
        queries = split_heads(held[slot, 0], pairs, head)
        total, tops = None, []
        for h in range(pairs):
            peak = None
            for frame in range(count):
                score = dot_nt(queries[h], held[frame ^ me, 1])
                scores[frame, h * rows : (h + 1) * rows] = score
                for at in range(0, rows, LANES):
                    piece = score[:, at : at + LANES]
                    peak = piece if peak is None else jnp.maximum(peak, piece)
            top = jnp.max(peak, axis=1, keepdims=True)
            tops.append(top)
            for frame in range(count):
                power = jnp.exp(scores[frame, h * rows : (h + 1) * rows] - top).astype(BF16)
                term = dot_nn(power, values[frame, h])
                total = term if total is None else total + term
        weight_sum = total[:, width:]
        result = total[:, :width] / weight_sum
        exact[slot] = result
        top = jnp.broadcast_to(tops[0], (rows, width))
        if pairs > 1:
            lane = lax.broadcasted_iota(jnp.int32, (rows, width), 1)
            for h in range(1, pairs):
                top = jnp.where(lane // head >= h, tops[h], top)
        turned = (top + jnp.log(weight_sum)).T
        logs[slot] = jnp.concatenate(
            [turned[h * head : h * head + 1] for h in range(pairs)], axis=1
        )

    def one_frame(frame, _):
        count = jnp.maximum(frame, context - 1) + 1
        for known in range(1, slots + 1):

            @pl.when(count == known)
            def _():
                attend(frame ^ me, known)

        return 0

    lax.fori_loop(0, slots, one_frame, 0)
    for slot in range(slots):
        outs[slot // 2][slot % 2] = exact[slot].astype(BF16)


def attend_call(meta, parts, head):
    zs = len(parts)
    slots = 2 * zs
    rows, width = parts[0].shape[-2:]
    pairs = width // head
    work = slots * slots * rows * rows
    return pl.pallas_call(
        functools.partial(attend_kernel, slots, head),
        out_shape=[shaped((2, rows, width), BF16)] * zs
        + [shaped((slots, rows, width), F32), shaped((slots, 1, pairs * rows), F32)],
        in_specs=[SMEM] + [ANY] * zs,
        out_specs=[VMEM] * (zs + 2),
        scratch_shapes=[
            pltpu.VMEM((slots, 3, rows, width), BF16),
            pltpu.VMEM((slots, pairs * rows, rows), F32),
            pltpu.VMEM((slots, pairs, rows, 2 * width), BF16),
            pltpu.SemaphoreType.DMA((zs,)),
        ],
        compiler_params=params(40),
        cost_estimate=cost(work * 16 * width, slots * rows * width * 12, work * pairs),
        name="attend",
    )(meta, *parts)


def attend_grad_kernel(slots, head, meta, *refs):
    zs = slots // 2
    parts, grads = refs[:zs], refs[zs:slots]
    exact, logs = refs[slots], refs[slots + 1]
    outs = refs[slots + 2 : slots + 2 + zs]
    held, grad, query_rows, grad_rows, delta, grad_q, grad_k, grad_v, sems, more = refs[
        slots + 2 + zs :
    ]
    copies = []
    for k in range(zs):
        pair = pl.ds(2 * k, 2)
        copies.append(pltpu.make_async_copy(parts[k], held.at[pair], sems.at[k]))
        copies.append(pltpu.make_async_copy(grads[k], grad.at[pair], more.at[k]))
    for copy in copies:
        copy.start()
    for copy in copies:
        copy.wait()
    me, context = meta[0], meta[1]
    rows, width = held.shape[2], held.shape[3]
    pairs = width // head

    def prepare(slot, _):
        query_rows[slot] = jnp.concatenate(split_heads(held[slot, 0], pairs, head), axis=0)
        grad_rows[slot] = jnp.concatenate(split_heads(grad[slot], pairs, head), axis=0)
        product = (grad[slot].astype(F32) * exact[slot]).T
        delta[slot] = jnp.concatenate(
            [
                jnp.sum(product[h * head : (h + 1) * head], axis=0, keepdims=True)
                for h in range(pairs)
            ],
            axis=1,
        )
        grad_q[slot] = jnp.zeros((rows, width), F32)
        return 0

    lax.fori_loop(0, slots, prepare, 0)

    def key_frame(frame, _):
        place = frame ^ me
        keys, values = held[place, 1], held[place, 2]
        head_keys = split_heads(keys, pairs, head)
        grad_k[...] = jnp.zeros_like(grad_k)
        grad_v[...] = jnp.zeros_like(grad_v)

        def query_frame(query, _):
            slot = query ^ me
            score = dot_nt(keys, query_rows[slot])
            grad_weight = dot_nt(values, grad_rows[slot])
            weight = jnp.exp(score - logs[slot])
            grad_score = (weight * (grad_weight - delta[slot])).astype(BF16)
            grad_v[...] += dot_nn(weight.astype(BF16), grad_rows[slot])
            grad_k[...] += dot_nn(grad_score, query_rows[slot])
            total = grad_q[slot]
            for h in range(pairs):
                total = total + dot_tn(grad_score[:, h * rows : (h + 1) * rows], head_keys[h])
            grad_q[slot] = total
            return 0

        lax.fori_loop(jnp.where(frame < context, 0, frame), slots, query_frame, 0)
        held[place, 1] = grad_k[...].astype(BF16)
        held[place, 2] = grad_v[...].astype(BF16)
        return 0

    lax.fori_loop(0, slots, key_frame, 0)
    for slot in range(slots):
        out, role = outs[slot // 2], slot % 2
        out[role, 0] = (grad_q[slot] * head**-0.5).astype(BF16)
        out[role, 1] = held[slot, 1]
        out[role, 2] = held[slot, 2]


def attend_grad_call(meta, parts, grads, exact, logs, head):
    zs = len(parts)
    slots = 2 * zs
    rows, width = parts[0].shape[-2:]
    pairs = width // head
    work = slots * slots * rows * rows
    return pl.pallas_call(
        functools.partial(attend_grad_kernel, slots, head),
        out_shape=[shaped((2, 3, rows, width), BF16)] * zs,
        in_specs=[SMEM] + [ANY] * slots + [VMEM, VMEM],
        out_specs=[VMEM] * zs,
        scratch_shapes=[
            pltpu.VMEM((slots, 3, rows, width), BF16),
            pltpu.VMEM((slots, rows, width), BF16),
            pltpu.VMEM((slots, pairs * rows, width), BF16),
            pltpu.VMEM((slots, pairs * rows, width), BF16),
            pltpu.VMEM((slots, 1, pairs * rows), F32),
            pltpu.VMEM((slots, rows, width), F32),
            pltpu.VMEM((rows, width), F32),
            pltpu.VMEM((rows, width), F32),
            pltpu.SemaphoreType.DMA((zs,)),
            pltpu.SemaphoreType.DMA((zs,)),
        ],
        compiler_params=params(40),
        cost_estimate=cost(work * 40 * width, slots * rows * width * 20, work * pairs),
        name="attend_grad",
    )(meta, *parts, *grads, exact, logs)


def forward_back_kernel(slots, clip, meta, tokens, cotangent, mod, proj_b, up_b, down_b, *refs):
    zs = slots // 2
    parts, swapped, (proj_hbm, up_hbm, down_hbm) = refs[:zs], refs[zs], refs[zs + 1 : zs + 4]
    (
        layer_out, grad_middle_out, row_grads, up_bgrad,
        att_own, att_far, gone_low,
        n2_own, n2_other, hid_low,
        act_own, act_other, gtwo_low,
        held, far, proj, up, down, slope, active, sems,
    ) = refs[zs + 4 :]
    proj_copy = pltpu.make_async_copy(proj_hbm, proj, sems.at[0])
    up_copy = pltpu.make_async_copy(up_hbm, up, sems.at[1])
    down_copy = pltpu.make_async_copy(down_hbm, down, sems.at[2])
    proj_copy.start()
    up_copy.start()
    down_copy.start()
    me = meta[0]
    parity = me % 2
    rows, width = tokens.shape[-2:]
    lanes = width // slots
    hidden_width = up.shape[1]
    gate_one, shift_two, scale_two, gate_two = (mod[clip, k : k + 1] for k in (2, 3, 4, 5))
    for k in range(zs):
        held[(2 * k) ^ me] = parts[k][0]
        held[(2 * k + 1) ^ me] = swapped[k]
        far[k ^ (me // 2)] = parts[k][1]
    attended = jnp.concatenate([held[k] for k in range(slots)], axis=1)
    att_own[...] = jnp.concatenate([held[2 * k + parity] for k in range(zs)], axis=1)
    att_far[...] = jnp.concatenate([far[k] for k in range(zs)], axis=1)
    proj_copy.wait()
    branch_one = dot_nn(attended, proj[...]) + proj_b[...].astype(F32)
    middle = tokens[...].reshape(rows, width).astype(F32) + gate_one * branch_one
    hat_two, inverse_two = norm_parts(middle)
    low_two = (hat_two * (1.0 + scale_two) + shift_two).astype(BF16)
    for block in range(slots):
        store_by_parity(
            n2_own, n2_other, slice(block // 2 * lanes, (block // 2 + 1) * lanes), parity, block,
            low_two[:, block * lanes : (block + 1) * lanes],
        )
    up_copy.wait()
    chunk = hidden_width // slots
    for block in range(hidden_width // FF_BLOCK):
        at = slice(block * FF_BLOCK, (block + 1) * FF_BLOCK)
        hidden = dot_nn(low_two, up[:, at]) + up_b[:, at].astype(F32)
        square = hidden * hidden
        bent = jnp.tanh(GELU_A * (hidden + GELU_B * square * hidden))
        half = 0.5 * (1.0 + bent)
        low = (hidden * half).astype(BF16)
        slope[:, at] = half + (0.5 * GELU_A) * hidden * (1.0 - bent * bent) * (
            1.0 + (3.0 * GELU_B) * square
        )
        active[:, at] = low
        for piece in range(FF_BLOCK // chunk):
            index = block * (FF_BLOCK // chunk) + piece
            store_by_parity(
                act_own, act_other, slice(index // 2 * chunk, (index // 2 + 1) * chunk), parity,
                index, low[:, piece * chunk : (piece + 1) * chunk],
            )
    down_copy.wait()
    branch_two = dot_nn(active[...], down[...]) + down_b[...].astype(F32)
    layer_out[...] = (middle + gate_two * branch_two).astype(BF16)
    grad_out = cotangent[...].reshape(rows, width).astype(F32)
    low_grad_two = (grad_out * gate_two).astype(BF16)
    gtwo_low[...] = low_grad_two
    row_grads[3:4] = jnp.sum(grad_out * branch_two, axis=0, keepdims=True)
    row_grads[4:5] = jnp.sum(low_grad_two.astype(F32), axis=0, keepdims=True)
    grad_normed = None
    for block in range(hidden_width // FF_BLOCK):
        at = slice(block * FF_BLOCK, (block + 1) * FF_BLOCK)
        low = (dot_nt(low_grad_two, down[at, :]) * slope[:, at]).astype(BF16)
        hid_low[:, at] = low
        up_bgrad[:, at] = jnp.sum(low.astype(F32), axis=0, keepdims=True)
        term = dot_nt(low, up[:, at])
        grad_normed = term if grad_normed is None else grad_normed + term
    grad_middle, grad_shift, grad_scale = norm_pull(grad_normed, hat_two, inverse_two, scale_two)
    grad_middle = grad_middle + grad_out
    grad_middle_out[...] = grad_middle
    low_grad_one = (grad_middle * gate_one).astype(BF16)
    gone_low[...] = low_grad_one
    row_grads[0:1] = jnp.sum(grad_middle * branch_one, axis=0, keepdims=True)
    row_grads[1:2] = grad_shift
    row_grads[2:3] = grad_scale
    row_grads[5:6] = jnp.sum(low_grad_one.astype(F32), axis=0, keepdims=True)
    row_grads[6:8] = jnp.zeros((2, width), F32)


def forward_back_call(
    meta, clip, tokens, cotangent, mod, proj_b, up_b, down_b, parts, swapped, proj, up, down
):
    zs = len(parts)
    slots = 2 * zs
    rows, width = tokens.shape[-2:]
    lanes = width // slots
    hidden = up.shape[1]
    half, half_hidden = width // 2, hidden // 2
    out_shape = [
        shaped((rows, width), BF16),
        shaped((rows, width), F32),
        shaped((8, width), F32),
        shaped((1, hidden), F32),
        shaped((rows, half), BF16),
        shaped((rows, half), BF16),
        shaped((rows, width), BF16),
        shaped((rows, half), BF16),
        shaped((rows, half), BF16),
        shaped((rows, hidden), BF16),
        shaped((rows, half_hidden), BF16),
        shaped((rows, half_hidden), BF16),
        shaped((rows, width), BF16),
    ]
    full = lambda shape: pl.BlockSpec(shape, lambda t: (0,) * len(shape))
    pick = pl.BlockSpec((1, 1, rows, width), lambda t: (clip, 0, 0, 0))
    return pl.pallas_call(
        functools.partial(forward_back_kernel, slots, clip),
        grid=(1,),
        out_shape=out_shape,
        in_specs=[SMEM, pick, pick]
        + [full(a.shape) for a in (mod, proj_b, up_b, down_b, *parts, swapped)]
        + [ANY] * 3,
        out_specs=[full(o.shape) for o in out_shape],
        scratch_shapes=[
            pltpu.VMEM((slots, rows, lanes), BF16),
            pltpu.VMEM((zs, rows, lanes), BF16),
            pltpu.VMEM(proj.shape, BF16),
            pltpu.VMEM(up.shape, BF16),
            pltpu.VMEM(down.shape, BF16),
            pltpu.VMEM((rows, hidden), F32),
            pltpu.VMEM((rows, hidden), BF16),
            pltpu.SemaphoreType.DMA((3,)),
        ],
        compiler_params=params(60),
        cost_estimate=cost(
            4 * rows * width * (width + 2 * hidden),
            4 * width * (width + 2 * hidden),
            rows * hidden,
        ),
        name="feed_forward",
    )(meta, tokens, cotangent, mod, proj_b, up_b, down_b, *parts, swapped, proj, up, down)


def proj_back_kernel(meta, near, far, proj, *outs):
    me = meta[0]
    rows, lanes = near.shape[0], outs[0].shape[2]
    for k, out in enumerate(outs):
        group = me ^ (2 * k)
        weight = proj[pl.ds(pl.multiple_of(group * lanes, lanes), lanes), :]
        out[0] = dot_nt(near[...], weight).astype(BF16)
        out[1] = dot_nt(far[...], weight).astype(BF16)


def proj_back_call(meta, near, far, proj, zs):
    rows, width = near.shape
    lanes = width // (2 * zs)
    return pl.pallas_call(
        proj_back_kernel,
        out_shape=[shaped((2, rows, lanes), BF16)] * zs,
        in_specs=[SMEM, VMEM, VMEM, VMEM],
        out_specs=[VMEM] * zs,
        compiler_params=params(32),
        cost_estimate=cost(2 * rows * width * width, 2 * width * width + 6 * rows * width),
        name="proj_back",
    )(meta, near, far, proj)


def qkv_grad_kernel(zs, head, clip, meta, cosine, sine, *refs):
    blocks = refs[zs].shape[0] // (2 * LANES)
    parts, weights = refs[:zs], refs[zs : zs + 3 * blocks]
    near_out, far_out, near_sum, far_sum, bias_out, held = refs[zs + 3 * blocks :]
    rows, width = near_sum.shape
    clips = cosine.shape[0] // 2
    z = meta[0] // 2
    for k in range(zs):
        held[k ^ z] = parts[k][...]
    totals = [None, None]
    bias_out[...] = jnp.zeros_like(bias_out)
    half = width // 2
    for kind in range(3):
        weight = jnp.concatenate([w[...] for w in weights[kind * blocks : (kind + 1) * blocks]], axis=1)
        sums = None
        for role, out in enumerate((near_out, far_out)):
            low = jnp.concatenate([held[k, role, kind] for k in range(zs)], axis=1)
            if kind < 2:
                row = role * clips + clip
                low = turn(low.astype(F32), cosine[row], sine[row], head, True).astype(BF16)
            out[:, kind * half : (kind + 1) * half] = low
            column = jnp.sum(low.astype(F32), axis=0, keepdims=True)
            sums = column if sums is None else sums + column
            term = dot_nt(low, weight)
            totals[role] = term if totals[role] is None else totals[role] + term
        bias_out[kind : kind + 1] = sums
    near_sum[...] = totals[0]
    far_sum[...] = totals[1]


def qkv_grad_call(meta, clip, cosine, sine, parts, weight, head, aligned):
    zs = len(parts)
    rows, lanes = parts[0].shape[-2:]
    width = 2 * zs * lanes
    blocks = width // (2 * LANES)
    whole = lambda shape: pl.BlockSpec(shape, lambda t, m: (0,) * len(shape))
    out_shape = [
        shaped((rows, 3 * width // 2), BF16),
        shaped((rows, 3 * width // 2), BF16),
        shaped((rows, width), F32),
        shaped((rows, width), F32),
        shaped((8, width // 2), F32),
    ]
    return pl.pallas_call(
        functools.partial(qkv_grad_kernel, zs, head, clip),
        out_shape=out_shape,
        grid_spec=pltpu.PrefetchScalarGridSpec(
            num_scalar_prefetch=1,
            grid=(1,),
            in_specs=[whole(a.shape) for a in (cosine, sine, *parts)]
            + half_specs(width, width, 2 * zs, aligned),
            out_specs=[whole(o.shape) for o in out_shape],
            scratch_shapes=[pltpu.VMEM((zs, 2, 3, rows, lanes), BF16)],
        ),
        compiler_params=params(48),
        cost_estimate=cost(6 * rows * width * width, 3 * width * width + 20 * rows * width),
        name="qkv_grad",
    )(meta, cosine, sine, *parts, *[weight] * (3 * blocks))


def norm_grad_kernel(tokens, mod, *refs):
    clips = tokens.shape[0]
    nears, fars, middles = refs[:clips], refs[clips : 2 * clips], refs[2 * clips : 3 * clips]
    tokens_grad, row_grads = refs[3 * clips :]
    for c in range(clips):
        hat, inverse = norm_parts(tokens[c, 0].astype(F32))
        grad, shift, scale = norm_pull(nears[c][...] + fars[c][...], hat, inverse, mod[c, 1:2])
        tokens_grad[c, 0] = grad + middles[c][...]
        row_grads[c, 0:1] = shift
        row_grads[c, 1:2] = scale
        row_grads[c, 2:8] = jnp.zeros((6, tokens.shape[-1]), F32)


def norm_grad_call(tokens, mod, nears, fars, middles):
    clips, _, rows, width = tokens.shape
    return pl.pallas_call(
        norm_grad_kernel,
        out_shape=[shaped(tokens.shape, F32), shaped((clips, 8, width), F32)],
        in_specs=[VMEM] * (2 + 3 * clips),
        out_specs=[VMEM, VMEM],
        compiler_params=params(40),
        cost_estimate=cost(clips * rows * width * 30, clips * rows * width * 18),
        name="norm_grad",
    )(tokens, mod, *nears, *fars, *middles)


def weight_grad_kernel(jobs, clip_size, zs, meta, *refs):
    count = sum(job[0] * (1 + job[1]) for job in jobs)
    outs = refs[count : count + 4]
    held, sems = refs[count + 4], refs[count + 5]
    turned_refs = refs[count + 6 :]
    step = pl.program_id(0) * pl.num_programs(1) + pl.program_id(1)
    last = pl.num_programs(0) * pl.num_programs(1) - 1
    slot = step % 2
    _, _, height, cols = held.shape
    tile = zs * height
    z = meta[0] // 2

    def drain(which):
        pltpu.make_async_copy(held.at[which], held.at[which], sems.at[which]).wait()

    def send_out(e, tiles, repeat, first, tall):
        for half, first_bit in enumerate((1, clip_size // 2)):
            keep, send = outs[2 * half], outs[2 * half + 1]
            rest = [k for k in range(clip_size) if not k & first_bit]
            out, place = (send, rest.index(e ^ first_bit)) if e & first_bit else (keep, rest.index(e))
            low, high = half * zs // 2, (half + 1) * zs // 2
            if not tall:
                pltpu.make_async_copy(
                    held.at[slot, pl.ds(low, zs // 2)],
                    out.at[place, :, pl.ds(first, height)],
                    sems.at[slot],
                ).start()
            else:
                for block in range(zs):
                    row = repeat * zs + block
                    k = row // tiles
                    if low <= k < high:
                        pltpu.make_async_copy(
                            held.at[slot, block],
                            out.at[place, k - low, pl.ds(first + row % tiles * height, height)],
                            sems.at[slot],
                        ).start()

    @pl.when(step >= 2)
    def _():
        drain(slot)

    at = index = 0
    for job, (lefts_n, lane_parts, tall, tiles, first) in enumerate(jobs):
        lefts = refs[at : at + lefts_n]
        rights = refs[at + lefts_n : at + lefts_n * (1 + lane_parts)]
        at += lefts_n * (1 + lane_parts)
        turned = turned_refs[job]
        total_rows = lefts[0].shape[1]
        depth = lefts[0].shape[0]
        block = total_rows // zs

        @pl.when(step == index)
        def _():
            for k in range(zs):
                place = pl.ds(pl.multiple_of((k ^ z) * block, block), block)
                for n, left in enumerate(lefts):
                    turned[place, n * depth : (n + 1) * depth] = left[
                        :, k * block : (k + 1) * block
                    ].T

        for repeat in range(tiles):

            @pl.when(pl.program_id(1) == index)
            def _():
                picked = turned[repeat * tile : (repeat + 1) * tile, :] if tall else turned[...]
                right = jnp.concatenate(
                    [
                        jnp.concatenate([rights[n * lane_parts + p][...] for p in range(lane_parts)], axis=1)
                        for n in range(lefts_n)
                    ],
                    axis=0,
                )
                held[slot] = dot_nn(picked, right).astype(BF16).reshape(held.shape[1:])
                offset = first if tall else first + repeat * height
                for e in range(clip_size):

                    @pl.when(pl.program_id(0) == e)
                    def _():
                        send_out(e, tiles, repeat, offset, tall)

            index += 1

    @pl.when(step == last)
    def _():
        drain(1 - slot)
        drain(slot)


def weight_grad_call(meta, products, clip_size, zs, name):
    jobs, specs, arrays, turned = [], [], [], []
    first = index = flops = 0
    tile = min(p[0][0].shape[1] for p in products)
    height = tile // zs
    piece = None
    for lefts, rights, lane_parts, tall in products:
        total = rights[0].shape[1]
        if tall:
            tiles, block = lefts[0].shape[1] // tile, total // clip_size
        elif lane_parts > 1:
            tiles, block = 1, total // (lane_parts * clip_size)
        else:
            tiles, block = total // (2 * tile), 2 * tile // clip_size
        piece = lane_parts * block
        jobs.append((len(lefts), lane_parts, tall, tiles, first))
        first += height * tiles
        for left in lefts:
            arrays.append(left)
            specs.append(pl.BlockSpec(left.shape, lambda e, t, m: (0, 0)))
            flops += 2 * left.shape[0] * left.shape[1] * total
        for right in rights:
            for part in range(lane_parts):
                arrays.append(right)

                def place(e, t, m, start=index, tiles=tiles, tall=tall, part=part):
                    group = part if tall or tiles == 1 else jnp.clip(t - start, 0, tiles - 1)
                    return (0, group * clip_size + (e ^ m[2]))

                specs.append(pl.BlockSpec((right.shape[0], block), place))
        turned.append(
            pltpu.VMEM((lefts[0].shape[1], len(lefts) * lefts[0].shape[0]), BF16)
        )
        index += tiles
    out = shaped((clip_size // 2, zs // 2, first, piece), BF16)
    return pl.pallas_call(
        functools.partial(weight_grad_kernel, tuple(jobs), clip_size, zs),
        out_shape=[out] * 4,
        grid_spec=pltpu.PrefetchScalarGridSpec(
            num_scalar_prefetch=1,
            grid=(clip_size, index),
            in_specs=specs,
            out_specs=[ANY] * 4,
            scratch_shapes=[
                pltpu.VMEM((2, zs, height, piece), BF16),
                pltpu.SemaphoreType.DMA((2,)),
            ]
            + turned,
        ),
        compiler_params=params(56),
        cost_estimate=cost(flops, sum(a.size * 2 for a in arrays) + 8 * out.size),
        name=name,
    )(meta, *arrays)


def place_kernel(jobs, pieces, meta, *refs):
    parts, outs = refs[:pieces], refs[pieces:]
    clip = meta[2]
    cols = parts[0].shape[1]
    for e in range(pieces):
        first = 0
        for out, (height, repeats, tall) in zip(outs, jobs):
            for repeat in range(repeats):
                base = 0 if tall else repeat * cols * pieces
                target = pl.ds(pl.multiple_of(base + (clip ^ e) * cols, cols), cols)
                value = parts[e][first : first + height].astype(F32)
                if tall:
                    out[repeat * height : (repeat + 1) * height, target] = value
                else:
                    out[:, target] = value
                first += height


def place_call(meta, parts, jobs, outs):
    return pl.pallas_call(
        functools.partial(place_kernel, jobs, len(parts)),
        out_shape=outs,
        in_specs=[SMEM] + [VMEM] * len(parts),
        out_specs=[VMEM] * len(outs),
        compiler_params=params(32),
        cost_estimate=cost(0, sum(o.size * 4 for o in outs)),
        name="place_grads",
    )(meta, *parts)


def place_qkv_kernel(meta, *refs):
    parts, out = refs[:-1], refs[-1]
    parity, clip = meta[0] % 2, meta[2]
    thirds = out.shape[1] // 3
    for e, part in enumerate(parts):
        for role in range(2):
            block = 2 * (clip ^ e) + (parity ^ role)
            for kind in range(3):
                at = pl.ds(pl.multiple_of(kind * thirds + block * LANES, LANES), LANES)
                out[:, at] = part[role, :, kind * LANES : (kind + 1) * LANES].astype(F32)


def place_qkv_call(meta, parts, out):
    return pl.pallas_call(
        place_qkv_kernel,
        out_shape=out,
        in_specs=[SMEM] + [VMEM] * len(parts),
        out_specs=VMEM,
        compiler_params=params(32),
        cost_estimate=cost(0, out.size * 6),
        name="place_qkv_grad",
    )(meta, *parts)


def exchange(array, axis, size, distance):
    return lax.ppermute(array, axis, [(k, k ^ distance) for k in range(size)])


def after(value, *others):
    return lax.optimization_barrier((value, *others))


def spread(slots_out, seq_size):
    return [slots_out[0]] + [
        exchange(slots_out[k], "seq", seq_size, 2 * k) for k in range(1, seq_size // 2)
    ]


def add_low(left, right):
    return (left.astype(F32) + right.astype(F32)).astype(BF16)


def halve(pair, bit, size):
    keep, send = pair
    arrived = exchange(send, "clip", size, bit)
    half = keep.shape[0] // 2
    if half == 0:
        return add_low(keep[0], arrived[0]), None
    return add_low(keep[:half], arrived[:half]), add_low(keep[half:], arrived[half:])


def clip_orders(clip_size):
    down = [1 << k for k in reversed(range(clip_size.bit_length() - 1))]
    return [1] + down[:-1], down


def sum_z(near, far, seq_size):
    zs = seq_size // 2
    half = zs // 2
    total = near[0].astype(F32)
    for k in range(1, zs):
        source = near[k] if k < half else far[k - half]
        total = total + exchange(source, "seq", seq_size, 2 * k).astype(F32)
    return total.astype(BF16)


def gather_pieces(piece, clip_size):
    return [piece] + [exchange(piece, "clip", clip_size, d) for d in range(1, clip_size)]


def gather_all(rows, clip_size, seq_size):
    both = jnp.stack([rows, exchange(rows, "seq", seq_size, 1)])
    by_seq = jnp.concatenate(
        [both] + [exchange(both, "seq", seq_size, 2 * k) for k in range(1, seq_size // 2)]
    )
    return jnp.concatenate(
        [by_seq] + [exchange(by_seq, "clip", clip_size, d) for d in range(1, clip_size)]
    )


def silu_act(values_in):
    return values_in * jax.nn.sigmoid(values_in)


def rotary_tables(stamps, patch_count, head):
    lane = jnp.arange(LANES, dtype=jnp.int32)
    quarter = head // 4
    pair = lane % (head // 2)
    freqs = 10000.0 ** (-(pair % quarter).astype(F32) / quarter)
    temporal = stamps.astype(F32)[:, None, None] * freqs[None, None, :]
    spatial = jnp.arange(patch_count).astype(F32)[None, :, None] * freqs[None, None, :]
    angles = jnp.where((pair < quarter)[None, None, :], temporal, spatial)
    sign = jnp.where(lane % head < head // 2, -1.0, 1.0).astype(F32)
    return jnp.cos(angles), jnp.sin(angles) * sign[None, None, :]


def on_device(
    tokens,
    cotangent,
    context_count,
    noise_level,
    frame_time,
    level_table,
    mod_weight,
    mod_bias,
    qkv_weight,
    qkv_bias,
    proj_weight,
    proj_bias,
    up_weight,
    up_bias,
    down_weight,
    down_bias,
):
    seq_size, clip_size = lax.axis_size("seq"), lax.axis_size("clip")
    me, mine = lax.axis_index("seq"), lax.axis_index("clip")
    clips, _, rows, width = tokens.shape
    head = width // HEADS
    hidden = up_weight.shape[1]
    zs = seq_size // 2
    me = me.astype(jnp.int32)
    mine = mine.astype(jnp.int32)
    parity = me % 2
    aligned = (width // seq_size) % LANES == 0
    metas = [jnp.stack([me, context_count[c], mine]) for c in range(clips)]
    stamps = jnp.stack([noise_level[:, 0], frame_time[:, 0]])
    other_stamps = exchange(stamps, "seq", seq_size, 1)
    other_tokens = exchange(tokens, "seq", seq_size, 1)
    both_levels = jnp.concatenate(
        [
            jnp.where(me < context_count, 0, stamps[0]),
            jnp.where((me ^ 1) < context_count, 0, other_stamps[0]),
        ]
    )
    levels_used = both_levels[:clips]
    picked = (
        both_levels[:, None] == jnp.arange(level_table.shape[0], dtype=jnp.int32)[None, :]
    ).astype(BF16)
    condition = jnp.dot(picked, level_table, preferred_element_type=F32)
    condition_low = silu_act(condition).astype(BF16)
    modulation = jnp.dot(
        condition_low, mod_weight, preferred_element_type=F32
    ) + mod_bias.astype(F32)
    mods = modulation.reshape(2 * clips, 6, width)
    cosine, sine = rotary_tables(jnp.concatenate([stamps[1], other_stamps[1]]), rows, head)
    qkv_bias_row = qkv_bias[None]
    if aligned:
        weight_half, bias_half = qkv_weight, qkv_bias_row
    else:
        weight_half = half_columns(qkv_weight, seq_size, parity)
        bias_half = half_columns(qkv_bias_row, seq_size, parity)

    parts, normed = [], []
    for c in range(clips):
        out = qkv_call(
            metas[c], c, tokens, other_tokens, mods, cosine, sine, weight_half, bias_half, zs,
            head, aligned,
        )
        parts.append(spread(out[:zs], seq_size))
        normed.append(out[zs:])
    attended, swapped, exact, logs = [], [], [], []
    for c in range(clips):
        out = attend_call(metas[c], parts[c], head)
        attended.append(spread(out[:zs], seq_size))
        crossing = jnp.stack([a[1] for a in attended[c]])
        swapped.append(exchange(crossing, "seq", seq_size, 1))
        exact.append(out[zs])
        logs.append(out[zs + 1])
    swap = lambda array: exchange(array, "seq", seq_size, 1)
    layer, middles, row_grads, up_bgrads, saved, grads, far_ones = [], [], [], [], [], [], []
    for c in range(clips):
        out = forward_back_call(
            metas[c], c, tokens, cotangent, mods, proj_bias[None], up_bias[None],
            down_bias[None], attended[c], swapped[c], proj_weight, up_weight, down_weight,
        )
        layer.append(out[0])
        middles.append(out[1])
        row_grads.append(out[2])
        up_bgrads.append(out[3])
        saved.append(out[4:13])
        far_ones.append(swap(out[6]))
        grads.append(spread(proj_back_call(metas[c], out[6], far_ones[c], proj_weight, zs), seq_size))
    products = [([], [], 1, False), ([], [], 1, True), ([], [], 1, False)]
    for c in range(clips):
        att_own, att_far, gone, n2_own, n2_other, hid, act_own, act_other, gtwo = saved[c]
        products[0][0].extend([n2_own, swap(n2_other)])
        products[0][1].extend([hid, swap(hid)])
        products[1][0].extend([act_own, swap(act_other)])
        products[1][1].extend([gtwo, swap(gtwo)])
        products[2][0].extend([att_own, att_far])
        products[2][1].extend([gone, far_ones[c]])
    shares = weight_grad_call(metas[0], products, clip_size, zs, "weight_grads")
    row = width // seq_size
    orders = clip_orders(clip_size)
    steps = len(orders[0])
    near, far = shares[:2], shares[2:]

    metas[0], near, far = after(metas[0], near, far)
    metas[1], near, far = after(metas[1], near, far)
    grad_rights, nears, fars, qkv_bgrads = [], [], [], []
    for c in range(clips):
        out = attend_grad_call(metas[c], parts[c], grads[c], exact[c], logs[c], head)
        if c < steps:
            near = halve(near, orders[0][c], clip_size)
            far = halve(far, orders[1][c], clip_size)
        metas[c], near, far = after(metas[c], near, far)
        out = qkv_grad_call(
            metas[c], c, cosine, sine, spread(out, seq_size), weight_half, head, aligned
        )
        grad_rights.extend(out[:2])
        nears.append(out[2])
        fars.append(swap(out[3]))
        qkv_bgrads.append(out[4][:3])
    tokens_grad, late_rows = norm_grad_call(tokens, mods, nears, fars, middles)
    for at in range(clips, steps):
        near = halve(near, orders[0][at], clip_size)
        far = halve(far, orders[1][at], clip_size)
    piece = sum_z(near[0], far[0], seq_size)
    up_wgrad, down_wgrad, proj_wgrad = place_call(
        metas[0],
        gather_pieces(piece, clip_size),
        (
            (row, hidden // width, False),
            (row, hidden // width, True),
            (row, 1, False),
        ),
        [shaped((row, hidden), F32), shaped((hidden // seq_size, width), F32), shaped((row, width), F32)],
    )
    lefts = [array for pair in normed for array in pair]
    if aligned:
        shares = weight_grad_call(
            metas[0], [(lefts, grad_rights, 3, False)], clip_size, zs, "qkv_weight_grad"
        )
        near, far = shares[:2], shares[2:]
        for at in range(steps):
            near = halve(near, orders[0][at], clip_size)
            far = halve(far, orders[1][at], clip_size)
        piece = sum_z(near[0], far[0], seq_size).reshape(2, row, 3 * LANES)
        own_rows = lax.dynamic_index_in_dim(piece, parity, 0, keepdims=False)
        far_rows = swap(lax.dynamic_index_in_dim(piece, 1 - parity, 0, keepdims=False))
        qkv_wgrad = place_qkv_call(
            metas[0],
            gather_pieces(jnp.stack([own_rows, far_rows]), clip_size),
            shaped((row, 3 * width), F32),
        )
    else:
        share = sum(
            lax.dot_general(left, right, (((0,), (0,)), ((), ())), preferred_element_type=F32)
            for left, right in zip(lefts, grad_rights)
        ).astype(BF16)
        share = share.reshape(width, 3, zs, 1, width // seq_size)
        blank = jnp.zeros_like(share)
        share = jnp.where(
            parity == 0,
            jnp.concatenate([share, blank], axis=3),
            jnp.concatenate([blank, share], axis=3),
        ).reshape(width, 3 * width)
        qkv_wgrad = lax.psum(
            lax.psum_scatter(share, "seq", scatter_dimension=0, tiled=True), "clip"
        ).astype(F32)

    level_rows = jnp.stack([levels_used // 32, levels_used % 32]).astype(F32)
    level_rows = jnp.concatenate([level_rows, jnp.zeros((2, width - clips), F32)], axis=1)
    mod_rows = []
    for c in range(clips):
        mod_rows += [late_rows[c, 0:2], row_grads[c][0:4]]
    bias_rows = [
        sum(qkv_bgrads).reshape(3 * width // 2),
        jnp.zeros((width // 2,), F32),
        sum(up_bgrads).reshape(hidden),
        sum(r[4] for r in row_grads),
        sum(r[5] for r in row_grads),
    ]
    bias_rows = jnp.concatenate(bias_rows).reshape(-1, width)
    late = jnp.concatenate([condition[:clips], level_rows] + mod_rows + [bias_rows], axis=0)
    used = late.shape[0]
    late = jnp.concatenate([late.astype(BF16), jnp.zeros((-used % 16, width), BF16)], axis=0)
    late = gather_all(late, clip_size, seq_size)
    devices = late.shape[0]
    start = clips + 2
    grad_modulation = late[:, start : start + 6 * clips].reshape(devices * clips, 6 * width)
    bias_all = late[:, start + 6 * clips : used].astype(F32).reshape(devices, -1)
    own_sums = jnp.sum(bias_all.reshape(devices // 2, 2, -1), axis=0)
    half_bias = own_sums[:, : 3 * width // 2].reshape(2, 3, zs, 1, width // seq_size)
    bias_sums = jnp.sum(own_sums, axis=0)[2 * width :]
    qkv_bias_sums = jnp.where(
        parity == 0,
        jnp.concatenate([half_bias[0], half_bias[1]], axis=2),
        jnp.concatenate([half_bias[1], half_bias[0]], axis=2),
    ).reshape(3 * width)
    all_condition = late[:, :clips].reshape(devices * clips, width).astype(F32)
    codes = late[:, clips:start, :clips].astype(jnp.int32)
    all_levels = (codes[:, 0] * 32 + codes[:, 1]).reshape(devices * clips)
    all_active, silu_pull = jax.vjp(silu_act, all_condition)
    my_active = lax.dynamic_slice_in_dim(all_active, me * row, row, axis=1).astype(BF16)
    mod_wgrad = lax.dot_general(
        my_active, grad_modulation, (((0,), (0,)), ((), ())), preferred_element_type=F32
    )
    (grad_condition,) = silu_pull(
        lax.dot_general(
            grad_modulation, mod_weight, (((1,), (1,)), ((), ())), preferred_element_type=F32
        )
    )
    table_row = level_table.shape[0] // seq_size
    onehot = (
        all_levels[:, None] == (me * table_row + jnp.arange(table_row, dtype=jnp.int32))[None, :]
    ).astype(F32)
    table_grad = lax.dot_general(
        onehot,
        grad_condition,
        (((0,), (0,)), ((), ())),
        precision=HIGHEST_PRECISION,
        preferred_element_type=F32,
    )
    mod_sums = jnp.sum(grad_modulation.astype(F32), axis=0)

    def own_part(vector):
        size = vector.shape[0] // seq_size
        return lax.dynamic_slice_in_dim(vector, me * size, size, axis=0)

    mod_bgrad = own_part(mod_sums)
    qkv_bgrad = own_part(qkv_bias_sums)
    up_bgrad = own_part(bias_sums[:hidden])
    down_bgrad = own_part(bias_sums[hidden : hidden + width])
    proj_bgrad = own_part(bias_sums[hidden + width : hidden + 2 * width])
    layer_out = jnp.stack(layer)[:, None]
    return (
        layer_out,
        tokens_grad,
        table_grad,
        mod_wgrad,
        mod_bgrad,
        qkv_wgrad,
        qkv_bgrad,
        proj_wgrad,
        proj_bgrad,
        up_wgrad,
        up_bgrad,
        down_wgrad,
        down_bgrad,
    )


def solution(mesh):
    placed = (
        P("clip", "seq", None, None),
        P("clip", "seq", None, None),
        P("clip"),
        P("clip", "seq"),
        P("clip", "seq"),
    ) + (P(),) * 11
    return jax.shard_map(
        on_device,
        mesh=mesh,
        in_specs=placed,
        out_specs=(
            P("clip", "seq", None, None),
            P("clip", "seq", None, None),
            P("seq", None),
            P("seq", None),
            P("seq"),
            P("seq", None),
            P("seq"),
            P("seq", None),
            P("seq"),
            P("seq", None),
            P("seq"),
            P("seq", None),
            P("seq"),
        ),
        check_vma=False,
    )
```

time: 734 us -> 566 us (0.77)
  waiting for transfers between devices: 223 us -> 150 us
  starting transfers between devices: 174 us -> 126 us
  local copies, waits for them, and re-layouts: 64.7 us -> 34.2 us
  Pallas kernels: 216 us -> 206 us
    ppermute x114 -> x68, waiting for transfers between devices: 223 us -> 150 us  [exchange(): return lax.ppermute(array, axis, [(k, k ^ distance) for k in range(size)])]
    ppermute x114 -> x68, starting transfers between devices: 174 us -> 126 us  [exchange(): return lax.ppermute(array, axis, [(k, k ^ distance) for k in range(size)])]
    unnamed x249 -> x168, local copies, waits for them, and re-layouts: 45.7 us -> 15.6 us
    pallas_call x10 -> x13, Pallas kernels: 123 us -> 123 us  [the longest x2 46.8 us: weight_grad_call(): pl.pallas_call(functools.partial(weight_grad_kernel, tuple(jobs), clip_si...]
  transfers between devices with their start and end apart: 114 -> 68, of which waited for: 20 -> 23; matrix products, arithmetic and copies ran while one was open for 9% -> 8% of each run, Pallas kernels for 29% -> 29%
where the time goes in v2:
time: 566 us; the launch traced here: 562 us
  Pallas kernels  206 us (36%)
  waiting for transfers between devices  150 us (27%)
  starting transfers between devices  126 us (22%)
  local copies, waits for them, and re-layouts  34.2 us (6%)
  other arithmetic  24 us (4%)
  matrix products  20.5 us (4%)
    ppermute x68, waiting for transfers between devices, exchange(): return lax.ppermute(array, axis, [(k, k ^ distance) for k in range(size)])  150 us
    ppermute x68, starting transfers between devices, exchange(): return lax.ppermute(array, axis, [(k, k ^ distance) for k in range(size)])  126 us
    pallas_call x2, Pallas kernels, attend_grad_call(): pl.pallas_call(functools.partial(attend_grad_kernel, slots, head), out_sh...  55.3 us
    pallas_call x2, Pallas kernels, weight_grad_call(): pl.pallas_call(functools.partial(weight_grad_kernel, tuple(jobs), clip_si...  46.8 us
    pallas_call x2, Pallas kernels, forward_back_call(): pl.pallas_call(functools.partial(forward_back_kernel, slots, clip), grid=...  42.7 us
    pallas_call x2, Pallas kernels, attend_call(): pl.pallas_call(functools.partial(attend_kernel, slots, head), out_shape=[...  27.6 us
    unnamed x168, local copies, waits for them, and re-layouts  15.6 us
  transfers between devices with their start and end apart: 68, of which 23 were waited for; matrix products, arithmetic and copies ran while one was open for 8% of the time, Pallas kernels for 29%

profile of v2, /device:TPU:0, one launch (start us, length us, event | category | flops | bytes accessed | tf_op | source)
XLA Modules:
  0.0 562.2 jit_solution(16900534670908501113)
XLA Ops:
  7.5 6.3 %convolution_add_fusion = f32[4,6144]{1,0:T(4,128)S(1)} fusion(bf16[1024,6144]{1,0:T(8,128)(2,1)} %param.22, f32[6144]{0:T(1024)S(1)} %convert_element_type.215, f32[4,1024]{1,0:T(4,128)S(1)} %fusion.25), kind=kOutput, calls=%fused_computation | convolution fusion | flops 50376704 | bytes 12722176 | tf_op jit(solution)/shard_map/dot_general | solution.py:953
  15.8 5.0 norm_qkv.2
  21.6 3.0 collective-permute-start.2
  24.7 2.6 collective-permute-start.3
  28.0 5.0 norm_qkv.3
  36.9 4.8 collective-permute-done.2.refs_1_
  41.8 29.5 %collective-permute-done.3.refs_2_ = bf16[2,3,256,128]{3,2,1,0:T(8,128)(2,1)S(1)} collective-permute-done((bf16[2,3,256,128]{3,2,1,0:T(8,128)(2,1)S(1)}, bf16[2,3,256,128]{3,2,1,0:T(8,128)(2,1)S(1)}, u32[]{:S(2)}, u32[]{:S(2)}) %collective-permute-start.3) | collective-permute-done | bytes 393248 | tf_op jit(solution)/shard_map/ppermute | solution.py:838
  71.3 15.4 %attend.2 = (bf16[2,256,128]{2,1,0:T(8,128)(2,1)S(1)}, bf16[2,256,128]{2,1,0:T(8,128)(2,1)S(1)}, bf16[2,256,128]{2,1,0:T(8,128)(2,1)S(1)}, bf16[2,256,128]{2,1,0...) custom-call(s32[3]{0:T(128)S(1)} %add_add_fusion.meta, ...), custom_call_target="tpu_custom_call" | custom-call | flops 8589934592 | bytes 3145728 | tf_op jit(solution)/shard_map/attend/pallas_call | solution.py:271
  87.7 9.0 %collective-permute-start.5 = (bf16[2,256,128]{2,1,0:T(8,128)(2,1)S(1)}, bf16[2,256,128]{2,1,0:T(8,128)(2,1)S(1)}, u32[]{:S(2)}, u32[]{:S(2)}) collective-permute-start(bf16[2,256,128]{2,1,0:T(8,128)(2,1)S(1)} %get-tuple-element.125), channel_id=1, source_target_pairs={{0,8},{4,12},{8,0},{12,4},{16,24},{20,28},{24,16},{28,20},{1,9},{5... | collective-permute-start | bytes 393224 | tf_op jit(solution)/shard_map/ppermute | solution.py:838
  97.7 2.7 collective-permute-done.5.refs_1_
  100.5 2.9 collective-permute-start.7
  103.4 4.2 collective-permute-done.6.refs_2_
  107.8 12.2 %attend.3 = (bf16[2,256,128]{2,1,0:T(8,128)(2,1)S(1)}, bf16[2,256,128]{2,1,0:T(8,128)(2,1)S(1)}, bf16[2,256,128]{2,1,0:T(8,128)(2,1)S(1)}, bf16[2,256,128]{2,1,0...) custom-call(s32[3]{0:T(128)S(1)} %add_add_fusion.1.meta, ...), custom_call_target="tpu_custom_call" | custom-call | flops 8589934592 | bytes 3145728 | tf_op jit(solution)/shard_map/attend/pallas_call | solution.py:271
  127.4 2.1 collective-permute-done.12.refs_1_
  129.4 6.5 %collective-permute-done.13.refs_2_ = bf16[2,256,128]{2,1,0:T(8,128)(2,1)S(1)} collective-permute-done((bf16[2,256,128]{2,1,0:T(8,128)(2,1)S(1)}, bf16[2,256,128]{2,1,0:T(8,128)(2,1)S(1)}, u32[]{:S(2)}, u32[]{:S(2)}) %collective-permute-start.13) | collective-permute-done | bytes 131104 | tf_op jit(solution)/shard_map/ppermute | solution.py:838
  136.8 21.2 %feed_forward.2 = (bf16[256,1024]{1,0:T(8,128)(2,1)}, f32[256,1024]{1,0:T(8,128)}, f32[8,1024]{1,0:T(8,128)}, f32[1,4096]{1,0:T(1,128)}, bf16[256,512]{1,0:T(8,1...) custom-call(s32[3]{0:T(128)} %copy-done.20, ...), custom_call_target="tpu_custom_call" | custom-call | flops 9663676416 | bytes 37748736 | tf_op jit(solution)/shard_map/feed_forward/pallas_call | solution.py:501
  159.4 21.5 %feed_forward.3 = (bf16[256,1024]{1,0:T(8,128)(2,1)}, f32[256,1024]{1,0:T(8,128)}, f32[8,1024]{1,0:T(8,128)}, f32[1,4096]{1,0:T(1,128)}, bf16[256,512]{1,0:T(8,1...) custom-call(s32[3]{0:T(128)} %copy-done.23, ...), custom_call_target="tpu_custom_call" | custom-call | flops 9663676416 | bytes 37748736 | tf_op jit(solution)/shard_map/feed_forward/pallas_call | solution.py:501
  181.9 3.5 collective-permute-done.16.refs_1_
  191.3 2.8 collective-permute-done.25.refs_23_.far
  195.0 37.0 %weight_grads.1 = (bf16[2,2,1152,256]{3,2,1,0:T(8,128)(2,1)}, bf16[2,2,1152,256]{3,2,1,0:T(8,128)(2,1)}, bf16[2,2,1152,256]{3,2,1,0:T(8,128)(2,1)}, bf16[2,2,1152,256]{3,2,1,0:T(8,128)(2,1)}) custom-call(s32[3]{0:T(128)} %copy-done.20, bf16[256,512]{1,0:T(8,128)(2,1)} %get-tuple-element.138.refs_0_, bf16[256,512]{1,0:T(8,128)(2,1)} %copy-done.73, ...), custom_call_target="tpu_custom_call" | custom-call | flops 9663676416 | bytes 28311552 | tf_op jit(solution)/shard_map/weight_grads/pallas_call | solution.py:763
  232.0 3.4 collective-permute-start.27
  240.7 2.7 collective-permute-start.28
  248.8 2.0 collective-permute-start.37
  250.8 5.5 collective-permute-done.29.refs_6_
  256.3 2.6 collective-permute-start.38
  258.9 31.4 %attend_grad.2 = (bf16[2,3,256,128]{3,2,1,0:T(8,128)(2,1)S(1)}, bf16[2,3,256,128]{3,2,1,0:T(8,128)(2,1)S(1)}, bf16[2,3,256,128]{3,2,1,0:T(8,128)(2,1)S(1)}, bf16[2,3,256,128]{3,2,1,0:T(8,128)(2,1)S(1)}) custom-call(s32[3]{0:T(128)S(1)} %copy-done.21, bf16[2,3,256,128]{3,2,1,0:T(8,128)(2,1)S(1)} %copy-done.38, bf16[2,3,256,128]{3,2,1,0:T(8,128)(2,1)S(1)} %copy-done.40, ...), custom_call_target="tpu_custom_call" | custom-call | flops 21474836480 | bytes 5242880 | tf_op jit(solution)/shard_map/attend_grad/pallas_call | solution.py:366
  290.4 6.5 %collective-permute-start.31 = (bf16[2,3,256,128]{3,2,1,0:T(8,128)(2,1)S(1)}, bf16[2,3,256,128]{3,2,1,0:T(8,128)(2,1)S(1)}, u32[]{:S(2)}, u32[]{:S(2)}) collective-permute-start(bf16[2,3,256,128]{3,2,1,0:T(8,128)(2,1)S(1)} %get-tuple-element.177), channel_id=1, source_target_pairs={{0,8},{4,12},{8,0},{12,4},{16,24},{20,28},{24,16},{28,20},{1,9},{5... | collective-permute-start | bytes 1179656 | tf_op jit(solution)/shard_map/ppermute | solution.py:838
  298.5 10.5 %collective-permute-done.26 = bf16[2,2,1152,256]{3,2,1,0:T(8,128)(2,1)} collective-permute-done((bf16[2,2,1152,256]{3,2,1,0:T(8,128)(2,1)}, bf16[2,2,1152,256]{3,2,1,0:T(8,128)(2,1)}, u32[]{:S(2)}, u32[]{:S(2)}) %collective-permute-start.26) | collective-permute-done | bytes 2359328 | tf_op jit(solution)/shard_map/ppermute | solution.py:838
  309.0 7.1 %collective-permute-start.32 = (bf16[2,3,256,128]{3,2,1,0:T(8,128)(2,1)S(1)}, bf16[2,3,256,128]{3,2,1,0:T(8,128)(2,1)S(1)}, u32[]{:S(2)}, u32[]{:S(2)}) collective-permute-start(bf16[2,3,256,128]{3,2,1,0:T(8,128)(2,1)S(1)} %get-tuple-element.178), channel_id=1, source_target_pairs={{0,16},{4,20},{8,24},{12,28},{16,0},{20,4},{24,8},{28,12},{1,17},{... | collective-permute-start | bytes 1179656 | tf_op jit(solution)/shard_map/ppermute | solution.py:838
  316.2 3.3 add_convert_fusion.4
  320.1 23.9 %attend_grad.3 = (bf16[2,3,256,128]{3,2,1,0:T(8,128)(2,1)S(1)}, bf16[2,3,256,128]{3,2,1,0:T(8,128)(2,1)S(1)}, bf16[2,3,256,128]{3,2,1,0:T(8,128)(2,1)S(1)}, bf16[2,3,256,128]{3,2,1,0:T(8,128)(2,1)S(1)}) custom-call(s32[3]{0:T(128)S(1)} %copy-done.24, bf16[2,3,256,128]{3,2,1,0:T(8,128)(2,1)S(1)} %copy-done.34, bf16[2,3,256,128]{3,2,1,0:T(8,128)(2,1)S(1)} %copy-done.36, ...), custom_call_target="tpu_custom_call" | custom-call | flops 21474836480 | bytes 5242880 | tf_op jit(solution)/shard_map/attend_grad/pallas_call | solution.py:366
  344.8 3.7 collective-permute-start.40
  348.6 5.5 qkv_grad.2
  359.5 4.2 collective-permute-start.64
  363.7 34.3 %collective-permute-done.40.refs_2_ = bf16[2,3,256,128]{3,2,1,0:T(8,128)(2,1)S(1)} collective-permute-done((bf16[2,3,256,128]{3,2,1,0:T(8,128)(2,1)S(1)}, bf16[2,3,256,128]{3,2,1,0:T(8,128)(2,1)S(1)}, u32[]{:S(2)}, u32[]{:S(2)}) %collective-permute-start.40) | collective-permute-done | bytes 393248 | tf_op jit(solution)/shard_map/ppermute | solution.py:838
  398.0 5.5 qkv_grad.3
  406.3 9.9 %qkv_weight_grad.1 = (bf16[2,2,256,384]{3,2,1,0:T(8,128)(2,1)}, bf16[2,2,256,384]{3,2,1,0:T(8,128)(2,1)}, bf16[2,2,256,384]{3,2,1,0:T(8,128)(2,1)}, bf16[2,2,256,384]{3,2,1,0:T(8,128)(2,1)}) custom-call(s32[3]{0:T(128)} %copy-done.20, bf16[256,1024]{1,0:T(8,128)(2,1)} %copy-done.29, bf16[256,1024]{1,0:T(8,128)(2,1)} %copy-done.30, ...), custom_call_target="tpu_custom_call" | custom-call | flops 3221225472 | bytes 14680064 | tf_op jit(solution)/shard_map/qkv_weight_grad/pallas_call | solution.py:763
  416.2 2.3 collective-permute-start.51
  420.3 12.7 %collective-permute-start.54 = (bf16[2,2,256,384]{3,2,1,0:T(8,128)(2,1)}, bf16[2,2,256,384]{3,2,1,0:T(8,128)(2,1)S(1)}, u32[]{:S(2)}, u32[]{:S(2)}) collective-permute-start(bf16[2,2,256,384]{3,2,1,0:T(8,128)(2,1)} %get-tuple-element.221), channel_id=1, source_target_pairs={{0,2},{1,3},{2,0},{3,1},{4,6},{5,7},{6,4},{7,5},{8,10},{9,11},{10,... | collective-permute-start | bytes 2359304 | tf_op jit(solution)/shard_map/ppermute | solution.py:838
  436.8 8.9 %collective-permute-start.52 = (bf16[1,2,256,384]{3,2,1,0:T(8,128)(2,1)}, bf16[1,2,256,384]{3,2,1,0:T(8,128)(2,1)}, u32[]{:S(2)}, u32[]{:S(2)}) collective-permute-start(bf16[1,2,256,384]{3,2,1,0:T(8,128)(2,1)} %add_convert_fusion.10), channel_id=1, source_target_pairs={{0,2},{1,3},{2,0},{3,1},{4,6},{5,7},{6,4},{7,5},{8,10},{9,11},{10,... | collective-permute-start | bytes 1179656 | tf_op jit(solution)/shard_map/ppermute | solution.py:838
  445.7 5.9 %collective-permute-done.54 = bf16[2,2,256,384]{3,2,1,0:T(8,128)(2,1)S(1)} collective-permute-done((bf16[2,2,256,384]{3,2,1,0:T(8,128)(2,1)}, bf16[2,2,256,384]{3,2,1,0:T(8,128)(2,1)S(1)}, u32[]{:S(2)}, u32[]{:S(2)}) %collective-permute-start.54) | collective-permute-done | bytes 786464 | tf_op jit(solution)/shard_map/ppermute | solution.py:838
  451.6 2.1 add_convert_fusion.7
  453.8 3.0 norm_grad.1
  456.8 2.6 concatenate.48
  460.8 9.1 %collective-permute-start.45 = (bf16[2,32,1024]{2,1,0:T(8,128)(2,1)S(1)}, bf16[2,32,1024]{2,1,0:T(8,128)(2,1)S(1)}, u32[]{:S(2)}, u32[]{:S(2)}) collective-permute-start(bf16[2,32,1024]{2,1,0:T(8,128)(2,1)S(1)} %pad_maximum_fusion.3), channel_id=1, source_target_pairs={{0,8},{4,12},{8,0},{12,4},{16,24},{20,28},{24,16},{28,20},{1,9},{5... | collective-permute-start | bytes 393224 | tf_op jit(solution)/shard_map/ppermute | solution.py:838
  473.0 2.0 collective-permute-start.53
  478.5 2.0 collective-permute-start.66
  481.2 3.2 collective-permute-done.53
  484.4 3.5 collective-permute-start.67
  487.9 4.7 collective-permute-done.56
  492.5 2.4 collective-permute-start.47
  495.2 4.2 collective-permute-done.47
  500.1 2.0 collective-permute-start.48
  502.3 2.1 collective-permute-start.49
  504.4 3.0 collective-permute-done.66.refs_2_
  507.4 3.5 collective-permute-start.50
  510.9 8.5 %collective-permute-done.59.refs_1_ = bf16[2,128,384]{2,1,0:T(8,128)(2,1)S(1)} collective-permute-done((bf16[2,128,384]{2,1,0:T(8,128)(2,1)S(1)}, bf16[2,128,384]{2,1,0:T(8,128)(2,1)S(1)}, u32[]{:S(2)}, u32[]{:S(2)}) %collective-permute-start.59) | collective-permute-done | bytes 196640 | tf_op jit(solution)/shard_map/ppermute | solution.py:838
  519.4 3.5 collective-permute-start.61
  522.9 2.3 maximum_bitcast_fusion
  525.2 3.7 place_grads.1
  528.9 7.7 %collective-permute-done.60.refs_2_ = bf16[2,128,384]{2,1,0:T(8,128)(2,1)S(1)} collective-permute-done((bf16[2,128,384]{2,1,0:T(8,128)(2,1)S(1)}, bf16[2,128,384]{2,1,0:T(8,128)(2,1)S(1)}, u32[]{:S(2)}, u32[]{:S(2)}) %collective-permute-start.60) | collective-permute-done | bytes 196640 | tf_op jit(solution)/shard_map/ppermute | solution.py:838
  541.9 9.2 %fusion.45 = f32[64,1024]{1,0:T(8,128)} fusion(bf16[64,6144]{1,0:T(8,128)(2,1)S(1)} %reshape.243, bf16[1024,6144]{1,0:T(8,128)(2,1)} %param.22), kind=kOutput, calls=%fused_computation.140 | convolution fusion | flops 805306368 | bytes 13631488 | tf_op jit(solution)/shard_map/dot_general | solution.py:1112
  554.2 2.3 fusion.19
  559.5 2.3 fusion.11
  (352 shorter events, 82.1 us)
Async XLA Ops:
  1.5 4.1 collective-permute-start
  1.9 13.8 %collective-permute-start.1 = (bf16[2,1,256,1024]{3,2,1,0:T(8,128)(2,1)}, bf16[2,1,256,1024]{3,2,1,0:T(8,128)(2,1)S(1)}, u32[]{:S(2)}, u32[]{:S(2)}) collective-permute-start(bf16[2,1,256,1024]{3,2,1,0:T(8,128)(2,1)} %tokens.9), channel_id=1, source_target_pairs={{0,4},{4,0},{8,12},{12,8},{16,20},{20,16},{24,28},{28,24},{1,5},{5... | collective-permute-start | bytes 3145736 | tf_op jit(solution)/shard_map/ppermute | solution.py:838
  21.6 20.1 %collective-permute-start.2 = (bf16[2,3,256,128]{3,2,1,0:T(8,128)(2,1)S(1)}, bf16[2,3,256,128]{3,2,1,0:T(8,128)(2,1)S(1)}, u32[]{:S(2)}, u32[]{:S(2)}) collective-permute-start(bf16[2,3,256,128]{3,2,1,0:T(8,128)(2,1)S(1)} %get-tuple-element.121), channel_id=1, source_target_pairs={{0,8},{4,12},{8,0},{12,4},{16,24},{20,28},{24,16},{28,20},{1,9},{5... | collective-permute-start | bytes 1179656 | tf_op jit(solution)/shard_map/ppermute | solution.py:838
  24.7 46.7 %collective-permute-start.3 = (bf16[2,3,256,128]{3,2,1,0:T(8,128)(2,1)S(1)}, bf16[2,3,256,128]{3,2,1,0:T(8,128)(2,1)S(1)}, u32[]{:S(2)}, u32[]{:S(2)}) collective-permute-start(bf16[2,3,256,128]{3,2,1,0:T(8,128)(2,1)S(1)} %get-tuple-element.122), channel_id=1, source_target_pairs={{0,16},{4,20},{8,24},{12,28},{16,0},{20,4},{24,8},{28,12},{1,17},{... | collective-permute-start | bytes 1179656 | tf_op jit(solution)/shard_map/ppermute | solution.py:838
  27.2 44.1 %collective-permute-start.4 = (bf16[2,3,256,128]{3,2,1,0:T(8,128)(2,1)S(1)}, bf16[2,3,256,128]{3,2,1,0:T(8,128)(2,1)S(1)}, u32[]{:S(2)}, u32[]{:S(2)}) collective-permute-start(bf16[2,3,256,128]{3,2,1,0:T(8,128)(2,1)S(1)} %get-tuple-element.123), channel_id=1, source_target_pairs={{0,24},{4,28},{8,16},{12,20},{16,8},{20,12},{24,0},{28,4},{1,25},{... | collective-permute-start | bytes 1179656 | tf_op jit(solution)/shard_map/ppermute | solution.py:838
  33.0 74.8 %collective-permute-start.10 = (bf16[2,3,256,128]{3,2,1,0:T(8,128)(2,1)S(1)}, bf16[2,3,256,128]{3,2,1,0:T(8,128)(2,1)S(1)}, u32[]{:S(2)}, u32[]{:S(2)}) collective-permute-start(bf16[2,3,256,128]{3,2,1,0:T(8,128)(2,1)S(1)} %get-tuple-element.131), channel_id=1, source_target_pairs={{0,16},{4,20},{8,24},{12,28},{16,0},{20,4},{24,8},{28,12},{1,17},{... | collective-permute-start | bytes 1179656 | tf_op jit(solution)/shard_map/ppermute | solution.py:838
  34.9 72.8 %collective-permute-start.11 = (bf16[2,3,256,128]{3,2,1,0:T(8,128)(2,1)S(1)}, bf16[2,3,256,128]{3,2,1,0:T(8,128)(2,1)S(1)}, u32[]{:S(2)}, u32[]{:S(2)}) collective-permute-start(bf16[2,3,256,128]{3,2,1,0:T(8,128)(2,1)S(1)} %get-tuple-element.132), channel_id=1, source_target_pairs={{0,24},{4,28},{8,16},{12,20},{16,8},{20,12},{24,0},{28,4},{1,25},{... | collective-permute-start | bytes 1179656 | tf_op jit(solution)/shard_map/ppermute | solution.py:838
  41.8 66.0 %collective-permute-start.9 = (bf16[2,3,256,128]{3,2,1,0:T(8,128)(2,1)S(1)}, bf16[2,3,256,128]{3,2,1,0:T(8,128)(2,1)S(1)}, u32[]{:S(2)}, u32[]{:S(2)}) collective-permute-start(bf16[2,3,256,128]{3,2,1,0:T(8,128)(2,1)S(1)} %get-tuple-element.130), channel_id=1, source_target_pairs={{0,8},{4,12},{8,0},{12,4},{16,24},{20,28},{24,16},{28,20},{1,9},{5... | collective-permute-start | bytes 1179656 | tf_op jit(solution)/shard_map/ppermute | solution.py:838
  87.7 12.7 %collective-permute-start.5 = (bf16[2,256,128]{2,1,0:T(8,128)(2,1)S(1)}, bf16[2,256,128]{2,1,0:T(8,128)(2,1)S(1)}, u32[]{:S(2)}, u32[]{:S(2)}) collective-permute-start(bf16[2,256,128]{2,1,0:T(8,128)(2,1)S(1)} %get-tuple-element.125), channel_id=1, source_target_pairs={{0,8},{4,12},{8,0},{12,4},{16,24},{20,28},{24,16},{28,20},{1,9},{5... | collective-permute-start | bytes 393224 | tf_op jit(solution)/shard_map/ppermute | solution.py:838
  96.7 10.8 %collective-permute-start.6 = (bf16[2,256,128]{2,1,0:T(8,128)(2,1)S(1)}, bf16[2,256,128]{2,1,0:T(8,128)(2,1)S(1)}, u32[]{:S(2)}, u32[]{:S(2)}) collective-permute-start(bf16[2,256,128]{2,1,0:T(8,128)(2,1)S(1)} %get-tuple-element.126), channel_id=1, source_target_pairs={{0,16},{4,20},{8,24},{12,28},{16,0},{20,4},{24,8},{28,12},{1,17},{... | collective-permute-start | bytes 393224 | tf_op jit(solution)/shard_map/ppermute | solution.py:838
  100.5 7.1 %collective-permute-start.7 = (bf16[2,256,128]{2,1,0:T(8,128)(2,1)S(1)}, bf16[2,256,128]{2,1,0:T(8,128)(2,1)S(1)}, u32[]{:S(2)}, u32[]{:S(2)}) collective-permute-start(bf16[2,256,128]{2,1,0:T(8,128)(2,1)S(1)} %get-tuple-element.127), channel_id=1, source_target_pairs={{0,24},{4,28},{8,16},{12,20},{16,8},{20,12},{24,0},{28,4},{1,25},{... | collective-permute-start | bytes 393224 | tf_op jit(solution)/shard_map/ppermute | solution.py:838
  107.7 28.4 %collective-permute-start.8 = (bf16[4,256,128]{2,1,0:T(8,128)(2,1)S(1)}, bf16[4,256,128]{2,1,0:T(8,128)(2,1)S(1)}, u32[]{:S(2)}, u32[]{:S(2)}) collective-permute-start(bf16[4,256,128]{2,1,0:T(8,128)(2,1)S(1)} %pad_maximum_fusion), channel_id=1, source_target_pairs={{0,4},{4,0},{8,12},{12,8},{16,20},{20,16},{24,28},{28,24},{1,5},{5... | collective-permute-start | bytes 786440 | tf_op jit(solution)/shard_map/ppermute | solution.py:838
  121.1 8.3 %collective-permute-start.12 = (bf16[2,256,128]{2,1,0:T(8,128)(2,1)S(1)}, bf16[2,256,128]{2,1,0:T(8,128)(2,1)S(1)}, u32[]{:S(2)}, u32[]{:S(2)}) collective-permute-start(bf16[2,256,128]{2,1,0:T(8,128)(2,1)S(1)} %get-tuple-element.134), channel_id=1, source_target_pairs={{0,8},{4,12},{8,0},{12,4},{16,24},{20,28},{24,16},{28,20},{1,9},{5... | collective-permute-start | bytes 393224 | tf_op jit(solution)/shard_map/ppermute | solution.py:838
  123.0 12.9 %collective-permute-start.13 = (bf16[2,256,128]{2,1,0:T(8,128)(2,1)S(1)}, bf16[2,256,128]{2,1,0:T(8,128)(2,1)S(1)}, u32[]{:S(2)}, u32[]{:S(2)}) collective-permute-start(bf16[2,256,128]{2,1,0:T(8,128)(2,1)S(1)} %get-tuple-element.135), channel_id=1, source_target_pairs={{0,16},{4,20},{8,24},{12,28},{16,0},{20,4},{24,8},{28,12},{1,17},{... | collective-permute-start | bytes 393224 | tf_op jit(solution)/shard_map/ppermute | solution.py:838
  124.3 11.7 %collective-permute-start.14 = (bf16[2,256,128]{2,1,0:T(8,128)(2,1)S(1)}, bf16[2,256,128]{2,1,0:T(8,128)(2,1)S(1)}, u32[]{:S(2)}, u32[]{:S(2)}) collective-permute-start(bf16[2,256,128]{2,1,0:T(8,128)(2,1)S(1)} %get-tuple-element.136), channel_id=1, source_target_pairs={{0,24},{4,28},{8,16},{12,20},{16,8},{20,12},{24,0},{28,4},{1,25},{... | collective-permute-start | bytes 393224 | tf_op jit(solution)/shard_map/ppermute | solution.py:838
  136.0 22.6 %collective-permute-start.15 = (bf16[4,256,128]{2,1,0:T(8,128)(2,1)S(1)}, bf16[4,256,128]{2,1,0:T(8,128)(2,1)S(1)}, u32[]{:S(2)}, u32[]{:S(2)}) collective-permute-start(bf16[4,256,128]{2,1,0:T(8,128)(2,1)S(1)} %pad_maximum_fusion.1), channel_id=1, source_target_pairs={{0,4},{4,0},{8,12},{12,8},{16,20},{20,16},{24,28},{28,24},{1,5},{5... | collective-permute-start | bytes 786440 | tf_op jit(solution)/shard_map/ppermute | solution.py:838
  158.1 36.0 %collective-permute-start.18 = (bf16[256,4096]{1,0:T(8,128)(2,1)}, bf16[256,4096]{1,0:T(8,128)(2,1)}, u32[]{:S(2)}, u32[]{:S(2)}) collective-permute-start(bf16[256,4096]{1,0:T(8,128)(2,1)} %get-tuple-element.142.refs_4_), channel_id=1, source_target_pairs={{0,4},{4,0},{8,12},{12,8},{16,20},{20,16},{24,28},{28,24},{1,5},{5... | collective-permute-start | bytes 6291464 | tf_op jit(solution)/shard_map/ppermute | solution.py:838
  180.8 13.3 %collective-permute-start.19 = (bf16[256,4096]{1,0:T(8,128)(2,1)}, bf16[256,4096]{1,0:T(8,128)(2,1)}, u32[]{:S(2)}, u32[]{:S(2)}) collective-permute-start(bf16[256,4096]{1,0:T(8,128)(2,1)} %get-tuple-element.143.refs_6_), channel_id=1, source_target_pairs={{0,4},{4,0},{8,12},{12,8},{16,20},{20,16},{24,28},{28,24},{1,5},{5... | collective-permute-start | bytes 6291464 | tf_op jit(solution)/shard_map/ppermute | solution.py:838
  180.9 4.5 collective-permute-start.16
  181.4 6.9 %collective-permute-start.22 = (bf16[256,1024]{1,0:T(8,128)(2,1)}, bf16[256,1024]{1,0:T(8,128)(2,1)S(1)}, u32[]{:S(2)}, u32[]{:S(2)}) collective-permute-start(bf16[256,1024]{1,0:T(8,128)(2,1)} %get-tuple-element.148.refs_12_), channel_id=1, source_target_pairs={{0,4},{4,0},{8,12},{12,8},{16,20},{20,16},{24,28},{28,24},{1,5},{5... | collective-permute-start | bytes 1572872 | tf_op jit(solution)/shard_map/ppermute | solution.py:838
  181.5 7.2 %collective-permute-start.24 = (bf16[256,1024]{1,0:T(8,128)(2,1)S(1)}, bf16[256,1024]{1,0:T(8,128)(2,1)S(1)}, u32[]{:S(2)}, u32[]{:S(2)}) collective-permute-start(bf16[256,1024]{1,0:T(8,128)(2,1)S(1)} %copy-done.11), channel_id=1, source_target_pairs={{0,4},{4,0},{8,12},{12,8},{16,20},{20,16},{24,28},{28,24},{1,5},{5... | collective-permute-start | bytes 1572872 | tf_op jit(solution)/shard_map/ppermute | solution.py:838
  188.3 5.7 %collective-permute-start.20 = (bf16[256,2048]{1,0:T(8,128)(2,1)}, bf16[256,2048]{1,0:T(8,128)(2,1)}, u32[]{:S(2)}, u32[]{:S(2)}) collective-permute-start(bf16[256,2048]{1,0:T(8,128)(2,1)} %get-tuple-element.145), channel_id=1, source_target_pairs={{0,4},{4,0},{8,12},{12,8},{16,20},{20,16},{24,28},{28,24},{1,5},{5... | collective-permute-start | bytes 3145736 | tf_op jit(solution)/shard_map/ppermute | solution.py:838
  188.7 5.4 collective-permute-start.21
  232.0 58.4 %collective-permute-start.27 = (bf16[2,2,1152,256]{3,2,1,0:T(8,128)(2,1)}, bf16[2,2,1152,256]{3,2,1,0:T(8,128)(2,1)S(1)}, u32[]{:S(2)}, u32[]{:S(2)}) collective-permute-start(bf16[2,2,1152,256]{3,2,1,0:T(8,128)(2,1)} %get-tuple-element.168), channel_id=1, source_target_pairs={{0,2},{1,3},{2,0},{3,1},{4,6},{5,7},{6,4},{7,5},{8,10},{9,11},{10,... | collective-permute-start | bytes 7077896 | tf_op jit(solution)/shard_map/ppermute | solution.py:838
  240.7 8.1 %collective-permute-start.28 = (bf16[2,256,128]{2,1,0:T(8,128)(2,1)S(1)}, bf16[2,256,128]{2,1,0:T(8,128)(2,1)S(1)}, u32[]{:S(2)}, u32[]{:S(2)}) collective-permute-start(bf16[2,256,128]{2,1,0:T(8,128)(2,1)S(1)} %get-tuple-element.171), channel_id=1, source_target_pairs={{0,8},{4,12},{8,0},{12,4},{16,24},{20,28},{24,16},{28,20},{1,9},{5... | collective-permute-start | bytes 393224 | tf_op jit(solution)/shard_map/ppermute | solution.py:838
  243.3 12.9 %collective-permute-start.29 = (bf16[2,256,128]{2,1,0:T(8,128)(2,1)S(1)}, bf16[2,256,128]{2,1,0:T(8,128)(2,1)S(1)}, u32[]{:S(2)}, u32[]{:S(2)}) collective-permute-start(bf16[2,256,128]{2,1,0:T(8,128)(2,1)S(1)} %get-tuple-element.172), channel_id=1, source_target_pairs={{0,16},{4,20},{8,24},{12,28},{16,0},{20,4},{24,8},{28,12},{1,17},{... | collective-permute-start | bytes 393224 | tf_op jit(solution)/shard_map/ppermute | solution.py:838
  244.5 14.4 %collective-permute-start.30 = (bf16[2,256,128]{2,1,0:T(8,128)(2,1)S(1)}, bf16[2,256,128]{2,1,0:T(8,128)(2,1)S(1)}, u32[]{:S(2)}, u32[]{:S(2)}) collective-permute-start(bf16[2,256,128]{2,1,0:T(8,128)(2,1)S(1)} %get-tuple-element.173), channel_id=1, source_target_pairs={{0,24},{4,28},{8,16},{12,20},{16,8},{20,12},{24,0},{28,4},{1,25},{... | collective-permute-start | bytes 393224 | tf_op jit(solution)/shard_map/ppermute | solution.py:838
  247.8 71.7 %collective-permute-start.36 = (bf16[2,256,128]{2,1,0:T(8,128)(2,1)S(1)}, bf16[2,256,128]{2,1,0:T(8,128)(2,1)S(1)}, u32[]{:S(2)}, u32[]{:S(2)}) collective-permute-start(bf16[2,256,128]{2,1,0:T(8,128)(2,1)S(1)} %get-tuple-element.188), channel_id=1, source_target_pairs={{0,8},{4,12},{8,0},{12,4},{16,24},{20,28},{24,16},{28,20},{1,9},{5... | collective-permute-start | bytes 393224 | tf_op jit(solution)/shard_map/ppermute | solution.py:838
  248.8 70.7 %collective-permute-start.37 = (bf16[2,256,128]{2,1,0:T(8,128)(2,1)S(1)}, bf16[2,256,128]{2,1,0:T(8,128)(2,1)S(1)}, u32[]{:S(2)}, u32[]{:S(2)}) collective-permute-start(bf16[2,256,128]{2,1,0:T(8,128)(2,1)S(1)} %get-tuple-element.189), channel_id=1, source_target_pairs={{0,16},{4,20},{8,24},{12,28},{16,0},{20,4},{24,8},{28,12},{1,17},{... | collective-permute-start | bytes 393224 | tf_op jit(solution)/shard_map/ppermute | solution.py:838
  256.3 63.5 %collective-permute-start.38 = (bf16[2,256,128]{2,1,0:T(8,128)(2,1)S(1)}, bf16[2,256,128]{2,1,0:T(8,128)(2,1)S(1)}, u32[]{:S(2)}, u32[]{:S(2)}) collective-permute-start(bf16[2,256,128]{2,1,0:T(8,128)(2,1)S(1)} %get-tuple-element.190), channel_id=1, source_target_pairs={{0,24},{4,28},{8,16},{12,20},{16,8},{20,12},{24,0},{28,4},{1,25},{... | collective-permute-start | bytes 393224 | tf_op jit(solution)/shard_map/ppermute | solution.py:838
  258.9 50.1 %collective-permute-start.26 = (bf16[2,2,1152,256]{3,2,1,0:T(8,128)(2,1)}, bf16[2,2,1152,256]{3,2,1,0:T(8,128)(2,1)}, u32[]{:S(2)}, u32[]{:S(2)}) collective-permute-start(bf16[2,2,1152,256]{3,2,1,0:T(8,128)(2,1)} %get-tuple-element.166), channel_id=1, source_target_pairs={{0,1},{1,0},{2,3},{3,2},{4,5},{5,4},{6,7},{7,6},{8,9},{9,8},{10,11... | collective-permute-start | bytes 7077896 | tf_op jit(solution)/shard_map/ppermute | solution.py:838
  290.4 53.7 %collective-permute-start.31 = (bf16[2,3,256,128]{3,2,1,0:T(8,128)(2,1)S(1)}, bf16[2,3,256,128]{3,2,1,0:T(8,128)(2,1)S(1)}, u32[]{:S(2)}, u32[]{:S(2)}) collective-permute-start(bf16[2,3,256,128]{3,2,1,0:T(8,128)(2,1)S(1)} %get-tuple-element.177), channel_id=1, source_target_pairs={{0,8},{4,12},{8,0},{12,4},{16,24},{20,28},{24,16},{28,20},{1,9},{5... | collective-permute-start | bytes 1179656 | tf_op jit(solution)/shard_map/ppermute | solution.py:838
  309.0 35.8 %collective-permute-start.32 = (bf16[2,3,256,128]{3,2,1,0:T(8,128)(2,1)S(1)}, bf16[2,3,256,128]{3,2,1,0:T(8,128)(2,1)S(1)}, u32[]{:S(2)}, u32[]{:S(2)}) collective-permute-start(bf16[2,3,256,128]{3,2,1,0:T(8,128)(2,1)S(1)} %get-tuple-element.178), channel_id=1, source_target_pairs={{0,16},{4,20},{8,24},{12,28},{16,0},{20,4},{24,8},{28,12},{1,17},{... | collective-permute-start | bytes 1179656 | tf_op jit(solution)/shard_map/ppermute | solution.py:838
  319.5 29.1 %collective-permute-start.33 = (bf16[2,3,256,128]{3,2,1,0:T(8,128)(2,1)S(1)}, bf16[2,3,256,128]{3,2,1,0:T(8,128)(2,1)S(1)}, u32[]{:S(2)}, u32[]{:S(2)}) collective-permute-start(bf16[2,3,256,128]{3,2,1,0:T(8,128)(2,1)S(1)} %get-tuple-element.179), channel_id=1, source_target_pairs={{0,24},{4,28},{8,16},{12,20},{16,8},{20,12},{24,0},{28,4},{1,25},{... | collective-permute-start | bytes 1179656 | tf_op jit(solution)/shard_map/ppermute | solution.py:838
  319.5 35.5 %collective-permute-start.35 = (bf16[1,2,1152,256]{3,2,1,0:T(8,128)(2,1)}, bf16[1,2,1152,256]{3,2,1,0:T(8,128)(2,1)S(1)}, u32[]{:S(2)}, u32[]{:S(2)}) collective-permute-start(bf16[1,2,1152,256]{3,2,1,0:T(8,128)(2,1)} %get-tuple-element.185), channel_id=1, source_target_pairs={{0,1},{1,0},{2,3},{3,2},{4,5},{5,4},{6,7},{7,6},{8,9},{9,8},{10,11... | collective-permute-start | bytes 3538952 | tf_op jit(solution)/shard_map/ppermute | solution.py:838
  319.8 35.5 %collective-permute-start.34 = (bf16[1,2,1152,256]{3,2,1,0:T(8,128)(2,1)}, bf16[1,2,1152,256]{3,2,1,0:T(8,128)(2,1)S(1)}, u32[]{:S(2)}, u32[]{:S(2)}) collective-permute-start(bf16[1,2,1152,256]{3,2,1,0:T(8,128)(2,1)} %get-tuple-element.183), channel_id=1, source_target_pairs={{0,2},{1,3},{2,0},{3,1},{4,6},{5,7},{6,4},{7,5},{8,10},{9,11},{10,... | collective-permute-start | bytes 3538952 | tf_op jit(solution)/shard_map/ppermute | solution.py:838
  344.1 15.4 %collective-permute-start.39 = (bf16[2,3,256,128]{3,2,1,0:T(8,128)(2,1)S(1)}, bf16[2,3,256,128]{3,2,1,0:T(8,128)(2,1)S(1)}, u32[]{:S(2)}, u32[]{:S(2)}) collective-permute-start(bf16[2,3,256,128]{3,2,1,0:T(8,128)(2,1)S(1)} %get-tuple-element.194), channel_id=1, source_target_pairs={{0,8},{4,12},{8,0},{12,4},{16,24},{20,28},{24,16},{28,20},{1,9},{5... | collective-permute-start | bytes 1179656 | tf_op jit(solution)/shard_map/ppermute | solution.py:838
  344.8 53.2 %collective-permute-start.40 = (bf16[2,3,256,128]{3,2,1,0:T(8,128)(2,1)S(1)}, bf16[2,3,256,128]{3,2,1,0:T(8,128)(2,1)S(1)}, u32[]{:S(2)}, u32[]{:S(2)}) collective-permute-start(bf16[2,3,256,128]{3,2,1,0:T(8,128)(2,1)S(1)} %get-tuple-element.195), channel_id=1, source_target_pairs={{0,16},{4,20},{8,24},{12,28},{16,0},{20,4},{24,8},{28,12},{1,17},{... | collective-permute-start | bytes 1179656 | tf_op jit(solution)/shard_map/ppermute | solution.py:838
  348.5 49.5 %collective-permute-start.41 = (bf16[2,3,256,128]{3,2,1,0:T(8,128)(2,1)S(1)}, bf16[2,3,256,128]{3,2,1,0:T(8,128)(2,1)S(1)}, u32[]{:S(2)}, u32[]{:S(2)}) collective-permute-start(bf16[2,3,256,128]{3,2,1,0:T(8,128)(2,1)S(1)} %get-tuple-element.196), channel_id=1, source_target_pairs={{0,24},{4,28},{8,16},{12,20},{16,8},{20,12},{24,0},{28,4},{1,25},{... | collective-permute-start | bytes 1179656 | tf_op jit(solution)/shard_map/ppermute | solution.py:838
  355.0 98.7 %collective-permute-start.42 = (f32[256,1024]{1,0:T(8,128)}, f32[256,1024]{1,0:T(8,128)S(1)}, u32[]{:S(2)}, u32[]{:S(2)}) collective-permute-start(f32[256,1024]{1,0:T(8,128)} %get-tuple-element.198), channel_id=1, source_target_pairs={{0,4},{4,0},{8,12},{12,8},{16,20},{20,16},{24,28},{28,24},{1,5},{5... | collective-permute-start | bytes 3145736 | tf_op jit(solution)/shard_map/ppermute | solution.py:838
  357.2 63.1 %collective-permute-start.63 = (bf16[1152,256]{1,0:T(8,128)(2,1)}, bf16[1152,256]{1,0:T(8,128)(2,1)}, u32[]{:S(2)}, u32[]{:S(2)}) collective-permute-start(bf16[1152,256]{1,0:T(8,128)(2,1)} %get-tuple-element.261), channel_id=1, source_target_pairs={{0,16},{4,20},{8,24},{12,28},{16,0},{20,4},{24,8},{28,12},{1,17},{... | collective-permute-start | bytes 1769480 | tf_op jit(solution)/shard_map/ppermute | solution.py:838
  359.5 60.8 %collective-permute-start.64 = (bf16[1152,256]{1,0:T(8,128)(2,1)}, bf16[1152,256]{1,0:T(8,128)(2,1)}, u32[]{:S(2)}, u32[]{:S(2)}) collective-permute-start(bf16[1152,256]{1,0:T(8,128)(2,1)} %get-tuple-element.262), channel_id=1, source_target_pairs={{0,24},{4,28},{8,16},{12,20},{16,8},{20,12},{24,0},{28,4},{1,25},{... | collective-permute-start | bytes 1769480 | tf_op jit(solution)/shard_map/ppermute | solution.py:838
  398.0 35.0 %collective-permute-start.62 = (bf16[1152,256]{1,0:T(8,128)(2,1)}, bf16[1152,256]{1,0:T(8,128)(2,1)}, u32[]{:S(2)}, u32[]{:S(2)}) collective-permute-start(bf16[1152,256]{1,0:T(8,128)(2,1)} %slice_bitcast_fusion.2), channel_id=1, source_target_pairs={{0,8},{4,12},{8,0},{12,4},{16,24},{20,28},{24,16},{28,20},{1,9},{5... | collective-permute-start | bytes 1769480 | tf_op jit(solution)/shard_map/ppermute | solution.py:838
  416.2 18.8 %collective-permute-start.51 = (bf16[2,2,256,384]{3,2,1,0:T(8,128)(2,1)}, bf16[2,2,256,384]{3,2,1,0:T(8,128)(2,1)}, u32[]{:S(2)}, u32[]{:S(2)}) collective-permute-start(bf16[2,2,256,384]{3,2,1,0:T(8,128)(2,1)} %get-tuple-element.219), channel_id=1, source_target_pairs={{0,1},{1,0},{2,3},{3,2},{4,5},{5,4},{6,7},{7,6},{8,9},{9,8},{10,11... | collective-permute-start | bytes 2359304 | tf_op jit(solution)/shard_map/ppermute | solution.py:838
  420.3 33.5 %collective-permute-start.43 = (f32[256,1024]{1,0:T(8,128)}, f32[256,1024]{1,0:T(8,128)S(1)}, u32[]{:S(2)}, u32[]{:S(2)}) collective-permute-start(f32[256,1024]{1,0:T(8,128)} %get-tuple-element.199), channel_id=1, source_target_pairs={{0,4},{4,0},{8,12},{12,8},{16,20},{20,16},{24,28},{28,24},{1,5},{5... | collective-permute-start | bytes 3145736 | tf_op jit(solution)/shard_map/ppermute | solution.py:838
  420.3 31.3 %collective-permute-start.54 = (bf16[2,2,256,384]{3,2,1,0:T(8,128)(2,1)}, bf16[2,2,256,384]{3,2,1,0:T(8,128)(2,1)S(1)}, u32[]{:S(2)}, u32[]{:S(2)}) collective-permute-start(bf16[2,2,256,384]{3,2,1,0:T(8,128)(2,1)} %get-tuple-element.221), channel_id=1, source_target_pairs={{0,2},{1,3},{2,0},{3,1},{4,6},{5,7},{6,4},{7,5},{8,10},{9,11},{10,... | collective-permute-start | bytes 2359304 | tf_op jit(solution)/shard_map/ppermute | solution.py:838
  434.9 67.4 %collective-permute-start.65 = (bf16[1152,256]{1,0:T(8,128)(2,1)S(1)}, bf16[1152,256]{1,0:T(8,128)(2,1)}, u32[]{:S(2)}, u32[]{:S(2)}) collective-permute-start(bf16[1152,256]{1,0:T(8,128)(2,1)S(1)} %fusion.4.refs_0_), channel_id=1, source_target_pairs={{0,1},{1,0},{2,3},{3,2},{4,5},{5,4},{6,7},{7,6},{8,9},{9,8},{10,11... | collective-permute-start | bytes 1769480 | tf_op jit(solution)/shard_map/ppermute | solution.py:838
  436.8 34.8 %collective-permute-start.52 = (bf16[1,2,256,384]{3,2,1,0:T(8,128)(2,1)}, bf16[1,2,256,384]{3,2,1,0:T(8,128)(2,1)}, u32[]{:S(2)}, u32[]{:S(2)}) collective-permute-start(bf16[1,2,256,384]{3,2,1,0:T(8,128)(2,1)} %add_convert_fusion.10), channel_id=1, source_target_pairs={{0,2},{1,3},{2,0},{3,1},{4,6},{5,7},{6,4},{7,5},{8,10},{9,11},{10,... | collective-permute-start | bytes 1179656 | tf_op jit(solution)/shard_map/ppermute | solution.py:838
  453.7 21.3 %collective-permute-start.55 = (bf16[1,2,256,384]{3,2,1,0:T(8,128)(2,1)}, bf16[1,2,256,384]{3,2,1,0:T(8,128)(2,1)S(1)}, u32[]{:S(2)}, u32[]{:S(2)}) collective-permute-start(bf16[1,2,256,384]{3,2,1,0:T(8,128)(2,1)} %add_convert_fusion.7), channel_id=1, source_target_pairs={{0,1},{1,0},{2,3},{3,2},{4,5},{5,4},{6,7},{7,6},{8,9},{9,8},{10,11... | collective-permute-start | bytes 1179656 | tf_op jit(solution)/shard_map/ppermute | solution.py:838
  460.8 15.2 %collective-permute-start.45 = (bf16[2,32,1024]{2,1,0:T(8,128)(2,1)S(1)}, bf16[2,32,1024]{2,1,0:T(8,128)(2,1)S(1)}, u32[]{:S(2)}, u32[]{:S(2)}) collective-permute-start(bf16[2,32,1024]{2,1,0:T(8,128)(2,1)S(1)} %pad_maximum_fusion.3), channel_id=1, source_target_pairs={{0,8},{4,12},{8,0},{12,4},{16,24},{20,28},{24,16},{28,20},{1,9},{5... | collective-permute-start | bytes 393224 | tf_op jit(solution)/shard_map/ppermute | solution.py:838
  469.9 8.6 %collective-permute-start.46 = (bf16[2,32,1024]{2,1,0:T(8,128)(2,1)S(1)}, bf16[2,32,1024]{2,1,0:T(8,128)(2,1)S(1)}, u32[]{:S(2)}, u32[]{:S(2)}) collective-permute-start(bf16[2,32,1024]{2,1,0:T(8,128)(2,1)S(1)} %pad_maximum_fusion.3), channel_id=1, source_target_pairs={{0,16},{4,20},{8,24},{12,28},{16,0},{20,4},{24,8},{28,12},{1,17},{... | collective-permute-start | bytes 393224 | tf_op jit(solution)/shard_map/ppermute | solution.py:838
  473.0 11.4 %collective-permute-start.53 = (bf16[256,384]{1,0:T(8,128)(2,1)S(1)}, bf16[256,384]{1,0:T(8,128)(2,1)S(1)}, u32[]{:S(2)}, u32[]{:S(2)}) collective-permute-start(bf16[256,384]{1,0:T(8,128)(2,1)S(1)} %slice_bitcast_fusion.5), channel_id=1, source_target_pairs={{0,8},{4,12},{8,0},{12,4},{16,24},{20,28},{24,16},{28,20},{1,9},{5... | collective-permute-start | bytes 589832 | tf_op jit(solution)/shard_map/ppermute | solution.py:838
  475.3 17.3 %collective-permute-start.56 = (bf16[256,384]{1,0:T(8,128)(2,1)S(1)}, bf16[256,384]{1,0:T(8,128)(2,1)S(1)}, u32[]{:S(2)}, u32[]{:S(2)}) collective-permute-start(bf16[256,384]{1,0:T(8,128)(2,1)S(1)} %get-tuple-element.263), channel_id=1, source_target_pairs={{0,16},{4,20},{8,24},{12,28},{16,0},{20,4},{24,8},{28,12},{1,17},{... | collective-permute-start | bytes 589832 | tf_op jit(solution)/shard_map/ppermute | solution.py:838
  476.1 18.9 %collective-permute-start.57 = (bf16[256,384]{1,0:T(8,128)(2,1)S(1)}, bf16[256,384]{1,0:T(8,128)(2,1)S(1)}, u32[]{:S(2)}, u32[]{:S(2)}) collective-permute-start(bf16[256,384]{1,0:T(8,128)(2,1)S(1)} %get-tuple-element.264), channel_id=1, source_target_pairs={{0,24},{4,28},{8,16},{12,20},{16,8},{20,12},{24,0},{28,4},{1,25},{... | collective-permute-start | bytes 589832 | tf_op jit(solution)/shard_map/ppermute | solution.py:838
  478.5 28.9 %collective-permute-start.66 = (bf16[1152,256]{1,0:T(8,128)(2,1)S(1)}, bf16[1152,256]{1,0:T(8,128)(2,1)S(1)}, u32[]{:S(2)}, u32[]{:S(2)}) collective-permute-start(bf16[1152,256]{1,0:T(8,128)(2,1)S(1)} %fusion.4.refs_0_), channel_id=1, source_target_pairs={{0,2},{1,3},{2,0},{3,1},{4,6},{5,7},{6,4},{7,5},{8,10},{9,11},{10,... | collective-permute-start | bytes 1769480 | tf_op jit(solution)/shard_map/ppermute | solution.py:838
  484.4 26.5 %collective-permute-start.67 = (bf16[1152,256]{1,0:T(8,128)(2,1)S(1)}, bf16[1152,256]{1,0:T(8,128)(2,1)S(1)}, u32[]{:S(2)}, u32[]{:S(2)}) collective-permute-start(bf16[1152,256]{1,0:T(8,128)(2,1)S(1)} %fusion.4.refs_0_), channel_id=1, source_target_pairs={{0,3},{1,2},{2,1},{3,0},{4,7},{5,6},{6,5},{7,4},{8,11},{9,10},{10,... | collective-permute-start | bytes 1769480 | tf_op jit(solution)/shard_map/ppermute | solution.py:838
  492.5 6.9 %collective-permute-start.47 = (bf16[2,32,1024]{2,1,0:T(8,128)(2,1)S(1)}, bf16[2,32,1024]{2,1,0:T(8,128)(2,1)S(1)}, u32[]{:S(2)}, u32[]{:S(2)}) collective-permute-start(bf16[2,32,1024]{2,1,0:T(8,128)(2,1)S(1)} %pad_maximum_fusion.3), channel_id=1, source_target_pairs={{0,24},{4,28},{8,16},{12,20},{16,8},{20,12},{24,0},{28,4},{1,25},{... | collective-permute-start | bytes 393224 | tf_op jit(solution)/shard_map/ppermute | solution.py:838
  495.1 7.1 %collective-permute-start.58 = (bf16[128,384]{1,0:T(8,128)(2,1)S(1)}, bf16[128,384]{1,0:T(8,128)(2,1)S(1)}, u32[]{:S(2)}, u32[]{:S(2)}) collective-permute-start(bf16[128,384]{1,0:T(8,128)(2,1)S(1)} %get-tuple-element.266), channel_id=1, source_target_pairs={{0,4},{4,0},{8,12},{12,8},{16,20},{20,16},{24,28},{28,24},{1,5},{5... | collective-permute-start | bytes 294920 | tf_op jit(solution)/shard_map/ppermute | solution.py:838
  500.1 38.3 %collective-permute-start.48 = (bf16[8,32,1024]{2,1,0:T(8,128)(2,1)}, bf16[8,32,1024]{2,1,0:T(8,128)(2,1)S(1)}, u32[]{:S(2)}, u32[]{:S(2)}) collective-permute-start(bf16[8,32,1024]{2,1,0:T(8,128)(2,1)} %get-tuple-element.269), channel_id=1, source_target_pairs={{0,1},{1,0},{2,3},{3,2},{4,5},{5,4},{6,7},{7,6},{8,9},{9,8},{10,11... | collective-permute-start | bytes 1572872 | tf_op jit(solution)/shard_map/ppermute | solution.py:838
  502.2 17.2 %collective-permute-start.59 = (bf16[2,128,384]{2,1,0:T(8,128)(2,1)S(1)}, bf16[2,128,384]{2,1,0:T(8,128)(2,1)S(1)}, u32[]{:S(2)}, u32[]{:S(2)}) collective-permute-start(bf16[2,128,384]{2,1,0:T(8,128)(2,1)S(1)} %pad_maximum_fusion.2.refs_0_), channel_id=1, source_target_pairs={{0,1},{1,0},{2,3},{3,2},{4,5},{5,4},{6,7},{7,6},{8,9},{9,8},{10,11... | collective-permute-start | bytes 589832 | tf_op jit(solution)/shard_map/ppermute | solution.py:838
  502.3 36.3 %collective-permute-start.49 = (bf16[8,32,1024]{2,1,0:T(8,128)(2,1)}, bf16[8,32,1024]{2,1,0:T(8,128)(2,1)S(1)}, u32[]{:S(2)}, u32[]{:S(2)}) collective-permute-start(bf16[8,32,1024]{2,1,0:T(8,128)(2,1)} %get-tuple-element.269), channel_id=1, source_target_pairs={{0,2},{1,3},{2,0},{3,1},{4,6},{5,7},{6,4},{7,5},{8,10},{9,11},{10,... | collective-permute-start | bytes 1572872 | tf_op jit(solution)/shard_map/ppermute | solution.py:838
  507.4 31.2 %collective-permute-start.50 = (bf16[8,32,1024]{2,1,0:T(8,128)(2,1)}, bf16[8,32,1024]{2,1,0:T(8,128)(2,1)}, u32[]{:S(2)}, u32[]{:S(2)}) collective-permute-start(bf16[8,32,1024]{2,1,0:T(8,128)(2,1)} %get-tuple-element.269), channel_id=1, source_target_pairs={{0,3},{1,2},{2,1},{3,0},{4,7},{5,6},{6,5},{7,4},{8,11},{9,10},{10,... | collective-permute-start | bytes 1572872 | tf_op jit(solution)/shard_map/ppermute | solution.py:838
  510.9 25.7 %collective-permute-start.60 = (bf16[2,128,384]{2,1,0:T(8,128)(2,1)S(1)}, bf16[2,128,384]{2,1,0:T(8,128)(2,1)S(1)}, u32[]{:S(2)}, u32[]{:S(2)}) collective-permute-start(bf16[2,128,384]{2,1,0:T(8,128)(2,1)S(1)} %pad_maximum_fusion.2.refs_0_), channel_id=1, source_target_pairs={{0,2},{1,3},{2,0},{3,1},{4,6},{5,7},{6,4},{7,5},{8,10},{9,11},{10,... | collective-permute-start | bytes 589832 | tf_op jit(solution)/shard_map/ppermute | solution.py:838
  519.4 17.2 %collective-permute-start.61 = (bf16[2,128,384]{2,1,0:T(8,128)(2,1)S(1)}, bf16[2,128,384]{2,1,0:T(8,128)(2,1)S(1)}, u32[]{:S(2)}, u32[]{:S(2)}) collective-permute-start(bf16[2,128,384]{2,1,0:T(8,128)(2,1)S(1)} %pad_maximum_fusion.2.refs_0_), channel_id=1, source_target_pairs={{0,3},{1,2},{2,1},{3,0},{4,7},{5,6},{6,5},{7,4},{8,11},{9,10},{10,... | collective-permute-start | bytes 589832 | tf_op jit(solution)/shard_map/ppermute | solution.py:838
  (82 other events, 1737.3 us)

commit v3 on v2

--- a/solution.py
+++ b/solution.py
@@ -17,9 +17,11 @@
 SMEM = pl.BlockSpec(memory_space=pltpu.SMEM)
 LANES = 128
 BLOCK = 256
-FF_BLOCK = 512
+FF_BLOCK = 1024
+IN_FLIGHT = 3
 GELU_A = 0.7978845608028654
 GELU_B = 0.044715
+WEIGHT = 1.0
 
 
 def shaped(shape, dtype):
@@ -32,7 +34,9 @@
 
 def cost(flops, moved, transcendentals=0):
     return pl.CostEstimate(
-        flops=int(flops), bytes_accessed=int(moved), transcendentals=int(transcendentals)
+        flops=int(flops * WEIGHT),
+        bytes_accessed=int(moved * WEIGHT),
+        transcendentals=int(transcendentals * WEIGHT),
     )
 
 
@@ -127,78 +131,77 @@
     return specs
 
 
-def qkv_kernel(zs, head, clip, meta, tokens, other_tokens, mod, cosine, sine, *refs):
+def qkv_kernel(zs, head, meta, tokens, other_tokens, mod, cosine, sine, *refs):
     blocks = tokens.shape[-1] // (2 * LANES)
     weights, biases = refs[: 3 * blocks], refs[3 * blocks : 6 * blocks]
-    outs, normed_outs, (normed, held) = refs[6 * blocks : 6 * blocks + zs], refs[-4:-2], refs[-2:]
-    rows, width = tokens.shape[-2:]
+    outs = refs[6 * blocks : 6 * blocks + zs]
+    normed_outs, (normed, held) = refs[6 * blocks + zs : -2], refs[-2:]
+    clips, _, rows, width = tokens.shape
     lanes = width // (2 * zs)
-    clips = mod.shape[0] // 2
     z = meta[0] // 2
-    for role, source in enumerate((tokens, other_tokens)):
-        row = role * clips + clip
-        hat, _ = norm_parts(source[...].reshape(rows, width).astype(F32))
+    for row in range(2 * clips):
+        role, clip = row // clips, row % clips
+        source = (tokens, other_tokens)[role]
+        hat, _ = norm_parts(source[clip, 0].astype(F32))
         low = (hat * (1.0 + mod[row, 1:2]) + mod[row, 0:1]).astype(BF16)
-        normed[role * rows : (role + 1) * rows] = low
-        normed_outs[role][...] = low
+        normed[row * rows : (row + 1) * rows] = low
+        normed_outs[row][...] = low
     for kind in range(3):
         pick = slice(kind * blocks, (kind + 1) * blocks)
         weight = jnp.concatenate([w[...] for w in weights[pick]], axis=1)
         bias = jnp.concatenate([b[...] for b in biases[pick]], axis=1).astype(F32)
-        for role in range(2):
-            row = role * clips + clip
-            value = dot_nn(normed[role * rows : (role + 1) * rows], weight) + bias
+        value = dot_nn(normed[...], weight) + bias
+        for row in range(2 * clips):
+            role, clip = row // clips, row % clips
+            part = value[row * rows : (row + 1) * rows]
             if kind < 2:
-                value = turn(value, cosine[row], sine[row], head, False)
-            value = value.astype(BF16)
+                part = turn(part, cosine[row], sine[row], head, False)
+            part = part.astype(BF16)
             if kind == 0:
-                value = value * jnp.asarray(head**-0.5, BF16)
+                part = part * jnp.asarray(head**-0.5, BF16)
             for group in range(zs):
-                held[group ^ z, role, kind] = value[:, group * lanes : (group + 1) * lanes]
+                held[group ^ z, clip, role, kind] = part[:, group * lanes : (group + 1) * lanes]
     for slot in range(zs):
         outs[slot][...] = held[slot]
 
 
-def qkv_call(meta, clip, tokens, other_tokens, mod, cosine, sine, weight, bias, zs, head, aligned):
-    rows, width = tokens.shape[-2:]
+def qkv_call(meta, tokens, other_tokens, mod, cosine, sine, weight, bias, zs, head, aligned):
+    clips, _, rows, width = tokens.shape
     lanes = width // (2 * zs)
-    whole = lambda a: pl.BlockSpec(a.shape, lambda t, m: (0,) * a.ndim)
+    whole = lambda shape: pl.BlockSpec(shape, lambda t, m: (0,) * len(shape))
     blocks = width // (2 * LANES)
-    flat = pl.BlockSpec((rows, width), lambda t, m: (0, 0))
+    message = (clips, 2, 3, rows, lanes)
+    out_shape = [shaped(message, BF16)] * zs + [shaped((rows, width), BF16)] * (2 * clips)
     return pl.pallas_call(
-        functools.partial(qkv_kernel, zs, head, clip),
-        out_shape=[shaped((2, 3, rows, lanes), BF16)] * zs + [shaped((rows, width), BF16)] * 2,
+        functools.partial(qkv_kernel, zs, head),
+        out_shape=out_shape,
         grid_spec=pltpu.PrefetchScalarGridSpec(
             num_scalar_prefetch=1,
             grid=(1,),
-            in_specs=[
-                pl.BlockSpec((1, 1, rows, width), lambda t, m: (clip, 0, 0, 0)),
-                pl.BlockSpec((1, 1, rows, width), lambda t, m: (clip, 0, 0, 0)),
-                whole(mod),
-                whole(cosine),
-                whole(sine),
-            ]
+            in_specs=[whole(a.shape) for a in (tokens, other_tokens, mod, cosine, sine)]
             + half_specs(width, width, 2 * zs, aligned)
             + half_specs(1, width, 2 * zs, aligned),
-            out_specs=[pl.BlockSpec((2, 3, rows, lanes), lambda t, m: (0, 0, 0, 0))] * zs
-            + [flat, flat],
+            out_specs=[whole(o.shape) for o in out_shape],
             scratch_shapes=[
-                pltpu.VMEM((2 * rows, width), BF16),
-                pltpu.VMEM((zs, 2, 3, rows, lanes), BF16),
+                pltpu.VMEM((2 * clips * rows, width), BF16),
+                pltpu.VMEM((zs, *message), BF16),
             ],
         ),
-        compiler_params=params(48),
-        cost_estimate=cost(6 * rows * width * width, 3 * width * width + 16 * rows * width),
+        compiler_params=params(56),
+        cost_estimate=cost(
+            6 * clips * rows * width * width, 3 * width * width + 32 * rows * width
+        ),
         name="norm_qkv",
     )(meta, tokens, other_tokens, mod, cosine, sine, *[weight] * (3 * blocks), *[bias] * (3 * blocks))
 
 
-def attend_kernel(slots, head, meta, *refs):
+def attend_kernel(slots, head, clip, meta, *refs):
     zs = slots // 2
     parts, outs = refs[:zs], refs[zs:slots]
     exact, logs, held, scores, values, sems = refs[slots:]
     copies = [
-        pltpu.make_async_copy(parts[k], held.at[pl.ds(2 * k, 2)], sems.at[k]) for k in range(zs)
+        pltpu.make_async_copy(parts[k].at[clip], held.at[pl.ds(2 * k, 2)], sems.at[k])
+        for k in range(zs)
     ]
     for copy in copies:
         copy.start()
@@ -262,14 +265,14 @@
         outs[slot // 2][slot % 2] = exact[slot].astype(BF16)
 
 
-def attend_call(meta, parts, head):
+def attend_call(meta, clip, parts, head):
     zs = len(parts)
     slots = 2 * zs
     rows, width = parts[0].shape[-2:]
     pairs = width // head
     work = slots * slots * rows * rows
     return pl.pallas_call(
-        functools.partial(attend_kernel, slots, head),
+        functools.partial(attend_kernel, slots, head, clip),
         out_shape=[shaped((2, rows, width), BF16)] * zs
         + [shaped((slots, rows, width), F32), shaped((slots, 1, pairs * rows), F32)],
         in_specs=[SMEM] + [ANY] * zs,
@@ -286,7 +289,7 @@
     )(meta, *parts)
 
 
-def attend_grad_kernel(slots, head, meta, *refs):
+def attend_grad_kernel(slots, head, clip, meta, *refs):
     zs = slots // 2
     parts, grads = refs[:zs], refs[zs:slots]
     exact, logs = refs[slots], refs[slots + 1]
@@ -297,7 +300,7 @@
     copies = []
     for k in range(zs):
         pair = pl.ds(2 * k, 2)
-        copies.append(pltpu.make_async_copy(parts[k], held.at[pair], sems.at[k]))
+        copies.append(pltpu.make_async_copy(parts[k].at[clip], held.at[pair], sems.at[k]))
         copies.append(pltpu.make_async_copy(grads[k], grad.at[pair], more.at[k]))
     for copy in copies:
         copy.start()
@@ -357,14 +360,14 @@
         out[role, 2] = held[slot, 2]
 
 
-def attend_grad_call(meta, parts, grads, exact, logs, head):
+def attend_grad_call(meta, clip, parts, grads, exact, logs, head):
     zs = len(parts)
     slots = 2 * zs
     rows, width = parts[0].shape[-2:]
     pairs = width // head
     work = slots * slots * rows * rows
     return pl.pallas_call(
-        functools.partial(attend_grad_kernel, slots, head),
+        functools.partial(attend_grad_kernel, slots, head, clip),
         out_shape=[shaped((2, 3, rows, width), BF16)] * zs,
         in_specs=[SMEM] + [ANY] * slots + [VMEM, VMEM],
         out_specs=[VMEM] * zs,
@@ -386,27 +389,44 @@
     )(meta, *parts, *grads, exact, logs)
 
 
+def mixed_places(width, hidden):
+    ends = [0]
+    for columns in (width // 2, hidden // 2, width, hidden):
+        ends.append(ends[-1] + columns)
+    return ends
+
+
 def forward_back_kernel(slots, clip, meta, tokens, cotangent, mod, proj_b, up_b, down_b, *refs):
     zs = slots // 2
+    width, hidden_width = tokens.shape[-1], refs[zs + 2].shape[1]
+    at_act, at_gtwo, at_hid = mixed_places(width, hidden_width)[1:4]
     parts, swapped, (proj_hbm, up_hbm, down_hbm) = refs[:zs], refs[zs], refs[zs + 1 : zs + 4]
     (
         layer_out, grad_middle_out, row_grads, up_bgrad,
-        att_own, att_far, gone_low,
-        n2_own, n2_other, hid_low,
-        act_own, act_other, gtwo_low,
-        held, far, proj, up, down, slope, active, sems,
+        att_own, att_far, gone_low, n2_own, act_own, mixed,
+        held, far, n2_other, gtwo_low, proj, up, down, slope, active, hid, sems,
     ) = refs[zs + 4 :]
-    proj_copy = pltpu.make_async_copy(proj_hbm, proj, sems.at[0])
-    up_copy = pltpu.make_async_copy(up_hbm, up, sems.at[1])
-    down_copy = pltpu.make_async_copy(down_hbm, down, sems.at[2])
-    proj_copy.start()
-    up_copy.start()
-    down_copy.start()
+    blocks = up.shape[1] // FF_BLOCK
+    fetches = [pltpu.make_async_copy(proj_hbm, proj, sems.at[4])]
+    for source, target, columns in ((up_hbm, up, True), (down_hbm, down, False)):
+        for block in range(blocks):
+            at = pl.ds(block * FF_BLOCK, FF_BLOCK)
+            at = (slice(None), at) if columns else (at, slice(None))
+            fetches.append(
+                pltpu.make_async_copy(source.at[at], target.at[at], sems.at[4 + len(fetches)])
+            )
+    for fetch in fetches[:IN_FLIGHT]:
+        fetch.start()
+
+    def fetched(number):
+        fetches[number].wait()
+        if number + IN_FLIGHT < len(fetches):
+            fetches[number + IN_FLIGHT].start()
+
     me = meta[0]
     parity = me % 2
-    rows, width = tokens.shape[-2:]
+    rows = tokens.shape[-2]
     lanes = width // slots
-    hidden_width = up.shape[1]
     gate_one, shift_two, scale_two, gate_two = (mod[clip, k : k + 1] for k in (2, 3, 4, 5))
     for k in range(zs):
         held[(2 * k) ^ me] = parts[k][0]
@@ -415,7 +435,7 @@
     attended = jnp.concatenate([held[k] for k in range(slots)], axis=1)
     att_own[...] = jnp.concatenate([held[2 * k + parity] for k in range(zs)], axis=1)
     att_far[...] = jnp.concatenate([far[k] for k in range(zs)], axis=1)
-    proj_copy.wait()
+    fetched(0)
     branch_one = dot_nn(attended, proj[...]) + proj_b[...].astype(F32)
     middle = tokens[...].reshape(rows, width).astype(F32) + gate_one * branch_one
     hat_two, inverse_two = norm_parts(middle)
@@ -425,10 +445,12 @@
             n2_own, n2_other, slice(block // 2 * lanes, (block // 2 + 1) * lanes), parity, block,
             low_two[:, block * lanes : (block + 1) * lanes],
         )
-    up_copy.wait()
+    n2_copy = pltpu.make_async_copy(n2_other, mixed.at[:, pl.ds(0, width // 2)], sems.at[2])
+    n2_copy.start()
     chunk = hidden_width // slots
-    for block in range(hidden_width // FF_BLOCK):
+    for block in range(blocks):
         at = slice(block * FF_BLOCK, (block + 1) * FF_BLOCK)
+        fetched(1 + block)
         hidden = dot_nn(low_two, up[:, at]) + up_b[:, at].astype(F32)
         square = hidden * hidden
         bent = jnp.tanh(GELU_A * (hidden + GELU_B * square * hidden))
@@ -438,25 +460,41 @@
             1.0 + (3.0 * GELU_B) * square
         )
         active[:, at] = low
-        for piece in range(FF_BLOCK // chunk):
-            index = block * (FF_BLOCK // chunk) + piece
-            store_by_parity(
-                act_own, act_other, slice(index // 2 * chunk, (index // 2 + 1) * chunk), parity,
-                index, low[:, piece * chunk : (piece + 1) * chunk],
-            )
-    down_copy.wait()
-    branch_two = dot_nn(active[...], down[...]) + down_b[...].astype(F32)
+        for index in range(block * FF_BLOCK // chunk, (block + 1) * FF_BLOCK // chunk):
+            piece = active.at[:, pl.ds(index * chunk, chunk)]
+            place = pl.ds(index // 2 * chunk, chunk)
+
+            @pl.when(parity == index % 2)
+            def _():
+                pltpu.make_async_copy(piece, act_own.at[:, place], sems.at[0]).start()
+
+            @pl.when(parity != index % 2)
+            def _():
+                pltpu.make_async_copy(
+                    piece, mixed.at[:, pl.ds(at_act + index // 2 * chunk, chunk)], sems.at[0]
+                ).start()
+
+    branch_two = down_b[...].astype(F32)
+    for block in range(blocks):
+        at = slice(block * FF_BLOCK, (block + 1) * FF_BLOCK)
+        fetched(1 + blocks + block)
+        branch_two = branch_two + dot_nn(active[:, at], down[at, :])
     layer_out[...] = (middle + gate_two * branch_two).astype(BF16)
     grad_out = cotangent[...].reshape(rows, width).astype(F32)
     low_grad_two = (grad_out * gate_two).astype(BF16)
     gtwo_low[...] = low_grad_two
+    gtwo_copy = pltpu.make_async_copy(gtwo_low, mixed.at[:, pl.ds(at_gtwo, width)], sems.at[3])
+    gtwo_copy.start()
     row_grads[3:4] = jnp.sum(grad_out * branch_two, axis=0, keepdims=True)
     row_grads[4:5] = jnp.sum(low_grad_two.astype(F32), axis=0, keepdims=True)
     grad_normed = None
-    for block in range(hidden_width // FF_BLOCK):
+    for block in range(blocks):
         at = slice(block * FF_BLOCK, (block + 1) * FF_BLOCK)
         low = (dot_nt(low_grad_two, down[at, :]) * slope[:, at]).astype(BF16)
-        hid_low[:, at] = low
+        hid[:, at] = low
+        pltpu.make_async_copy(
+            hid.at[:, at], mixed.at[:, pl.ds(at_hid + block * FF_BLOCK, FF_BLOCK)], sems.at[1]
+        ).start()
         up_bgrad[:, at] = jnp.sum(low.astype(F32), axis=0, keepdims=True)
         term = dot_nt(low, up[:, at])
         grad_normed = term if grad_normed is None else grad_normed + term
@@ -470,6 +508,10 @@
     row_grads[2:3] = grad_scale
     row_grads[5:6] = jnp.sum(low_grad_one.astype(F32), axis=0, keepdims=True)
     row_grads[6:8] = jnp.zeros((2, width), F32)
+    n2_copy.wait()
+    gtwo_copy.wait()
+    pltpu.make_async_copy(active, active, sems.at[0]).wait()
+    pltpu.make_async_copy(hid, hid, sems.at[1]).wait()
 
 
 def forward_back_call(
@@ -490,11 +532,8 @@
         shaped((rows, half), BF16),
         shaped((rows, width), BF16),
         shaped((rows, half), BF16),
-        shaped((rows, half), BF16),
-        shaped((rows, hidden), BF16),
         shaped((rows, half_hidden), BF16),
-        shaped((rows, half_hidden), BF16),
-        shaped((rows, width), BF16),
+        shaped((rows, mixed_places(width, hidden)[4]), BF16),
     ]
     full = lambda shape: pl.BlockSpec(shape, lambda t: (0,) * len(shape))
     pick = pl.BlockSpec((1, 1, rows, width), lambda t: (clip, 0, 0, 0))
@@ -505,16 +544,19 @@
         in_specs=[SMEM, pick, pick]
         + [full(a.shape) for a in (mod, proj_b, up_b, down_b, *parts, swapped)]
         + [ANY] * 3,
-        out_specs=[full(o.shape) for o in out_shape],
+        out_specs=[ANY if k in (8, 9) else full(o.shape) for k, o in enumerate(out_shape)],
         scratch_shapes=[
             pltpu.VMEM((slots, rows, lanes), BF16),
             pltpu.VMEM((zs, rows, lanes), BF16),
+            pltpu.VMEM((rows, half), BF16),
+            pltpu.VMEM((rows, width), BF16),
             pltpu.VMEM(proj.shape, BF16),
             pltpu.VMEM(up.shape, BF16),
             pltpu.VMEM(down.shape, BF16),
             pltpu.VMEM((rows, hidden), F32),
             pltpu.VMEM((rows, hidden), BF16),
-            pltpu.SemaphoreType.DMA((3,)),
+            pltpu.VMEM((rows, hidden), BF16),
+            pltpu.SemaphoreType.DMA((5 + 2 * hidden // FF_BLOCK,)),
         ],
         compiler_params=params(60),
         cost_estimate=cost(
@@ -637,145 +679,141 @@
 
 
 def weight_grad_kernel(jobs, clip_size, zs, meta, *refs):
-    count = sum(job[0] * (1 + job[1]) for job in jobs)
-    outs = refs[count : count + 4]
-    held, sems = refs[count + 4], refs[count + 5]
-    turned_refs = refs[count + 6 :]
-    step = pl.program_id(0) * pl.num_programs(1) + pl.program_id(1)
-    last = pl.num_programs(0) * pl.num_programs(1) - 1
-    slot = step % 2
-    _, _, height, cols = held.shape
+    arrays_n = sum(2 * job[0] for job in jobs)
+    arrays, outs = refs[:arrays_n], refs[arrays_n : arrays_n + 4]
+    held, out_sems, in_sems = refs[arrays_n + 4 : arrays_n + 7]
+    scratch = refs[arrays_n + 7 :]
+    _, _, _, height, cols = held.shape
     tile = zs * height
     z = meta[0] // 2
-
-    def drain(which):
-        pltpu.make_async_copy(held.at[which], held.at[which], sems.at[which]).wait()
-
-    def send_out(e, tiles, repeat, first, tall):
-        for half, first_bit in enumerate((1, clip_size // 2)):
-            keep, send = outs[2 * half], outs[2 * half + 1]
-            rest = [k for k in range(clip_size) if not k & first_bit]
-            out, place = (send, rest.index(e ^ first_bit)) if e & first_bit else (keep, rest.index(e))
-            low, high = half * zs // 2, (half + 1) * zs // 2
-            if not tall:
-                pltpu.make_async_copy(
-                    held.at[slot, pl.ds(low, zs // 2)],
-                    out.at[place, :, pl.ds(first, height)],
-                    sems.at[slot],
-                ).start()
-            else:
+    clip = meta[2]
+
+    def send_out(slot, tiles, repeat, first, tall):
+        for e in range(clip_size):
+            for half, first_bit in enumerate((1, clip_size // 2)):
+                keep, send = outs[2 * half], outs[2 * half + 1]
+                rest = [k for k in range(clip_size) if not k & first_bit]
+                if e & first_bit:
+                    out, place = send, rest.index(e ^ first_bit)
+                else:
+                    out, place = keep, rest.index(e)
+                low, high = half * zs // 2, (half + 1) * zs // 2
+                if not tall:
+                    pltpu.make_async_copy(
+                        held.at[slot, e, pl.ds(low, zs // 2)],
+                        out.at[place, :, pl.ds(first, height)],
+                        out_sems.at[slot],
+                    ).start()
+                    continue
                 for block in range(zs):
                     row = repeat * zs + block
                     k = row // tiles
                     if low <= k < high:
                         pltpu.make_async_copy(
-                            held.at[slot, block],
+                            held.at[slot, e, block],
                             out.at[place, k - low, pl.ds(first + row % tiles * height, height)],
-                            sems.at[slot],
+                            out_sems.at[slot],
                         ).start()
 
-    @pl.when(step >= 2)
-    def _():
-        drain(slot)
-
-    at = index = 0
-    for job, (lefts_n, lane_parts, tall, tiles, first) in enumerate(jobs):
-        lefts = refs[at : at + lefts_n]
-        rights = refs[at + lefts_n : at + lefts_n * (1 + lane_parts)]
-        at += lefts_n * (1 + lane_parts)
-        turned = turned_refs[job]
-        total_rows = lefts[0].shape[1]
-        depth = lefts[0].shape[0]
-        block = total_rows // zs
-
-        @pl.when(step == index)
-        def _():
-            for k in range(zs):
-                place = pl.ds(pl.multiple_of((k ^ z) * block, block), block)
-                for n, left in enumerate(lefts):
-                    turned[place, n * depth : (n + 1) * depth] = left[
-                        :, k * block : (k + 1) * block
-                    ].T
-
+    copies = []
+    at = 0
+    for job, (count, _, _, _, _, places) in enumerate(jobs):
+        left, right = scratch[2 * job : 2 * job + 2]
+        depth = left.shape[0] // count
+        for n in range(2 * count):
+            target = left if n < count else right
+            source = arrays[at + n]
+            if source.shape[1] != target.shape[1]:
+                source = source.at[:, pl.ds(places[n], target.shape[1])]
+            copies.append(
+                pltpu.make_async_copy(
+                    source,
+                    target.at[pl.ds(n % count * depth, depth)],
+                    in_sems.at[at + n],
+                )
+            )
+        at += 2 * count
+    for copy in copies:
+        copy.start()
+
+    at = number = 0
+    for job, (count, lane_parts, tall, tiles, first, _) in enumerate(jobs):
+        left, right = scratch[2 * job : 2 * job + 2]
+        block = left.shape[1] // zs
+        for n in range(2 * count):
+            copies[at + n].wait()
+        at += 2 * count
+        wide = right.shape[1] // (tiles * lane_parts if not tall else 1)
+        part = wide // clip_size
         for repeat in range(tiles):
-
-            @pl.when(pl.program_id(1) == index)
-            def _():
-                picked = turned[repeat * tile : (repeat + 1) * tile, :] if tall else turned[...]
-                right = jnp.concatenate(
-                    [
-                        jnp.concatenate([rights[n * lane_parts + p][...] for p in range(lane_parts)], axis=1)
-                        for n in range(lefts_n)
-                    ],
-                    axis=0,
-                )
-                held[slot] = dot_nn(picked, right).astype(BF16).reshape(held.shape[1:])
-                offset = first if tall else first + repeat * height
-                for e in range(clip_size):
-
-                    @pl.when(pl.program_id(0) == e)
-                    def _():
-                        send_out(e, tiles, repeat, offset, tall)
-
-            index += 1
-
-    @pl.when(step == last)
-    def _():
-        drain(1 - slot)
-        drain(slot)
+            slot = number % 2
+            if number >= 2:
+                pltpu.make_async_copy(held.at[slot], held.at[slot], out_sems.at[slot]).wait()
+            for lane_part in range(lane_parts):
+                if tall:
+                    per = zs // tiles
+                    rows = [
+                        left[:, pl.ds(pl.multiple_of(((repeat * per + n) ^ z) * block, block), block)]
+                        for n in range(per)
+                    ]
+                    rows = rows[0] if per == 1 else jnp.concatenate(rows, axis=1)
+                    value = dot_tn(rows, right[...]).astype(BF16)
+                else:
+                    group = repeat + lane_part
+                    value = dot_tn(
+                        left[...], right[:, group * wide : (group + 1) * wide]
+                    ).astype(BF16)
+                for p in range(clip_size):
+                    lanes = slice(lane_part * part, (lane_part + 1) * part)
+                    piece = value[:, p * part : (p + 1) * part]
+                    for k in range(zs):
+                        source = piece[k * height : (k + 1) * height]
+                        held[slot, p ^ clip, k if tall else k ^ z, :, lanes] = source
+            send_out(slot, tiles, repeat, first if tall else first + repeat * height, tall)
+            number += 1
+    for slot in range(min(number, 2)):
+        pltpu.make_async_copy(held.at[slot], held.at[slot], out_sems.at[slot]).wait()
 
 
 def weight_grad_call(meta, products, clip_size, zs, name):
-    jobs, specs, arrays, turned = [], [], [], []
-    first = index = flops = 0
-    tile = min(p[0][0].shape[1] for p in products)
+    jobs, arrays, scratch = [], [], []
+    first = flops = 0
+    tile = min(p[0][0][2] for p in products)
     height = tile // zs
     piece = None
     for lefts, rights, lane_parts, tall in products:
-        total = rights[0].shape[1]
+        depth, total = rights[0][0].shape[0], rights[0][2]
+        rows = lefts[0][2]
         if tall:
-            tiles, block = lefts[0].shape[1] // tile, total // clip_size
+            tiles, piece = rows // tile, total // clip_size
         elif lane_parts > 1:
-            tiles, block = 1, total // (lane_parts * clip_size)
+            tiles, piece = 1, total // clip_size
         else:
-            tiles, block = total // (2 * tile), 2 * tile // clip_size
-        piece = lane_parts * block
-        jobs.append((len(lefts), lane_parts, tall, tiles, first))
+            tiles, piece = total // (2 * tile), 2 * tile // clip_size
+        count = len(lefts)
+        places = tuple(a[1] for a in lefts + rights)
+        jobs.append((count, lane_parts, tall, tiles, first, places))
         first += height * tiles
-        for left in lefts:
-            arrays.append(left)
-            specs.append(pl.BlockSpec(left.shape, lambda e, t, m: (0, 0)))
-            flops += 2 * left.shape[0] * left.shape[1] * total
-        for right in rights:
-            for part in range(lane_parts):
-                arrays.append(right)
-
-                def place(e, t, m, start=index, tiles=tiles, tall=tall, part=part):
-                    group = part if tall or tiles == 1 else jnp.clip(t - start, 0, tiles - 1)
-                    return (0, group * clip_size + (e ^ m[2]))
-
-                specs.append(pl.BlockSpec((right.shape[0], block), place))
-        turned.append(
-            pltpu.VMEM((lefts[0].shape[1], len(lefts) * lefts[0].shape[0]), BF16)
-        )
-        index += tiles
+        arrays += [a[0] for a in lefts + rights]
+        flops += 2 * count * depth * rows * total
+        scratch += [
+            pltpu.VMEM((count * depth, rows), BF16),
+            pltpu.VMEM((count * depth, total), BF16),
+        ]
     out = shaped((clip_size // 2, zs // 2, first, piece), BF16)
     return pl.pallas_call(
         functools.partial(weight_grad_kernel, tuple(jobs), clip_size, zs),
         out_shape=[out] * 4,
-        grid_spec=pltpu.PrefetchScalarGridSpec(
-            num_scalar_prefetch=1,
-            grid=(clip_size, index),
-            in_specs=specs,
-            out_specs=[ANY] * 4,
-            scratch_shapes=[
-                pltpu.VMEM((2, zs, height, piece), BF16),
-                pltpu.SemaphoreType.DMA((2,)),
-            ]
-            + turned,
-        ),
-        compiler_params=params(56),
-        cost_estimate=cost(flops, sum(a.size * 2 for a in arrays) + 8 * out.size),
+        in_specs=[SMEM] + [ANY] * len(arrays),
+        out_specs=[ANY] * 4,
+        scratch_shapes=[
+            pltpu.VMEM((2, clip_size, zs, height, piece), BF16),
+            pltpu.SemaphoreType.DMA((2,)),
+            pltpu.SemaphoreType.DMA((len(arrays),)),
+        ]
+        + scratch,
+        compiler_params=params(60),
+        cost_estimate=cost(flops, flops / 512 + 8 * out.size),
         name=name,
     )(meta, *arrays)
 
@@ -852,13 +890,19 @@
     return (left.astype(F32) + right.astype(F32)).astype(BF16)
 
 
-def halve(pair, bit, size):
-    keep, send = pair
-    arrived = exchange(send, "clip", size, bit)
-    half = keep.shape[0] // 2
-    if half == 0:
-        return add_low(keep[0], arrived[0]), None
-    return add_low(keep[:half], arrived[:half]), add_low(keep[half:], arrived[half:])
+def step_out(pairs, bits, size):
+    return [exchange(send, "clip", size, bit) for (_, send), bit in zip(pairs, bits)]
+
+
+def step_in(pairs, arrived):
+    left = []
+    for (keep, _), new in zip(pairs, arrived):
+        half = keep.shape[0] // 2
+        if half:
+            left.append((add_low(keep[:half], new[:half]), add_low(keep[half:], new[half:])))
+        else:
+            left.append((add_low(keep[0], new[0]), None))
+    return left
 
 
 def clip_orders(clip_size):
@@ -866,13 +910,19 @@
     return [1] + down[:-1], down
 
 
-def sum_z(near, far, seq_size):
-    zs = seq_size // 2
-    half = zs // 2
-    total = near[0].astype(F32)
-    for k in range(1, zs):
-        source = near[k] if k < half else far[k - half]
-        total = total + exchange(source, "seq", seq_size, 2 * k).astype(F32)
+def z_out(pairs, seq_size):
+    near, far = pairs[0][0], pairs[1][0]
+    half = seq_size // 4
+    return [
+        exchange(near[k] if k < half else far[k - half], "seq", seq_size, 2 * k)
+        for k in range(1, seq_size // 2)
+    ]
+
+
+def z_in(pairs, arrived):
+    total = pairs[0][0][0].astype(F32)
+    for part in arrived:
+        total = total + part.astype(F32)
     return total.astype(BF16)
 
 
@@ -880,14 +930,12 @@
     return [piece] + [exchange(piece, "clip", clip_size, d) for d in range(1, clip_size)]
 
 
-def gather_all(rows, clip_size, seq_size):
-    both = jnp.stack([rows, exchange(rows, "seq", seq_size, 1)])
-    by_seq = jnp.concatenate(
-        [both] + [exchange(both, "seq", seq_size, 2 * k) for k in range(1, seq_size // 2)]
-    )
-    return jnp.concatenate(
-        [by_seq] + [exchange(by_seq, "clip", clip_size, d) for d in range(1, clip_size)]
-    )
+def double(array, axis, size):
+    bit = 1
+    while bit < size:
+        array = jnp.concatenate([array, exchange(array, axis, size, bit)])
+        bit *= 2
+    return array
 
 
 def silu_act(values_in):
@@ -962,100 +1010,132 @@
         weight_half = half_columns(qkv_weight, seq_size, parity)
         bias_half = half_columns(qkv_bias_row, seq_size, parity)
 
-    parts, normed = [], []
+    out = qkv_call(
+        metas[0], tokens, other_tokens, mods, cosine, sine, weight_half, bias_half, zs, head, aligned
+    )
+    parts = spread(out[:zs], seq_size)
+    normed = out[zs:]
+    swap = lambda array: exchange(array, "seq", seq_size, 1)
+    full = lambda array: (array, 0, array.shape[1])
+    at_n2, at_act, at_gtwo, at_hid, _ = mixed_places(width, hidden)
+    exact, logs, attended, crossed = [], [], [], []
     for c in range(clips):
-        out = qkv_call(
-            metas[c], c, tokens, other_tokens, mods, cosine, sine, weight_half, bias_half, zs,
-            head, aligned,
-        )
-        parts.append(spread(out[:zs], seq_size))
-        normed.append(out[zs:])
-    attended, swapped, exact, logs = [], [], [], []
-    for c in range(clips):
-        out = attend_call(metas[c], parts[c], head)
-        attended.append(spread(out[:zs], seq_size))
-        crossing = jnp.stack([a[1] for a in attended[c]])
-        swapped.append(exchange(crossing, "seq", seq_size, 1))
+        meta = metas[c]
+        if c:
+            meta, logs[-1] = after(meta, logs[-1])
+        out = attend_call(meta, c, parts, head)
         exact.append(out[zs])
         logs.append(out[zs + 1])
-    swap = lambda array: exchange(array, "seq", seq_size, 1)
-    layer, middles, row_grads, up_bgrads, saved, grads, far_ones = [], [], [], [], [], [], []
+        sends = out[:zs]
+        if c:
+            sends, attended[-1] = after(sends, attended[-1])
+            crossed.append(swap(jnp.stack([a[1] for a in attended[-1]])))
+        attended.append(spread(sends, seq_size))
+    layer, middles, row_grads, up_bgrads, saved, mixed, far_ones, grads = ([] for _ in range(8))
     for c in range(clips):
+        meta = metas[c]
+        if c:
+            meta, grads[-1][0] = after(meta, grads[-1][0])
         out = forward_back_call(
-            metas[c], c, tokens, cotangent, mods, proj_bias[None], up_bias[None],
-            down_bias[None], attended[c], swapped[c], proj_weight, up_weight, down_weight,
+            meta, c, tokens, cotangent, mods, proj_bias[None], up_bias[None],
+            down_bias[None], attended[c], crossed[c], proj_weight, up_weight, down_weight,
         )
         layer.append(out[0])
         middles.append(out[1])
         row_grads.append(out[2])
         up_bgrads.append(out[3])
-        saved.append(out[4:13])
-        far_ones.append(swap(out[6]))
-        grads.append(spread(proj_back_call(metas[c], out[6], far_ones[c], proj_weight, zs), seq_size))
-    products = [([], [], 1, False), ([], [], 1, True), ([], [], 1, False)]
-    for c in range(clips):
-        att_own, att_far, gone, n2_own, n2_other, hid, act_own, act_other, gtwo = saved[c]
-        products[0][0].extend([n2_own, swap(n2_other)])
-        products[0][1].extend([hid, swap(hid)])
-        products[1][0].extend([act_own, swap(act_other)])
-        products[1][1].extend([gtwo, swap(gtwo)])
-        products[2][0].extend([att_own, att_far])
-        products[2][1].extend([gone, far_ones[c]])
-    shares = weight_grad_call(metas[0], products, clip_size, zs, "weight_grads")
+        gone, mine_mixed = out[6], out[9]
+        if c < clips - 1:
+            gone, mine_mixed, attended[c + 1] = after(gone, mine_mixed, attended[c + 1])
+            crossed.append(swap(jnp.stack([a[1] for a in attended[c + 1]])))
+        if c:
+            gone, mine_mixed, grads[-1], mixed[-1] = after(gone, mine_mixed, grads[-1], mixed[-1])
+        far_ones.append(swap(gone))
+        mixed.append([mine_mixed, swap(mine_mixed)])
+        saved.append((out[4], out[5], gone, out[7], out[8]))
+        back = proj_back_call(metas[c], gone, far_ones[c], proj_weight, zs)
+        grads.append(spread(back, seq_size))
     row = width // seq_size
     orders = clip_orders(clip_size)
     steps = len(orders[0])
-    near, far = shares[:2], shares[2:]
-
-    metas[0], near, far = after(metas[0], near, far)
-    metas[1], near, far = after(metas[1], near, far)
+    returned = []
+    for c in range(clips):
+        if c:
+            meta, shares[0] = after(metas[c], shares[0])
+        else:
+            meta, grads[-1][0] = after(metas[c], grads[-1][0])
+        out = attend_grad_call(meta, c, parts, grads[c], exact[c], logs[c], head)
+        if c < clips - 1:
+            out, grads[-1], mixed[-1] = after(out, grads[-1], mixed[-1])
+        else:
+            out, returned[-1] = after(out, returned[-1])
+        returned.append(spread(out, seq_size))
+        if c == 0:
+            products = [([], [], 1, False), ([], [], 1, True), ([], [], 1, False)]
+            for k in range(clips):
+                att_own, att_far, gone, n2_own, act_own = saved[k]
+                own, far = mixed[k]
+                products[0][0].extend([full(att_own), full(att_far)])
+                products[0][1].extend([full(gone), full(far_ones[k])])
+                products[1][0].extend([full(act_own), (far, at_act, hidden // 2)])
+                products[1][1].extend([(own, at_gtwo, width), (far, at_gtwo, width)])
+                products[2][0].extend([full(n2_own), (far, at_n2, width // 2)])
+                products[2][1].extend([(own, at_hid, hidden), (far, at_hid, hidden)])
+            shares = weight_grad_call(metas[c], products, clip_size, zs, "weight_grads")
+            shares = list(shares)
+    pairs = [shares[:2], shares[2:]]
+    turns = list(zip(*orders))
     grad_rights, nears, fars, qkv_bgrads = [], [], [], []
     for c in range(clips):
-        out = attend_grad_call(metas[c], parts[c], grads[c], exact[c], logs[c], head)
-        if c < steps:
-            near = halve(near, orders[0][c], clip_size)
-            far = halve(far, orders[1][c], clip_size)
-        metas[c], near, far = after(metas[c], near, far)
-        out = qkv_grad_call(
-            metas[c], c, cosine, sine, spread(out, seq_size), weight_half, head, aligned
-        )
+        if c:
+            kept = [pair[0] for pair in pairs]
+            kept, qkv_bgrads[0] = after(kept, qkv_bgrads[0])
+            pairs = [(keep, pair[1]) for keep, pair in zip(kept, pairs)]
+            pairs = step_in(pairs, step_out(pairs, turns[0], clip_size))
+            meta, pairs = after(metas[c], pairs)
+        else:
+            meta, returned[-1][0] = after(metas[c], returned[-1][0])
+        out = qkv_grad_call(meta, c, cosine, sine, returned[c], weight_half, head, aligned)
         grad_rights.extend(out[:2])
         nears.append(out[2])
         fars.append(swap(out[3]))
         qkv_bgrads.append(out[4][:3])
     tokens_grad, late_rows = norm_grad_call(tokens, mods, nears, fars, middles)
-    for at in range(clips, steps):
-        near = halve(near, orders[0][at], clip_size)
-        far = halve(far, orders[1][at], clip_size)
-    piece = sum_z(near[0], far[0], seq_size)
-    up_wgrad, down_wgrad, proj_wgrad = place_call(
-        metas[0],
-        gather_pieces(piece, clip_size),
-        (
-            (row, hidden // width, False),
-            (row, hidden // width, True),
-            (row, 1, False),
-        ),
-        [shaped((row, hidden), F32), shaped((hidden // seq_size, width), F32), shaped((row, width), F32)],
-    )
-    lefts = [array for pair in normed for array in pair]
+    lefts = [normed[role * clips + c] for c in range(clips) for role in range(2)]
+    last_steps = turns[1:]
     if aligned:
         shares = weight_grad_call(
-            metas[0], [(lefts, grad_rights, 3, False)], clip_size, zs, "qkv_weight_grad"
+            metas[0],
+            [([full(a) for a in lefts], [full(a) for a in grad_rights], 3, False)],
+            clip_size,
+            zs,
+            "qkv_weight_grad",
         )
-        near, far = shares[:2], shares[2:]
-        for at in range(steps):
-            near = halve(near, orders[0][at], clip_size)
-            far = halve(far, orders[1][at], clip_size)
-        piece = sum_z(near[0], far[0], seq_size).reshape(2, row, 3 * LANES)
+        if last_steps:
+            arrived = step_out(pairs, last_steps[0], clip_size)
+            arrived, shares = after(arrived, shares)
+            pairs = step_in(pairs, arrived)
+            last_steps = last_steps[1:]
+    for bits in last_steps:
+        pairs = step_in(pairs, step_out(pairs, bits, clip_size))
+    landed = z_out(pairs, seq_size)
+    if aligned:
+        pairs_qkv = [shares[:2], shares[2:]]
+        for bits in turns:
+            pairs_qkv = step_in(pairs_qkv, step_out(pairs_qkv, bits, clip_size))
+        pairs_qkv, landed = after(pairs_qkv, landed)
+        pieces = gather_pieces(z_in(pairs, landed), clip_size)
+        piece = z_in(pairs_qkv, z_out(pairs_qkv, seq_size)).reshape(2, row, 3 * LANES)
         own_rows = lax.dynamic_index_in_dim(piece, parity, 0, keepdims=False)
         far_rows = swap(lax.dynamic_index_in_dim(piece, 1 - parity, 0, keepdims=False))
+        far_rows, pieces = after(far_rows, pieces)
         qkv_wgrad = place_qkv_call(
             metas[0],
             gather_pieces(jnp.stack([own_rows, far_rows]), clip_size),
             shaped((row, 3 * width), F32),
         )
     else:
+        pieces = gather_pieces(z_in(pairs, landed), clip_size)
         share = sum(
             lax.dot_general(left, right, (((0,), (0,)), ((), ())), preferred_element_type=F32)
             for left, right in zip(lefts, grad_rights)
@@ -1085,14 +1165,20 @@
     ]
     bias_rows = jnp.concatenate(bias_rows).reshape(-1, width)
     late = jnp.concatenate([condition[:clips], level_rows] + mod_rows + [bias_rows], axis=0)
-    used = late.shape[0]
-    late = jnp.concatenate([late.astype(BF16), jnp.zeros((-used % 16, width), BF16)], axis=0)
-    late = gather_all(late, clip_size, seq_size)
-    devices = late.shape[0]
-    start = clips + 2
-    grad_modulation = late[:, start : start + 6 * clips].reshape(devices * clips, 6 * width)
-    bias_all = late[:, start + 6 * clips : used].astype(F32).reshape(devices, -1)
-    own_sums = jnp.sum(bias_all.reshape(devices // 2, 2, -1), axis=0)
+    start, stop = clips + 2, clips + 2 + 6 * clips
+    late = double(late.astype(BF16)[None], "seq", seq_size)
+    own_sums = jnp.sum(
+        late[:, stop:].astype(F32).reshape(zs, 2, late.shape[1] - stop, width), axis=0
+    ).astype(BF16)
+    sums_rows = 2 * own_sums.shape[1]
+    message = jnp.concatenate(
+        [late[:, :stop].reshape(seq_size * stop, width), own_sums.reshape(sums_rows, width)]
+    )
+    late = double(message[None], "clip", clip_size)
+    own_sums = jnp.sum(late[:, seq_size * stop :].astype(F32), axis=0).reshape(2, -1)
+    late = late[:, : seq_size * stop].reshape(clip_size * seq_size, stop, width)
+    devices = clip_size * seq_size
+    grad_modulation = late[:, start:].reshape(devices * clips, 6 * width)
     half_bias = own_sums[:, : 3 * width // 2].reshape(2, 3, zs, 1, width // seq_size)
     bias_sums = jnp.sum(own_sums, axis=0)[2 * width :]
     qkv_bias_sums = jnp.where(
@@ -1135,6 +1221,17 @@
     up_bgrad = own_part(bias_sums[:hidden])
     down_bgrad = own_part(bias_sums[hidden : hidden + width])
     proj_bgrad = own_part(bias_sums[hidden + width : hidden + 2 * width])
+    meta, mod_wgrad, table_grad, qkv_wgrad = after(metas[0], mod_wgrad, table_grad, qkv_wgrad)
+    proj_wgrad, down_wgrad, up_wgrad = place_call(
+        meta,
+        pieces,
+        (
+            (row, 1, False),
+            (row, hidden // width, True),
+            (row, hidden // width, False),
+        ),
+        [shaped((row, width), F32), shaped((hidden // seq_size, width), F32), shaped((row, hidden), F32)],
+    )
     layer_out = jnp.stack(layer)[:, None]
     return (
         layer_out,

time: 566 us -> 524 us (0.926)
  starting transfers between devices: 126 us -> 94 us
  Pallas kernels: 206 us -> 185 us
  local copies, waits for them, and re-layouts: 34.2 us -> 43.6 us
  waiting for transfers between devices: 150 us -> 141 us
    ppermute x68 -> x57, starting transfers between devices: 126 us -> 94 us  [exchange(): return lax.ppermute(array, axis, [(k, k ^ distance) for k in range(size)])]
    pallas_call x2, Pallas kernels: 46.8 us -> 25.3 us  [weight_grad_call(): pl.pallas_call(functools.partial(weight_grad_kernel, tuple(jobs), clip_si...]
    unnamed x168 -> x184, local copies, waits for them, and re-layouts: 15.6 us -> 25.9 us
    ppermute x68 -> x57, waiting for transfers between devices: 150 us -> 141 us  [exchange(): return lax.ppermute(array, axis, [(k, k ^ distance) for k in range(size)])]
    pallas_call x6 -> x5, Pallas kernels: 92.9 us -> 97.3 us  [the longest x2 58.2 us: attend_grad_call(): pl.pallas_call(functools.partial(attend_grad_kernel, slots, head, clip),...]
  transfers between devices with their start and end apart: 68 -> 57, of which waited for: 23 -> 19; matrix products, arithmetic and copies ran while one was open for 8% -> 13% of each run, Pallas kernels for 29% -> 27%
where the time goes in v3:
time: 524 us; the launch traced here: 515 us
  Pallas kernels  185 us (35%)
  waiting for transfers between devices  141 us (27%)
  starting transfers between devices  94 us (18%)
  local copies, waits for them, and re-layouts  43.6 us (8%)
  other arithmetic  29.3 us (6%)
  matrix products  19.5 us (4%)
    ppermute x57, waiting for transfers between devices, exchange(): return lax.ppermute(array, axis, [(k, k ^ distance) for k in range(size)])  141 us
    ppermute x57, starting transfers between devices, exchange(): return lax.ppermute(array, axis, [(k, k ^ distance) for k in range(size)])  94 us
    pallas_call x2, Pallas kernels, attend_grad_call(): pl.pallas_call(functools.partial(attend_grad_kernel, slots, head, clip),...  58.2 us
    pallas_call x2, Pallas kernels, forward_back_call(): pl.pallas_call(functools.partial(forward_back_kernel, slots, clip), grid=...  38.1 us
    pallas_call x2, Pallas kernels, attend_call(): pl.pallas_call(functools.partial(attend_kernel, slots, head, clip), out_s...  28.7 us
    unnamed x184, local copies, waits for them, and re-layouts  25.9 us
    pallas_call x2, Pallas kernels, weight_grad_call(): pl.pallas_call(functools.partial(weight_grad_kernel, tuple(jobs), clip_si...  25.3 us
    convert_element_type x8, other arithmetic, add_low(): return (left.astype(F32) + right.astype(F32)).astype(BF16)  16.1 us
  transfers between devices with their start and end apart: 57, of which 19 were waited for; matrix products, arithmetic and copies ran while one was open for 13% of the time, Pallas kernels for 27%

profile of v3, /device:TPU:0, one launch (start us, length us, event | category | flops | bytes accessed | tf_op | source)
XLA Modules:
  0.0 514.8 jit_solution(6690097147371521780)
XLA Ops:
  9.2 6.3 %convolution_add_fusion = f32[4,6144]{1,0:T(4,128)S(1)} fusion(bf16[1024,6144]{1,0:T(8,128)(2,1)} %param.22, f32[6144]{0:T(1024)S(1)} %convert_element_type.230, f32[4,1024]{1,0:T(4,128)S(1)} %fusion.24), kind=kOutput, calls=%fused_computation | convolution fusion | flops 50376704 | bytes 12722176 | tf_op jit(solution)/shard_map/dot_general | solution.py:1001
  16.3 2.7 fusion.3
  20.0 10.4 %norm_qkv.1 = (bf16[2,2,3,256,128]{4,3,2,1,0:T(8,128)(2,1)}, bf16[2,2,3,256,128]{4,3,2,1,0:T(8,128)(2,1)}, bf16[2,2,3,256,128]{4,3,2,1,0:T(8,128)(2,1)}, bf16[2,...) custom-call(s32[3]{0:T(128)} %add_add_fusion.meta, ...), custom_call_target="tpu_custom_call" | custom-call | flops 3221225472 | bytes 11534336 | tf_op jit(solution)/shard_map/norm_qkv/pallas_call | solution.py:175
  30.4 3.1 collective-permute-start.2
  33.4 2.6 collective-permute-start.3
  36.8 30.9 %collective-permute-done.2.refs_1_ = bf16[2,2,3,256,128]{4,3,2,1,0:T(8,128)(2,1)S(1)} collective-permute-done((bf16[2,2,3,256,128]{4,3,2,1,0:T(8,128)(2,1)}, bf16[2,2,3,256,128]{4,3,2,1,0:T(8,128)(2,1)S(1)}, u32[]{:S(2)}, u32[]{:S(2)}) %collective-permute-start.2) | collective-permute-done | bytes 786464 | tf_op jit(solution)/shard_map/ppermute | solution.py:876
  67.6 21.0 %collective-permute-done.3.refs_2_ = bf16[2,2,3,256,128]{4,3,2,1,0:T(8,128)(2,1)S(1)} collective-permute-done((bf16[2,2,3,256,128]{4,3,2,1,0:T(8,128)(2,1)}, bf16[2,2,3,256,128]{4,3,2,1,0:T(8,128)(2,1)S(1)}, u32[]{:S(2)}, u32[]{:S(2)}) %collective-permute-start.3) | collective-permute-done | bytes 786464 | tf_op jit(solution)/shard_map/ppermute | solution.py:876
  88.7 1.7 copy-done.26
  90.4 12.4 %attend.2 = (bf16[2,256,128]{2,1,0:T(8,128)(2,1)S(1)}, bf16[2,256,128]{2,1,0:T(8,128)(2,1)S(1)}, bf16[2,256,128]{2,1,0:T(8,128)(2,1)S(1)}, bf16[2,256,128]{2,1,0...) custom-call(s32[3]{0:T(128)S(1)} %copy-done.20, bf16[2,2,3,256,128]{4,3,2,1,0:T(8,128)(2,1)S(1)} %copy-done.26, ...), custom_call_target="tpu_custom_call" | custom-call | flops 8589934592 | bytes 3145728 | tf_op jit(solution)/shard_map/attend/pallas_call | solution.py:274
  103.8 16.0 %collective-permute-start.5 = (bf16[2,256,128]{2,1,0:T(8,128)(2,1)S(1)}, bf16[2,256,128]{2,1,0:T(8,128)(2,1)S(1)}, u32[]{:S(2)}, u32[]{:S(2)}) collective-permute-start(bf16[2,256,128]{2,1,0:T(8,128)(2,1)S(1)} %get-tuple-element.181), channel_id=1, source_target_pairs={{0,8},{4,12},{8,0},{12,4},{16,24},{20,28},{24,16},{28,20},{1,9},{5... | collective-permute-start | bytes 393224 | tf_op jit(solution)/shard_map/ppermute | solution.py:876
  120.8 1.5 collective-permute-start.7
  122.4 16.3 %attend.3 = (bf16[2,256,128]{2,1,0:T(8,128)(2,1)S(1)}, bf16[2,256,128]{2,1,0:T(8,128)(2,1)S(1)}, bf16[2,256,128]{2,1,0:T(8,128)(2,1)S(1)}, bf16[2,256,128]{2,1,0...) custom-call(s32[3]{0:T(128)S(1)} %add_add_fusion.1.meta, ...), custom_call_target="tpu_custom_call" | custom-call | flops 8589934592 | bytes 3145728 | tf_op jit(solution)/shard_map/attend/pallas_call | solution.py:274
  142.6 1.9 collective-permute-start.10
  144.6 1.5 collective-permute-start.11
  146.1 19.3 %feed_forward.2 = (bf16[256,1024]{1,0:T(8,128)(2,1)}, f32[256,1024]{1,0:T(8,128)}, f32[8,1024]{1,0:T(8,128)}, f32[1,4096]{1,0:T(1,128)}, bf16[256,512]{1,0:T(8,1...) custom-call(s32[3]{0:T(128)} %add_add_fusion.meta, ...), custom_call_target="tpu_custom_call" | custom-call | flops 9663676416 | bytes 37748736 | tf_op jit(solution)/shard_map/feed_forward/pallas_call | solution.py:540
  166.3 6.8 %collective-permute-done.12.far.refs_5_ = bf16[256,1024]{1,0:T(8,128)(2,1)S(1)} collective-permute-done((bf16[256,1024]{1,0:T(8,128)(2,1)}, bf16[256,1024]{1,0:T(8,128)(2,1)S(1)}, u32[]{:S(2)}, u32[]{:S(2)}) %collective-permute-start.12) | collective-permute-done | bytes 524320 | tf_op jit(solution)/shard_map/ppermute | solution.py:876
  174.1 1.8 proj_back.2
  176.0 2.8 collective-permute-start.15
  178.9 1.5 collective-permute-start.16
  180.4 18.8 %feed_forward.3 = (bf16[256,1024]{1,0:T(8,128)(2,1)}, f32[256,1024]{1,0:T(8,128)}, f32[8,1024]{1,0:T(8,128)}, f32[1,4096]{1,0:T(1,128)}, bf16[256,512]{1,0:T(8,1...) custom-call(s32[3]{0:T(128)} %copy-done.24, ...), custom_call_target="tpu_custom_call" | custom-call | flops 9663676416 | bytes 37748736 | tf_op jit(solution)/shard_map/feed_forward/pallas_call | solution.py:540
  202.4 4.7 collective-permute-done.18.far.refs_7_
  208.2 1.8 proj_back.3
  210.6 2.9 collective-permute-start.20
  213.5 1.5 collective-permute-start.21
  220.5 23.3 %attend_grad.2 = (bf16[2,3,256,128]{3,2,1,0:T(8,128)(2,1)S(1)}, bf16[2,3,256,128]{3,2,1,0:T(8,128)(2,1)S(1)}, bf16[2,3,256,128]{3,2,1,0:T(8,128)(2,1)S(1)}, bf16[2,3,256,128]{3,2,1,0:T(8,128)(2,1)S(1)}) custom-call(s32[3]{0:T(128)S(1)} %copy-done.21, bf16[2,2,3,256,128]{4,3,2,1,0:T(8,128)(2,1)S(1)} %copy-done.27, ...), custom_call_target="tpu_custom_call" | custom-call | flops 21474836480 | bytes 5242880 | tf_op jit(solution)/shard_map/attend_grad/pallas_call | solution.py:369
  246.6 16.5 %weight_grads.1 = (bf16[2,2,1152,256]{3,2,1,0:T(8,128)(2,1)}, bf16[2,2,1152,256]{3,2,1,0:T(8,128)(2,1)}, bf16[2,2,1152,256]{3,2,1,0:T(8,128)(2,1)}, bf16[2,2,1152,256]{3,2,1,0:T(8,128)(2,1)}) custom-call(s32[3]{0:T(128)} %add_add_fusion.meta, bf16[256,512]{1,0:T(8,128)(2,1)} %get-tuple-element.203.refs_0_, bf16[256,512]{1,0:T(8,128)(2,1)} %get-tuple-element.204.refs_1_, ...), custom_call_target="tpu_custom_call" | custom-call | flops 9663676416 | bytes 28311552 | tf_op jit(solution)/shard_map/weight_grads/pallas_call | solution.py:804
  263.1 5.9 %collective-permute-start.26 = (bf16[2,2,1152,256]{3,2,1,0:T(8,128)(2,1)}, bf16[2,2,1152,256]{3,2,1,0:T(8,128)(2,1)S(1)}, u32[]{:S(2)}, u32[]{:S(2)}) collective-permute-start(bf16[2,2,1152,256]{3,2,1,0:T(8,128)(2,1)} %get-tuple-element.267), channel_id=1, source_target_pairs={{0,1},{1,0},{2,3},{3,2},{4,5},{5,4},{6,7},{7,6},{8,9},{9,8},{10,11... | collective-permute-start | bytes 7077896 | tf_op jit(solution)/shard_map/ppermute | solution.py:876
  269.8 2.9 collective-permute-start.24
  276.6 34.9 %attend_grad.3 = (bf16[2,3,256,128]{3,2,1,0:T(8,128)(2,1)S(1)}, bf16[2,3,256,128]{3,2,1,0:T(8,128)(2,1)S(1)}, bf16[2,3,256,128]{3,2,1,0:T(8,128)(2,1)S(1)}, bf16[2,3,256,128]{3,2,1,0:T(8,128)(2,1)S(1)}) custom-call(s32[3]{0:T(128)S(1)} %copy-done.25, bf16[2,2,3,256,128]{4,3,2,1,0:T(8,128)(2,1)S(1)} %copy-done.28, ...), custom_call_target="tpu_custom_call" | custom-call | flops 21474836480 | bytes 5242880 | tf_op jit(solution)/shard_map/attend_grad/pallas_call | solution.py:369
  311.6 2.9 collective-permute-start.29
  316.0 5.7 %qkv_grad.2 = (bf16[256,1536]{1,0:T(8,128)(2,1)S(1)}, bf16[256,1536]{1,0:T(8,128)(2,1)S(1)}, f32[256,1024]{1,0:T(8,128)S(1)}, f32[256,1024]{1,0:T(8,128)}, f32[8,512]{1,0:T(8,128)S(1)}) custom-call(s32[3]{0:T(128)S(1)} %copy-done.22, f32[4,256,128]{2,1,0:T(8,128)S(1)} %copy-done.3, f32[4,256,128]{2,1,0:T(8,128)S(1)} %copy-done.2, ...), custom_call_target="tpu_custom_call" | custom-call | flops 1610612736 | bytes 8388608 | tf_op jit(solution)/shard_map/qkv_grad/pallas_call | solution.py:638
  323.2 3.9 add_convert_fusion.4
  327.1 3.7 add_convert_fusion.2
  330.8 10.7 %collective-permute-done.29.refs_2_ = bf16[2,3,256,128]{3,2,1,0:T(8,128)(2,1)S(1)} collective-permute-done((bf16[2,3,256,128]{3,2,1,0:T(8,128)(2,1)S(1)}, bf16[2,3,256,128]{3,2,1,0:T(8,128)(2,1)S(1)}, u32[]{:S(2)}, u32[]{:S(2)}) %collective-permute-start.29) | collective-permute-done | bytes 393248 | tf_op jit(solution)/shard_map/ppermute | solution.py:876
  341.5 5.6 %qkv_grad.3 = (bf16[256,1536]{1,0:T(8,128)(2,1)S(1)}, bf16[256,1536]{1,0:T(8,128)(2,1)S(1)}, f32[256,1024]{1,0:T(8,128)S(1)}, f32[256,1024]{1,0:T(8,128)}, f32[8,512]{1,0:T(8,128)S(1)}) custom-call(s32[3]{0:T(128)S(1)} %copy-done.25, f32[4,256,128]{2,1,0:T(8,128)S(1)} %copy-done.3, f32[4,256,128]{2,1,0:T(8,128)S(1)} %copy-done.2, ...), custom_call_target="tpu_custom_call" | custom-call | flops 1610612736 | bytes 8388608 | tf_op jit(solution)/shard_map/qkv_grad/pallas_call | solution.py:638
  355.4 4.6 norm_grad.1
  360.7 8.8 %qkv_weight_grad.1 = (bf16[2,2,256,384]{3,2,1,0:T(8,128)(2,1)}, bf16[2,2,256,384]{3,2,1,0:T(8,128)(2,1)}, bf16[2,2,256,384]{3,2,1,0:T(8,128)(2,1)}, bf16[2,2,256,384]{3,2,1,0:T(8,128)(2,1)}) custom-call(s32[3]{0:T(128)} %add_add_fusion.meta, bf16[256,1024]{1,0:T(8,128)(2,1)} %get-tuple-element.290.refs_0_, bf16[256,1024]{1,0:T(8,128)(2,1)} %get-tuple-element.291.refs_1_, ...), custom_call_target="tpu_custom_call" | custom-call | flops 3221225472 | bytes 9437184 | tf_op jit(solution)/shard_map/qkv_weight_grad/pallas_call | solution.py:804
  369.6 6.2 %collective-permute-start.34 = (bf16[2,24,1024]{2,1,0:T(8,128)(2,1)S(1)}, bf16[2,24,1024]{2,1,0:T(8,128)(2,1)S(1)}, u32[]{:S(2)}, u32[]{:S(2)}) collective-permute-start(bf16[2,24,1024]{2,1,0:T(8,128)(2,1)S(1)} %pad_maximum_fusion.8), channel_id=1, source_target_pairs={{0,8},{4,12},{8,0},{12,4},{16,24},{20,28},{24,16},{28,20},{1,9},{5... | collective-permute-start | bytes 294920 | tf_op jit(solution)/shard_map/ppermute | solution.py:876
  375.8 4.8 collective-permute-done.38
  381.0 1.5 add_convert_fusion
  382.6 7.1 %collective-permute-start.35 = (bf16[4,24,1024]{2,1,0:T(8,128)(2,1)S(1)}, bf16[4,24,1024]{2,1,0:T(8,128)(2,1)S(1)}, u32[]{:S(2)}, u32[]{:S(2)}) collective-permute-start(bf16[4,24,1024]{2,1,0:T(8,128)(2,1)S(1)} %pad_maximum_fusion.5), channel_id=1, source_target_pairs={{0,16},{4,20},{8,24},{12,28},{16,0},{20,4},{24,8},{28,12},{1,17},{... | collective-permute-start | bytes 589832 | tf_op jit(solution)/shard_map/ppermute | solution.py:876
  389.6 1.6 add_convert_fusion.1
  391.2 7.2 %collective-permute-done.35 = bf16[4,24,1024]{2,1,0:T(8,128)(2,1)S(1)} collective-permute-done((bf16[4,24,1024]{2,1,0:T(8,128)(2,1)S(1)}, bf16[4,24,1024]{2,1,0:T(8,128)(2,1)S(1)}, u32[]{:S(2)}, u32[]{:S(2)}) %collective-permute-start.35) | collective-permute-done | bytes 196640 | tf_op jit(solution)/shard_map/ppermute | solution.py:876
  398.6 1.6 collective-permute-start.36
  402.7 3.8 collective-permute-done.36
  408.9 6.0 %collective-permute-start.44 = (bf16[1152,256]{1,0:T(8,128)(2,1)}, bf16[1152,256]{1,0:T(8,128)(2,1)}, u32[]{:S(2)}, u32[]{:S(2)}) collective-permute-start(bf16[1152,256]{1,0:T(8,128)(2,1)} %slice_bitcast_fusion.3), channel_id=1, source_target_pairs={{0,8},{4,12},{8,0},{12,4},{16,24},{20,28},{24,16},{28,20},{1,9},{5... | collective-permute-start | bytes 1769480 | tf_op jit(solution)/shard_map/ppermute | solution.py:876
  414.8 2.3 collective-permute-start.46
  417.1 1.8 add_convert_fusion.10
  419.0 2.9 collective-permute-done.42
  424.1 10.4 %collective-permute-done.37 = bf16[2,144,1024]{2,1,0:T(8,128)(2,1)S(1)} collective-permute-done((bf16[2,144,1024]{2,1,0:T(8,128)(2,1)S(1)}, bf16[2,144,1024]{2,1,0:T(8,128)(2,1)S(1)}, u32[]{:S(2)}, u32[]{:S(2)}) %collective-permute-start.37) | collective-permute-done | bytes 589856 | tf_op jit(solution)/shard_map/ppermute | solution.py:876
  436.8 2.3 reshape.351
  439.2 9.2 %fusion.46 = f32[64,1024]{1,0:T(8,128)} fusion(bf16[64,6144]{1,0:T(8,128)(2,1)S(1)} %reshape.351, bf16[1024,6144]{1,0:T(8,128)(2,1)} %param.22), kind=kOutput, calls=%fused_computation.128 | convolution fusion | flops 805306368 | bytes 13631488 | tf_op jit(solution)/shard_map/dot_general | solution.py:1198
  448.4 2.3 fusion.18
  455.0 10.8 %collective-permute-done.45 = bf16[1152,256]{1,0:T(8,128)(2,1)} collective-permute-done((bf16[1152,256]{1,0:T(8,128)(2,1)}, bf16[1152,256]{1,0:T(8,128)(2,1)}, u32[]{:S(2)}, u32[]{:S(2)}) %collective-permute-start.45) | collective-permute-done | bytes 589856 | tf_op jit(solution)/shard_map/ppermute | solution.py:876
  466.0 2.9 collective-permute-start.48
  470.4 1.7 fusion.2.refs_0_
  477.0 4.5 collective-permute-done.48
  483.0 6.3 %collective-permute-done.53.refs_3_ = bf16[1152,256]{1,0:T(8,128)(2,1)S(1)} collective-permute-done((bf16[1152,256]{1,0:T(8,128)(2,1)S(1)}, bf16[1152,256]{1,0:T(8,128)(2,1)S(1)}, u32[]{:S(2)}, u32[]{:S(2)}) %collective-permute-start.53) | collective-permute-done | bytes 589856 | tf_op jit(solution)/shard_map/ppermute | solution.py:876
  489.3 8.0 %collective-permute-done.52.refs_2_ = bf16[1152,256]{1,0:T(8,128)(2,1)S(1)} collective-permute-done((bf16[1152,256]{1,0:T(8,128)(2,1)S(1)}, bf16[1152,256]{1,0:T(8,128)(2,1)S(1)}, u32[]{:S(2)}, u32[]{:S(2)}) %collective-permute-start.52) | collective-permute-done | bytes 589856 | tf_op jit(solution)/shard_map/ppermute | solution.py:876
  497.3 1.7 collective-permute-start.56
  502.2 3.9 collective-permute-done.56.refs_3_
  506.1 3.2 collective-permute-done.55.refs_2_
  509.3 1.9 place_qkv_grad.1
  511.2 3.0 place_grads.1
  (353 shorter events, 73.8 us)
Async XLA Ops:
  1.5 5.3 %collective-permute-start = (s32[2,2]{1,0:T(2,128)S(1)}, s32[2,2]{1,0:T(2,128)S(1)}, u32[]{:S(2)}, u32[]{:S(2)}) collective-permute-start(s32[2,2]{1,0:T(2,128)S(1)} %pad_add_fusion), channel_id=1, source_target_pairs={{0,4},{4,0},{8,12},{12,8},{16,20},{20,16},{24,28},{28,24},{1,5},{5... | collective-permute-start | bytes 56 | tf_op jit(solution)/shard_map/ppermute | solution.py:876
  1.9 17.1 %collective-permute-start.1 = (bf16[2,1,256,1024]{3,2,1,0:T(8,128)(2,1)}, bf16[2,1,256,1024]{3,2,1,0:T(8,128)(2,1)S(1)}, u32[]{:S(2)}, u32[]{:S(2)}) collective-permute-start(bf16[2,1,256,1024]{3,2,1,0:T(8,128)(2,1)} %tokens.7), channel_id=1, source_target_pairs={{0,4},{4,0},{8,12},{12,8},{16,20},{20,16},{24,28},{28,24},{1,5},{5... | collective-permute-start | bytes 3145736 | tf_op jit(solution)/shard_map/ppermute | solution.py:876
  20.0 68.7 %copy-start.20 = (s32[3]{0:T(128)S(1)}, s32[3]{0:T(128)}, u32[]{:S(2)}) copy-start(s32[3]{0:T(128)} %add_add_fusion.meta) | copy-start | bytes 40
  30.4 37.3 %collective-permute-start.2 = (bf16[2,2,3,256,128]{4,3,2,1,0:T(8,128)(2,1)}, bf16[2,2,3,256,128]{4,3,2,1,0:T(8,128)(2,1)S(1)}, u32[]{:S(2)}, u32[]{:S(2)}) collective-permute-start(bf16[2,2,3,256,128]{4,3,2,1,0:T(8,128)(2,1)} %get-tuple-element.171), channel_id=1, source_target_pairs={{0,8},{4,12},{8,0},{12,4},{16,24},{20,28},{24,16},{28,20},{1,9},{5... | collective-permute-start | bytes 2359304 | tf_op jit(solution)/shard_map/ppermute | solution.py:876
  33.4 55.3 %collective-permute-start.3 = (bf16[2,2,3,256,128]{4,3,2,1,0:T(8,128)(2,1)}, bf16[2,2,3,256,128]{4,3,2,1,0:T(8,128)(2,1)S(1)}, u32[]{:S(2)}, u32[]{:S(2)}) collective-permute-start(bf16[2,2,3,256,128]{4,3,2,1,0:T(8,128)(2,1)} %get-tuple-element.172), channel_id=1, source_target_pairs={{0,16},{4,20},{8,24},{12,28},{16,0},{20,4},{24,8},{28,12},{1,17},{... | collective-permute-start | bytes 2359304 | tf_op jit(solution)/shard_map/ppermute | solution.py:876
  36.0 52.7 %collective-permute-start.4 = (bf16[2,2,3,256,128]{4,3,2,1,0:T(8,128)(2,1)}, bf16[2,2,3,256,128]{4,3,2,1,0:T(8,128)(2,1)S(1)}, u32[]{:S(2)}, u32[]{:S(2)}) collective-permute-start(bf16[2,2,3,256,128]{4,3,2,1,0:T(8,128)(2,1)} %get-tuple-element.173), channel_id=1, source_target_pairs={{0,24},{4,28},{8,16},{12,20},{16,8},{20,12},{24,0},{28,4},{1,25},{... | collective-permute-start | bytes 2359304 | tf_op jit(solution)/shard_map/ppermute | solution.py:876
  36.8 85.6 %copy-start.24 = (s32[3]{0:T(128)}, s32[3]{0:T(128)S(1)}, u32[]{:S(2)}) copy-start(s32[3]{0:T(128)S(1)} %add_add_fusion.1.meta) | copy-start | bytes 40
  67.6 54.7 %copy-start.29 = (bf16[2,2,3,256,128]{4,3,2,1,0:T(8,128)(2,1)}, bf16[2,2,3,256,128]{4,3,2,1,0:T(8,128)(2,1)S(1)}, u32[]{:S(2)}) copy-start(bf16[2,2,3,256,128]{4,3,2,1,0:T(8,128)(2,1)S(1)} %collective-permute-done.2.refs_1_) | copy-start | bytes 2359300
  103.8 35.8 %collective-permute-start.5 = (bf16[2,256,128]{2,1,0:T(8,128)(2,1)S(1)}, bf16[2,256,128]{2,1,0:T(8,128)(2,1)S(1)}, u32[]{:S(2)}, u32[]{:S(2)}) collective-permute-start(bf16[2,256,128]{2,1,0:T(8,128)(2,1)S(1)} %get-tuple-element.181), channel_id=1, source_target_pairs={{0,8},{4,12},{8,0},{12,4},{16,24},{20,28},{24,16},{28,20},{1,9},{5... | collective-permute-start | bytes 393224 | tf_op jit(solution)/shard_map/ppermute | solution.py:876
  119.8 19.9 %collective-permute-start.6 = (bf16[2,256,128]{2,1,0:T(8,128)(2,1)S(1)}, bf16[2,256,128]{2,1,0:T(8,128)(2,1)S(1)}, u32[]{:S(2)}, u32[]{:S(2)}) collective-permute-start(bf16[2,256,128]{2,1,0:T(8,128)(2,1)S(1)} %get-tuple-element.182), channel_id=1, source_target_pairs={{0,16},{4,20},{8,24},{12,28},{16,0},{20,4},{24,8},{28,12},{1,17},{... | collective-permute-start | bytes 393224 | tf_op jit(solution)/shard_map/ppermute | solution.py:876
  120.8 18.9 %collective-permute-start.7 = (bf16[2,256,128]{2,1,0:T(8,128)(2,1)S(1)}, bf16[2,256,128]{2,1,0:T(8,128)(2,1)S(1)}, u32[]{:S(2)}, u32[]{:S(2)}) collective-permute-start(bf16[2,256,128]{2,1,0:T(8,128)(2,1)S(1)} %get-tuple-element.183), channel_id=1, source_target_pairs={{0,24},{4,28},{8,16},{12,20},{16,8},{20,12},{24,0},{28,4},{1,25},{... | collective-permute-start | bytes 393224 | tf_op jit(solution)/shard_map/ppermute | solution.py:876
  139.8 6.3 %collective-permute-start.8 = (bf16[4,256,128]{2,1,0:T(8,128)(2,1)S(1)}, bf16[4,256,128]{2,1,0:T(8,128)(2,1)}, u32[]{:S(2)}, u32[]{:S(2)}) collective-permute-start(bf16[4,256,128]{2,1,0:T(8,128)(2,1)S(1)} %pad_maximum_fusion.3), channel_id=1, source_target_pairs={{0,4},{4,0},{8,12},{12,8},{16,20},{20,16},{24,28},{28,24},{1,5},{5... | collective-permute-start | bytes 786440 | tf_op jit(solution)/shard_map/ppermute | solution.py:876
  141.7 23.7 %collective-permute-start.9 = (bf16[2,256,128]{2,1,0:T(8,128)(2,1)S(1)}, bf16[2,256,128]{2,1,0:T(8,128)(2,1)S(1)}, u32[]{:S(2)}, u32[]{:S(2)}) collective-permute-start(bf16[2,256,128]{2,1,0:T(8,128)(2,1)S(1)} %get-tuple-element.192), channel_id=1, source_target_pairs={{0,8},{4,12},{8,0},{12,4},{16,24},{20,28},{24,16},{28,20},{1,9},{5... | collective-permute-start | bytes 393224 | tf_op jit(solution)/shard_map/ppermute | solution.py:876
  142.6 22.8 %collective-permute-start.10 = (bf16[2,256,128]{2,1,0:T(8,128)(2,1)S(1)}, bf16[2,256,128]{2,1,0:T(8,128)(2,1)S(1)}, u32[]{:S(2)}, u32[]{:S(2)}) collective-permute-start(bf16[2,256,128]{2,1,0:T(8,128)(2,1)S(1)} %get-tuple-element.193), channel_id=1, source_target_pairs={{0,16},{4,20},{8,24},{12,28},{16,0},{20,4},{24,8},{28,12},{1,17},{... | collective-permute-start | bytes 393224 | tf_op jit(solution)/shard_map/ppermute | solution.py:876
  144.6 20.9 %collective-permute-start.11 = (bf16[2,256,128]{2,1,0:T(8,128)(2,1)S(1)}, bf16[2,256,128]{2,1,0:T(8,128)(2,1)S(1)}, u32[]{:S(2)}, u32[]{:S(2)}) collective-permute-start(bf16[2,256,128]{2,1,0:T(8,128)(2,1)S(1)} %get-tuple-element.194), channel_id=1, source_target_pairs={{0,24},{4,28},{8,16},{12,20},{16,8},{20,12},{24,0},{28,4},{1,25},{... | collective-permute-start | bytes 393224 | tf_op jit(solution)/shard_map/ppermute | solution.py:876
  165.5 33.8 %collective-permute-start.17 = (bf16[256,7680]{1,0:T(8,128)(2,1)}, bf16[256,7680]{1,0:T(8,128)(2,1)}, u32[]{:S(2)}, u32[]{:S(2)}) collective-permute-start(bf16[256,7680]{1,0:T(8,128)(2,1)} %get-tuple-element.236.refs_12_.refs_20_), channel_id=1, source_target_pairs={{0,4},{4,0},{8,12},{12,8},{16,20},{20,16},{24,28},{28,24},{1,5},{5... | collective-permute-start | bytes 11796488 | tf_op jit(solution)/shard_map/ppermute | solution.py:876
  165.6 7.5 %collective-permute-start.12 = (bf16[256,1024]{1,0:T(8,128)(2,1)}, bf16[256,1024]{1,0:T(8,128)(2,1)S(1)}, u32[]{:S(2)}, u32[]{:S(2)}) collective-permute-start(bf16[256,1024]{1,0:T(8,128)(2,1)} %get-tuple-element.195.near.refs_4_), channel_id=1, source_target_pairs={{0,4},{4,0},{8,12},{12,8},{16,20},{20,16},{24,28},{28,24},{1,5},{5... | collective-permute-start | bytes 1572872 | tf_op jit(solution)/shard_map/ppermute | solution.py:876
  166.2 14.2 %collective-permute-start.13 = (bf16[4,256,128]{2,1,0:T(8,128)(2,1)S(1)}, bf16[4,256,128]{2,1,0:T(8,128)(2,1)}, u32[]{:S(2)}, u32[]{:S(2)}) collective-permute-start(bf16[4,256,128]{2,1,0:T(8,128)(2,1)S(1)} %pad_maximum_fusion.4), channel_id=1, source_target_pairs={{0,4},{4,0},{8,12},{12,8},{16,20},{20,16},{24,28},{28,24},{1,5},{5... | collective-permute-start | bytes 786440 | tf_op jit(solution)/shard_map/ppermute | solution.py:876
  175.9 23.3 %collective-permute-start.14 = (bf16[2,256,128]{2,1,0:T(8,128)(2,1)S(1)}, bf16[2,256,128]{2,1,0:T(8,128)(2,1)S(1)}, u32[]{:S(2)}, u32[]{:S(2)}) collective-permute-start(bf16[2,256,128]{2,1,0:T(8,128)(2,1)S(1)} %get-tuple-element.210), channel_id=1, source_target_pairs={{0,8},{4,12},{8,0},{12,4},{16,24},{20,28},{24,16},{28,20},{1,9},{5... | collective-permute-start | bytes 393224 | tf_op jit(solution)/shard_map/ppermute | solution.py:876
  176.0 23.2 %collective-permute-start.15 = (bf16[2,256,128]{2,1,0:T(8,128)(2,1)S(1)}, bf16[2,256,128]{2,1,0:T(8,128)(2,1)S(1)}, u32[]{:S(2)}, u32[]{:S(2)}) collective-permute-start(bf16[2,256,128]{2,1,0:T(8,128)(2,1)S(1)} %get-tuple-element.211), channel_id=1, source_target_pairs={{0,16},{4,20},{8,24},{12,28},{16,0},{20,4},{24,8},{28,12},{1,17},{... | collective-permute-start | bytes 393224 | tf_op jit(solution)/shard_map/ppermute | solution.py:876
  178.9 20.4 %collective-permute-start.16 = (bf16[2,256,128]{2,1,0:T(8,128)(2,1)S(1)}, bf16[2,256,128]{2,1,0:T(8,128)(2,1)S(1)}, u32[]{:S(2)}, u32[]{:S(2)}) collective-permute-start(bf16[2,256,128]{2,1,0:T(8,128)(2,1)S(1)} %get-tuple-element.212), channel_id=1, source_target_pairs={{0,24},{4,28},{8,16},{12,20},{16,8},{20,12},{24,0},{28,4},{1,25},{... | collective-permute-start | bytes 393224 | tf_op jit(solution)/shard_map/ppermute | solution.py:876
  199.3 47.2 %collective-permute-start.22 = (bf16[256,7680]{1,0:T(8,128)(2,1)}, bf16[256,7680]{1,0:T(8,128)(2,1)}, u32[]{:S(2)}, u32[]{:S(2)}) collective-permute-start(bf16[256,7680]{1,0:T(8,128)(2,1)} %get-tuple-element.237.refs_14_.refs_22_), channel_id=1, source_target_pairs={{0,4},{4,0},{8,12},{12,8},{16,20},{20,16},{24,28},{28,24},{1,5},{5... | collective-permute-start | bytes 11796488 | tf_op jit(solution)/shard_map/ppermute | solution.py:876
  200.0 7.1 %collective-permute-start.18 = (bf16[256,1024]{1,0:T(8,128)(2,1)}, bf16[256,1024]{1,0:T(8,128)(2,1)S(1)}, u32[]{:S(2)}, u32[]{:S(2)}) collective-permute-start(bf16[256,1024]{1,0:T(8,128)(2,1)} %get-tuple-element.214.near.refs_6_), channel_id=1, source_target_pairs={{0,4},{4,0},{8,12},{12,8},{16,20},{20,16},{24,28},{28,24},{1,5},{5... | collective-permute-start | bytes 1572872 | tf_op jit(solution)/shard_map/ppermute | solution.py:876
  210.6 33.9 %collective-permute-start.19 = (bf16[2,256,128]{2,1,0:T(8,128)(2,1)S(1)}, bf16[2,256,128]{2,1,0:T(8,128)(2,1)S(1)}, u32[]{:S(2)}, u32[]{:S(2)}) collective-permute-start(bf16[2,256,128]{2,1,0:T(8,128)(2,1)S(1)} %get-tuple-element.231), channel_id=1, source_target_pairs={{0,8},{4,12},{8,0},{12,4},{16,24},{20,28},{24,16},{28,20},{1,9},{5... | collective-permute-start | bytes 393224 | tf_op jit(solution)/shard_map/ppermute | solution.py:876
  210.6 34.6 %collective-permute-start.20 = (bf16[2,256,128]{2,1,0:T(8,128)(2,1)S(1)}, bf16[2,256,128]{2,1,0:T(8,128)(2,1)S(1)}, u32[]{:S(2)}, u32[]{:S(2)}) collective-permute-start(bf16[2,256,128]{2,1,0:T(8,128)(2,1)S(1)} %get-tuple-element.232), channel_id=1, source_target_pairs={{0,16},{4,20},{8,24},{12,28},{16,0},{20,4},{24,8},{28,12},{1,17},{... | collective-permute-start | bytes 393224 | tf_op jit(solution)/shard_map/ppermute | solution.py:876
  213.5 32.4 %collective-permute-start.21 = (bf16[2,256,128]{2,1,0:T(8,128)(2,1)S(1)}, bf16[2,256,128]{2,1,0:T(8,128)(2,1)S(1)}, u32[]{:S(2)}, u32[]{:S(2)}) collective-permute-start(bf16[2,256,128]{2,1,0:T(8,128)(2,1)S(1)} %get-tuple-element.233), channel_id=1, source_target_pairs={{0,24},{4,28},{8,16},{12,20},{16,8},{20,12},{24,0},{28,4},{1,25},{... | collective-permute-start | bytes 393224 | tf_op jit(solution)/shard_map/ppermute | solution.py:876
  263.1 58.6 %collective-permute-start.26 = (bf16[2,2,1152,256]{3,2,1,0:T(8,128)(2,1)}, bf16[2,2,1152,256]{3,2,1,0:T(8,128)(2,1)S(1)}, u32[]{:S(2)}, u32[]{:S(2)}) collective-permute-start(bf16[2,2,1152,256]{3,2,1,0:T(8,128)(2,1)} %get-tuple-element.267), channel_id=1, source_target_pairs={{0,1},{1,0},{2,3},{3,2},{4,5},{5,4},{6,7},{7,6},{8,9},{9,8},{10,11... | collective-permute-start | bytes 7077896 | tf_op jit(solution)/shard_map/ppermute | solution.py:876
  269.8 41.7 %collective-permute-start.23 = (bf16[2,3,256,128]{3,2,1,0:T(8,128)(2,1)}, bf16[2,3,256,128]{3,2,1,0:T(8,128)(2,1)S(1)}, u32[]{:S(2)}, u32[]{:S(2)}) collective-permute-start(bf16[2,3,256,128]{3,2,1,0:T(8,128)(2,1)} %copy-done.44), channel_id=1, source_target_pairs={{0,8},{4,12},{8,0},{12,4},{16,24},{20,28},{24,16},{28,20},{1,9},{5... | collective-permute-start | bytes 1179656 | tf_op jit(solution)/shard_map/ppermute | solution.py:876
  269.8 41.7 %collective-permute-start.24 = (bf16[2,3,256,128]{3,2,1,0:T(8,128)(2,1)S(1)}, bf16[2,3,256,128]{3,2,1,0:T(8,128)(2,1)S(1)}, u32[]{:S(2)}, u32[]{:S(2)}) collective-permute-start(bf16[2,3,256,128]{3,2,1,0:T(8,128)(2,1)S(1)} %copy-done.43), channel_id=1, source_target_pairs={{0,16},{4,20},{8,24},{12,28},{16,0},{20,4},{24,8},{28,12},{1,17},{... | collective-permute-start | bytes 1179656 | tf_op jit(solution)/shard_map/ppermute | solution.py:876
  272.7 38.9 %collective-permute-start.25 = (bf16[2,3,256,128]{3,2,1,0:T(8,128)(2,1)S(1)}, bf16[2,3,256,128]{3,2,1,0:T(8,128)(2,1)S(1)}, u32[]{:S(2)}, u32[]{:S(2)}) collective-permute-start(bf16[2,3,256,128]{3,2,1,0:T(8,128)(2,1)S(1)} %get-tuple-element.255), channel_id=1, source_target_pairs={{0,24},{4,28},{8,16},{12,20},{16,8},{20,12},{24,0},{28,4},{1,25},{... | collective-permute-start | bytes 1179656 | tf_op jit(solution)/shard_map/ppermute | solution.py:876
  274.2 52.9 %collective-permute-start.27 = (bf16[2,2,1152,256]{3,2,1,0:T(8,128)(2,1)}, bf16[2,2,1152,256]{3,2,1,0:T(8,128)(2,1)}, u32[]{:S(2)}, u32[]{:S(2)}) collective-permute-start(bf16[2,2,1152,256]{3,2,1,0:T(8,128)(2,1)} %get-tuple-element.269), channel_id=1, source_target_pairs={{0,2},{1,3},{2,0},{3,1},{4,6},{5,7},{6,4},{7,5},{8,10},{9,11},{10,... | collective-permute-start | bytes 7077896 | tf_op jit(solution)/shard_map/ppermute | solution.py:876
  276.6 39.4 %copy-start.2 = (f32[4,256,128]{2,1,0:T(8,128)S(1)}, f32[4,256,128]{2,1,0:T(8,128)}, u32[]{:S(2)}) copy-start(f32[4,256,128]{2,1,0:T(8,128)} %get-tuple-element.393.sine) | copy-start | bytes 1572868
  276.6 39.4 %copy-start.3 = (f32[4,256,128]{2,1,0:T(8,128)S(1)}, f32[4,256,128]{2,1,0:T(8,128)}, u32[]{:S(2)}) copy-start(f32[4,256,128]{2,1,0:T(8,128)} %get-tuple-element.394.cosine) | copy-start | bytes 1572868
  276.6 39.4 %copy-start.22 = (s32[3]{0:T(128)S(1)}, s32[3]{0:T(128)}, u32[]{:S(2)}) copy-start(s32[3]{0:T(128)} %add_add_fusion.meta) | copy-start | bytes 40
  311.5 19.2 %collective-permute-start.28 = (bf16[2,3,256,128]{3,2,1,0:T(8,128)(2,1)S(1)}, bf16[2,3,256,128]{3,2,1,0:T(8,128)(2,1)S(1)}, u32[]{:S(2)}, u32[]{:S(2)}) collective-permute-start(bf16[2,3,256,128]{3,2,1,0:T(8,128)(2,1)S(1)} %get-tuple-element.272), channel_id=1, source_target_pairs={{0,8},{4,12},{8,0},{12,4},{16,24},{20,28},{24,16},{28,20},{1,9},{5... | collective-permute-start | bytes 1179656 | tf_op jit(solution)/shard_map/ppermute | solution.py:876
  311.6 29.9 %collective-permute-start.29 = (bf16[2,3,256,128]{3,2,1,0:T(8,128)(2,1)S(1)}, bf16[2,3,256,128]{3,2,1,0:T(8,128)(2,1)S(1)}, u32[]{:S(2)}, u32[]{:S(2)}) collective-permute-start(bf16[2,3,256,128]{3,2,1,0:T(8,128)(2,1)S(1)} %get-tuple-element.273), channel_id=1, source_target_pairs={{0,16},{4,20},{8,24},{12,28},{16,0},{20,4},{24,8},{28,12},{1,17},{... | collective-permute-start | bytes 1179656 | tf_op jit(solution)/shard_map/ppermute | solution.py:876
  314.5 27.0 %collective-permute-start.30 = (bf16[2,3,256,128]{3,2,1,0:T(8,128)(2,1)S(1)}, bf16[2,3,256,128]{3,2,1,0:T(8,128)(2,1)S(1)}, u32[]{:S(2)}, u32[]{:S(2)}) collective-permute-start(bf16[2,3,256,128]{3,2,1,0:T(8,128)(2,1)S(1)} %get-tuple-element.274), channel_id=1, source_target_pairs={{0,24},{4,28},{8,16},{12,20},{16,8},{20,12},{24,0},{28,4},{1,25},{... | collective-permute-start | bytes 1179656 | tf_op jit(solution)/shard_map/ppermute | solution.py:876
  323.2 29.5 %collective-permute-start.31 = (f32[256,1024]{1,0:T(8,128)}, f32[256,1024]{1,0:T(8,128)}, u32[]{:S(2)}, u32[]{:S(2)}) collective-permute-start(f32[256,1024]{1,0:T(8,128)} %get-tuple-element.276), channel_id=1, source_target_pairs={{0,4},{4,0},{8,12},{12,8},{16,20},{20,16},{24,28},{28,24},{1,5},{5... | collective-permute-start | bytes 3145736 | tf_op jit(solution)/shard_map/ppermute | solution.py:876
  349.9 3.0 collective-permute-start.32
  352.0 28.6 %collective-permute-start.38 = (bf16[1,2,1152,256]{3,2,1,0:T(8,128)(2,1)}, bf16[1,2,1152,256]{3,2,1,0:T(8,128)(2,1)}, u32[]{:S(2)}, u32[]{:S(2)}) collective-permute-start(bf16[1,2,1152,256]{3,2,1,0:T(8,128)(2,1)} %get-tuple-element.288), channel_id=1, source_target_pairs={{0,2},{1,3},{2,0},{3,1},{4,6},{5,7},{6,4},{7,5},{8,10},{9,11},{10,... | collective-permute-start | bytes 3538952 | tf_op jit(solution)/shard_map/ppermute | solution.py:876
  352.0 28.7 %collective-permute-start.39 = (bf16[1,2,1152,256]{3,2,1,0:T(8,128)(2,1)}, bf16[1,2,1152,256]{3,2,1,0:T(8,128)(2,1)}, u32[]{:S(2)}, u32[]{:S(2)}) collective-permute-start(bf16[1,2,1152,256]{3,2,1,0:T(8,128)(2,1)} %get-tuple-element.289), channel_id=1, source_target_pairs={{0,1},{1,0},{2,3},{3,2},{4,5},{5,4},{6,7},{7,6},{8,9},{9,8},{10,11... | collective-permute-start | bytes 3538952 | tf_op jit(solution)/shard_map/ppermute | solution.py:876
  360.4 9.1 %collective-permute-start.33 = (bf16[1,24,1024]{2,1,0:T(8,128)(2,1)S(1)}, bf16[1,24,1024]{2,1,0:T(8,128)(2,1)S(1)}, u32[]{:S(2)}, u32[]{:S(2)}) collective-permute-start(bf16[1,24,1024]{2,1,0:T(8,128)(2,1)S(1)} %concatenate.80), channel_id=1, source_target_pairs={{0,4},{4,0},{8,12},{12,8},{16,20},{20,16},{24,28},{28,24},{1,5},{5... | collective-permute-start | bytes 147464 | tf_op jit(solution)/shard_map/ppermute | solution.py:876
  369.6 12.9 %collective-permute-start.34 = (bf16[2,24,1024]{2,1,0:T(8,128)(2,1)S(1)}, bf16[2,24,1024]{2,1,0:T(8,128)(2,1)S(1)}, u32[]{:S(2)}, u32[]{:S(2)}) collective-permute-start(bf16[2,24,1024]{2,1,0:T(8,128)(2,1)S(1)} %pad_maximum_fusion.8), channel_id=1, source_target_pairs={{0,8},{4,12},{8,0},{12,4},{16,24},{20,28},{24,16},{28,20},{1,9},{5... | collective-permute-start | bytes 294920 | tf_op jit(solution)/shard_map/ppermute | solution.py:876
  380.7 36.4 %collective-permute-start.40 = (bf16[2,2,256,384]{3,2,1,0:T(8,128)(2,1)}, bf16[2,2,256,384]{3,2,1,0:T(8,128)(2,1)}, u32[]{:S(2)}, u32[]{:S(2)}) collective-permute-start(bf16[2,2,256,384]{3,2,1,0:T(8,128)(2,1)} %get-tuple-element.303), channel_id=1, source_target_pairs={{0,1},{1,0},{2,3},{3,2},{4,5},{5,4},{6,7},{7,6},{8,9},{9,8},{10,11... | collective-permute-start | bytes 2359304 | tf_op jit(solution)/shard_map/ppermute | solution.py:876
  382.6 15.9 %collective-permute-start.35 = (bf16[4,24,1024]{2,1,0:T(8,128)(2,1)S(1)}, bf16[4,24,1024]{2,1,0:T(8,128)(2,1)S(1)}, u32[]{:S(2)}, u32[]{:S(2)}) collective-permute-start(bf16[4,24,1024]{2,1,0:T(8,128)(2,1)S(1)} %pad_maximum_fusion.5), channel_id=1, source_target_pairs={{0,16},{4,20},{8,24},{12,28},{16,0},{20,4},{24,8},{28,12},{1,17},{... | collective-permute-start | bytes 589832 | tf_op jit(solution)/shard_map/ppermute | solution.py:876
  398.6 7.9 %collective-permute-start.36 = (bf16[1,144,1024]{2,1,0:T(8,128)(2,1)S(1)}, bf16[1,144,1024]{2,1,0:T(8,128)(2,1)S(1)}, u32[]{:S(2)}, u32[]{:S(2)}) collective-permute-start(bf16[1,144,1024]{2,1,0:T(8,128)(2,1)S(1)} %maximum_bitcast_fusion.1), channel_id=1, source_target_pairs={{0,1},{1,0},{2,3},{3,2},{4,5},{5,4},{6,7},{7,6},{8,9},{9,8},{10,11... | collective-permute-start | bytes 884744 | tf_op jit(solution)/shard_map/ppermute | solution.py:876
  401.4 20.5 %collective-permute-start.42 = (bf16[2,2,256,384]{3,2,1,0:T(8,128)(2,1)S(1)}, bf16[2,2,256,384]{3,2,1,0:T(8,128)(2,1)S(1)}, u32[]{:S(2)}, u32[]{:S(2)}) collective-permute-start(bf16[2,2,256,384]{3,2,1,0:T(8,128)(2,1)S(1)} %copy-done.88), channel_id=1, source_target_pairs={{0,2},{1,3},{2,0},{3,1},{4,6},{5,7},{6,4},{7,5},{8,10},{9,11},{10,... | collective-permute-start | bytes 2359304 | tf_op jit(solution)/shard_map/ppermute | solution.py:876
  406.6 27.9 %collective-permute-start.37 = (bf16[2,144,1024]{2,1,0:T(8,128)(2,1)S(1)}, bf16[2,144,1024]{2,1,0:T(8,128)(2,1)S(1)}, u32[]{:S(2)}, u32[]{:S(2)}) collective-permute-start(bf16[2,144,1024]{2,1,0:T(8,128)(2,1)S(1)} %pad_maximum_fusion.1), channel_id=1, source_target_pairs={{0,2},{1,3},{2,0},{3,1},{4,6},{5,7},{6,4},{7,5},{8,10},{9,11},{10,... | collective-permute-start | bytes 1769480 | tf_op jit(solution)/shard_map/ppermute | solution.py:876
  408.9 46.1 %collective-permute-start.44 = (bf16[1152,256]{1,0:T(8,128)(2,1)}, bf16[1152,256]{1,0:T(8,128)(2,1)}, u32[]{:S(2)}, u32[]{:S(2)}) collective-permute-start(bf16[1152,256]{1,0:T(8,128)(2,1)} %slice_bitcast_fusion.3), channel_id=1, source_target_pairs={{0,8},{4,12},{8,0},{12,4},{16,24},{20,28},{24,16},{28,20},{1,9},{5... | collective-permute-start | bytes 1769480 | tf_op jit(solution)/shard_map/ppermute | solution.py:876
  414.8 40.2 %collective-permute-start.46 = (bf16[1152,256]{1,0:T(8,128)(2,1)}, bf16[1152,256]{1,0:T(8,128)(2,1)}, u32[]{:S(2)}, u32[]{:S(2)}) collective-permute-start(bf16[1152,256]{1,0:T(8,128)(2,1)} %get-tuple-element.387), channel_id=1, source_target_pairs={{0,24},{4,28},{8,16},{12,20},{16,8},{20,12},{24,0},{28,4},{1,25},{... | collective-permute-start | bytes 1769480 | tf_op jit(solution)/shard_map/ppermute | solution.py:876
  417.1 48.7 %collective-permute-start.45 = (bf16[1152,256]{1,0:T(8,128)(2,1)}, bf16[1152,256]{1,0:T(8,128)(2,1)}, u32[]{:S(2)}, u32[]{:S(2)}) collective-permute-start(bf16[1152,256]{1,0:T(8,128)(2,1)} %get-tuple-element.388), channel_id=1, source_target_pairs={{0,16},{4,20},{8,24},{12,28},{16,0},{20,4},{24,8},{28,12},{1,17},{... | collective-permute-start | bytes 1769480 | tf_op jit(solution)/shard_map/ppermute | solution.py:876
  421.9 30.3 %collective-permute-start.41 = (bf16[1,2,256,384]{3,2,1,0:T(8,128)(2,1)}, bf16[1,2,256,384]{3,2,1,0:T(8,128)(2,1)}, u32[]{:S(2)}, u32[]{:S(2)}) collective-permute-start(bf16[1,2,256,384]{3,2,1,0:T(8,128)(2,1)} %add_convert_fusion.10), channel_id=1, source_target_pairs={{0,2},{1,3},{2,0},{3,1},{4,6},{5,7},{6,4},{7,5},{8,10},{9,11},{10,... | collective-permute-start | bytes 1179656 | tf_op jit(solution)/shard_map/ppermute | solution.py:876
  434.5 19.1 %collective-permute-start.43 = (bf16[1,2,256,384]{3,2,1,0:T(8,128)(2,1)}, bf16[1,2,256,384]{3,2,1,0:T(8,128)(2,1)}, u32[]{:S(2)}, u32[]{:S(2)}) collective-permute-start(bf16[1,2,256,384]{3,2,1,0:T(8,128)(2,1)} %add_convert_fusion.7), channel_id=1, source_target_pairs={{0,1},{1,0},{2,3},{3,2},{4,5},{5,4},{6,7},{7,6},{8,9},{9,8},{10,11... | collective-permute-start | bytes 1179656 | tf_op jit(solution)/shard_map/ppermute | solution.py:876
  465.9 8.7 %collective-permute-start.47 = (bf16[256,384]{1,0:T(8,128)(2,1)S(1)}, bf16[256,384]{1,0:T(8,128)(2,1)S(1)}, u32[]{:S(2)}, u32[]{:S(2)}) collective-permute-start(bf16[256,384]{1,0:T(8,128)(2,1)S(1)} %slice_bitcast_fusion.6), channel_id=1, source_target_pairs={{0,8},{4,12},{8,0},{12,4},{16,24},{20,28},{24,16},{28,20},{1,9},{5... | collective-permute-start | bytes 589832 | tf_op jit(solution)/shard_map/ppermute | solution.py:876
  466.0 15.5 %collective-permute-start.48 = (bf16[256,384]{1,0:T(8,128)(2,1)S(1)}, bf16[256,384]{1,0:T(8,128)(2,1)S(1)}, u32[]{:S(2)}, u32[]{:S(2)}) collective-permute-start(bf16[256,384]{1,0:T(8,128)(2,1)S(1)} %get-tuple-element.389), channel_id=1, source_target_pairs={{0,16},{4,20},{8,24},{12,28},{16,0},{20,4},{24,8},{28,12},{1,17},{... | collective-permute-start | bytes 589832 | tf_op jit(solution)/shard_map/ppermute | solution.py:876
  468.9 12.7 %collective-permute-start.49 = (bf16[256,384]{1,0:T(8,128)(2,1)S(1)}, bf16[256,384]{1,0:T(8,128)(2,1)S(1)}, u32[]{:S(2)}, u32[]{:S(2)}) collective-permute-start(bf16[256,384]{1,0:T(8,128)(2,1)S(1)} %get-tuple-element.390), channel_id=1, source_target_pairs={{0,24},{4,28},{8,16},{12,20},{16,8},{20,12},{24,0},{28,4},{1,25},{... | collective-permute-start | bytes 589832 | tf_op jit(solution)/shard_map/ppermute | solution.py:876
  472.1 37.2 %copy-start.23 = (s32[3]{0:T(128)S(1)}, s32[3]{0:T(128)}, u32[]{:S(2)}) copy-start(s32[3]{0:T(128)} %add_add_fusion.meta) | copy-start | bytes 40
  472.1 17.2 %collective-permute-start.53 = (bf16[1152,256]{1,0:T(8,128)(2,1)S(1)}, bf16[1152,256]{1,0:T(8,128)(2,1)S(1)}, u32[]{:S(2)}, u32[]{:S(2)}) collective-permute-start(bf16[1152,256]{1,0:T(8,128)(2,1)S(1)} %fusion.2.refs_0_), channel_id=1, source_target_pairs={{0,3},{1,2},{2,1},{3,0},{4,7},{5,6},{6,5},{7,4},{8,11},{9,10},{10,... | collective-permute-start | bytes 1769480 | tf_op jit(solution)/shard_map/ppermute | solution.py:876
  473.3 24.0 %collective-permute-start.52 = (bf16[1152,256]{1,0:T(8,128)(2,1)S(1)}, bf16[1152,256]{1,0:T(8,128)(2,1)S(1)}, u32[]{:S(2)}, u32[]{:S(2)}) collective-permute-start(bf16[1152,256]{1,0:T(8,128)(2,1)S(1)} %fusion.2.refs_0_), channel_id=1, source_target_pairs={{0,2},{1,3},{2,0},{3,1},{4,6},{5,7},{6,4},{7,5},{8,10},{9,11},{10,... | collective-permute-start | bytes 1769480 | tf_op jit(solution)/shard_map/ppermute | solution.py:876
  474.6 22.7 %collective-permute-start.51 = (bf16[1152,256]{1,0:T(8,128)(2,1)S(1)}, bf16[1152,256]{1,0:T(8,128)(2,1)S(1)}, u32[]{:S(2)}, u32[]{:S(2)}) collective-permute-start(bf16[1152,256]{1,0:T(8,128)(2,1)S(1)} %fusion.2.refs_0_), channel_id=1, source_target_pairs={{0,1},{1,0},{2,3},{3,2},{4,5},{5,4},{6,7},{7,6},{8,9},{9,8},{10,11... | collective-permute-start | bytes 1769480 | tf_op jit(solution)/shard_map/ppermute | solution.py:876
  481.7 1.4 collective-permute-start.50
  497.3 8.8 %collective-permute-start.56 = (bf16[2,128,384]{2,1,0:T(8,128)(2,1)S(1)}, bf16[2,128,384]{2,1,0:T(8,128)(2,1)S(1)}, u32[]{:S(2)}, u32[]{:S(2)}) collective-permute-start(bf16[2,128,384]{2,1,0:T(8,128)(2,1)S(1)} %pad_maximum_fusion.6.refs_0_), channel_id=1, source_target_pairs={{0,3},{1,2},{2,1},{3,0},{4,7},{5,6},{6,5},{7,4},{8,11},{9,10},{10,... | collective-permute-start | bytes 589832 | tf_op jit(solution)/shard_map/ppermute | solution.py:876
  499.1 10.3 %collective-permute-start.55 = (bf16[2,128,384]{2,1,0:T(8,128)(2,1)S(1)}, bf16[2,128,384]{2,1,0:T(8,128)(2,1)S(1)}, u32[]{:S(2)}, u32[]{:S(2)}) collective-permute-start(bf16[2,128,384]{2,1,0:T(8,128)(2,1)S(1)} %pad_maximum_fusion.6.refs_0_), channel_id=1, source_target_pairs={{0,2},{1,3},{2,0},{3,1},{4,6},{5,7},{6,4},{7,5},{8,10},{9,11},{10,... | collective-permute-start | bytes 589832 | tf_op jit(solution)/shard_map/ppermute | solution.py:876
  500.1 9.2 %collective-permute-start.54 = (bf16[2,128,384]{2,1,0:T(8,128)(2,1)S(1)}, bf16[2,128,384]{2,1,0:T(8,128)(2,1)S(1)}, u32[]{:S(2)}, u32[]{:S(2)}) collective-permute-start(bf16[2,128,384]{2,1,0:T(8,128)(2,1)S(1)} %pad_maximum_fusion.6.refs_0_), channel_id=1, source_target_pairs={{0,1},{1,0},{2,3},{3,2},{4,5},{5,4},{6,7},{7,6},{8,9},{9,8},{10,11... | collective-permute-start | bytes 589832 | tf_op jit(solution)/shard_map/ppermute | solution.py:876
  (84 other events, 1028.4 us)

commit v4 on v3

--- a/solution.py
+++ b/solution.py
@@ -12,24 +12,26 @@
 HIGHEST_PRECISION = lax.Precision.HIGHEST
 F32 = jnp.float32
 BF16 = jnp.bfloat16
-ANY = pl.BlockSpec(memory_space=pl.ANY)
+ANY = pl.BlockSpec(memory_space=pltpu.HBM)
 VMEM = pl.BlockSpec(memory_space=pltpu.VMEM)
 SMEM = pl.BlockSpec(memory_space=pltpu.SMEM)
 LANES = 128
 BLOCK = 256
 FF_BLOCK = 1024
 IN_FLIGHT = 3
+GROUPS = (8, 4, 2, 1)
 GELU_A = 0.7978845608028654
 GELU_B = 0.044715
 WEIGHT = 1.0
+VMEM_BYTES = 62 << 20
 
 
 def shaped(shape, dtype):
     return jax.ShapeDtypeStruct(shape, dtype)
 
 
-def params(mib):
-    return pltpu.CompilerParams(vmem_limit_bytes=mib << 20)
+def params():
+    return pltpu.CompilerParams(vmem_limit_bytes=VMEM_BYTES)
 
 
 def cost(flops, moved, transcendentals=0):
@@ -103,6 +105,51 @@
     @pl.when(jnp.logical_not(own))
     def _():
         other_ref[:, where] = value
+
+
+def modulation_kernel(meta, table, weight, bias, out, condition_out, low):
+    rows, levels = out.shape[1], table.shape[0]
+
+    @pl.when(pl.program_id(0) == 0)
+    def _():
+        lane = lax.broadcasted_iota(jnp.int32, (1, levels), 1)
+        picked = jnp.concatenate(
+            [jnp.where(lane == meta[row], 1.0, 0.0) for row in range(rows)], axis=0
+        )
+        condition = dot_nn(picked.astype(BF16), table[...])
+        condition_out[...] = condition
+        low[...] = silu_act(condition).astype(BF16)
+
+    out[0] = dot_nn(low[...], weight[...]) + bias[...].astype(F32)
+
+
+def modulation_call(levels, table, weight, bias, first, parts):
+    rows, width = levels.shape[0], table.shape[1]
+    return pl.pallas_call(
+        modulation_kernel,
+        grid=(parts,),
+        out_shape=[shaped((parts, rows, width), F32), shaped((rows, width), F32)],
+        in_specs=[
+            SMEM,
+            pl.BlockSpec(table.shape, lambda t: (0, 0)),
+            pl.BlockSpec((width, width), lambda t: (0, first + t)),
+            pl.BlockSpec((1, width), lambda t: (0, first + t)),
+        ],
+        out_specs=[
+            pl.BlockSpec((1, rows, width), lambda t: (t, 0, 0)),
+            pl.BlockSpec((rows, width), lambda t: (0, 0)),
+        ],
+        scratch_shapes=[pltpu.VMEM((rows, width), BF16)],
+        compiler_params=params(),
+        cost_estimate=cost(0, 2 * (parts + 1) * width * width),
+        name="modulation",
+    )(levels, table, weight, bias)
+
+
+def turn_table(temporal, spatial, row, head):
+    lane = lax.broadcasted_iota(jnp.int32, spatial.shape, 1)
+    timed = lax.rem(lane, head // 2) < head // 4
+    return jnp.where(timed, temporal[row : row + 1], spatial[...])
 
 
 def half_columns(weight, groups, parity):
@@ -131,19 +178,22 @@
     return specs
 
 
-def qkv_kernel(zs, head, meta, tokens, other_tokens, mod, cosine, sine, *refs):
+def qkv_kernel(zs, head, meta, tokens, other_tokens, mod, *refs):
+    tables, refs = refs[:4], refs[4:]
     blocks = tokens.shape[-1] // (2 * LANES)
     weights, biases = refs[: 3 * blocks], refs[3 * blocks : 6 * blocks]
-    outs = refs[6 * blocks : 6 * blocks + zs]
-    normed_outs, (normed, held) = refs[6 * blocks + zs : -2], refs[-2:]
     clips, _, rows, width = tokens.shape
+    outs = refs[6 * blocks : 6 * blocks + zs * clips]
+    normed_outs, (normed, held) = refs[6 * blocks + zs * clips : -2], refs[-2:]
+    cosines = [turn_table(tables[0], tables[2], row, head) for row in range(2 * clips)]
+    sines = [turn_table(tables[1], tables[3], row, head) for row in range(2 * clips)]
     lanes = width // (2 * zs)
     z = meta[0] // 2
     for row in range(2 * clips):
         role, clip = row // clips, row % clips
         source = (tokens, other_tokens)[role]
         hat, _ = norm_parts(source[clip, 0].astype(F32))
-        low = (hat * (1.0 + mod[row, 1:2]) + mod[row, 0:1]).astype(BF16)
+        low = (hat * (1.0 + mod[1, row : row + 1]) + mod[0, row : row + 1]).astype(BF16)
         normed[row * rows : (row + 1) * rows] = low
         normed_outs[row][...] = low
     for kind in range(3):
@@ -155,44 +205,45 @@
             role, clip = row // clips, row % clips
             part = value[row * rows : (row + 1) * rows]
             if kind < 2:
-                part = turn(part, cosine[row], sine[row], head, False)
+                part = turn(part, cosines[row], sines[row], head, False)
             part = part.astype(BF16)
             if kind == 0:
                 part = part * jnp.asarray(head**-0.5, BF16)
             for group in range(zs):
-                held[group ^ z, clip, role, kind] = part[:, group * lanes : (group + 1) * lanes]
-    for slot in range(zs):
-        outs[slot][...] = held[slot]
-
-
-def qkv_call(meta, tokens, other_tokens, mod, cosine, sine, weight, bias, zs, head, aligned):
+                held[clip, group ^ z, role, kind] = part[:, group * lanes : (group + 1) * lanes]
+    for n, out in enumerate(outs):
+        out[...] = held[n // zs, n % zs]
+
+
+def qkv_call(meta, tokens, other_tokens, mod, tables, weight, bias, zs, head, aligned):
     clips, _, rows, width = tokens.shape
     lanes = width // (2 * zs)
     whole = lambda shape: pl.BlockSpec(shape, lambda t, m: (0,) * len(shape))
     blocks = width // (2 * LANES)
-    message = (clips, 2, 3, rows, lanes)
-    out_shape = [shaped(message, BF16)] * zs + [shaped((rows, width), BF16)] * (2 * clips)
+    message = (2, 3, rows, lanes)
+    out_shape = [shaped(message, BF16)] * (zs * clips)
+    out_shape += [shaped((rows, width), BF16)] * (2 * clips)
     return pl.pallas_call(
         functools.partial(qkv_kernel, zs, head),
         out_shape=out_shape,
         grid_spec=pltpu.PrefetchScalarGridSpec(
             num_scalar_prefetch=1,
             grid=(1,),
-            in_specs=[whole(a.shape) for a in (tokens, other_tokens, mod, cosine, sine)]
+            in_specs=[whole(a.shape) for a in (tokens, other_tokens, mod, *tables)]
             + half_specs(width, width, 2 * zs, aligned)
             + half_specs(1, width, 2 * zs, aligned),
             out_specs=[whole(o.shape) for o in out_shape],
             scratch_shapes=[
                 pltpu.VMEM((2 * clips * rows, width), BF16),
-                pltpu.VMEM((zs, *message), BF16),
+                pltpu.VMEM((clips, zs, *message), BF16),
             ],
         ),
-        compiler_params=params(56),
+        compiler_params=params(),
         cost_estimate=cost(
             6 * clips * rows * width * width, 3 * width * width + 32 * rows * width
         ),
         name="norm_qkv",
-    )(meta, tokens, other_tokens, mod, cosine, sine, *[weight] * (3 * blocks), *[bias] * (3 * blocks))
+    )(meta, tokens, other_tokens, mod, *tables, *[weight] * (3 * blocks), *[bias] * (3 * blocks))
 
 
 def attend_kernel(slots, head, clip, meta, *refs):
@@ -200,14 +251,14 @@
     parts, outs = refs[:zs], refs[zs:slots]
     exact, logs, held, scores, values, sems = refs[slots:]
     copies = [
-        pltpu.make_async_copy(parts[k].at[clip], held.at[pl.ds(2 * k, 2)], sems.at[k])
+        pltpu.make_async_copy(parts[k], held.at[pl.ds(2 * k, 2)], sems.at[k])
         for k in range(zs)
     ]
     for copy in copies:
         copy.start()
     for copy in copies:
         copy.wait()
-    me, context = meta[0], meta[1]
+    me, context = meta[0], meta[2 + clip]
     rows, width = held.shape[2], held.shape[3]
     pairs = width // head
 
@@ -283,7 +334,7 @@
             pltpu.VMEM((slots, pairs, rows, 2 * width), BF16),
             pltpu.SemaphoreType.DMA((zs,)),
         ],
-        compiler_params=params(40),
+        compiler_params=params(),
         cost_estimate=cost(work * 16 * width, slots * rows * width * 12, work * pairs),
         name="attend",
     )(meta, *parts)
@@ -300,13 +351,13 @@
     copies = []
     for k in range(zs):
         pair = pl.ds(2 * k, 2)
-        copies.append(pltpu.make_async_copy(parts[k].at[clip], held.at[pair], sems.at[k]))
+        copies.append(pltpu.make_async_copy(parts[k], held.at[pair], sems.at[k]))
         copies.append(pltpu.make_async_copy(grads[k], grad.at[pair], more.at[k]))
     for copy in copies:
         copy.start()
     for copy in copies:
         copy.wait()
-    me, context = meta[0], meta[1]
+    me, context = meta[0], meta[2 + clip]
     rows, width = held.shape[2], held.shape[3]
     pairs = width // head
 
@@ -333,21 +384,37 @@
         grad_k[...] = jnp.zeros_like(grad_k)
         grad_v[...] = jnp.zeros_like(grad_v)
 
-        def query_frame(query, _):
-            slot = query ^ me
-            score = dot_nt(keys, query_rows[slot])
-            grad_weight = dot_nt(values, grad_rows[slot])
-            weight = jnp.exp(score - logs[slot])
-            grad_score = (weight * (grad_weight - delta[slot])).astype(BF16)
-            grad_v[...] += dot_nn(weight.astype(BF16), grad_rows[slot])
-            grad_k[...] += dot_nn(grad_score, query_rows[slot])
-            total = grad_q[slot]
-            for h in range(pairs):
-                total = total + dot_tn(grad_score[:, h * rows : (h + 1) * rows], head_keys[h])
-            grad_q[slot] = total
-            return 0
-
-        lax.fori_loop(jnp.where(frame < context, 0, frame), slots, query_frame, 0)
+        def query_frames(first, count):
+            add_k = add_v = None
+            for n in range(count):
+                slot = (first + n) ^ me
+                score = dot_nt(keys, query_rows[slot])
+                grad_weight = dot_nt(values, grad_rows[slot])
+                weight = jnp.exp(score - logs[slot])
+                grad_score = (weight * (grad_weight - delta[slot])).astype(BF16)
+                term_v = dot_nn(weight.astype(BF16), grad_rows[slot])
+                term_k = dot_nn(grad_score, query_rows[slot])
+                add_v = term_v if add_v is None else add_v + term_v
+                add_k = term_k if add_k is None else add_k + term_k
+                total = grad_q[slot]
+                for h in range(pairs):
+                    total = total + dot_tn(grad_score[:, h * rows : (h + 1) * rows], head_keys[h])
+                grad_q[slot] = total
+            grad_v[...] += add_v
+            grad_k[...] += add_k
+
+        first = jnp.where(frame < context, 0, frame)
+        for size in GROUPS:
+            if size > slots:
+                continue
+            count = (slots - first) // size
+
+            def group_step(n, _, first=first, size=size):
+                query_frames(first + n * size, size)
+                return 0
+
+            lax.fori_loop(0, count, group_step, 0)
+            first = first + count * size
         held[place, 1] = grad_k[...].astype(BF16)
         held[place, 2] = grad_v[...].astype(BF16)
         return 0
@@ -383,7 +450,7 @@
             pltpu.SemaphoreType.DMA((zs,)),
             pltpu.SemaphoreType.DMA((zs,)),
         ],
-        compiler_params=params(40),
+        compiler_params=params(),
         cost_estimate=cost(work * 40 * width, slots * rows * width * 20, work * pairs),
         name="attend_grad",
     )(meta, *parts, *grads, exact, logs)
@@ -427,7 +494,7 @@
     parity = me % 2
     rows = tokens.shape[-2]
     lanes = width // slots
-    gate_one, shift_two, scale_two, gate_two = (mod[clip, k : k + 1] for k in (2, 3, 4, 5))
+    gate_one, shift_two, scale_two, gate_two = (mod[k, clip : clip + 1] for k in range(4))
     for k in range(zs):
         held[(2 * k) ^ me] = parts[k][0]
         held[(2 * k + 1) ^ me] = swapped[k]
@@ -558,7 +625,7 @@
             pltpu.VMEM((rows, hidden), BF16),
             pltpu.SemaphoreType.DMA((5 + 2 * hidden // FF_BLOCK,)),
         ],
-        compiler_params=params(60),
+        compiler_params=params(),
         cost_estimate=cost(
             4 * rows * width * (width + 2 * hidden),
             4 * width * (width + 2 * hidden),
@@ -571,11 +638,13 @@
 def proj_back_kernel(meta, near, far, proj, *outs):
     me = meta[0]
     rows, lanes = near.shape[0], outs[0].shape[2]
+    groups = [pl.multiple_of((me ^ (2 * k)) * lanes, lanes) for k in range(len(outs))]
+    weight = jnp.concatenate([proj[pl.ds(group, lanes), :] for group in groups], axis=0)
+    both = jnp.concatenate([near[...], far[...]], axis=0)
+    value = dot_nt(both, weight).astype(BF16)
     for k, out in enumerate(outs):
-        group = me ^ (2 * k)
-        weight = proj[pl.ds(pl.multiple_of(group * lanes, lanes), lanes), :]
-        out[0] = dot_nt(near[...], weight).astype(BF16)
-        out[1] = dot_nt(far[...], weight).astype(BF16)
+        for role in range(2):
+            out[role] = value[role * rows : (role + 1) * rows, k * lanes : (k + 1) * lanes]
 
 
 def proj_back_call(meta, near, far, proj, zs):
@@ -586,19 +655,22 @@
         out_shape=[shaped((2, rows, lanes), BF16)] * zs,
         in_specs=[SMEM, VMEM, VMEM, VMEM],
         out_specs=[VMEM] * zs,
-        compiler_params=params(32),
+        compiler_params=params(),
         cost_estimate=cost(2 * rows * width * width, 2 * width * width + 6 * rows * width),
         name="proj_back",
     )(meta, near, far, proj)
 
 
-def qkv_grad_kernel(zs, head, clip, meta, cosine, sine, *refs):
+def qkv_grad_kernel(zs, head, clip, meta, *refs):
+    tables, refs = refs[:4], refs[4:]
     blocks = refs[zs].shape[0] // (2 * LANES)
     parts, weights = refs[:zs], refs[zs : zs + 3 * blocks]
     near_out, far_out, near_sum, far_sum, bias_out, held = refs[zs + 3 * blocks :]
     rows, width = near_sum.shape
-    clips = cosine.shape[0] // 2
+    clips = tables[0].shape[0] // 2
     z = meta[0] // 2
+    cosines = [turn_table(tables[0], tables[2], role * clips + clip, head) for role in range(2)]
+    sines = [turn_table(tables[1], tables[3], role * clips + clip, head) for role in range(2)]
     for k in range(zs):
         held[k ^ z] = parts[k][...]
     totals = [None, None]
@@ -610,8 +682,7 @@
         for role, out in enumerate((near_out, far_out)):
             low = jnp.concatenate([held[k, role, kind] for k in range(zs)], axis=1)
             if kind < 2:
-                row = role * clips + clip
-                low = turn(low.astype(F32), cosine[row], sine[row], head, True).astype(BF16)
+                low = turn(low.astype(F32), cosines[role], sines[role], head, True).astype(BF16)
             out[:, kind * half : (kind + 1) * half] = low
             column = jnp.sum(low.astype(F32), axis=0, keepdims=True)
             sums = column if sums is None else sums + column
@@ -622,7 +693,7 @@
     far_sum[...] = totals[1]
 
 
-def qkv_grad_call(meta, clip, cosine, sine, parts, weight, head, aligned):
+def qkv_grad_call(meta, clip, tables, parts, weight, head, aligned):
     zs = len(parts)
     rows, lanes = parts[0].shape[-2:]
     width = 2 * zs * lanes
@@ -641,15 +712,15 @@
         grid_spec=pltpu.PrefetchScalarGridSpec(
             num_scalar_prefetch=1,
             grid=(1,),
-            in_specs=[whole(a.shape) for a in (cosine, sine, *parts)]
+            in_specs=[whole(a.shape) for a in (*tables, *parts)]
             + half_specs(width, width, 2 * zs, aligned),
             out_specs=[whole(o.shape) for o in out_shape],
             scratch_shapes=[pltpu.VMEM((zs, 2, 3, rows, lanes), BF16)],
         ),
-        compiler_params=params(48),
+        compiler_params=params(),
         cost_estimate=cost(6 * rows * width * width, 3 * width * width + 20 * rows * width),
         name="qkv_grad",
-    )(meta, cosine, sine, *parts, *[weight] * (3 * blocks))
+    )(meta, *tables, *parts, *[weight] * (3 * blocks))
 
 
 def norm_grad_kernel(tokens, mod, *refs):
@@ -658,7 +729,9 @@
     tokens_grad, row_grads = refs[3 * clips :]
     for c in range(clips):
         hat, inverse = norm_parts(tokens[c, 0].astype(F32))
-        grad, shift, scale = norm_pull(nears[c][...] + fars[c][...], hat, inverse, mod[c, 1:2])
+        grad, shift, scale = norm_pull(
+            nears[c][...] + fars[c][...], hat, inverse, mod[1, c : c + 1]
+        )
         tokens_grad[c, 0] = grad + middles[c][...]
         row_grads[c, 0:1] = shift
         row_grads[c, 1:2] = scale
@@ -672,7 +745,7 @@
         out_shape=[shaped(tokens.shape, F32), shaped((clips, 8, width), F32)],
         in_specs=[VMEM] * (2 + 3 * clips),
         out_specs=[VMEM, VMEM],
-        compiler_params=params(40),
+        compiler_params=params(),
         cost_estimate=cost(clips * rows * width * 30, clips * rows * width * 18),
         name="norm_grad",
     )(tokens, mod, *nears, *fars, *middles)
@@ -686,7 +759,7 @@
     _, _, _, height, cols = held.shape
     tile = zs * height
     z = meta[0] // 2
-    clip = meta[2]
+    clip = meta[1]
 
     def send_out(slot, tiles, repeat, first, tall):
         for e in range(clip_size):
@@ -812,7 +885,7 @@
             pltpu.SemaphoreType.DMA((len(arrays),)),
         ]
         + scratch,
-        compiler_params=params(60),
+        compiler_params=params(),
         cost_estimate=cost(flops, flops / 512 + 8 * out.size),
         name=name,
     )(meta, *arrays)
@@ -820,7 +893,7 @@
 
 def place_kernel(jobs, pieces, meta, *refs):
     parts, outs = refs[:pieces], refs[pieces:]
-    clip = meta[2]
+    clip = meta[1]
     cols = parts[0].shape[1]
     for e in range(pieces):
         first = 0
@@ -842,7 +915,7 @@
         out_shape=outs,
         in_specs=[SMEM] + [VMEM] * len(parts),
         out_specs=[VMEM] * len(outs),
-        compiler_params=params(32),
+        compiler_params=params(),
         cost_estimate=cost(0, sum(o.size * 4 for o in outs)),
         name="place_grads",
     )(meta, *parts)
@@ -850,7 +923,7 @@
 
 def place_qkv_kernel(meta, *refs):
     parts, out = refs[:-1], refs[-1]
-    parity, clip = meta[0] % 2, meta[2]
+    parity, clip = meta[0] % 2, meta[1]
     thirds = out.shape[1] // 3
     for e, part in enumerate(parts):
         for role in range(2):
@@ -866,7 +939,7 @@
         out_shape=out,
         in_specs=[SMEM] + [VMEM] * len(parts),
         out_specs=VMEM,
-        compiler_params=params(32),
+        compiler_params=params(),
         cost_estimate=cost(0, out.size * 6),
         name="place_qkv_grad",
     )(meta, *parts)
@@ -910,20 +983,15 @@
     return [1] + down[:-1], down
 
 
-def z_out(pairs, seq_size):
-    near, far = pairs[0][0], pairs[1][0]
-    half = seq_size // 4
-    return [
-        exchange(near[k] if k < half else far[k - half], "seq", seq_size, 2 * k)
-        for k in range(1, seq_size // 2)
-    ]
-
-
-def z_in(pairs, arrived):
-    total = pairs[0][0][0].astype(F32)
-    for part in arrived:
-        total = total + part.astype(F32)
-    return total.astype(BF16)
+def sum_z(pairs, seq_size):
+    blocks = [*pairs[0][0], *pairs[1][0]]
+    bit = 1
+    while len(blocks) > 1:
+        kept, sent = blocks[0::2], blocks[1::2]
+        arrived = exchange(jnp.stack(sent), "seq", seq_size, 2 * bit)
+        blocks = [add_low(keep, new) for keep, new in zip(kept, arrived)]
+        bit *= 2
+    return blocks[0]
 
 
 def gather_pieces(piece, clip_size):
@@ -945,13 +1013,13 @@
 def rotary_tables(stamps, patch_count, head):
     lane = jnp.arange(LANES, dtype=jnp.int32)
     quarter = head // 4
-    pair = lane % (head // 2)
-    freqs = 10000.0 ** (-(pair % quarter).astype(F32) / quarter)
-    temporal = stamps.astype(F32)[:, None, None] * freqs[None, None, :]
-    spatial = jnp.arange(patch_count).astype(F32)[None, :, None] * freqs[None, None, :]
-    angles = jnp.where((pair < quarter)[None, None, :], temporal, spatial)
+    freqs = 10000.0 ** (-(lane % quarter).astype(F32) / quarter)
     sign = jnp.where(lane % head < head // 2, -1.0, 1.0).astype(F32)
-    return jnp.cos(angles), jnp.sin(angles) * sign[None, None, :]
+    tables = []
+    for places in (stamps, jnp.arange(patch_count, dtype=jnp.int32)):
+        angles = places.astype(F32)[:, None] * freqs[None, :]
+        tables += [jnp.cos(angles), jnp.sin(angles) * sign[None, :]]
+    return tables
 
 
 def on_device(
@@ -982,27 +1050,21 @@
     mine = mine.astype(jnp.int32)
     parity = me % 2
     aligned = (width // seq_size) % LANES == 0
-    metas = [jnp.stack([me, context_count[c], mine]) for c in range(clips)]
     stamps = jnp.stack([noise_level[:, 0], frame_time[:, 0]])
     other_stamps = exchange(stamps, "seq", seq_size, 1)
     other_tokens = exchange(tokens, "seq", seq_size, 1)
-    both_levels = jnp.concatenate(
+    meta = jnp.concatenate([jnp.stack([me, mine]), context_count])
+    levels = jnp.concatenate(
         [
             jnp.where(me < context_count, 0, stamps[0]),
             jnp.where((me ^ 1) < context_count, 0, other_stamps[0]),
         ]
     )
-    levels_used = both_levels[:clips]
-    picked = (
-        both_levels[:, None] == jnp.arange(level_table.shape[0], dtype=jnp.int32)[None, :]
-    ).astype(BF16)
-    condition = jnp.dot(picked, level_table, preferred_element_type=F32)
-    condition_low = silu_act(condition).astype(BF16)
-    modulation = jnp.dot(
-        condition_low, mod_weight, preferred_element_type=F32
-    ) + mod_bias.astype(F32)
-    mods = modulation.reshape(2 * clips, 6, width)
-    cosine, sine = rotary_tables(jnp.concatenate([stamps[1], other_stamps[1]]), rows, head)
+    levels_used = levels[:clips]
+    mod_bias_row = mod_bias[None]
+    mod_one, condition = modulation_call(levels, level_table, mod_weight, mod_bias_row, 0, 2)
+    condition = condition[:clips]
+    tables = rotary_tables(jnp.concatenate([stamps[1], other_stamps[1]]), rows, head)
     qkv_bias_row = qkv_bias[None]
     if aligned:
         weight_half, bias_half = qkv_weight, qkv_bias_row
@@ -1010,34 +1072,40 @@
         weight_half = half_columns(qkv_weight, seq_size, parity)
         bias_half = half_columns(qkv_bias_row, seq_size, parity)
 
-    out = qkv_call(
-        metas[0], tokens, other_tokens, mods, cosine, sine, weight_half, bias_half, zs, head, aligned
-    )
-    parts = spread(out[:zs], seq_size)
-    normed = out[zs:]
     swap = lambda array: exchange(array, "seq", seq_size, 1)
     full = lambda array: (array, 0, array.shape[1])
     at_n2, at_act, at_gtwo, at_hid, _ = mixed_places(width, hidden)
+    out = qkv_call(
+        meta, tokens, other_tokens, mod_one, tables, weight_half, bias_half, zs, head, aligned
+    )
+    normed = out[zs * clips :]
+    parts = [spread(out[:zs], seq_size)]
+    mod_two, _ = modulation_call(
+        levels[:clips], level_table, mod_weight, mod_bias_row, 2, 4
+    )
+    parts[0], mod_two = after(parts[0], mod_two)
     exact, logs, attended, crossed = [], [], [], []
     for c in range(clips):
-        meta = metas[c]
-        if c:
-            meta, logs[-1] = after(meta, logs[-1])
-        out = attend_call(meta, c, parts, head)
-        exact.append(out[zs])
-        logs.append(out[zs + 1])
-        sends = out[:zs]
+        sends = out[(c + 1) * zs : (c + 2) * zs] if c < clips - 1 else None
+        if c < clips - 1:
+            parts[c], sends = after(parts[c], sends)
+            parts.append(spread(sends, seq_size))
+        done = attend_call(meta, c, parts[c], head)
+        exact.append(done[zs])
+        logs.append(done[zs + 1])
+        sends = done[:zs]
+        if c < clips - 1:
+            sends, parts[c + 1] = after(sends, parts[c + 1])
         if c:
             sends, attended[-1] = after(sends, attended[-1])
             crossed.append(swap(jnp.stack([a[1] for a in attended[-1]])))
         attended.append(spread(sends, seq_size))
     layer, middles, row_grads, up_bgrads, saved, mixed, far_ones, grads = ([] for _ in range(8))
     for c in range(clips):
-        meta = metas[c]
         if c:
             meta, grads[-1][0] = after(meta, grads[-1][0])
         out = forward_back_call(
-            meta, c, tokens, cotangent, mods, proj_bias[None], up_bias[None],
+            meta, c, tokens, cotangent, mod_two, proj_bias[None], up_bias[None],
             down_bias[None], attended[c], crossed[c], proj_weight, up_weight, down_weight,
         )
         layer.append(out[0])
@@ -1051,9 +1119,12 @@
         if c:
             gone, mine_mixed, grads[-1], mixed[-1] = after(gone, mine_mixed, grads[-1], mixed[-1])
         far_ones.append(swap(gone))
+        if c < clips - 1:
+            far_ones[-1], crossed[-1] = after(far_ones[-1], crossed[-1])
+        saved.append((out[4], out[5], gone, out[7], out[8]))
+        back = list(proj_back_call(meta, gone, far_ones[c], proj_weight, zs))
+        back[0], mine_mixed = after(back[0], mine_mixed)
         mixed.append([mine_mixed, swap(mine_mixed)])
-        saved.append((out[4], out[5], gone, out[7], out[8]))
-        back = proj_back_call(metas[c], gone, far_ones[c], proj_weight, zs)
         grads.append(spread(back, seq_size))
     row = width // seq_size
     orders = clip_orders(clip_size)
@@ -1061,10 +1132,10 @@
     returned = []
     for c in range(clips):
         if c:
-            meta, shares[0] = after(metas[c], shares[0])
+            meta, shares[0] = after(meta, shares[0])
         else:
-            meta, grads[-1][0] = after(metas[c], grads[-1][0])
-        out = attend_grad_call(meta, c, parts, grads[c], exact[c], logs[c], head)
+            meta, grads[-1][0] = after(meta, grads[-1][0])
+        out = attend_grad_call(meta, c, parts[c], grads[c], exact[c], logs[c], head)
         if c < clips - 1:
             out, grads[-1], mixed[-1] = after(out, grads[-1], mixed[-1])
         else:
@@ -1081,7 +1152,7 @@
                 products[1][1].extend([(own, at_gtwo, width), (far, at_gtwo, width)])
                 products[2][0].extend([full(n2_own), (far, at_n2, width // 2)])
                 products[2][1].extend([(own, at_hid, hidden), (far, at_hid, hidden)])
-            shares = weight_grad_call(metas[c], products, clip_size, zs, "weight_grads")
+            shares = weight_grad_call(meta, products, clip_size, zs, "weight_grads")
             shares = list(shares)
     pairs = [shares[:2], shares[2:]]
     turns = list(zip(*orders))
@@ -1092,65 +1163,21 @@
             kept, qkv_bgrads[0] = after(kept, qkv_bgrads[0])
             pairs = [(keep, pair[1]) for keep, pair in zip(kept, pairs)]
             pairs = step_in(pairs, step_out(pairs, turns[0], clip_size))
-            meta, pairs = after(metas[c], pairs)
+            meta, pairs, returned[c] = after(meta, pairs, returned[c])
         else:
-            meta, returned[-1][0] = after(metas[c], returned[-1][0])
-        out = qkv_grad_call(meta, c, cosine, sine, returned[c], weight_half, head, aligned)
+            meta, returned[-1][0] = after(meta, returned[-1][0])
+        out = qkv_grad_call(meta, c, tables, returned[c], weight_half, head, aligned)
         grad_rights.extend(out[:2])
         nears.append(out[2])
         fars.append(swap(out[3]))
         qkv_bgrads.append(out[4][:3])
-    tokens_grad, late_rows = norm_grad_call(tokens, mods, nears, fars, middles)
-    lefts = [normed[role * clips + c] for c in range(clips) for role in range(2)]
-    last_steps = turns[1:]
-    if aligned:
-        shares = weight_grad_call(
-            metas[0],
-            [([full(a) for a in lefts], [full(a) for a in grad_rights], 3, False)],
-            clip_size,
-            zs,
-            "qkv_weight_grad",
-        )
-        if last_steps:
-            arrived = step_out(pairs, last_steps[0], clip_size)
-            arrived, shares = after(arrived, shares)
-            pairs = step_in(pairs, arrived)
-            last_steps = last_steps[1:]
-    for bits in last_steps:
+    tokens_grad, late_rows = norm_grad_call(tokens, mod_one, nears, fars, middles)
+    if len(turns) > 1:
+        arrived = step_out(pairs, turns[1], clip_size)
+        tokens_grad, arrived = after(tokens_grad, arrived)
+        pairs = step_in(pairs, arrived)
+    for bits in turns[2:]:
         pairs = step_in(pairs, step_out(pairs, bits, clip_size))
-    landed = z_out(pairs, seq_size)
-    if aligned:
-        pairs_qkv = [shares[:2], shares[2:]]
-        for bits in turns:
-            pairs_qkv = step_in(pairs_qkv, step_out(pairs_qkv, bits, clip_size))
-        pairs_qkv, landed = after(pairs_qkv, landed)
-        pieces = gather_pieces(z_in(pairs, landed), clip_size)
-        piece = z_in(pairs_qkv, z_out(pairs_qkv, seq_size)).reshape(2, row, 3 * LANES)
-        own_rows = lax.dynamic_index_in_dim(piece, parity, 0, keepdims=False)
-        far_rows = swap(lax.dynamic_index_in_dim(piece, 1 - parity, 0, keepdims=False))
-        far_rows, pieces = after(far_rows, pieces)
-        qkv_wgrad = place_qkv_call(
-            metas[0],
-            gather_pieces(jnp.stack([own_rows, far_rows]), clip_size),
-            shaped((row, 3 * width), F32),
-        )
-    else:
-        pieces = gather_pieces(z_in(pairs, landed), clip_size)
-        share = sum(
-            lax.dot_general(left, right, (((0,), (0,)), ((), ())), preferred_element_type=F32)
-            for left, right in zip(lefts, grad_rights)
-        ).astype(BF16)
-        share = share.reshape(width, 3, zs, 1, width // seq_size)
-        blank = jnp.zeros_like(share)
-        share = jnp.where(
-            parity == 0,
-            jnp.concatenate([share, blank], axis=3),
-            jnp.concatenate([blank, share], axis=3),
-        ).reshape(width, 3 * width)
-        qkv_wgrad = lax.psum(
-            lax.psum_scatter(share, "seq", scatter_dimension=0, tiled=True), "clip"
-        ).astype(F32)
-
     level_rows = jnp.stack([levels_used // 32, levels_used % 32]).astype(F32)
     level_rows = jnp.concatenate([level_rows, jnp.zeros((2, width - clips), F32)], axis=1)
     mod_rows = []
@@ -1164,9 +1191,27 @@
         sum(r[5] for r in row_grads),
     ]
     bias_rows = jnp.concatenate(bias_rows).reshape(-1, width)
-    late = jnp.concatenate([condition[:clips], level_rows] + mod_rows + [bias_rows], axis=0)
+    late = jnp.concatenate([condition, level_rows] + mod_rows + [bias_rows], axis=0)
     start, stop = clips + 2, clips + 2 + 6 * clips
     late = double(late.astype(BF16)[None], "seq", seq_size)
+    pairs, late = after(pairs, late)
+    piece = sum_z(pairs, seq_size)
+    lefts = [normed[role * clips + c] for c in range(clips) for role in range(2)]
+    if aligned:
+        meta, late_rows = after(meta, late_rows)
+        shares = weight_grad_call(
+            meta,
+            [([full(a) for a in lefts], [full(a) for a in grad_rights], 3, False)],
+            clip_size,
+            zs,
+            "qkv_weight_grad",
+        )
+        pairs_qkv = [shares[:2], shares[2:]]
+        arrived = step_out(pairs_qkv, turns[0], clip_size)
+        arrived, late = after(arrived, late)
+        pairs_qkv = step_in(pairs_qkv, arrived)
+        for bits in turns[1:]:
+            pairs_qkv = step_in(pairs_qkv, step_out(pairs_qkv, bits, clip_size))
     own_sums = jnp.sum(
         late[:, stop:].astype(F32).reshape(zs, 2, late.shape[1] - stop, width), axis=0
     ).astype(BF16)
@@ -1175,6 +1220,8 @@
         [late[:, :stop].reshape(seq_size * stop, width), own_sums.reshape(sums_rows, width)]
     )
     late = double(message[None], "clip", clip_size)
+    if aligned:
+        pairs_qkv, piece, late = after(pairs_qkv, piece, late)
     own_sums = jnp.sum(late[:, seq_size * stop :].astype(F32), axis=0).reshape(2, -1)
     late = late[:, : seq_size * stop].reshape(clip_size * seq_size, stop, width)
     devices = clip_size * seq_size
@@ -1221,7 +1268,30 @@
     up_bgrad = own_part(bias_sums[:hidden])
     down_bgrad = own_part(bias_sums[hidden : hidden + width])
     proj_bgrad = own_part(bias_sums[hidden + width : hidden + 2 * width])
-    meta, mod_wgrad, table_grad, qkv_wgrad = after(metas[0], mod_wgrad, table_grad, qkv_wgrad)
+    if aligned:
+        pieces = gather_pieces(piece, clip_size)
+        piece = sum_z(pairs_qkv, seq_size).reshape(2, row, 3 * LANES)
+        own_rows = lax.dynamic_index_in_dim(piece, parity, 0, keepdims=False)
+        far_rows = swap(lax.dynamic_index_in_dim(piece, 1 - parity, 0, keepdims=False))
+        far_rows, pieces, mod_wgrad, table_grad = after(far_rows, pieces, mod_wgrad, table_grad)
+        pieces_qkv = gather_pieces(jnp.stack([own_rows, far_rows]), clip_size)
+    else:
+        pieces = gather_pieces(piece, clip_size)
+        share = sum(
+            lax.dot_general(left, right, (((0,), (0,)), ((), ())), preferred_element_type=F32)
+            for left, right in zip(lefts, grad_rights)
+        ).astype(BF16)
+        share = share.reshape(width, 3, zs, 1, width // seq_size)
+        blank = jnp.zeros_like(share)
+        share = jnp.where(
+            parity == 0,
+            jnp.concatenate([share, blank], axis=3),
+            jnp.concatenate([blank, share], axis=3),
+        ).reshape(width, 3 * width)
+        qkv_wgrad = lax.psum(
+            lax.psum_scatter(share, "seq", scatter_dimension=0, tiled=True), "clip"
+        ).astype(F32)
+
     proj_wgrad, down_wgrad, up_wgrad = place_call(
         meta,
         pieces,
@@ -1232,6 +1302,9 @@
         ),
         [shaped((row, width), F32), shaped((hidden // seq_size, width), F32), shaped((row, hidden), F32)],
     )
+    if aligned:
+        pieces_qkv, proj_wgrad = after(pieces_qkv, proj_wgrad)
+        qkv_wgrad = place_qkv_call(meta, pieces_qkv, shaped((row, 3 * width), F32))
     layer_out = jnp.stack(layer)[:, None]
     return (
         layer_out,

time: 524 us -> 475 us (0.906)
  waiting for transfers between devices: 141 us -> 117 us
  local copies, waits for them, and re-layouts: 43.6 us -> 19.9 us
  Pallas kernels: 185 us -> 195 us
  matrix products: 19.5 us -> 12.1 us
    ppermute x57 -> x58, waiting for transfers between devices: 141 us -> 117 us  [exchange(): return lax.ppermute(array, axis, [(k, k ^ distance) for k in range(size)])]
    unnamed x184 -> x118, local copies, waits for them, and re-layouts: 25.9 us -> 6.54 us
    pallas_call x0 -> x2, Pallas kernels: none -> 10.5 us  [modulation_call(): pl.pallas_call(modulation_kernel, grid=(parts,), out_shape=[shaped((parts...]
    pallas_call x2, Pallas kernels: 58.2 us -> 48.1 us  [attend_grad_call(): pl.pallas_call(functools.partial(attend_grad_kernel, slots, head, clip),...]
    dot_general x2 -> x0, matrix products: 6.72 us -> none  [the longest x1 6.31 us: on_device(): jnp.dot(condition_low, mod_weight, preferred_element_type=F32)]
    ppermute x57 -> x58, starting transfers between devices: 94 us -> 92.6 us  [exchange(): return lax.ppermute(array, axis, [(k, k ^ distance) for k in range(size)])]
    convert_element_type x8 -> x12, other arithmetic: 16.1 us -> 15.6 us  [add_low(): return (left.astype(F32) + right.astype(F32)).astype(BF16)]
  transfers between devices with their start and end apart: 57 -> 58, of which waited for: 19 -> 18; matrix products, arithmetic and copies ran while one was open for 13% -> 12% of each run, Pallas kernels for 27% -> 34%
where the time goes in v4:
time: 475 us; the launch traced here: 470 us
  Pallas kernels  195 us (41%)
  waiting for transfers between devices  117 us (25%)
  starting transfers between devices  92.6 us (19%)
  other arithmetic  31.6 us (7%)
  local copies, waits for them, and re-layouts  19.9 us (4%)
  matrix products  12.1 us (3%)
    ppermute x58, waiting for transfers between devices, exchange(): return lax.ppermute(array, axis, [(k, k ^ distance) for k in range(size)])  117 us
    ppermute x58, starting transfers between devices, exchange(): return lax.ppermute(array, axis, [(k, k ^ distance) for k in range(size)])  92.6 us
    pallas_call x2, Pallas kernels, attend_grad_call(): pl.pallas_call(functools.partial(attend_grad_kernel, slots, head, clip),...  48.1 us
    pallas_call x2, Pallas kernels, forward_back_call(): pl.pallas_call(functools.partial(forward_back_kernel, slots, clip), grid=...  38.3 us
    pallas_call x2, Pallas kernels, attend_call(): pl.pallas_call(functools.partial(attend_kernel, slots, head, clip), out_s...  30.2 us
    pallas_call x2, Pallas kernels, weight_grad_call(): pl.pallas_call(functools.partial(weight_grad_kernel, tuple(jobs), clip_si...  25.1 us
    convert_element_type x12, other arithmetic, add_low(): return (left.astype(F32) + right.astype(F32)).astype(BF16)  15.6 us
    pallas_call x2, Pallas kernels, qkv_grad_call(): pl.pallas_call(functools.partial(qkv_grad_kernel, zs, head, clip), out_sh...  13.2 us
  transfers between devices with their start and end apart: 58, of which 18 were waited for; matrix products, arithmetic and copies ran while one was open for 12% of the time, Pallas kernels for 34%

profile of v4, /device:TPU:0, one launch (start us, length us, event | category | flops | bytes accessed | tf_op | source)
XLA Modules:
  0.0 469.9 jit_solution(7120595482967768056)
XLA Ops:
  9.0 4.0 modulation.2
  14.7 10.0 %norm_qkv.1 = (bf16[2,3,256,128]{3,2,1,0:T(8,128)(2,1)}, bf16[2,3,256,128]{3,2,1,0:T(8,128)(2,1)}, bf16[2,3,256,128]{3,2,1,0:T(8,128)(2,1)}, bf16[2,3,256,128]{3...) custom-call(s32[4]{0:T(128)} %pad_add_fusion.1.meta, ...), custom_call_target="tpu_custom_call" | custom-call | flops 3221225472 | bytes 11534336 | tf_op jit(solution)/shard_map/norm_qkv/pallas_call | solution.py:226
  24.7 3.1 collective-permute-start.2
  27.7 2.6 collective-permute-start.3
  30.3 6.5 %modulation.3 = (f32[4,2,1024]{2,1,0:T(2,128)}, f32[2,1024]{1,0:T(2,128)}) custom-call(s32[2]{0:T(128)} %copy-done.37, bf16[1024,1024]{1,0:T(8,128)(2,1)} %table.3, bf16[1024,6144]{1,0:T(8,128)(2,1)} %weight.3, bf16[1,6144]{1,0:T(2,128)(2,1)} %broadcast_in_dim.50.bias), custom_call_target="tpu_custom_call" | custom-call | bytes 10485760 | tf_op jit(solution)/shard_map/modulation/pallas_call | solution.py:128
  36.8 8.3 %collective-permute-done.2.refs_1_ = bf16[2,3,256,128]{3,2,1,0:T(8,128)(2,1)S(1)} collective-permute-done((bf16[2,3,256,128]{3,2,1,0:T(8,128)(2,1)}, bf16[2,3,256,128]{3,2,1,0:T(8,128)(2,1)S(1)}, u32[]{:S(2)}, u32[]{:S(2)}) %collective-permute-start.2) | collective-permute-done | bytes 393248 | tf_op jit(solution)/shard_map/ppermute | solution.py:949
  45.1 12.6 %collective-permute-done.3.refs_2_ = bf16[2,3,256,128]{3,2,1,0:T(8,128)(2,1)S(1)} collective-permute-done((bf16[2,3,256,128]{3,2,1,0:T(8,128)(2,1)}, bf16[2,3,256,128]{3,2,1,0:T(8,128)(2,1)S(1)}, u32[]{:S(2)}, u32[]{:S(2)}) %collective-permute-start.3) | collective-permute-done | bytes 393248 | tf_op jit(solution)/shard_map/ppermute | solution.py:949
  57.7 7.8 %collective-permute-start.5 = (bf16[2,3,256,128]{3,2,1,0:T(8,128)(2,1)}, bf16[2,3,256,128]{3,2,1,0:T(8,128)(2,1)S(1)}, u32[]{:S(2)}, u32[]{:S(2)}) collective-permute-start(bf16[2,3,256,128]{3,2,1,0:T(8,128)(2,1)} %get-tuple-element.236), channel_id=1, source_target_pairs={{0,8},{4,12},{8,0},{12,4},{16,24},{20,28},{24,16},{28,20},{1,9},{5... | collective-permute-start | bytes 1179656 | tf_op jit(solution)/shard_map/ppermute | solution.py:949
  65.5 1.8 collective-permute-start.6
  68.6 14.3 %attend.2 = (bf16[2,256,128]{2,1,0:T(8,128)(2,1)}, bf16[2,256,128]{2,1,0:T(8,128)(2,1)}, bf16[2,256,128]{2,1,0:T(8,128)(2,1)}, bf16[2,256,128]{2,1,0:T(8,128)(2,...) custom-call(s32[4]{0:T(128)} %pad_add_fusion.1.meta, bf16[2,3,256,128]{3,2,1,0:T(8,128)(2,1)} %get-tuple-element.227.refs_0_, ...), custom_call_target="tpu_custom_call" | custom-call | flops 8589934592 | bytes 3145728 | tf_op jit(solution)/shard_map/attend/pallas_call | solution.py:325
  83.0 12.6 %collective-permute-done.6.refs_2_ = bf16[2,3,256,128]{3,2,1,0:T(8,128)(2,1)S(1)} collective-permute-done((bf16[2,3,256,128]{3,2,1,0:T(8,128)(2,1)}, bf16[2,3,256,128]{3,2,1,0:T(8,128)(2,1)S(1)}, u32[]{:S(2)}, u32[]{:S(2)}) %collective-permute-start.6) | collective-permute-done | bytes 393248 | tf_op jit(solution)/shard_map/ppermute | solution.py:949
  95.6 6.7 %collective-permute-start.8 = (bf16[2,256,128]{2,1,0:T(8,128)(2,1)}, bf16[2,256,128]{2,1,0:T(8,128)(2,1)S(1)}, u32[]{:S(2)}, u32[]{:S(2)}) collective-permute-start(bf16[2,256,128]{2,1,0:T(8,128)(2,1)} %get-tuple-element.248), channel_id=1, source_target_pairs={{0,8},{4,12},{8,0},{12,4},{16,24},{20,28},{24,16},{28,20},{1,9},{5... | collective-permute-start | bytes 393224 | tf_op jit(solution)/shard_map/ppermute | solution.py:949
  104.8 15.9 %attend.3 = (bf16[2,256,128]{2,1,0:T(8,128)(2,1)}, bf16[2,256,128]{2,1,0:T(8,128)(2,1)}, bf16[2,256,128]{2,1,0:T(8,128)(2,1)}, bf16[2,256,128]{2,1,0:T(8,128)(2,...) custom-call(s32[4]{0:T(128)} %pad_add_fusion.1.meta, bf16[2,3,256,128]{3,2,1,0:T(8,128)(2,1)} %get-tuple-element.239.refs_0_, ...), custom_call_target="tpu_custom_call" | custom-call | flops 8589934592 | bytes 3145728 | tf_op jit(solution)/shard_map/attend/pallas_call | solution.py:325
  123.7 2.0 collective-permute-start.13
  127.9 19.0 %feed_forward.2 = (bf16[256,1024]{1,0:T(8,128)(2,1)}, f32[256,1024]{1,0:T(8,128)}, f32[8,1024]{1,0:T(8,128)}, f32[1,4096]{1,0:T(1,128)}, bf16[256,512]{1,0:T(8,1...) custom-call(s32[4]{0:T(128)} %pad_add_fusion.1.meta, ...), custom_call_target="tpu_custom_call" | custom-call | flops 9663676416 | bytes 37748736 | tf_op jit(solution)/shard_map/feed_forward/pallas_call | solution.py:607
  147.7 1.6 collective-permute-done.16.refs_4_
  150.2 3.5 proj_back.2
  154.0 2.9 collective-permute-start.18
  158.3 19.2 %feed_forward.3 = (bf16[256,1024]{1,0:T(8,128)(2,1)}, f32[256,1024]{1,0:T(8,128)}, f32[8,1024]{1,0:T(8,128)}, f32[1,4096]{1,0:T(1,128)}, bf16[256,512]{1,0:T(8,1...) custom-call(s32[4]{0:T(128)} %pad_add_fusion.1.meta, ...), custom_call_target="tpu_custom_call" | custom-call | flops 9663676416 | bytes 37748736 | tf_op jit(solution)/shard_map/feed_forward/pallas_call | solution.py:607
  177.7 2.1 collective-permute-done.21.far.refs_7_
  180.6 3.5 proj_back.3
  184.4 3.0 collective-permute-start.23
  188.8 22.5 %attend_grad.2 = (bf16[2,3,256,128]{3,2,1,0:T(8,128)(2,1)}, bf16[2,3,256,128]{3,2,1,0:T(8,128)(2,1)}, bf16[2,3,256,128]{3,2,1,0:T(8,128)(2,1)}, bf16[2,3,256,128]{3,2,1,0:T(8,128)(2,1)}) custom-call(s32[4]{0:T(128)} %pad_add_fusion.1.meta, bf16[2,3,256,128]{3,2,1,0:T(8,128)(2,1)} %get-tuple-element.227.refs_0_, bf16[2,3,256,128]{3,2,1,0:T(8,128)(2,1)} %copy-done.44, ...), custom_call_target="tpu_custom_call" | custom-call | flops 21474836480 | bytes 5242880 | tf_op jit(solution)/shard_map/attend_grad/pallas_call | solution.py:436
  211.4 16.4 %weight_grads.1 = (bf16[2,2,1152,256]{3,2,1,0:T(8,128)(2,1)}, bf16[2,2,1152,256]{3,2,1,0:T(8,128)(2,1)}, bf16[2,2,1152,256]{3,2,1,0:T(8,128)(2,1)}, bf16[2,2,1152,256]{3,2,1,0:T(8,128)(2,1)}) custom-call(s32[4]{0:T(128)} %pad_add_fusion.1.meta, bf16[256,512]{1,0:T(8,128)(2,1)} %get-tuple-element.286.refs_0_, bf16[256,512]{1,0:T(8,128)(2,1)} %get-tuple-element.287.refs_1_, ...), custom_call_target="tpu_custom_call" | custom-call | flops 9663676416 | bytes 28311552 | tf_op jit(solution)/shard_map/weight_grads/pallas_call | solution.py:877
  227.8 9.1 %collective-permute-start.29 = (bf16[2,2,1152,256]{3,2,1,0:T(8,128)(2,1)}, bf16[2,2,1152,256]{3,2,1,0:T(8,128)(2,1)}, u32[]{:S(2)}, u32[]{:S(2)}) collective-permute-start(bf16[2,2,1152,256]{3,2,1,0:T(8,128)(2,1)} %get-tuple-element.340), channel_id=1, source_target_pairs={{0,1},{1,0},{2,3},{3,2},{4,5},{5,4},{6,7},{7,6},{8,9},{9,8},{10,11... | collective-permute-start | bytes 7077896 | tf_op jit(solution)/shard_map/ppermute | solution.py:949
  237.6 3.0 collective-permute-start.27
  242.0 25.7 %attend_grad.3 = (bf16[2,3,256,128]{3,2,1,0:T(8,128)(2,1)}, bf16[2,3,256,128]{3,2,1,0:T(8,128)(2,1)}, bf16[2,3,256,128]{3,2,1,0:T(8,128)(2,1)}, bf16[2,3,256,128]{3,2,1,0:T(8,128)(2,1)}) custom-call(s32[4]{0:T(128)} %pad_add_fusion.1.meta, bf16[2,3,256,128]{3,2,1,0:T(8,128)(2,1)} %get-tuple-element.239.refs_0_, bf16[2,3,256,128]{3,2,1,0:T(8,128)(2,1)} %copy-done.41, ...), custom_call_target="tpu_custom_call" | custom-call | flops 21474836480 | bytes 5242880 | tf_op jit(solution)/shard_map/attend_grad/pallas_call | solution.py:436
  267.7 7.0 %collective-permute-start.31 = (bf16[2,3,256,128]{3,2,1,0:T(8,128)(2,1)}, bf16[2,3,256,128]{3,2,1,0:T(8,128)(2,1)S(1)}, u32[]{:S(2)}, u32[]{:S(2)}) collective-permute-start(bf16[2,3,256,128]{3,2,1,0:T(8,128)(2,1)} %get-tuple-element.344), channel_id=1, source_target_pairs={{0,8},{4,12},{8,0},{12,4},{16,24},{20,28},{24,16},{28,20},{1,9},{5... | collective-permute-start | bytes 1179656 | tf_op jit(solution)/shard_map/ppermute | solution.py:949
  275.7 1.5 collective-permute-start.33
  277.2 6.5 %qkv_grad.2 = (bf16[256,1536]{1,0:T(8,128)(2,1)}, bf16[256,1536]{1,0:T(8,128)(2,1)}, f32[256,1024]{1,0:T(8,128)}, f32[256,1024]{1,0:T(8,128)}, f32[8,512]{1,0:T(8,128)}) custom-call(s32[4]{0:T(128)} %pad_add_fusion.1.meta, f32[4,128]{1,0:T(4,128)} %get-tuple-element.482.refs_0_, f32[4,128]{1,0:T(4,128)} %get-tuple-element.481.refs_1_, ...), custom_call_target="tpu_custom_call" | custom-call | flops 1610612736 | bytes 8388608 | tf_op jit(solution)/shard_map/qkv_grad/pallas_call | solution.py:709
  284.5 3.7 collective-permute-done.29
  288.1 4.1 add_convert_fusion.4
  292.2 1.7 collective-permute-done.30
  293.9 3.6 add_convert_fusion.2
  297.5 7.3 %collective-permute-done.32.refs_6_ = bf16[2,3,256,128]{3,2,1,0:T(8,128)(2,1)S(1)} collective-permute-done((bf16[2,3,256,128]{3,2,1,0:T(8,128)(2,1)}, bf16[2,3,256,128]{3,2,1,0:T(8,128)(2,1)S(1)}, u32[]{:S(2)}, u32[]{:S(2)}) %collective-permute-start.32) | collective-permute-done | bytes 393248 | tf_op jit(solution)/shard_map/ppermute | solution.py:949
  305.6 6.7 %qkv_grad.3 = (bf16[256,1536]{1,0:T(8,128)(2,1)}, bf16[256,1536]{1,0:T(8,128)(2,1)}, f32[256,1024]{1,0:T(8,128)}, f32[256,1024]{1,0:T(8,128)}, f32[8,512]{1,0:T(8,128)}) custom-call(s32[4]{0:T(128)} %pad_add_fusion.1.meta, f32[4,128]{1,0:T(4,128)} %get-tuple-element.482.refs_0_, f32[4,128]{1,0:T(4,128)} %get-tuple-element.481.refs_1_, ...), custom_call_target="tpu_custom_call" | custom-call | flops 1610612736 | bytes 8388608 | tf_op jit(solution)/shard_map/qkv_grad/pallas_call | solution.py:709
  316.3 6.2 %norm_grad.1 = (f32[2,1,256,1024]{3,2,1,0:T(8,128)}, f32[2,8,1024]{2,1,0:T(8,128)}) custom-call(bf16[2,1,256,1024]{3,2,1,0:T(8,128)(2,1)} %tokens.7, f32[2,4,1024]{2,1,0:T(4,128)} %get-tuple-element.212.mod, f32[256,1024]{1,0:T(8,128)} %get-tuple-element.335.refs_0_, f32[256,1024]{1,0:T(8,128)} %get-tuple-element.352.refs_1_, ...), custom_call_target="tpu_custom_call" | custom-call | flops 15728640 | bytes 9437184 | tf_op jit(solution)/shard_map/norm_grad/pallas_call | solution.py:743
  324.0 8.7 %qkv_weight_grad.1 = (bf16[2,2,256,384]{3,2,1,0:T(8,128)(2,1)}, bf16[2,2,256,384]{3,2,1,0:T(8,128)(2,1)}, bf16[2,2,256,384]{3,2,1,0:T(8,128)(2,1)}, bf16[2,2,256,384]{3,2,1,0:T(8,128)(2,1)}) custom-call(s32[4]{0:T(128)} %pad_add_fusion.1.meta, bf16[256,1024]{1,0:T(8,128)(2,1)} %get-tuple-element.363.refs_0_, bf16[256,1024]{1,0:T(8,128)(2,1)} %get-tuple-element.364.refs_1_, ...), custom_call_target="tpu_custom_call" | custom-call | flops 3221225472 | bytes 9437184 | tf_op jit(solution)/shard_map/qkv_weight_grad/pallas_call | solution.py:877
  332.7 1.8 collective-permute-start.38
  334.5 1.8 collective-permute-start.39
  337.1 5.6 %collective-permute-start.41 = (bf16[2,24,1024]{2,1,0:T(8,128)(2,1)S(1)}, bf16[2,24,1024]{2,1,0:T(8,128)(2,1)S(1)}, u32[]{:S(2)}, u32[]{:S(2)}) collective-permute-start(bf16[2,24,1024]{2,1,0:T(8,128)(2,1)S(1)} %pad_maximum_fusion.9), channel_id=1, source_target_pairs={{0,8},{4,12},{8,0},{12,4},{16,24},{20,28},{24,16},{28,20},{1,9},{5... | collective-permute-start | bytes 294920 | tf_op jit(solution)/shard_map/ppermute | solution.py:949
  343.8 1.9 fusion.1
  346.5 6.6 %collective-permute-start.42 = (bf16[4,24,1024]{2,1,0:T(8,128)(2,1)S(1)}, bf16[4,24,1024]{2,1,0:T(8,128)(2,1)S(1)}, u32[]{:S(2)}, u32[]{:S(2)}) collective-permute-start(bf16[4,24,1024]{2,1,0:T(8,128)(2,1)S(1)} %pad_maximum_fusion.7), channel_id=1, source_target_pairs={{0,16},{4,20},{8,24},{12,28},{16,0},{20,4},{24,8},{28,12},{1,17},{... | collective-permute-start | bytes 589832 | tf_op jit(solution)/shard_map/ppermute | solution.py:949
  353.1 1.5 fusion
  354.6 7.0 %collective-permute-done.42 = bf16[4,24,1024]{2,1,0:T(8,128)(2,1)S(1)} collective-permute-done((bf16[4,24,1024]{2,1,0:T(8,128)(2,1)S(1)}, bf16[4,24,1024]{2,1,0:T(8,128)(2,1)S(1)}, u32[]{:S(2)}, u32[]{:S(2)}) %collective-permute-start.42) | collective-permute-done | bytes 196640 | tf_op jit(solution)/shard_map/ppermute | solution.py:949
  363.8 2.3 maximum_bitcast_fusion
  370.4 1.5 collective-permute-start.44
  373.0 1.5 collective-permute-start.43
  374.5 4.0 collective-permute-done.47
  378.7 1.5 collective-permute-start.48
  380.1 10.5 %collective-permute-done.45 = bf16[2,1152,256]{2,1,0:T(8,128)(2,1)S(1)} collective-permute-done((bf16[2,1152,256]{2,1,0:T(8,128)(2,1)}, bf16[2,1152,256]{2,1,0:T(8,128)(2,1)S(1)}, u32[]{:S(2)}, u32[]{:S(2)}) %collective-permute-start.45) | collective-permute-done | bytes 1179680 | tf_op jit(solution)/shard_map/ppermute | solution.py:949
  391.0 1.5 fusion.4
  392.8 2.3 collective-permute-done.48
  395.2 22.4 %collective-permute-done.46 = bf16[1,1152,256]{2,1,0:T(8,128)(2,1)S(1)} collective-permute-done((bf16[1,1152,256]{2,1,0:T(8,128)(2,1)S(1)}, bf16[1,1152,256]{2,1,0:T(8,128)(2,1)S(1)}, u32[]{:S(2)}, u32[]{:S(2)}) %collective-permute-start.46) | collective-permute-done | bytes 589856 | tf_op jit(solution)/shard_map/ppermute | solution.py:949
  418.5 1.5 collective-permute-start.54
  420.6 1.4 collective-permute-start.52
  423.4 8.5 %fusion.36 = f32[64,1024]{1,0:T(8,128)S(1)} fusion(bf16[64,6144]{1,0:T(8,128)(2,1)S(1)} %reshape.272, bf16[1024,6144]{1,0:T(8,128)(2,1)} %weight.3), kind=kOutput, calls=%fused_computation.109 | convolution fusion | flops 805306368 | bytes 13631488 | tf_op jit(solution)/shard_map/dot_general | solution.py:1245
  432.1 2.3 fusion.15
  434.4 7.9 %collective-permute-done.49 = bf16[2,256,384]{2,1,0:T(8,128)(2,1)S(1)} collective-permute-done((bf16[2,256,384]{2,1,0:T(8,128)(2,1)S(1)}, bf16[2,256,384]{2,1,0:T(8,128)(2,1)S(1)}, u32[]{:S(2)}, u32[]{:S(2)}) %collective-permute-start.49) | collective-permute-done | bytes 393248 | tf_op jit(solution)/shard_map/ppermute | solution.py:949
  443.9 8.9 %collective-permute-done.50 = bf16[1,256,384]{2,1,0:T(8,128)(2,1)S(1)} collective-permute-done((bf16[1,256,384]{2,1,0:T(8,128)(2,1)S(1)}, bf16[1,256,384]{2,1,0:T(8,128)(2,1)S(1)}, u32[]{:S(2)}, u32[]{:S(2)}) %collective-permute-start.50) | collective-permute-done | bytes 196640 | tf_op jit(solution)/shard_map/ppermute | solution.py:949
  454.3 1.5 collective-permute-start.57
  456.4 1.4 collective-permute-start.55
  461.1 4.1 place_grads.1
  467.2 2.6 place_qkv_grad.1
  (288 shorter events, 57.6 us)
Async XLA Ops:
  1.3 5.7 %collective-permute-start.1 = (s32[2,2]{1,0:T(2,128)S(1)}, s32[2,2]{1,0:T(2,128)S(1)}, u32[]{:S(2)}, u32[]{:S(2)}) collective-permute-start(s32[2,2]{1,0:T(2,128)S(1)} %pad_add_fusion), channel_id=1, source_target_pairs={{0,4},{4,0},{8,12},{12,8},{16,20},{20,16},{24,28},{28,24},{1,5},{5... | collective-permute-start | bytes 56 | tf_op jit(solution)/shard_map/ppermute | solution.py:949
  1.8 11.9 %collective-permute-start = (bf16[2,1,256,1024]{3,2,1,0:T(8,128)(2,1)}, bf16[2,1,256,1024]{3,2,1,0:T(8,128)(2,1)S(1)}, u32[]{:S(2)}, u32[]{:S(2)}) collective-permute-start(bf16[2,1,256,1024]{3,2,1,0:T(8,128)(2,1)} %tokens.7), channel_id=1, source_target_pairs={{0,4},{4,0},{8,12},{12,8},{16,20},{20,16},{24,28},{28,24},{1,5},{5... | collective-permute-start | bytes 3145736 | tf_op jit(solution)/shard_map/ppermute | solution.py:949
  24.7 20.4 %collective-permute-start.2 = (bf16[2,3,256,128]{3,2,1,0:T(8,128)(2,1)}, bf16[2,3,256,128]{3,2,1,0:T(8,128)(2,1)S(1)}, u32[]{:S(2)}, u32[]{:S(2)}) collective-permute-start(bf16[2,3,256,128]{3,2,1,0:T(8,128)(2,1)} %get-tuple-element.214), channel_id=1, source_target_pairs={{0,8},{4,12},{8,0},{12,4},{16,24},{20,28},{24,16},{28,20},{1,9},{5... | collective-permute-start | bytes 1179656 | tf_op jit(solution)/shard_map/ppermute | solution.py:949
  27.7 30.0 %collective-permute-start.3 = (bf16[2,3,256,128]{3,2,1,0:T(8,128)(2,1)}, bf16[2,3,256,128]{3,2,1,0:T(8,128)(2,1)S(1)}, u32[]{:S(2)}, u32[]{:S(2)}) collective-permute-start(bf16[2,3,256,128]{3,2,1,0:T(8,128)(2,1)} %get-tuple-element.215), channel_id=1, source_target_pairs={{0,16},{4,20},{8,24},{12,28},{16,0},{20,4},{24,8},{28,12},{1,17},{... | collective-permute-start | bytes 1179656 | tf_op jit(solution)/shard_map/ppermute | solution.py:949
  30.3 27.4 %collective-permute-start.4 = (bf16[2,3,256,128]{3,2,1,0:T(8,128)(2,1)}, bf16[2,3,256,128]{3,2,1,0:T(8,128)(2,1)S(1)}, u32[]{:S(2)}, u32[]{:S(2)}) collective-permute-start(bf16[2,3,256,128]{3,2,1,0:T(8,128)(2,1)} %get-tuple-element.216), channel_id=1, source_target_pairs={{0,24},{4,28},{8,16},{12,20},{16,8},{20,12},{24,0},{28,4},{1,25},{... | collective-permute-start | bytes 1179656 | tf_op jit(solution)/shard_map/ppermute | solution.py:949
  57.7 25.3 %collective-permute-start.5 = (bf16[2,3,256,128]{3,2,1,0:T(8,128)(2,1)}, bf16[2,3,256,128]{3,2,1,0:T(8,128)(2,1)S(1)}, u32[]{:S(2)}, u32[]{:S(2)}) collective-permute-start(bf16[2,3,256,128]{3,2,1,0:T(8,128)(2,1)} %get-tuple-element.236), channel_id=1, source_target_pairs={{0,8},{4,12},{8,0},{12,4},{16,24},{20,28},{24,16},{28,20},{1,9},{5... | collective-permute-start | bytes 1179656 | tf_op jit(solution)/shard_map/ppermute | solution.py:949
  65.5 30.0 %collective-permute-start.6 = (bf16[2,3,256,128]{3,2,1,0:T(8,128)(2,1)}, bf16[2,3,256,128]{3,2,1,0:T(8,128)(2,1)S(1)}, u32[]{:S(2)}, u32[]{:S(2)}) collective-permute-start(bf16[2,3,256,128]{3,2,1,0:T(8,128)(2,1)} %get-tuple-element.237), channel_id=1, source_target_pairs={{0,16},{4,20},{8,24},{12,28},{16,0},{20,4},{24,8},{28,12},{1,17},{... | collective-permute-start | bytes 1179656 | tf_op jit(solution)/shard_map/ppermute | solution.py:949
  67.3 28.3 %collective-permute-start.7 = (bf16[2,3,256,128]{3,2,1,0:T(8,128)(2,1)}, bf16[2,3,256,128]{3,2,1,0:T(8,128)(2,1)S(1)}, u32[]{:S(2)}, u32[]{:S(2)}) collective-permute-start(bf16[2,3,256,128]{3,2,1,0:T(8,128)(2,1)} %get-tuple-element.238), channel_id=1, source_target_pairs={{0,24},{4,28},{8,16},{12,20},{16,8},{20,12},{24,0},{28,4},{1,25},{... | collective-permute-start | bytes 1179656 | tf_op jit(solution)/shard_map/ppermute | solution.py:949
  95.6 26.0 %copy-start.40 = (bf16[1024]{0:T(1024)(128)(2,1)S(1)}, bf16[1024]{0:T(1024)(128)(2,1)}, u32[]{:S(2)}) copy-start(bf16[1024]{0:T(1024)(128)(2,1)} %param.31) | copy-start | bytes 6148
  95.6 26.5 %copy-start.36 = (bf16[4096]{0:T(1024)(128)(2,1)S(1)}, bf16[4096]{0:T(1024)(128)(2,1)}, u32[]{:S(2)}) copy-start(bf16[4096]{0:T(1024)(128)(2,1)} %param.29) | copy-start | bytes 24580
  95.6 25.1 %collective-permute-start.8 = (bf16[2,256,128]{2,1,0:T(8,128)(2,1)}, bf16[2,256,128]{2,1,0:T(8,128)(2,1)S(1)}, u32[]{:S(2)}, u32[]{:S(2)}) collective-permute-start(bf16[2,256,128]{2,1,0:T(8,128)(2,1)} %get-tuple-element.248), channel_id=1, source_target_pairs={{0,8},{4,12},{8,0},{12,4},{16,24},{20,28},{24,16},{28,20},{1,9},{5... | collective-permute-start | bytes 393224 | tf_op jit(solution)/shard_map/ppermute | solution.py:949
  102.3 18.4 %collective-permute-start.9 = (bf16[2,256,128]{2,1,0:T(8,128)(2,1)}, bf16[2,256,128]{2,1,0:T(8,128)(2,1)S(1)}, u32[]{:S(2)}, u32[]{:S(2)}) collective-permute-start(bf16[2,256,128]{2,1,0:T(8,128)(2,1)} %get-tuple-element.249), channel_id=1, source_target_pairs={{0,16},{4,20},{8,24},{12,28},{16,0},{20,4},{24,8},{28,12},{1,17},{... | collective-permute-start | bytes 393224 | tf_op jit(solution)/shard_map/ppermute | solution.py:949
  103.4 17.3 %collective-permute-start.10 = (bf16[2,256,128]{2,1,0:T(8,128)(2,1)}, bf16[2,256,128]{2,1,0:T(8,128)(2,1)S(1)}, u32[]{:S(2)}, u32[]{:S(2)}) collective-permute-start(bf16[2,256,128]{2,1,0:T(8,128)(2,1)} %get-tuple-element.250), channel_id=1, source_target_pairs={{0,24},{4,28},{8,16},{12,20},{16,8},{20,12},{24,0},{28,4},{1,25},{... | collective-permute-start | bytes 393224 | tf_op jit(solution)/shard_map/ppermute | solution.py:949
  120.9 6.3 %collective-permute-start.11 = (bf16[4,256,128]{2,1,0:T(8,128)(2,1)S(1)}, bf16[4,256,128]{2,1,0:T(8,128)(2,1)S(1)}, u32[]{:S(2)}, u32[]{:S(2)}) collective-permute-start(bf16[4,256,128]{2,1,0:T(8,128)(2,1)S(1)} %pad_maximum_fusion.5), channel_id=1, source_target_pairs={{0,4},{4,0},{8,12},{12,8},{16,20},{20,16},{24,28},{28,24},{1,5},{5... | collective-permute-start | bytes 786440 | tf_op jit(solution)/shard_map/ppermute | solution.py:949
  122.8 24.2 %collective-permute-start.12 = (bf16[2,256,128]{2,1,0:T(8,128)(2,1)}, bf16[2,256,128]{2,1,0:T(8,128)(2,1)S(1)}, u32[]{:S(2)}, u32[]{:S(2)}) collective-permute-start(bf16[2,256,128]{2,1,0:T(8,128)(2,1)} %get-tuple-element.259), channel_id=1, source_target_pairs={{0,8},{4,12},{8,0},{12,4},{16,24},{20,28},{24,16},{28,20},{1,9},{5... | collective-permute-start | bytes 393224 | tf_op jit(solution)/shard_map/ppermute | solution.py:949
  123.7 23.2 %collective-permute-start.13 = (bf16[2,256,128]{2,1,0:T(8,128)(2,1)}, bf16[2,256,128]{2,1,0:T(8,128)(2,1)S(1)}, u32[]{:S(2)}, u32[]{:S(2)}) collective-permute-start(bf16[2,256,128]{2,1,0:T(8,128)(2,1)} %get-tuple-element.260), channel_id=1, source_target_pairs={{0,16},{4,20},{8,24},{12,28},{16,0},{20,4},{24,8},{28,12},{1,17},{... | collective-permute-start | bytes 393224 | tf_op jit(solution)/shard_map/ppermute | solution.py:949
  125.8 21.2 %collective-permute-start.14 = (bf16[2,256,128]{2,1,0:T(8,128)(2,1)}, bf16[2,256,128]{2,1,0:T(8,128)(2,1)S(1)}, u32[]{:S(2)}, u32[]{:S(2)}) collective-permute-start(bf16[2,256,128]{2,1,0:T(8,128)(2,1)} %get-tuple-element.261), channel_id=1, source_target_pairs={{0,24},{4,28},{8,16},{12,20},{16,8},{20,12},{24,0},{28,4},{1,25},{... | collective-permute-start | bytes 393224 | tf_op jit(solution)/shard_map/ppermute | solution.py:949
  147.0 2.4 collective-permute-start.15
  147.2 2.2 collective-permute-start.16
  153.7 23.9 %collective-permute-start.20 = (bf16[256,7680]{1,0:T(8,128)(2,1)}, bf16[256,7680]{1,0:T(8,128)(2,1)}, u32[]{:S(2)}, u32[]{:S(2)}) collective-permute-start(bf16[256,7680]{1,0:T(8,128)(2,1)} %get-tuple-element.309.refs_12_.refs_20_), channel_id=1, source_target_pairs={{0,4},{4,0},{8,12},{12,8},{16,20},{20,16},{24,28},{28,24},{1,5},{5... | collective-permute-start | bytes 11796488 | tf_op jit(solution)/shard_map/ppermute | solution.py:949
  153.9 23.6 %collective-permute-start.17 = (bf16[2,256,128]{2,1,0:T(8,128)(2,1)}, bf16[2,256,128]{2,1,0:T(8,128)(2,1)S(1)}, u32[]{:S(2)}, u32[]{:S(2)}) collective-permute-start(bf16[2,256,128]{2,1,0:T(8,128)(2,1)} %get-tuple-element.277), channel_id=1, source_target_pairs={{0,8},{4,12},{8,0},{12,4},{16,24},{20,28},{24,16},{28,20},{1,9},{5... | collective-permute-start | bytes 393224 | tf_op jit(solution)/shard_map/ppermute | solution.py:949
  154.0 23.6 %collective-permute-start.18 = (bf16[2,256,128]{2,1,0:T(8,128)(2,1)}, bf16[2,256,128]{2,1,0:T(8,128)(2,1)S(1)}, u32[]{:S(2)}, u32[]{:S(2)}) collective-permute-start(bf16[2,256,128]{2,1,0:T(8,128)(2,1)} %get-tuple-element.278), channel_id=1, source_target_pairs={{0,16},{4,20},{8,24},{12,28},{16,0},{20,4},{24,8},{28,12},{1,17},{... | collective-permute-start | bytes 393224 | tf_op jit(solution)/shard_map/ppermute | solution.py:949
  156.9 20.7 %collective-permute-start.19 = (bf16[2,256,128]{2,1,0:T(8,128)(2,1)}, bf16[2,256,128]{2,1,0:T(8,128)(2,1)S(1)}, u32[]{:S(2)}, u32[]{:S(2)}) collective-permute-start(bf16[2,256,128]{2,1,0:T(8,128)(2,1)} %get-tuple-element.279), channel_id=1, source_target_pairs={{0,24},{4,28},{8,16},{12,20},{16,8},{20,12},{24,0},{28,4},{1,25},{... | collective-permute-start | bytes 393224 | tf_op jit(solution)/shard_map/ppermute | solution.py:949
  177.6 2.2 collective-permute-start.21
  184.1 27.2 %collective-permute-start.25 = (bf16[256,7680]{1,0:T(8,128)(2,1)}, bf16[256,7680]{1,0:T(8,128)(2,1)}, u32[]{:S(2)}, u32[]{:S(2)}) collective-permute-start(bf16[256,7680]{1,0:T(8,128)(2,1)} %get-tuple-element.310.refs_14_.refs_22_), channel_id=1, source_target_pairs={{0,4},{4,0},{8,12},{12,8},{16,20},{20,16},{24,28},{28,24},{1,5},{5... | collective-permute-start | bytes 11796488 | tf_op jit(solution)/shard_map/ppermute | solution.py:949
  184.3 27.0 %collective-permute-start.22 = (bf16[2,256,128]{2,1,0:T(8,128)(2,1)}, bf16[2,256,128]{2,1,0:T(8,128)(2,1)S(1)}, u32[]{:S(2)}, u32[]{:S(2)}) collective-permute-start(bf16[2,256,128]{2,1,0:T(8,128)(2,1)} %get-tuple-element.304), channel_id=1, source_target_pairs={{0,8},{4,12},{8,0},{12,4},{16,24},{20,28},{24,16},{28,20},{1,9},{5... | collective-permute-start | bytes 393224 | tf_op jit(solution)/shard_map/ppermute | solution.py:949
  184.4 26.9 %collective-permute-start.23 = (bf16[2,256,128]{2,1,0:T(8,128)(2,1)}, bf16[2,256,128]{2,1,0:T(8,128)(2,1)S(1)}, u32[]{:S(2)}, u32[]{:S(2)}) collective-permute-start(bf16[2,256,128]{2,1,0:T(8,128)(2,1)} %get-tuple-element.305), channel_id=1, source_target_pairs={{0,16},{4,20},{8,24},{12,28},{16,0},{20,4},{24,8},{28,12},{1,17},{... | collective-permute-start | bytes 393224 | tf_op jit(solution)/shard_map/ppermute | solution.py:949
  187.4 23.9 %collective-permute-start.24 = (bf16[2,256,128]{2,1,0:T(8,128)(2,1)}, bf16[2,256,128]{2,1,0:T(8,128)(2,1)S(1)}, u32[]{:S(2)}, u32[]{:S(2)}) collective-permute-start(bf16[2,256,128]{2,1,0:T(8,128)(2,1)} %get-tuple-element.306), channel_id=1, source_target_pairs={{0,24},{4,28},{8,16},{12,20},{16,8},{20,12},{24,0},{28,4},{1,25},{... | collective-permute-start | bytes 393224 | tf_op jit(solution)/shard_map/ppermute | solution.py:949
  211.4 26.3 %copy-start.48 = (bf16[2,3,256,128]{3,2,1,0:T(8,128)(2,1)S(1)}, bf16[2,3,256,128]{3,2,1,0:T(8,128)(2,1)}, u32[]{:S(2)}) copy-start(bf16[2,3,256,128]{3,2,1,0:T(8,128)(2,1)} %get-tuple-element.327) | copy-start | bytes 1179652
  211.4 29.3 %copy-start.47 = (bf16[2,3,256,128]{3,2,1,0:T(8,128)(2,1)S(1)}, bf16[2,3,256,128]{3,2,1,0:T(8,128)(2,1)}, u32[]{:S(2)}) copy-start(bf16[2,3,256,128]{3,2,1,0:T(8,128)(2,1)} %get-tuple-element.328) | copy-start | bytes 1179652
  227.8 60.3 %collective-permute-start.29 = (bf16[2,2,1152,256]{3,2,1,0:T(8,128)(2,1)}, bf16[2,2,1152,256]{3,2,1,0:T(8,128)(2,1)}, u32[]{:S(2)}, u32[]{:S(2)}) collective-permute-start(bf16[2,2,1152,256]{3,2,1,0:T(8,128)(2,1)} %get-tuple-element.340), channel_id=1, source_target_pairs={{0,1},{1,0},{2,3},{3,2},{4,5},{5,4},{6,7},{7,6},{8,9},{9,8},{10,11... | collective-permute-start | bytes 7077896 | tf_op jit(solution)/shard_map/ppermute | solution.py:949
  237.6 30.1 %collective-permute-start.26 = (bf16[2,3,256,128]{3,2,1,0:T(8,128)(2,1)}, bf16[2,3,256,128]{3,2,1,0:T(8,128)(2,1)S(1)}, u32[]{:S(2)}, u32[]{:S(2)}) collective-permute-start(bf16[2,3,256,128]{3,2,1,0:T(8,128)(2,1)} %get-tuple-element.326), channel_id=1, source_target_pairs={{0,8},{4,12},{8,0},{12,4},{16,24},{20,28},{24,16},{28,20},{1,9},{5... | collective-permute-start | bytes 1179656 | tf_op jit(solution)/shard_map/ppermute | solution.py:949
  237.6 30.1 %collective-permute-start.27 = (bf16[2,3,256,128]{3,2,1,0:T(8,128)(2,1)S(1)}, bf16[2,3,256,128]{3,2,1,0:T(8,128)(2,1)S(1)}, u32[]{:S(2)}, u32[]{:S(2)}) collective-permute-start(bf16[2,3,256,128]{3,2,1,0:T(8,128)(2,1)S(1)} %copy-done.48), channel_id=1, source_target_pairs={{0,16},{4,20},{8,24},{12,28},{16,0},{20,4},{24,8},{28,12},{1,17},{... | collective-permute-start | bytes 1179656 | tf_op jit(solution)/shard_map/ppermute | solution.py:949
  240.6 27.1 %collective-permute-start.28 = (bf16[2,3,256,128]{3,2,1,0:T(8,128)(2,1)S(1)}, bf16[2,3,256,128]{3,2,1,0:T(8,128)(2,1)S(1)}, u32[]{:S(2)}, u32[]{:S(2)}) collective-permute-start(bf16[2,3,256,128]{3,2,1,0:T(8,128)(2,1)S(1)} %copy-done.47), channel_id=1, source_target_pairs={{0,24},{4,28},{8,16},{12,20},{16,8},{20,12},{24,0},{28,4},{1,25},{... | collective-permute-start | bytes 1179656 | tf_op jit(solution)/shard_map/ppermute | solution.py:949
  242.0 51.9 %collective-permute-start.30 = (bf16[2,2,1152,256]{3,2,1,0:T(8,128)(2,1)}, bf16[2,2,1152,256]{3,2,1,0:T(8,128)(2,1)}, u32[]{:S(2)}, u32[]{:S(2)}) collective-permute-start(bf16[2,2,1152,256]{3,2,1,0:T(8,128)(2,1)} %get-tuple-element.342), channel_id=1, source_target_pairs={{0,2},{1,3},{2,0},{3,1},{4,6},{5,7},{6,4},{7,5},{8,10},{9,11},{10,... | collective-permute-start | bytes 7077896 | tf_op jit(solution)/shard_map/ppermute | solution.py:949
  267.7 29.7 %collective-permute-start.31 = (bf16[2,3,256,128]{3,2,1,0:T(8,128)(2,1)}, bf16[2,3,256,128]{3,2,1,0:T(8,128)(2,1)S(1)}, u32[]{:S(2)}, u32[]{:S(2)}) collective-permute-start(bf16[2,3,256,128]{3,2,1,0:T(8,128)(2,1)} %get-tuple-element.344), channel_id=1, source_target_pairs={{0,8},{4,12},{8,0},{12,4},{16,24},{20,28},{24,16},{28,20},{1,9},{5... | collective-permute-start | bytes 1179656 | tf_op jit(solution)/shard_map/ppermute | solution.py:949
  274.8 30.0 %collective-permute-start.32 = (bf16[2,3,256,128]{3,2,1,0:T(8,128)(2,1)}, bf16[2,3,256,128]{3,2,1,0:T(8,128)(2,1)S(1)}, u32[]{:S(2)}, u32[]{:S(2)}) collective-permute-start(bf16[2,3,256,128]{3,2,1,0:T(8,128)(2,1)} %get-tuple-element.345), channel_id=1, source_target_pairs={{0,16},{4,20},{8,24},{12,28},{16,0},{20,4},{24,8},{28,12},{1,17},{... | collective-permute-start | bytes 1179656 | tf_op jit(solution)/shard_map/ppermute | solution.py:949
  275.7 29.1 %collective-permute-start.33 = (bf16[2,3,256,128]{3,2,1,0:T(8,128)(2,1)}, bf16[2,3,256,128]{3,2,1,0:T(8,128)(2,1)}, u32[]{:S(2)}, u32[]{:S(2)}) collective-permute-start(bf16[2,3,256,128]{3,2,1,0:T(8,128)(2,1)} %get-tuple-element.346), channel_id=1, source_target_pairs={{0,24},{4,28},{8,16},{12,20},{16,8},{20,12},{24,0},{28,4},{1,25},{... | collective-permute-start | bytes 1179656 | tf_op jit(solution)/shard_map/ppermute | solution.py:949
  288.1 28.2 %collective-permute-start.34 = (f32[256,1024]{1,0:T(8,128)}, f32[256,1024]{1,0:T(8,128)}, u32[]{:S(2)}, u32[]{:S(2)}) collective-permute-start(f32[256,1024]{1,0:T(8,128)} %get-tuple-element.353), channel_id=1, source_target_pairs={{0,4},{4,0},{8,12},{12,8},{16,20},{20,16},{24,28},{28,24},{1,5},{5... | collective-permute-start | bytes 3145736 | tf_op jit(solution)/shard_map/ppermute | solution.py:949
  312.2 4.1 collective-permute-start.35
  314.7 29.1 %collective-permute-start.36 = (bf16[1,2,1152,256]{3,2,1,0:T(8,128)(2,1)}, bf16[1,2,1152,256]{3,2,1,0:T(8,128)(2,1)}, u32[]{:S(2)}, u32[]{:S(2)}) collective-permute-start(bf16[1,2,1152,256]{3,2,1,0:T(8,128)(2,1)} %get-tuple-element.358), channel_id=1, source_target_pairs={{0,2},{1,3},{2,0},{3,1},{4,6},{5,7},{6,4},{7,5},{8,10},{9,11},{10,... | collective-permute-start | bytes 3538952 | tf_op jit(solution)/shard_map/ppermute | solution.py:949
  314.7 29.1 %collective-permute-start.37 = (bf16[1,2,1152,256]{3,2,1,0:T(8,128)(2,1)}, bf16[1,2,1152,256]{3,2,1,0:T(8,128)(2,1)}, u32[]{:S(2)}, u32[]{:S(2)}) collective-permute-start(bf16[1,2,1152,256]{3,2,1,0:T(8,128)(2,1)} %get-tuple-element.359), channel_id=1, source_target_pairs={{0,1},{1,0},{2,3},{3,2},{4,5},{5,4},{6,7},{7,6},{8,9},{9,8},{10,11... | collective-permute-start | bytes 3538952 | tf_op jit(solution)/shard_map/ppermute | solution.py:949
  323.7 12.6 %collective-permute-start.40 = (bf16[1,24,1024]{2,1,0:T(8,128)(2,1)S(1)}, bf16[1,24,1024]{2,1,0:T(8,128)(2,1)}, u32[]{:S(2)}, u32[]{:S(2)}) collective-permute-start(bf16[1,24,1024]{2,1,0:T(8,128)(2,1)S(1)} %concatenate.84), channel_id=1, source_target_pairs={{0,4},{4,0},{8,12},{12,8},{16,20},{20,16},{24,28},{28,24},{1,5},{5... | collective-permute-start | bytes 147464 | tf_op jit(solution)/shard_map/ppermute | solution.py:949
  332.7 33.4 %collective-permute-start.38 = (bf16[2,2,256,384]{3,2,1,0:T(8,128)(2,1)}, bf16[2,2,256,384]{3,2,1,0:T(8,128)(2,1)S(1)}, u32[]{:S(2)}, u32[]{:S(2)}) collective-permute-start(bf16[2,2,256,384]{3,2,1,0:T(8,128)(2,1)} %get-tuple-element.372), channel_id=1, source_target_pairs={{0,1},{1,0},{2,3},{3,2},{4,5},{5,4},{6,7},{7,6},{8,9},{9,8},{10,11... | collective-permute-start | bytes 2359304 | tf_op jit(solution)/shard_map/ppermute | solution.py:949
  334.5 31.6 %collective-permute-start.39 = (bf16[2,2,256,384]{3,2,1,0:T(8,128)(2,1)}, bf16[2,2,256,384]{3,2,1,0:T(8,128)(2,1)}, u32[]{:S(2)}, u32[]{:S(2)}) collective-permute-start(bf16[2,2,256,384]{3,2,1,0:T(8,128)(2,1)} %get-tuple-element.373), channel_id=1, source_target_pairs={{0,2},{1,3},{2,0},{3,1},{4,6},{5,7},{6,4},{7,5},{8,10},{9,11},{10,... | collective-permute-start | bytes 2359304 | tf_op jit(solution)/shard_map/ppermute | solution.py:949
  337.1 8.6 %collective-permute-start.41 = (bf16[2,24,1024]{2,1,0:T(8,128)(2,1)S(1)}, bf16[2,24,1024]{2,1,0:T(8,128)(2,1)S(1)}, u32[]{:S(2)}, u32[]{:S(2)}) collective-permute-start(bf16[2,24,1024]{2,1,0:T(8,128)(2,1)S(1)} %pad_maximum_fusion.9), channel_id=1, source_target_pairs={{0,8},{4,12},{8,0},{12,4},{16,24},{20,28},{24,16},{28,20},{1,9},{5... | collective-permute-start | bytes 294920 | tf_op jit(solution)/shard_map/ppermute | solution.py:949
  346.5 15.2 %collective-permute-start.42 = (bf16[4,24,1024]{2,1,0:T(8,128)(2,1)S(1)}, bf16[4,24,1024]{2,1,0:T(8,128)(2,1)S(1)}, u32[]{:S(2)}, u32[]{:S(2)}) collective-permute-start(bf16[4,24,1024]{2,1,0:T(8,128)(2,1)S(1)} %pad_maximum_fusion.7), channel_id=1, source_target_pairs={{0,16},{4,20},{8,24},{12,28},{16,0},{20,4},{24,8},{28,12},{1,17},{... | collective-permute-start | bytes 589832 | tf_op jit(solution)/shard_map/ppermute | solution.py:949
  363.8 26.9 %collective-permute-start.45 = (bf16[2,1152,256]{2,1,0:T(8,128)(2,1)}, bf16[2,1152,256]{2,1,0:T(8,128)(2,1)S(1)}, u32[]{:S(2)}, u32[]{:S(2)}) collective-permute-start(bf16[2,1152,256]{2,1,0:T(8,128)(2,1)} %pad_maximum_fusion), channel_id=1, source_target_pairs={{0,8},{4,12},{8,0},{12,4},{16,24},{20,28},{24,16},{28,20},{1,9},{5... | collective-permute-start | bytes 3538952 | tf_op jit(solution)/shard_map/ppermute | solution.py:949
  368.6 10.0 %collective-permute-start.47 = (bf16[1,144,1024]{2,1,0:T(8,128)(2,1)S(1)}, bf16[1,144,1024]{2,1,0:T(8,128)(2,1)S(1)}, u32[]{:S(2)}, u32[]{:S(2)}) collective-permute-start(bf16[1,144,1024]{2,1,0:T(8,128)(2,1)S(1)} %maximum_bitcast_fusion.1), channel_id=1, source_target_pairs={{0,1},{1,0},{2,3},{3,2},{4,5},{5,4},{6,7},{7,6},{8,9},{9,8},{10,11... | collective-permute-start | bytes 884744 | tf_op jit(solution)/shard_map/ppermute | solution.py:949
  370.4 20.6 %collective-permute-start.44 = (bf16[1,2,256,384]{3,2,1,0:T(8,128)(2,1)S(1)}, bf16[1,2,256,384]{3,2,1,0:T(8,128)(2,1)S(1)}, u32[]{:S(2)}, u32[]{:S(2)}) collective-permute-start(bf16[1,2,256,384]{3,2,1,0:T(8,128)(2,1)S(1)} %add_convert_fusion.10), channel_id=1, source_target_pairs={{0,1},{1,0},{2,3},{3,2},{4,5},{5,4},{6,7},{7,6},{8,9},{9,8},{10,11... | collective-permute-start | bytes 1179656 | tf_op jit(solution)/shard_map/ppermute | solution.py:949
  373.0 19.5 %collective-permute-start.43 = (bf16[1,2,256,384]{3,2,1,0:T(8,128)(2,1)S(1)}, bf16[1,2,256,384]{3,2,1,0:T(8,128)(2,1)S(1)}, u32[]{:S(2)}, u32[]{:S(2)}) collective-permute-start(bf16[1,2,256,384]{3,2,1,0:T(8,128)(2,1)S(1)} %add_convert_fusion.13), channel_id=1, source_target_pairs={{0,2},{1,3},{2,0},{3,1},{4,6},{5,7},{6,4},{7,5},{8,10},{9,11},{10,... | collective-permute-start | bytes 1179656 | tf_op jit(solution)/shard_map/ppermute | solution.py:949
  378.7 16.4 %collective-permute-start.48 = (bf16[2,144,1024]{2,1,0:T(8,128)(2,1)S(1)}, bf16[2,144,1024]{2,1,0:T(8,128)(2,1)S(1)}, u32[]{:S(2)}, u32[]{:S(2)}) collective-permute-start(bf16[2,144,1024]{2,1,0:T(8,128)(2,1)S(1)} %pad_maximum_fusion.2), channel_id=1, source_target_pairs={{0,2},{1,3},{2,0},{3,1},{4,6},{5,7},{6,4},{7,5},{8,10},{9,11},{10,... | collective-permute-start | bytes 1769480 | tf_op jit(solution)/shard_map/ppermute | solution.py:949
  390.9 26.8 %collective-permute-start.46 = (bf16[1,1152,256]{2,1,0:T(8,128)(2,1)S(1)}, bf16[1,1152,256]{2,1,0:T(8,128)(2,1)S(1)}, u32[]{:S(2)}, u32[]{:S(2)}) collective-permute-start(bf16[1,1152,256]{2,1,0:T(8,128)(2,1)S(1)} %add_convert_fusion.7), channel_id=1, source_target_pairs={{0,16},{4,20},{8,24},{12,28},{16,0},{20,4},{24,8},{28,12},{1,17},{... | collective-permute-start | bytes 1769480 | tf_op jit(solution)/shard_map/ppermute | solution.py:949
  392.5 29.7 %copy-start.8 = (bf16[2,256,384]{2,1,0:T(8,128)(2,1)}, bf16[2,256,384]{2,1,0:T(8,128)(2,1)S(1)}, u32[]{:S(2)}) copy-start(bf16[2,256,384]{2,1,0:T(8,128)(2,1)S(1)} %fusion.4) | copy-start | bytes 1179652
  392.7 29.5 %copy-start.6 = (bf16[2,256,384]{2,1,0:T(8,128)(2,1)}, bf16[2,256,384]{2,1,0:T(8,128)(2,1)S(1)}, u32[]{:S(2)}) copy-start(bf16[2,256,384]{2,1,0:T(8,128)(2,1)S(1)} %fusion.3) | copy-start | bytes 1179652
  418.5 34.5 %collective-permute-start.54 = (bf16[1152,256]{1,0:T(8,128)(2,1)S(1)}, bf16[1152,256]{1,0:T(8,128)(2,1)}, u32[]{:S(2)}, u32[]{:S(2)}) collective-permute-start(bf16[1152,256]{1,0:T(8,128)(2,1)S(1)} %fusion.2.refs_0_), channel_id=1, source_target_pairs={{0,3},{1,2},{2,1},{3,0},{4,7},{5,6},{6,5},{7,4},{8,11},{9,10},{10,... | collective-permute-start | bytes 1769480 | tf_op jit(solution)/shard_map/ppermute | solution.py:949
  420.0 33.0 %collective-permute-start.53 = (bf16[1152,256]{1,0:T(8,128)(2,1)S(1)}, bf16[1152,256]{1,0:T(8,128)(2,1)}, u32[]{:S(2)}, u32[]{:S(2)}) collective-permute-start(bf16[1152,256]{1,0:T(8,128)(2,1)S(1)} %fusion.2.refs_0_), channel_id=1, source_target_pairs={{0,2},{1,3},{2,0},{3,1},{4,6},{5,7},{6,4},{7,5},{8,10},{9,11},{10,... | collective-permute-start | bytes 1769480 | tf_op jit(solution)/shard_map/ppermute | solution.py:949
  420.6 32.4 %collective-permute-start.52 = (bf16[1152,256]{1,0:T(8,128)(2,1)S(1)}, bf16[1152,256]{1,0:T(8,128)(2,1)}, u32[]{:S(2)}, u32[]{:S(2)}) collective-permute-start(bf16[1152,256]{1,0:T(8,128)(2,1)S(1)} %fusion.2.refs_0_), channel_id=1, source_target_pairs={{0,1},{1,0},{2,3},{3,2},{4,5},{5,4},{6,7},{7,6},{8,9},{9,8},{10,11... | collective-permute-start | bytes 1769480 | tf_op jit(solution)/shard_map/ppermute | solution.py:949
  432.1 10.3 %collective-permute-start.49 = (bf16[2,256,384]{2,1,0:T(8,128)(2,1)S(1)}, bf16[2,256,384]{2,1,0:T(8,128)(2,1)S(1)}, u32[]{:S(2)}, u32[]{:S(2)}) collective-permute-start(bf16[2,256,384]{2,1,0:T(8,128)(2,1)S(1)} %pad_maximum_fusion.4), channel_id=1, source_target_pairs={{0,8},{4,12},{8,0},{12,4},{16,24},{20,28},{24,16},{28,20},{1,9},{5... | collective-permute-start | bytes 1179656 | tf_op jit(solution)/shard_map/ppermute | solution.py:949
  442.4 10.3 %collective-permute-start.50 = (bf16[1,256,384]{2,1,0:T(8,128)(2,1)S(1)}, bf16[1,256,384]{2,1,0:T(8,128)(2,1)S(1)}, u32[]{:S(2)}, u32[]{:S(2)}) collective-permute-start(bf16[1,256,384]{2,1,0:T(8,128)(2,1)S(1)} %add_convert_fusion.16), channel_id=1, source_target_pairs={{0,16},{4,20},{8,24},{12,28},{16,0},{20,4},{24,8},{28,12},{1,17},{... | collective-permute-start | bytes 589832 | tf_op jit(solution)/shard_map/ppermute | solution.py:949
  452.8 1.4 collective-permute-start.51
  454.3 11.0 %collective-permute-start.57 = (bf16[2,128,384]{2,1,0:T(8,128)(2,1)S(1)}, bf16[2,128,384]{2,1,0:T(8,128)(2,1)S(1)}, u32[]{:S(2)}, u32[]{:S(2)}) collective-permute-start(bf16[2,128,384]{2,1,0:T(8,128)(2,1)S(1)} %pad_maximum_fusion.8.refs_0_), channel_id=1, source_target_pairs={{0,3},{1,2},{2,1},{3,0},{4,7},{5,6},{6,5},{7,4},{8,11},{9,10},{10,... | collective-permute-start | bytes 589832 | tf_op jit(solution)/shard_map/ppermute | solution.py:949
  455.7 10.6 %collective-permute-start.56 = (bf16[2,128,384]{2,1,0:T(8,128)(2,1)S(1)}, bf16[2,128,384]{2,1,0:T(8,128)(2,1)S(1)}, u32[]{:S(2)}, u32[]{:S(2)}) collective-permute-start(bf16[2,128,384]{2,1,0:T(8,128)(2,1)S(1)} %pad_maximum_fusion.8.refs_0_), channel_id=1, source_target_pairs={{0,2},{1,3},{2,0},{3,1},{4,6},{5,7},{6,4},{7,5},{8,10},{9,11},{10,... | collective-permute-start | bytes 589832 | tf_op jit(solution)/shard_map/ppermute | solution.py:949
  456.4 10.0 %collective-permute-start.55 = (bf16[2,128,384]{2,1,0:T(8,128)(2,1)S(1)}, bf16[2,128,384]{2,1,0:T(8,128)(2,1)S(1)}, u32[]{:S(2)}, u32[]{:S(2)}) collective-permute-start(bf16[2,128,384]{2,1,0:T(8,128)(2,1)S(1)} %pad_maximum_fusion.8.refs_0_), channel_id=1, source_target_pairs={{0,1},{1,0},{2,3},{3,2},{4,5},{5,4},{6,7},{7,6},{8,9},{9,8},{10,11... | collective-permute-start | bytes 589832 | tf_op jit(solution)/shard_map/ppermute | solution.py:949
  (53 other events, 498.7 us)

commit v5 on v4

--- a/solution.py
+++ b/solution.py
@@ -451,7 +451,7 @@
             pltpu.SemaphoreType.DMA((zs,)),
         ],
         compiler_params=params(),
-        cost_estimate=cost(work * 40 * width, slots * rows * width * 20, work * pairs),
+        cost_estimate=cost(work * 4 * width, slots * rows * width * 2, work * pairs / 10),
         name="attend_grad",
     )(meta, *parts, *grads, exact, logs)
 
@@ -718,7 +718,7 @@
             scratch_shapes=[pltpu.VMEM((zs, 2, 3, rows, lanes), BF16)],
         ),
         compiler_params=params(),
-        cost_estimate=cost(6 * rows * width * width, 3 * width * width + 20 * rows * width),
+        cost_estimate=cost(0.6 * rows * width * width, width * width),
         name="qkv_grad",
     )(meta, *tables, *parts, *[weight] * (3 * blocks))
 
@@ -746,34 +746,36 @@
         in_specs=[VMEM] * (2 + 3 * clips),
         out_specs=[VMEM, VMEM],
         compiler_params=params(),
-        cost_estimate=cost(clips * rows * width * 30, clips * rows * width * 18),
+        cost_estimate=cost(clips * rows * width * 3, clips * rows * width * 2),
         name="norm_grad",
     )(tokens, mod, *nears, *fars, *middles)
 
 
-def weight_grad_kernel(jobs, clip_size, zs, meta, *refs):
+def weight_grad_kernel(jobs, clip_size, zs, split, meta, *refs):
     arrays_n = sum(2 * job[0] for job in jobs)
-    arrays, outs = refs[:arrays_n], refs[arrays_n : arrays_n + 4]
-    held, out_sems, in_sems = refs[arrays_n + 4 : arrays_n + 7]
-    scratch = refs[arrays_n + 7 :]
+    outs_n = 4 if split else 1
+    arrays, outs = refs[:arrays_n], refs[arrays_n : arrays_n + outs_n]
+    held, out_sems, in_sems = refs[arrays_n + outs_n : arrays_n + outs_n + 3]
+    scratch = refs[arrays_n + outs_n + 3 :]
     _, _, _, height, cols = held.shape
     tile = zs * height
     z = meta[0] // 2
-    clip = meta[1]
+    clip = meta[1] if split else 0
 
     def send_out(slot, tiles, repeat, first, tall):
         for e in range(clip_size):
-            for half, first_bit in enumerate((1, clip_size // 2)):
-                keep, send = outs[2 * half], outs[2 * half + 1]
+            for half, first_bit in enumerate((1, clip_size // 2) if split else (0,)):
+                keep, send = (outs[2 * half], outs[2 * half + 1]) if split else (outs[0], None)
                 rest = [k for k in range(clip_size) if not k & first_bit]
                 if e & first_bit:
                     out, place = send, rest.index(e ^ first_bit)
                 else:
                     out, place = keep, rest.index(e)
-                low, high = half * zs // 2, (half + 1) * zs // 2
+                span = zs // 2 if split else zs
+                low, high = half * span, (half + 1) * span
                 if not tall:
                     pltpu.make_async_copy(
-                        held.at[slot, e, pl.ds(low, zs // 2)],
+                        held.at[slot, e, pl.ds(low, span)],
                         out.at[place, :, pl.ds(first, height)],
                         out_sems.at[slot],
                     ).start()
@@ -848,7 +850,7 @@
         pltpu.make_async_copy(held.at[slot], held.at[slot], out_sems.at[slot]).wait()
 
 
-def weight_grad_call(meta, products, clip_size, zs, name):
+def weight_grad_call(meta, products, clip_size, zs, split, name):
     jobs, arrays, scratch = [], [], []
     first = flops = 0
     tile = min(p[0][0][2] for p in products)
@@ -873,12 +875,15 @@
             pltpu.VMEM((count * depth, rows), BF16),
             pltpu.VMEM((count * depth, total), BF16),
         ]
-    out = shaped((clip_size // 2, zs // 2, first, piece), BF16)
+    if split:
+        outs = [shaped((clip_size // 2, zs // 2, first, piece), BF16)] * 4
+    else:
+        outs = [shaped((clip_size, zs, first, piece), BF16)]
     return pl.pallas_call(
-        functools.partial(weight_grad_kernel, tuple(jobs), clip_size, zs),
-        out_shape=[out] * 4,
+        functools.partial(weight_grad_kernel, tuple(jobs), clip_size, zs, split),
+        out_shape=outs,
         in_specs=[SMEM] + [ANY] * len(arrays),
-        out_specs=[ANY] * 4,
+        out_specs=[ANY] * len(outs),
         scratch_shapes=[
             pltpu.VMEM((2, clip_size, zs, height, piece), BF16),
             pltpu.SemaphoreType.DMA((2,)),
@@ -886,7 +891,7 @@
         ]
         + scratch,
         compiler_params=params(),
-        cost_estimate=cost(flops, flops / 512 + 8 * out.size),
+        cost_estimate=cost(flops, flops / 512),
         name=name,
     )(meta, *arrays)
 
@@ -983,14 +988,17 @@
     return [1] + down[:-1], down
 
 
-def sum_z(pairs, seq_size):
-    blocks = [*pairs[0][0], *pairs[1][0]]
-    bit = 1
+def z_out(blocks, seq_size):
+    return exchange(jnp.stack(blocks[1::2]), "seq", seq_size, seq_size // len(blocks))
+
+
+def z_in(blocks, arrived):
+    return [add_low(keep, new) for keep, new in zip(blocks[0::2], arrived)]
+
+
+def sum_z(blocks, seq_size):
     while len(blocks) > 1:
-        kept, sent = blocks[0::2], blocks[1::2]
-        arrived = exchange(jnp.stack(sent), "seq", seq_size, 2 * bit)
-        blocks = [add_low(keep, new) for keep, new in zip(kept, arrived)]
-        bit *= 2
+        blocks = z_in(blocks, z_out(blocks, seq_size))
     return blocks[0]
 
 
@@ -1083,12 +1091,14 @@
     mod_two, _ = modulation_call(
         levels[:clips], level_table, mod_weight, mod_bias_row, 2, 4
     )
-    parts[0], mod_two = after(parts[0], mod_two)
+    proj_row, up_row, down_row = proj_bias[None], up_bias[None], down_bias[None]
+    parts[0], mod_two, proj_row, up_row, down_row = after(
+        parts[0], mod_two, proj_row, up_row, down_row
+    )
     exact, logs, attended, crossed = [], [], [], []
     for c in range(clips):
         sends = out[(c + 1) * zs : (c + 2) * zs] if c < clips - 1 else None
         if c < clips - 1:
-            parts[c], sends = after(parts[c], sends)
             parts.append(spread(sends, seq_size))
         done = attend_call(meta, c, parts[c], head)
         exact.append(done[zs])
@@ -1105,8 +1115,8 @@
         if c:
             meta, grads[-1][0] = after(meta, grads[-1][0])
         out = forward_back_call(
-            meta, c, tokens, cotangent, mod_two, proj_bias[None], up_bias[None],
-            down_bias[None], attended[c], crossed[c], proj_weight, up_weight, down_weight,
+            meta, c, tokens, cotangent, mod_two, proj_row, up_row, down_row, attended[c],
+            crossed[c], proj_weight, up_weight, down_weight,
         )
         layer.append(out[0])
         middles.append(out[1])
@@ -1129,42 +1139,36 @@
     row = width // seq_size
     orders = clip_orders(clip_size)
     steps = len(orders[0])
+    products = [([], [], 1, False), ([], [], 1, True), ([], [], 1, False)]
+    for c in range(clips):
+        att_own, att_far, gone, n2_own, act_own = saved[c]
+        own, far = mixed[c]
+        products[0][0].extend([full(att_own), full(att_far)])
+        products[0][1].extend([full(gone), full(far_ones[c])])
+        products[1][0].extend([full(act_own), (far, at_act, hidden // 2)])
+        products[1][1].extend([(own, at_gtwo, width), (far, at_gtwo, width)])
+        products[2][0].extend([full(n2_own), (far, at_n2, width // 2)])
+        products[2][1].extend([(own, at_hid, hidden), (far, at_hid, hidden)])
+    meta, grads[-1][0] = after(meta, grads[-1][0])
+    (shares,) = weight_grad_call(meta, products, clip_size, zs, False, "weight_grads")
+    meta, shares = after(meta, shares)
+    summed = lax.psum_scatter(
+        shares.reshape(-1, shares.shape[-1]), "clip", scatter_dimension=0, tiled=True
+    ).reshape(shares.shape[1:])
     returned = []
     for c in range(clips):
         if c:
-            meta, shares[0] = after(meta, shares[0])
-        else:
-            meta, grads[-1][0] = after(meta, grads[-1][0])
+            meta, returned[-1][0] = after(meta, returned[-1][0])
         out = attend_grad_call(meta, c, parts[c], grads[c], exact[c], logs[c], head)
         if c < clips - 1:
-            out, grads[-1], mixed[-1] = after(out, grads[-1], mixed[-1])
+            out, grads[c + 1] = after(out, grads[c + 1])
         else:
             out, returned[-1] = after(out, returned[-1])
         returned.append(spread(out, seq_size))
-        if c == 0:
-            products = [([], [], 1, False), ([], [], 1, True), ([], [], 1, False)]
-            for k in range(clips):
-                att_own, att_far, gone, n2_own, act_own = saved[k]
-                own, far = mixed[k]
-                products[0][0].extend([full(att_own), full(att_far)])
-                products[0][1].extend([full(gone), full(far_ones[k])])
-                products[1][0].extend([full(act_own), (far, at_act, hidden // 2)])
-                products[1][1].extend([(own, at_gtwo, width), (far, at_gtwo, width)])
-                products[2][0].extend([full(n2_own), (far, at_n2, width // 2)])
-                products[2][1].extend([(own, at_hid, hidden), (far, at_hid, hidden)])
-            shares = weight_grad_call(meta, products, clip_size, zs, "weight_grads")
-            shares = list(shares)
-    pairs = [shares[:2], shares[2:]]
     turns = list(zip(*orders))
     grad_rights, nears, fars, qkv_bgrads = [], [], [], []
     for c in range(clips):
-        if c:
-            kept = [pair[0] for pair in pairs]
-            kept, qkv_bgrads[0] = after(kept, qkv_bgrads[0])
-            pairs = [(keep, pair[1]) for keep, pair in zip(kept, pairs)]
-            pairs = step_in(pairs, step_out(pairs, turns[0], clip_size))
-            meta, pairs, returned[c] = after(meta, pairs, returned[c])
-        else:
+        if c == 0:
             meta, returned[-1][0] = after(meta, returned[-1][0])
         out = qkv_grad_call(meta, c, tables, returned[c], weight_half, head, aligned)
         grad_rights.extend(out[:2])
@@ -1172,12 +1176,11 @@
         fars.append(swap(out[3]))
         qkv_bgrads.append(out[4][:3])
     tokens_grad, late_rows = norm_grad_call(tokens, mod_one, nears, fars, middles)
-    if len(turns) > 1:
-        arrived = step_out(pairs, turns[1], clip_size)
-        tokens_grad, arrived = after(tokens_grad, arrived)
-        pairs = step_in(pairs, arrived)
-    for bits in turns[2:]:
-        pairs = step_in(pairs, step_out(pairs, bits, clip_size))
+    blocks = list(summed)
+    if len(blocks) > 1:
+        landed = z_out(blocks, seq_size)
+        late_rows, landed = after(late_rows, landed)
+        blocks = z_in(blocks, landed)
     level_rows = jnp.stack([levels_used // 32, levels_used % 32]).astype(F32)
     level_rows = jnp.concatenate([level_rows, jnp.zeros((2, width - clips), F32)], axis=1)
     mod_rows = []
@@ -1194,22 +1197,19 @@
     late = jnp.concatenate([condition, level_rows] + mod_rows + [bias_rows], axis=0)
     start, stop = clips + 2, clips + 2 + 6 * clips
     late = double(late.astype(BF16)[None], "seq", seq_size)
-    pairs, late = after(pairs, late)
-    piece = sum_z(pairs, seq_size)
+    blocks = list(summed)
     lefts = [normed[role * clips + c] for c in range(clips) for role in range(2)]
     if aligned:
-        meta, late_rows = after(meta, late_rows)
         shares = weight_grad_call(
             meta,
             [([full(a) for a in lefts], [full(a) for a in grad_rights], 3, False)],
             clip_size,
             zs,
+            True,
             "qkv_weight_grad",
         )
         pairs_qkv = [shares[:2], shares[2:]]
-        arrived = step_out(pairs_qkv, turns[0], clip_size)
-        arrived, late = after(arrived, late)
-        pairs_qkv = step_in(pairs_qkv, arrived)
+        pairs_qkv = step_in(pairs_qkv, step_out(pairs_qkv, turns[0], clip_size))
         for bits in turns[1:]:
             pairs_qkv = step_in(pairs_qkv, step_out(pairs_qkv, bits, clip_size))
     own_sums = jnp.sum(
@@ -1220,6 +1220,7 @@
         [late[:, :stop].reshape(seq_size * stop, width), own_sums.reshape(sums_rows, width)]
     )
     late = double(message[None], "clip", clip_size)
+    piece = sum_z(blocks, seq_size)
     if aligned:
         pairs_qkv, piece, late = after(pairs_qkv, piece, late)
     own_sums = jnp.sum(late[:, seq_size * stop :].astype(F32), axis=0).reshape(2, -1)
@@ -1270,7 +1271,8 @@
     proj_bgrad = own_part(bias_sums[hidden + width : hidden + 2 * width])
     if aligned:
         pieces = gather_pieces(piece, clip_size)
-        piece = sum_z(pairs_qkv, seq_size).reshape(2, row, 3 * LANES)
+        piece = sum_z([*pairs_qkv[0][0], *pairs_qkv[1][0]], seq_size)
+        piece = piece.reshape(2, row, 3 * LANES)
         own_rows = lax.dynamic_index_in_dim(piece, parity, 0, keepdims=False)
         far_rows = swap(lax.dynamic_index_in_dim(piece, 1 - parity, 0, keepdims=False))
         far_rows, pieces, mod_wgrad, table_grad = after(far_rows, pieces, mod_wgrad, table_grad)

time: 475 us -> 464 us (0.977)
  between operations: 2 us -> 15.7 us
  starting transfers between devices: 92.6 us -> 79.3 us
  other arithmetic: 31.6 us -> 21.2 us
  Pallas kernels: 195 us -> 201 us
  waiting for transfers between devices: 117 us -> 111 us
    ppermute x58 -> x54, waiting for transfers between devices: 117 us -> 89.2 us  [exchange(): return lax.ppermute(array, axis, [(k, k ^ distance) for k in range(size)])]
    reduce_scatter x0 -> x1, waiting for transfers between devices: none -> 21.9 us  [on_device(): lax.psum_scatter(shares.reshape(-1, shares.shape[-1]), 'clip', scatter_di...]
    ppermute x58 -> x54, starting transfers between devices: 92.6 us -> 79.3 us  [exchange(): return lax.ppermute(array, axis, [(k, k ^ distance) for k in range(size)])]
    convert_element_type x12 -> x8, other arithmetic: 15.6 us -> 7.71 us  [add_low(): return (left.astype(F32) + right.astype(F32)).astype(BF16)]
  transfers between devices with their start and end apart: 58 -> 55, of which waited for: 18 -> 16; matrix products, arithmetic and copies ran while one was open for 12% -> 10% of each run, Pallas kernels for 34% -> 36%
where the time goes in v5:
time: 464 us; the launch traced here: 458 us
  Pallas kernels  201 us (43%)
  waiting for transfers between devices  111 us (24%)
  starting transfers between devices  79.3 us (17%)
  other arithmetic  21.2 us (5%)
  local copies, waits for them, and re-layouts  17.4 us (4%)
  between operations  15.7 us (3%)
  matrix products  12.1 us (3%)
    ppermute x54, waiting for transfers between devices, exchange(): return lax.ppermute(array, axis, [(k, k ^ distance) for k in range(size)])  89.2 us
    ppermute x54, starting transfers between devices, exchange(): return lax.ppermute(array, axis, [(k, k ^ distance) for k in range(size)])  79.3 us
    pallas_call x2, Pallas kernels, attend_grad_call(): pl.pallas_call(functools.partial(attend_grad_kernel, slots, head, clip),...  52.2 us
    pallas_call x2, Pallas kernels, forward_back_call(): pl.pallas_call(functools.partial(forward_back_kernel, slots, clip), grid=...  38 us
    pallas_call x2, Pallas kernels, attend_call(): pl.pallas_call(functools.partial(attend_kernel, slots, head, clip), out_s...  32.3 us
    pallas_call x2, Pallas kernels, weight_grad_call(): pl.pallas_call(functools.partial(weight_grad_kernel, tuple(jobs), clip_si...  24.8 us
    reduce_scatter x1, waiting for transfers between devices, on_device(): lax.psum_scatter(shares.reshape(-1, shares.shape[-1]), 'clip', scatter_di...  21.9 us
    pallas_call x2, Pallas kernels, qkv_grad_call(): pl.pallas_call(functools.partial(qkv_grad_kernel, zs, head, clip), out_sh...  13.1 us
  transfers between devices with their start and end apart: 55, of which 16 were waited for; matrix products, arithmetic and copies ran while one was open for 10% of the time, Pallas kernels for 36%

profile of v5, /device:TPU:0, one launch (start us, length us, event | category | flops | bytes accessed | tf_op | source)
XLA Modules:
  0.0 457.6 jit_solution(6010012826195470400)
XLA Ops:
  15.6 4.0 modulation.2
  21.3 10.1 %norm_qkv.1 = (bf16[2,3,256,128]{3,2,1,0:T(8,128)(2,1)}, bf16[2,3,256,128]{3,2,1,0:T(8,128)(2,1)}, bf16[2,3,256,128]{3,2,1,0:T(8,128)(2,1)}, bf16[2,3,256,128]{3...) custom-call(s32[4]{0:T(128)} %pad_add_fusion.1.meta, ...), custom_call_target="tpu_custom_call" | custom-call | flops 3221225472 | bytes 11534336 | tf_op jit(solution)/shard_map/norm_qkv/pallas_call | solution.py:226
  31.4 3.1 collective-permute-start.2
  34.5 2.6 collective-permute-start.3
  38.9 6.4 %modulation.3 = (f32[4,2,1024]{2,1,0:T(2,128)}, f32[2,1024]{1,0:T(2,128)}) custom-call(s32[2]{0:T(128)} %copy-done.34, bf16[1024,1024]{1,0:T(8,128)(2,1)} %table.3, bf16[1024,6144]{1,0:T(8,128)(2,1)} %weight.3, bf16[1,6144]{1,0:T(2,128)(2,1)} %broadcast_in_dim.47.bias), custom_call_target="tpu_custom_call" | custom-call | bytes 10485760 | tf_op jit(solution)/shard_map/modulation/pallas_call | solution.py:128
  46.2 3.5 collective-permute-start.6
  49.7 2.7 collective-permute-done.2.refs_1_
  52.4 4.1 collective-permute-start.7
  56.5 8.1 %collective-permute-done.3.refs_2_ = bf16[2,3,256,128]{3,2,1,0:T(8,128)(2,1)} collective-permute-done((bf16[2,3,256,128]{3,2,1,0:T(8,128)(2,1)}, bf16[2,3,256,128]{3,2,1,0:T(8,128)(2,1)}, u32[]{:S(2)}, u32[]{:S(2)}) %collective-permute-start.3) | collective-permute-done | bytes 393248 | tf_op jit(solution)/shard_map/ppermute | solution.py:954
  64.6 18.2 %attend.2 = (bf16[2,256,128]{2,1,0:T(8,128)(2,1)}, bf16[2,256,128]{2,1,0:T(8,128)(2,1)}, bf16[2,256,128]{2,1,0:T(8,128)(2,1)}, bf16[2,256,128]{2,1,0:T(8,128)(2,...) custom-call(s32[4]{0:T(128)} %pad_add_fusion.1.meta, bf16[2,3,256,128]{3,2,1,0:T(8,128)(2,1)} %get-tuple-element.192.refs_0_, ...), custom_call_target="tpu_custom_call" | custom-call | flops 8589934592 | bytes 3145728 | tf_op jit(solution)/shard_map/attend/pallas_call | solution.py:325
  82.8 15.4 %collective-permute-done.6.refs_2_ = bf16[2,3,256,128]{3,2,1,0:T(8,128)(2,1)S(1)} collective-permute-done((bf16[2,3,256,128]{3,2,1,0:T(8,128)(2,1)}, bf16[2,3,256,128]{3,2,1,0:T(8,128)(2,1)S(1)}, u32[]{:S(2)}, u32[]{:S(2)}) %collective-permute-start.6) | collective-permute-done | bytes 393248 | tf_op jit(solution)/shard_map/ppermute | solution.py:954
  98.2 10.5 %collective-permute-start.8 = (bf16[2,256,128]{2,1,0:T(8,128)(2,1)}, bf16[2,256,128]{2,1,0:T(8,128)(2,1)S(1)}, u32[]{:S(2)}, u32[]{:S(2)}) collective-permute-start(bf16[2,256,128]{2,1,0:T(8,128)(2,1)} %get-tuple-element.213), channel_id=1, source_target_pairs={{0,8},{4,12},{8,0},{12,4},{16,24},{20,28},{24,16},{28,20},{1,9},{5... | collective-permute-start | bytes 393224 | tf_op jit(solution)/shard_map/ppermute | solution.py:954
  109.8 1.4 collective-permute-start.10
  111.2 14.1 %attend.3 = (bf16[2,256,128]{2,1,0:T(8,128)(2,1)}, bf16[2,256,128]{2,1,0:T(8,128)(2,1)}, bf16[2,256,128]{2,1,0:T(8,128)(2,1)}, bf16[2,256,128]{2,1,0:T(8,128)(2,...) custom-call(s32[4]{0:T(128)} %pad_add_fusion.1.meta, bf16[2,3,256,128]{3,2,1,0:T(8,128)(2,1)} %get-tuple-element.204.refs_0_, ...), custom_call_target="tpu_custom_call" | custom-call | flops 8589934592 | bytes 3145728 | tf_op jit(solution)/shard_map/attend/pallas_call | solution.py:325
  126.7 2.0 collective-permute-start.13
  128.6 1.4 collective-permute-start.14
  130.8 19.0 %feed_forward.2 = (bf16[256,1024]{1,0:T(8,128)(2,1)}, f32[256,1024]{1,0:T(8,128)}, f32[8,1024]{1,0:T(8,128)}, f32[1,4096]{1,0:T(1,128)}, bf16[256,512]{1,0:T(8,1...) custom-call(s32[4]{0:T(128)} %pad_add_fusion.1.meta, ...), custom_call_target="tpu_custom_call" | custom-call | flops 9663676416 | bytes 37748736 | tf_op jit(solution)/shard_map/feed_forward/pallas_call | solution.py:607
  150.5 1.6 collective-permute-done.16.refs_4_
  153.0 3.5 proj_back.2
  156.9 2.9 collective-permute-start.18
  159.8 1.4 collective-permute-start.19
  161.1 19.0 %feed_forward.3 = (bf16[256,1024]{1,0:T(8,128)(2,1)}, f32[256,1024]{1,0:T(8,128)}, f32[8,1024]{1,0:T(8,128)}, f32[1,4096]{1,0:T(1,128)}, bf16[256,512]{1,0:T(8,1...) custom-call(s32[4]{0:T(128)} %pad_add_fusion.1.meta, ...), custom_call_target="tpu_custom_call" | custom-call | flops 9663676416 | bytes 37748736 | tf_op jit(solution)/shard_map/feed_forward/pallas_call | solution.py:607
  180.3 2.1 collective-permute-done.21.far.refs_7_
  183.2 3.5 proj_back.3
  186.8 7.0 %collective-permute-done.22.refs_11_.refs_15_.refs_19_.refs_23_ = bf16[256,7680]{1,0:T(8,128)(2,1)} collective-permute-done((bf16[256,7680]{1,0:T(8,128)(2,1)}, bf16[256,7680]{1,0:T(8,128)(2,1)}, u32[]{:S(2)}, u32[]{:S(2)}) %collective-permute-start.22) | collective-permute-done | bytes 3932192 | tf_op jit(solution)/shard_map/ppermute | solution.py:954
  193.8 16.1 %weight_grads.1 = bf16[4,4,1152,256]{3,2,1,0:T(8,128)(2,1)} custom-call(s32[4]{0:T(128)} %pad_add_fusion.1.meta, bf16[256,512]{1,0:T(8,128)(2,1)} %get-tuple-element.251.refs_0_, bf16[256,512]{1,0:T(8,128)(2,1)} %get-tuple-element.252.refs_1_, bf16[256,512]{1,0:T(8,128)(2,1)} %get-tuple-element.253.refs_2_, bf16[256,512]{1,0:T(8,128)(2,1)} %get-tuple-element.254.refs_3_, ...), custom_call_target="tpu_custom_call" | custom-call | flops 9663676416 | bytes 18874368 | tf_op jit(solution)/shard_map/weight_grads/pallas_call | solution.py:882
  211.4 3.0 collective-permute-start.24
  214.4 1.4 collective-permute-start.25
  215.8 29.4 %attend_grad.2 = (bf16[2,3,256,128]{3,2,1,0:T(8,128)(2,1)}, bf16[2,3,256,128]{3,2,1,0:T(8,128)(2,1)}, bf16[2,3,256,128]{3,2,1,0:T(8,128)(2,1)}, bf16[2,3,256,128]{3,2,1,0:T(8,128)(2,1)}) custom-call(s32[4]{0:T(128)} %pad_add_fusion.1.meta, bf16[2,3,256,128]{3,2,1,0:T(8,128)(2,1)} %get-tuple-element.192.refs_0_, bf16[2,3,256,128]{3,2,1,0:T(8,128)(2,1)} %copy-done.42, ...), custom_call_target="tpu_custom_call" | custom-call | flops 2147483648 | bytes 524288 | tf_op jit(solution)/shard_map/attend_grad/pallas_call | solution.py:436
  245.4 2.4 collective-permute-start.27
  247.7 2.0 collective-permute-start.28
  250.6 22.8 %attend_grad.3 = (bf16[2,3,256,128]{3,2,1,0:T(8,128)(2,1)}, bf16[2,3,256,128]{3,2,1,0:T(8,128)(2,1)}, bf16[2,3,256,128]{3,2,1,0:T(8,128)(2,1)}, bf16[2,3,256,128]{3,2,1,0:T(8,128)(2,1)}) custom-call(s32[4]{0:T(128)} %pad_add_fusion.1.meta, bf16[2,3,256,128]{3,2,1,0:T(8,128)(2,1)} %get-tuple-element.204.refs_0_, bf16[2,3,256,128]{3,2,1,0:T(8,128)(2,1)} %copy-done.39, ...), custom_call_target="tpu_custom_call" | custom-call | flops 2147483648 | bytes 524288 | tf_op jit(solution)/shard_map/attend_grad/pallas_call | solution.py:436
  273.5 2.0 collective-permute-done.27.refs_6_
  275.4 6.7 %collective-permute-start.29 = (bf16[2,3,256,128]{3,2,1,0:T(8,128)(2,1)}, bf16[2,3,256,128]{3,2,1,0:T(8,128)(2,1)}, u32[]{:S(2)}, u32[]{:S(2)}) collective-permute-start(bf16[2,3,256,128]{3,2,1,0:T(8,128)(2,1)} %get-tuple-element.301), channel_id=1, source_target_pairs={{0,8},{4,12},{8,0},{12,4},{16,24},{20,28},{24,16},{28,20},{1,9},{5... | collective-permute-start | bytes 1179656 | tf_op jit(solution)/shard_map/ppermute | solution.py:954
  283.1 1.5 collective-permute-start.31
  284.5 21.9 %reduce-scatter.2.cloned.1.call-done = bf16[4608,256]{1,0:T(8,128)(2,1)} async-done(((bf16[18432,256]{1,0:T(8,128)(2,1)}), bf16[4608,256]{1,0:T(8,128)(2,1)}) %reduce-scatter.2.cloned.1.call-update) | async-done | bytes 2359312 | tf_op jit(solution)/shard_map/reduce_scatter | solution.py:1155
  308.9 1.5 collective-permute-start.38
  310.4 6.5 %qkv_grad.2 = (bf16[256,1536]{1,0:T(8,128)(2,1)}, bf16[256,1536]{1,0:T(8,128)(2,1)}, f32[256,1024]{1,0:T(8,128)}, f32[256,1024]{1,0:T(8,128)}, f32[8,512]{1,0:T(8,128)}) custom-call(s32[4]{0:T(128)} %pad_add_fusion.1.meta, f32[4,128]{1,0:T(4,128)} %get-tuple-element.420.refs_0_, f32[4,128]{1,0:T(4,128)} %get-tuple-element.419.refs_1_, ...), custom_call_target="tpu_custom_call" | custom-call | flops 161061280 | bytes 1048576 | tf_op jit(solution)/shard_map/qkv_grad/pallas_call | solution.py:709
  317.1 6.6 %qkv_grad.3 = (bf16[256,1536]{1,0:T(8,128)(2,1)}, bf16[256,1536]{1,0:T(8,128)(2,1)}, f32[256,1024]{1,0:T(8,128)}, f32[256,1024]{1,0:T(8,128)}, f32[8,512]{1,0:T(8,128)}) custom-call(s32[4]{0:T(128)} %pad_add_fusion.1.meta, f32[4,128]{1,0:T(4,128)} %get-tuple-element.420.refs_0_, f32[4,128]{1,0:T(4,128)} %get-tuple-element.419.refs_1_, ...), custom_call_target="tpu_custom_call" | custom-call | flops 161061280 | bytes 1048576 | tf_op jit(solution)/shard_map/qkv_grad/pallas_call | solution.py:709
  325.6 8.7 %qkv_weight_grad.1 = (bf16[2,2,256,384]{3,2,1,0:T(8,128)(2,1)}, bf16[2,2,256,384]{3,2,1,0:T(8,128)(2,1)}, bf16[2,2,256,384]{3,2,1,0:T(8,128)(2,1)}, bf16[2,2,256,384]{3,2,1,0:T(8,128)(2,1)}) custom-call(s32[4]{0:T(128)} %pad_add_fusion.1.meta, bf16[256,1024]{1,0:T(8,128)(2,1)} %get-tuple-element.310.refs_0_, bf16[256,1024]{1,0:T(8,128)(2,1)} %get-tuple-element.311.refs_1_, ...), custom_call_target="tpu_custom_call" | custom-call | flops 3221225472 | bytes 6291456 | tf_op jit(solution)/shard_map/qkv_weight_grad/pallas_call | solution.py:882
  334.4 1.4 collective-permute-start.34
  337.0 6.2 %norm_grad.1 = (f32[2,1,256,1024]{3,2,1,0:T(8,128)}, f32[2,8,1024]{2,1,0:T(8,128)}) custom-call(bf16[2,1,256,1024]{3,2,1,0:T(8,128)(2,1)} %tokens.7, f32[2,4,1024]{2,1,0:T(4,128)} %get-tuple-element.182.mod, f32[256,1024]{1,0:T(8,128)} %get-tuple-element.299.refs_0_, f32[256,1024]{1,0:T(8,128)} %get-tuple-element.304.refs_1_, ...), custom_call_target="tpu_custom_call" | custom-call | flops 1572864 | bytes 1048576 | tf_op jit(solution)/shard_map/norm_grad/pallas_call | solution.py:743
  344.8 2.3 maximum_bitcast_fusion
  347.1 3.7 collective-permute-start.41
  350.8 3.3 collective-permute-done.34
  355.1 1.4 collective-permute-start.35
  356.5 2.8 collective-permute-start.42
  359.3 1.8 add_convert_fusion.1
  361.2 1.7 collective-permute-start.37
  362.9 5.1 %collective-permute-done.42 = bf16[4,24,1024]{2,1,0:T(8,128)(2,1)S(1)} collective-permute-done((bf16[4,24,1024]{2,1,0:T(8,128)(2,1)S(1)}, bf16[4,24,1024]{2,1,0:T(8,128)(2,1)S(1)}, u32[]{:S(2)}, u32[]{:S(2)}) %collective-permute-start.42) | collective-permute-done | bytes 196640 | tf_op jit(solution)/shard_map/ppermute | solution.py:954
  368.2 1.9 collective-permute-start.43
  371.4 1.3 fusion.3
  372.8 5.2 %collective-permute-done.43 = bf16[1,144,1024]{2,1,0:T(8,128)(2,1)S(1)} collective-permute-done((bf16[1,144,1024]{2,1,0:T(8,128)(2,1)S(1)}, bf16[1,144,1024]{2,1,0:T(8,128)(2,1)S(1)}, u32[]{:S(2)}, u32[]{:S(2)}) %collective-permute-start.43) | collective-permute-done | bytes 294944 | tf_op jit(solution)/shard_map/ppermute | solution.py:954
  378.4 2.0 fusion.4
  380.4 18.5 %collective-permute-done.39 = bf16[1,1152,256]{2,1,0:T(8,128)(2,1)S(1)} collective-permute-done((bf16[1,1152,256]{2,1,0:T(8,128)(2,1)S(1)}, bf16[1,1152,256]{2,1,0:T(8,128)(2,1)S(1)}, u32[]{:S(2)}, u32[]{:S(2)}) %collective-permute-start.39) | collective-permute-done | bytes 589856 | tf_op jit(solution)/shard_map/ppermute | solution.py:954
  399.9 1.8 collective-permute-start.49
  401.7 1.7 collective-permute-start.48
  404.7 8.5 %fusion.36 = f32[64,1024]{1,0:T(8,128)S(1)} fusion(bf16[64,6144]{1,0:T(8,128)(2,1)S(1)} %reshape.274, bf16[1024,6144]{1,0:T(8,128)(2,1)} %weight.3), kind=kOutput, calls=%fused_computation.108 | convolution fusion | flops 805306368 | bytes 13631488 | tf_op jit(solution)/shard_map/dot_general | solution.py:1246
  413.5 2.3 fusion.15
  415.8 7.7 %collective-permute-done.45 = bf16[2,256,384]{2,1,0:T(8,128)(2,1)S(1)} collective-permute-done((bf16[2,256,384]{2,1,0:T(8,128)(2,1)S(1)}, bf16[2,256,384]{2,1,0:T(8,128)(2,1)S(1)}, u32[]{:S(2)}, u32[]{:S(2)}) %collective-permute-start.45) | collective-permute-done | bytes 393248 | tf_op jit(solution)/shard_map/ppermute | solution.py:954
  425.2 8.5 %collective-permute-done.46 = bf16[1,256,384]{2,1,0:T(8,128)(2,1)S(1)} collective-permute-done((bf16[1,256,384]{2,1,0:T(8,128)(2,1)S(1)}, bf16[1,256,384]{2,1,0:T(8,128)(2,1)S(1)}, u32[]{:S(2)}, u32[]{:S(2)}) %collective-permute-start.46) | collective-permute-done | bytes 196640 | tf_op jit(solution)/shard_map/ppermute | solution.py:954
  437.0 1.8 collective-permute-start.51
  442.2 4.1 place_grads.1
  447.6 2.6 place_qkv_grad.1
  (273 shorter events, 44.2 us)
Async XLA Ops:
  7.2 299.2 %reduce-scatter.2.cloned.1.call-start = ((), (), s32[]{:S(2)}) async-start(), calls=%async_computation.1 | async-start | bytes 11796480 | tf_op jit(solution)/shard_map/reduce_scatter | solution.py:1155
  7.9 5.7 %collective-permute-start.1 = (s32[2,2]{1,0:T(2,128)S(1)}, s32[2,2]{1,0:T(2,128)S(1)}, u32[]{:S(2)}, u32[]{:S(2)}) collective-permute-start(s32[2,2]{1,0:T(2,128)S(1)} %pad_add_fusion), channel_id=1, source_target_pairs={{0,4},{4,0},{8,12},{12,8},{16,20},{20,16},{24,28},{28,24},{1,5},{5... | collective-permute-start | bytes 56 | tf_op jit(solution)/shard_map/ppermute | solution.py:954
  8.4 11.9 %collective-permute-start = (bf16[2,1,256,1024]{3,2,1,0:T(8,128)(2,1)}, bf16[2,1,256,1024]{3,2,1,0:T(8,128)(2,1)S(1)}, u32[]{:S(2)}, u32[]{:S(2)}) collective-permute-start(bf16[2,1,256,1024]{3,2,1,0:T(8,128)(2,1)} %tokens.7), channel_id=1, source_target_pairs={{0,4},{4,0},{8,12},{12,8},{16,20},{20,16},{24,28},{28,24},{1,5},{5... | collective-permute-start | bytes 3145736 | tf_op jit(solution)/shard_map/ppermute | solution.py:954
  31.4 21.0 %collective-permute-start.2 = (bf16[2,3,256,128]{3,2,1,0:T(8,128)(2,1)}, bf16[2,3,256,128]{3,2,1,0:T(8,128)(2,1)S(1)}, u32[]{:S(2)}, u32[]{:S(2)}) collective-permute-start(bf16[2,3,256,128]{3,2,1,0:T(8,128)(2,1)} %get-tuple-element.184), channel_id=1, source_target_pairs={{0,8},{4,12},{8,0},{12,4},{16,24},{20,28},{24,16},{28,20},{1,9},{5... | collective-permute-start | bytes 1179656 | tf_op jit(solution)/shard_map/ppermute | solution.py:954
  34.5 30.1 %collective-permute-start.3 = (bf16[2,3,256,128]{3,2,1,0:T(8,128)(2,1)}, bf16[2,3,256,128]{3,2,1,0:T(8,128)(2,1)}, u32[]{:S(2)}, u32[]{:S(2)}) collective-permute-start(bf16[2,3,256,128]{3,2,1,0:T(8,128)(2,1)} %get-tuple-element.185), channel_id=1, source_target_pairs={{0,16},{4,20},{8,24},{12,28},{16,0},{20,4},{24,8},{28,12},{1,17},{... | collective-permute-start | bytes 1179656 | tf_op jit(solution)/shard_map/ppermute | solution.py:954
  37.0 27.5 %collective-permute-start.4 = (bf16[2,3,256,128]{3,2,1,0:T(8,128)(2,1)}, bf16[2,3,256,128]{3,2,1,0:T(8,128)(2,1)}, u32[]{:S(2)}, u32[]{:S(2)}) collective-permute-start(bf16[2,3,256,128]{3,2,1,0:T(8,128)(2,1)} %get-tuple-element.186), channel_id=1, source_target_pairs={{0,24},{4,28},{8,16},{12,20},{16,8},{20,12},{24,0},{28,4},{1,25},{... | collective-permute-start | bytes 1179656 | tf_op jit(solution)/shard_map/ppermute | solution.py:954
  45.3 37.5 %collective-permute-start.5 = (bf16[2,3,256,128]{3,2,1,0:T(8,128)(2,1)}, bf16[2,3,256,128]{3,2,1,0:T(8,128)(2,1)S(1)}, u32[]{:S(2)}, u32[]{:S(2)}) collective-permute-start(bf16[2,3,256,128]{3,2,1,0:T(8,128)(2,1)} %get-tuple-element.201), channel_id=1, source_target_pairs={{0,8},{4,12},{8,0},{12,4},{16,24},{20,28},{24,16},{28,20},{1,9},{5... | collective-permute-start | bytes 1179656 | tf_op jit(solution)/shard_map/ppermute | solution.py:954
  46.2 52.0 %collective-permute-start.6 = (bf16[2,3,256,128]{3,2,1,0:T(8,128)(2,1)}, bf16[2,3,256,128]{3,2,1,0:T(8,128)(2,1)S(1)}, u32[]{:S(2)}, u32[]{:S(2)}) collective-permute-start(bf16[2,3,256,128]{3,2,1,0:T(8,128)(2,1)} %get-tuple-element.202), channel_id=1, source_target_pairs={{0,16},{4,20},{8,24},{12,28},{16,0},{20,4},{24,8},{28,12},{1,17},{... | collective-permute-start | bytes 1179656 | tf_op jit(solution)/shard_map/ppermute | solution.py:954
  52.4 45.8 %collective-permute-start.7 = (bf16[2,3,256,128]{3,2,1,0:T(8,128)(2,1)}, bf16[2,3,256,128]{3,2,1,0:T(8,128)(2,1)S(1)}, u32[]{:S(2)}, u32[]{:S(2)}) collective-permute-start(bf16[2,3,256,128]{3,2,1,0:T(8,128)(2,1)} %get-tuple-element.203), channel_id=1, source_target_pairs={{0,24},{4,28},{8,16},{12,20},{16,8},{20,12},{24,0},{28,4},{1,25},{... | collective-permute-start | bytes 1179656 | tf_op jit(solution)/shard_map/ppermute | solution.py:954
  82.8 28.4 %copy-start.39 = (bf16[2,3,256,128]{3,2,1,0:T(8,128)(2,1)}, bf16[2,3,256,128]{3,2,1,0:T(8,128)(2,1)S(1)}, u32[]{:S(2)}) copy-start(bf16[2,3,256,128]{3,2,1,0:T(8,128)(2,1)S(1)} %collective-permute-done.5.refs_1_) | copy-start | bytes 1179652
  98.2 27.1 %collective-permute-start.8 = (bf16[2,256,128]{2,1,0:T(8,128)(2,1)}, bf16[2,256,128]{2,1,0:T(8,128)(2,1)S(1)}, u32[]{:S(2)}, u32[]{:S(2)}) collective-permute-start(bf16[2,256,128]{2,1,0:T(8,128)(2,1)} %get-tuple-element.213), channel_id=1, source_target_pairs={{0,8},{4,12},{8,0},{12,4},{16,24},{20,28},{24,16},{28,20},{1,9},{5... | collective-permute-start | bytes 393224 | tf_op jit(solution)/shard_map/ppermute | solution.py:954
  108.7 16.6 %collective-permute-start.9 = (bf16[2,256,128]{2,1,0:T(8,128)(2,1)}, bf16[2,256,128]{2,1,0:T(8,128)(2,1)S(1)}, u32[]{:S(2)}, u32[]{:S(2)}) collective-permute-start(bf16[2,256,128]{2,1,0:T(8,128)(2,1)} %get-tuple-element.214), channel_id=1, source_target_pairs={{0,16},{4,20},{8,24},{12,28},{16,0},{20,4},{24,8},{28,12},{1,17},{... | collective-permute-start | bytes 393224 | tf_op jit(solution)/shard_map/ppermute | solution.py:954
  109.8 15.6 %collective-permute-start.10 = (bf16[2,256,128]{2,1,0:T(8,128)(2,1)}, bf16[2,256,128]{2,1,0:T(8,128)(2,1)S(1)}, u32[]{:S(2)}, u32[]{:S(2)}) collective-permute-start(bf16[2,256,128]{2,1,0:T(8,128)(2,1)} %get-tuple-element.215), channel_id=1, source_target_pairs={{0,24},{4,28},{8,16},{12,20},{16,8},{20,12},{24,0},{28,4},{1,25},{... | collective-permute-start | bytes 393224 | tf_op jit(solution)/shard_map/ppermute | solution.py:954
  125.5 4.5 collective-permute-start.11
  125.6 24.2 %collective-permute-start.12 = (bf16[2,256,128]{2,1,0:T(8,128)(2,1)}, bf16[2,256,128]{2,1,0:T(8,128)(2,1)S(1)}, u32[]{:S(2)}, u32[]{:S(2)}) collective-permute-start(bf16[2,256,128]{2,1,0:T(8,128)(2,1)} %get-tuple-element.224), channel_id=1, source_target_pairs={{0,8},{4,12},{8,0},{12,4},{16,24},{20,28},{24,16},{28,20},{1,9},{5... | collective-permute-start | bytes 393224 | tf_op jit(solution)/shard_map/ppermute | solution.py:954
  126.7 23.1 %collective-permute-start.13 = (bf16[2,256,128]{2,1,0:T(8,128)(2,1)}, bf16[2,256,128]{2,1,0:T(8,128)(2,1)S(1)}, u32[]{:S(2)}, u32[]{:S(2)}) collective-permute-start(bf16[2,256,128]{2,1,0:T(8,128)(2,1)} %get-tuple-element.225), channel_id=1, source_target_pairs={{0,16},{4,20},{8,24},{12,28},{16,0},{20,4},{24,8},{28,12},{1,17},{... | collective-permute-start | bytes 393224 | tf_op jit(solution)/shard_map/ppermute | solution.py:954
  128.6 21.1 %collective-permute-start.14 = (bf16[2,256,128]{2,1,0:T(8,128)(2,1)}, bf16[2,256,128]{2,1,0:T(8,128)(2,1)S(1)}, u32[]{:S(2)}, u32[]{:S(2)}) collective-permute-start(bf16[2,256,128]{2,1,0:T(8,128)(2,1)} %get-tuple-element.226), channel_id=1, source_target_pairs={{0,24},{4,28},{8,16},{12,20},{16,8},{20,12},{24,0},{28,4},{1,25},{... | collective-permute-start | bytes 393224 | tf_op jit(solution)/shard_map/ppermute | solution.py:954
  149.8 2.4 collective-permute-start.15
  150.0 2.2 collective-permute-start.16
  156.5 23.7 %collective-permute-start.20 = (bf16[256,7680]{1,0:T(8,128)(2,1)}, bf16[256,7680]{1,0:T(8,128)(2,1)}, u32[]{:S(2)}, u32[]{:S(2)}) collective-permute-start(bf16[256,7680]{1,0:T(8,128)(2,1)} %get-tuple-element.259.refs_12_.refs_20_), channel_id=1, source_target_pairs={{0,4},{4,0},{8,12},{12,8},{16,20},{20,16},{24,28},{28,24},{1,5},{5... | collective-permute-start | bytes 11796488 | tf_op jit(solution)/shard_map/ppermute | solution.py:954
  156.7 23.4 %collective-permute-start.17 = (bf16[2,256,128]{2,1,0:T(8,128)(2,1)}, bf16[2,256,128]{2,1,0:T(8,128)(2,1)S(1)}, u32[]{:S(2)}, u32[]{:S(2)}) collective-permute-start(bf16[2,256,128]{2,1,0:T(8,128)(2,1)} %get-tuple-element.242), channel_id=1, source_target_pairs={{0,8},{4,12},{8,0},{12,4},{16,24},{20,28},{24,16},{28,20},{1,9},{5... | collective-permute-start | bytes 393224 | tf_op jit(solution)/shard_map/ppermute | solution.py:954
  156.9 23.3 %collective-permute-start.18 = (bf16[2,256,128]{2,1,0:T(8,128)(2,1)}, bf16[2,256,128]{2,1,0:T(8,128)(2,1)S(1)}, u32[]{:S(2)}, u32[]{:S(2)}) collective-permute-start(bf16[2,256,128]{2,1,0:T(8,128)(2,1)} %get-tuple-element.243), channel_id=1, source_target_pairs={{0,16},{4,20},{8,24},{12,28},{16,0},{20,4},{24,8},{28,12},{1,17},{... | collective-permute-start | bytes 393224 | tf_op jit(solution)/shard_map/ppermute | solution.py:954
  159.8 20.5 %collective-permute-start.19 = (bf16[2,256,128]{2,1,0:T(8,128)(2,1)}, bf16[2,256,128]{2,1,0:T(8,128)(2,1)S(1)}, u32[]{:S(2)}, u32[]{:S(2)}) collective-permute-start(bf16[2,256,128]{2,1,0:T(8,128)(2,1)} %get-tuple-element.244), channel_id=1, source_target_pairs={{0,24},{4,28},{8,16},{12,20},{16,8},{20,12},{24,0},{28,4},{1,25},{... | collective-permute-start | bytes 393224 | tf_op jit(solution)/shard_map/ppermute | solution.py:954
  180.2 29.8 %copy-start.45 = (bf16[2,256,128]{2,1,0:T(8,128)(2,1)}, bf16[2,256,128]{2,1,0:T(8,128)(2,1)S(1)}, u32[]{:S(2)}) copy-start(bf16[2,256,128]{2,1,0:T(8,128)(2,1)S(1)} %collective-permute-done.17.refs_5_) | copy-start | bytes 393220
  180.2 29.8 %copy-start.46 = (bf16[2,256,128]{2,1,0:T(8,128)(2,1)}, bf16[2,256,128]{2,1,0:T(8,128)(2,1)S(1)}, u32[]{:S(2)}) copy-start(bf16[2,256,128]{2,1,0:T(8,128)(2,1)S(1)} %collective-permute-done.18.refs_6_) | copy-start | bytes 393220
  180.2 29.7 %copy-start.47 = (bf16[2,256,128]{2,1,0:T(8,128)(2,1)}, bf16[2,256,128]{2,1,0:T(8,128)(2,1)S(1)}, u32[]{:S(2)}) copy-start(bf16[2,256,128]{2,1,0:T(8,128)(2,1)S(1)} %collective-permute-done.19.refs_7_) | copy-start | bytes 393220
  180.2 2.2 collective-permute-start.21
  186.7 7.1 %collective-permute-start.22 = (bf16[256,7680]{1,0:T(8,128)(2,1)}, bf16[256,7680]{1,0:T(8,128)(2,1)}, u32[]{:S(2)}, u32[]{:S(2)}) collective-permute-start(bf16[256,7680]{1,0:T(8,128)(2,1)} %get-tuple-element.258.refs_14_.refs_22_), channel_id=1, source_target_pairs={{0,4},{4,0},{8,12},{12,8},{16,20},{20,16},{24,28},{28,24},{1,5},{5... | collective-permute-start | bytes 11796488 | tf_op jit(solution)/shard_map/ppermute | solution.py:954
  211.4 33.8 %collective-permute-start.23 = (bf16[2,256,128]{2,1,0:T(8,128)(2,1)S(1)}, bf16[2,256,128]{2,1,0:T(8,128)(2,1)S(1)}, u32[]{:S(2)}, u32[]{:S(2)}) collective-permute-start(bf16[2,256,128]{2,1,0:T(8,128)(2,1)S(1)} %copy-done.50), channel_id=1, source_target_pairs={{0,8},{4,12},{8,0},{12,4},{16,24},{20,28},{24,16},{28,20},{1,9},{5... | collective-permute-start | bytes 393224 | tf_op jit(solution)/shard_map/ppermute | solution.py:954
  211.4 33.8 %collective-permute-start.24 = (bf16[2,256,128]{2,1,0:T(8,128)(2,1)S(1)}, bf16[2,256,128]{2,1,0:T(8,128)(2,1)S(1)}, u32[]{:S(2)}, u32[]{:S(2)}) collective-permute-start(bf16[2,256,128]{2,1,0:T(8,128)(2,1)S(1)} %copy-done.49), channel_id=1, source_target_pairs={{0,16},{4,20},{8,24},{12,28},{16,0},{20,4},{24,8},{28,12},{1,17},{... | collective-permute-start | bytes 393224 | tf_op jit(solution)/shard_map/ppermute | solution.py:954
  214.4 30.9 %collective-permute-start.25 = (bf16[2,256,128]{2,1,0:T(8,128)(2,1)S(1)}, bf16[2,256,128]{2,1,0:T(8,128)(2,1)S(1)}, u32[]{:S(2)}, u32[]{:S(2)}) collective-permute-start(bf16[2,256,128]{2,1,0:T(8,128)(2,1)S(1)} %copy-done.48), channel_id=1, source_target_pairs={{0,24},{4,28},{8,16},{12,20},{16,8},{20,12},{24,0},{28,4},{1,25},{... | collective-permute-start | bytes 393224 | tf_op jit(solution)/shard_map/ppermute | solution.py:954
  215.8 34.0 %copy-start.33 = (f32[8,1024]{1,0:T(8,128)S(1)}, f32[8,1024]{1,0:T(8,128)}, u32[]{:S(2)}) copy-start(f32[8,1024]{1,0:T(8,128)} %get-tuple-element.326) | copy-start | bytes 98308
  245.3 28.2 %collective-permute-start.26 = (bf16[2,3,256,128]{3,2,1,0:T(8,128)(2,1)}, bf16[2,3,256,128]{3,2,1,0:T(8,128)(2,1)S(1)}, u32[]{:S(2)}, u32[]{:S(2)}) collective-permute-start(bf16[2,3,256,128]{3,2,1,0:T(8,128)(2,1)} %get-tuple-element.290), channel_id=1, source_target_pairs={{0,8},{4,12},{8,0},{12,4},{16,24},{20,28},{24,16},{28,20},{1,9},{5... | collective-permute-start | bytes 1179656 | tf_op jit(solution)/shard_map/ppermute | solution.py:954
  245.4 30.1 %collective-permute-start.27 = (bf16[2,3,256,128]{3,2,1,0:T(8,128)(2,1)}, bf16[2,3,256,128]{3,2,1,0:T(8,128)(2,1)S(1)}, u32[]{:S(2)}, u32[]{:S(2)}) collective-permute-start(bf16[2,3,256,128]{3,2,1,0:T(8,128)(2,1)} %get-tuple-element.291), channel_id=1, source_target_pairs={{0,16},{4,20},{8,24},{12,28},{16,0},{20,4},{24,8},{28,12},{1,17},{... | collective-permute-start | bytes 1179656 | tf_op jit(solution)/shard_map/ppermute | solution.py:954
  247.7 27.7 %collective-permute-start.28 = (bf16[2,3,256,128]{3,2,1,0:T(8,128)(2,1)}, bf16[2,3,256,128]{3,2,1,0:T(8,128)(2,1)S(1)}, u32[]{:S(2)}, u32[]{:S(2)}) collective-permute-start(bf16[2,3,256,128]{3,2,1,0:T(8,128)(2,1)} %get-tuple-element.292), channel_id=1, source_target_pairs={{0,24},{4,28},{8,16},{12,20},{16,8},{20,12},{24,0},{28,4},{1,25},{... | collective-permute-start | bytes 1179656 | tf_op jit(solution)/shard_map/ppermute | solution.py:954
  273.5 35.4 %copy-start.16 = (bf16[2,3,256,128]{3,2,1,0:T(8,128)(2,1)}, bf16[2,3,256,128]{3,2,1,0:T(8,128)(2,1)S(1)}, u32[]{:S(2)}) copy-start(bf16[2,3,256,128]{3,2,1,0:T(8,128)(2,1)S(1)} %collective-permute-done.26.refs_5_) | copy-start | bytes 1179652
  275.4 33.5 %copy-start.17 = (bf16[2,3,256,128]{3,2,1,0:T(8,128)(2,1)}, bf16[2,3,256,128]{3,2,1,0:T(8,128)(2,1)S(1)}, u32[]{:S(2)}) copy-start(bf16[2,3,256,128]{3,2,1,0:T(8,128)(2,1)S(1)} %collective-permute-done.27.refs_6_) | copy-start | bytes 1179652
  275.4 32.3 %copy-start.18 = (bf16[2,3,256,128]{3,2,1,0:T(8,128)(2,1)}, bf16[2,3,256,128]{3,2,1,0:T(8,128)(2,1)S(1)}, u32[]{:S(2)}) copy-start(bf16[2,3,256,128]{3,2,1,0:T(8,128)(2,1)S(1)} %collective-permute-done.28.refs_7_) | copy-start | bytes 1179652
  275.4 41.6 %collective-permute-start.29 = (bf16[2,3,256,128]{3,2,1,0:T(8,128)(2,1)}, bf16[2,3,256,128]{3,2,1,0:T(8,128)(2,1)}, u32[]{:S(2)}, u32[]{:S(2)}) collective-permute-start(bf16[2,3,256,128]{3,2,1,0:T(8,128)(2,1)} %get-tuple-element.301), channel_id=1, source_target_pairs={{0,8},{4,12},{8,0},{12,4},{16,24},{20,28},{24,16},{28,20},{1,9},{5... | collective-permute-start | bytes 1179656 | tf_op jit(solution)/shard_map/ppermute | solution.py:954
  282.1 35.0 %collective-permute-start.30 = (bf16[2,3,256,128]{3,2,1,0:T(8,128)(2,1)}, bf16[2,3,256,128]{3,2,1,0:T(8,128)(2,1)}, u32[]{:S(2)}, u32[]{:S(2)}) collective-permute-start(bf16[2,3,256,128]{3,2,1,0:T(8,128)(2,1)} %get-tuple-element.302), channel_id=1, source_target_pairs={{0,16},{4,20},{8,24},{12,28},{16,0},{20,4},{24,8},{28,12},{1,17},{... | collective-permute-start | bytes 1179656 | tf_op jit(solution)/shard_map/ppermute | solution.py:954
  283.1 34.0 %collective-permute-start.31 = (bf16[2,3,256,128]{3,2,1,0:T(8,128)(2,1)}, bf16[2,3,256,128]{3,2,1,0:T(8,128)(2,1)}, u32[]{:S(2)}, u32[]{:S(2)}) collective-permute-start(bf16[2,3,256,128]{3,2,1,0:T(8,128)(2,1)} %get-tuple-element.303), channel_id=1, source_target_pairs={{0,24},{4,28},{8,16},{12,20},{16,8},{20,12},{24,0},{28,4},{1,25},{... | collective-permute-start | bytes 1179656 | tf_op jit(solution)/shard_map/ppermute | solution.py:954
  308.9 34.3 %collective-permute-start.38 = (bf16[2,1152,256]{2,1,0:T(8,128)(2,1)}, bf16[2,1152,256]{2,1,0:T(8,128)(2,1)S(1)}, u32[]{:S(2)}, u32[]{:S(2)}) collective-permute-start(bf16[2,1152,256]{2,1,0:T(8,128)(2,1)} %pad_maximum_fusion), channel_id=1, source_target_pairs={{0,8},{4,12},{8,0},{12,4},{16,24},{20,28},{24,16},{28,20},{1,9},{5... | collective-permute-start | bytes 3538952 | tf_op jit(solution)/shard_map/ppermute | solution.py:954
  317.0 20.0 %collective-permute-start.32 = (f32[256,1024]{1,0:T(8,128)}, f32[256,1024]{1,0:T(8,128)}, u32[]{:S(2)}, u32[]{:S(2)}) collective-permute-start(f32[256,1024]{1,0:T(8,128)} %get-tuple-element.305), channel_id=1, source_target_pairs={{0,4},{4,0},{8,12},{12,8},{16,20},{20,16},{24,28},{28,24},{1,5},{5... | collective-permute-start | bytes 3145736 | tf_op jit(solution)/shard_map/ppermute | solution.py:954
  323.7 13.3 %collective-permute-start.33 = (f32[256,1024]{1,0:T(8,128)}, f32[256,1024]{1,0:T(8,128)}, u32[]{:S(2)}, u32[]{:S(2)}) collective-permute-start(f32[256,1024]{1,0:T(8,128)} %get-tuple-element.306), channel_id=1, source_target_pairs={{0,4},{4,0},{8,12},{12,8},{16,20},{20,16},{24,28},{28,24},{1,5},{5... | collective-permute-start | bytes 3145736 | tf_op jit(solution)/shard_map/ppermute | solution.py:954
  334.4 19.8 %collective-permute-start.34 = (bf16[2,2,256,384]{3,2,1,0:T(8,128)(2,1)}, bf16[2,2,256,384]{3,2,1,0:T(8,128)(2,1)S(1)}, u32[]{:S(2)}, u32[]{:S(2)}) collective-permute-start(bf16[2,2,256,384]{3,2,1,0:T(8,128)(2,1)} %get-tuple-element.319), channel_id=1, source_target_pairs={{0,1},{1,0},{2,3},{3,2},{4,5},{5,4},{6,7},{7,6},{8,9},{9,8},{10,11... | collective-permute-start | bytes 2359304 | tf_op jit(solution)/shard_map/ppermute | solution.py:954
  336.3 23.0 %collective-permute-start.36 = (bf16[2,2,256,384]{3,2,1,0:T(8,128)(2,1)}, bf16[2,2,256,384]{3,2,1,0:T(8,128)(2,1)}, u32[]{:S(2)}, u32[]{:S(2)}) collective-permute-start(bf16[2,2,256,384]{3,2,1,0:T(8,128)(2,1)} %get-tuple-element.321), channel_id=1, source_target_pairs={{0,2},{1,3},{2,0},{3,1},{4,6},{5,7},{6,4},{7,5},{8,10},{9,11},{10,... | collective-permute-start | bytes 2359304 | tf_op jit(solution)/shard_map/ppermute | solution.py:954
  344.7 2.4 collective-permute-start.40
  347.1 9.4 %collective-permute-start.41 = (bf16[2,24,1024]{2,1,0:T(8,128)(2,1)S(1)}, bf16[2,24,1024]{2,1,0:T(8,128)(2,1)S(1)}, u32[]{:S(2)}, u32[]{:S(2)}) collective-permute-start(bf16[2,24,1024]{2,1,0:T(8,128)(2,1)S(1)} %pad_maximum_fusion.10), channel_id=1, source_target_pairs={{0,8},{4,12},{8,0},{12,4},{16,24},{20,28},{24,16},{28,20},{1,9},{5... | collective-permute-start | bytes 294920 | tf_op jit(solution)/shard_map/ppermute | solution.py:954
  355.1 16.3 %collective-permute-start.35 = (bf16[1,2,256,384]{3,2,1,0:T(8,128)(2,1)}, bf16[1,2,256,384]{3,2,1,0:T(8,128)(2,1)}, u32[]{:S(2)}, u32[]{:S(2)}) collective-permute-start(bf16[1,2,256,384]{3,2,1,0:T(8,128)(2,1)} %add_convert_fusion.4), channel_id=1, source_target_pairs={{0,2},{1,3},{2,0},{3,1},{4,6},{5,7},{6,4},{7,5},{8,10},{9,11},{10,... | collective-permute-start | bytes 1179656 | tf_op jit(solution)/shard_map/ppermute | solution.py:954
  356.5 11.5 %collective-permute-start.42 = (bf16[4,24,1024]{2,1,0:T(8,128)(2,1)S(1)}, bf16[4,24,1024]{2,1,0:T(8,128)(2,1)S(1)}, u32[]{:S(2)}, u32[]{:S(2)}) collective-permute-start(bf16[4,24,1024]{2,1,0:T(8,128)(2,1)S(1)} %pad_maximum_fusion.7), channel_id=1, source_target_pairs={{0,16},{4,20},{8,24},{12,28},{16,0},{20,4},{24,8},{28,12},{1,17},{... | collective-permute-start | bytes 589832 | tf_op jit(solution)/shard_map/ppermute | solution.py:954
  361.2 17.2 %collective-permute-start.37 = (bf16[1,2,256,384]{3,2,1,0:T(8,128)(2,1)}, bf16[1,2,256,384]{3,2,1,0:T(8,128)(2,1)}, u32[]{:S(2)}, u32[]{:S(2)}) collective-permute-start(bf16[1,2,256,384]{3,2,1,0:T(8,128)(2,1)} %add_convert_fusion.1), channel_id=1, source_target_pairs={{0,1},{1,0},{2,3},{3,2},{4,5},{5,4},{6,7},{7,6},{8,9},{9,8},{10,11... | collective-permute-start | bytes 1179656 | tf_op jit(solution)/shard_map/ppermute | solution.py:954
  368.2 9.8 %collective-permute-start.43 = (bf16[1,144,1024]{2,1,0:T(8,128)(2,1)S(1)}, bf16[1,144,1024]{2,1,0:T(8,128)(2,1)S(1)}, u32[]{:S(2)}, u32[]{:S(2)}) collective-permute-start(bf16[1,144,1024]{2,1,0:T(8,128)(2,1)S(1)} %maximum_bitcast_fusion.1), channel_id=1, source_target_pairs={{0,1},{1,0},{2,3},{3,2},{4,5},{5,4},{6,7},{7,6},{8,9},{9,8},{10,11... | collective-permute-start | bytes 884744 | tf_op jit(solution)/shard_map/ppermute | solution.py:954
  371.3 27.5 %collective-permute-start.39 = (bf16[1,1152,256]{2,1,0:T(8,128)(2,1)S(1)}, bf16[1,1152,256]{2,1,0:T(8,128)(2,1)S(1)}, u32[]{:S(2)}, u32[]{:S(2)}) collective-permute-start(bf16[1,1152,256]{2,1,0:T(8,128)(2,1)S(1)} %fusion.1), channel_id=1, source_target_pairs={{0,16},{4,20},{8,24},{12,28},{16,0},{20,4},{24,8},{28,12},{1,17},{... | collective-permute-start | bytes 1769480 | tf_op jit(solution)/shard_map/ppermute | solution.py:954
  372.8 30.9 %copy-start.4 = (bf16[2,256,384]{2,1,0:T(8,128)(2,1)}, bf16[2,256,384]{2,1,0:T(8,128)(2,1)S(1)}, u32[]{:S(2)}) copy-start(bf16[2,256,384]{2,1,0:T(8,128)(2,1)S(1)} %fusion.3) | copy-start | bytes 1179652
  378.0 21.1 %collective-permute-start.44 = (bf16[2,144,1024]{2,1,0:T(8,128)(2,1)S(1)}, bf16[2,144,1024]{2,1,0:T(8,128)(2,1)S(1)}, u32[]{:S(2)}, u32[]{:S(2)}) collective-permute-start(bf16[2,144,1024]{2,1,0:T(8,128)(2,1)S(1)} %pad_maximum_fusion.2), channel_id=1, source_target_pairs={{0,2},{1,3},{2,0},{3,1},{4,6},{5,7},{6,4},{7,5},{8,10},{9,11},{10,... | collective-permute-start | bytes 1769480 | tf_op jit(solution)/shard_map/ppermute | solution.py:954
  399.8 34.1 %collective-permute-start.50 = (bf16[1152,256]{1,0:T(8,128)(2,1)S(1)}, bf16[1152,256]{1,0:T(8,128)(2,1)}, u32[]{:S(2)}, u32[]{:S(2)}) collective-permute-start(bf16[1152,256]{1,0:T(8,128)(2,1)S(1)} %fusion.refs_0_), channel_id=1, source_target_pairs={{0,3},{1,2},{2,1},{3,0},{4,7},{5,6},{6,5},{7,4},{8,11},{9,10},{10,... | collective-permute-start | bytes 1769480 | tf_op jit(solution)/shard_map/ppermute | solution.py:954
  399.9 34.1 %collective-permute-start.49 = (bf16[1152,256]{1,0:T(8,128)(2,1)S(1)}, bf16[1152,256]{1,0:T(8,128)(2,1)}, u32[]{:S(2)}, u32[]{:S(2)}) collective-permute-start(bf16[1152,256]{1,0:T(8,128)(2,1)S(1)} %fusion.refs_0_), channel_id=1, source_target_pairs={{0,2},{1,3},{2,0},{3,1},{4,6},{5,7},{6,4},{7,5},{8,10},{9,11},{10,... | collective-permute-start | bytes 1769480 | tf_op jit(solution)/shard_map/ppermute | solution.py:954
  401.7 32.3 %collective-permute-start.48 = (bf16[1152,256]{1,0:T(8,128)(2,1)S(1)}, bf16[1152,256]{1,0:T(8,128)(2,1)}, u32[]{:S(2)}, u32[]{:S(2)}) collective-permute-start(bf16[1152,256]{1,0:T(8,128)(2,1)S(1)} %fusion.refs_0_), channel_id=1, source_target_pairs={{0,1},{1,0},{2,3},{3,2},{4,5},{5,4},{6,7},{7,6},{8,9},{9,8},{10,11... | collective-permute-start | bytes 1769480 | tf_op jit(solution)/shard_map/ppermute | solution.py:954
  413.5 10.1 %collective-permute-start.45 = (bf16[2,256,384]{2,1,0:T(8,128)(2,1)S(1)}, bf16[2,256,384]{2,1,0:T(8,128)(2,1)S(1)}, u32[]{:S(2)}, u32[]{:S(2)}) collective-permute-start(bf16[2,256,384]{2,1,0:T(8,128)(2,1)S(1)} %pad_maximum_fusion.4), channel_id=1, source_target_pairs={{0,8},{4,12},{8,0},{12,4},{16,24},{20,28},{24,16},{28,20},{1,9},{5... | collective-permute-start | bytes 1179656 | tf_op jit(solution)/shard_map/ppermute | solution.py:954
  423.6 10.2 %collective-permute-start.46 = (bf16[1,256,384]{2,1,0:T(8,128)(2,1)S(1)}, bf16[1,256,384]{2,1,0:T(8,128)(2,1)S(1)}, u32[]{:S(2)}, u32[]{:S(2)}) collective-permute-start(bf16[1,256,384]{2,1,0:T(8,128)(2,1)S(1)} %add_convert_fusion.7), channel_id=1, source_target_pairs={{0,16},{4,20},{8,24},{12,28},{16,0},{20,4},{24,8},{28,12},{1,17},{... | collective-permute-start | bytes 589832 | tf_op jit(solution)/shard_map/ppermute | solution.py:954
  433.9 1.4 collective-permute-start.47
  435.3 11.0 %collective-permute-start.53 = (bf16[2,128,384]{2,1,0:T(8,128)(2,1)S(1)}, bf16[2,128,384]{2,1,0:T(8,128)(2,1)S(1)}, u32[]{:S(2)}, u32[]{:S(2)}) collective-permute-start(bf16[2,128,384]{2,1,0:T(8,128)(2,1)S(1)} %pad_maximum_fusion.8.refs_0_), channel_id=1, source_target_pairs={{0,3},{1,2},{2,1},{3,0},{4,7},{5,6},{6,5},{7,4},{8,11},{9,10},{10,... | collective-permute-start | bytes 589832 | tf_op jit(solution)/shard_map/ppermute | solution.py:954
  436.0 10.9 %collective-permute-start.52 = (bf16[2,128,384]{2,1,0:T(8,128)(2,1)S(1)}, bf16[2,128,384]{2,1,0:T(8,128)(2,1)S(1)}, u32[]{:S(2)}, u32[]{:S(2)}) collective-permute-start(bf16[2,128,384]{2,1,0:T(8,128)(2,1)S(1)} %pad_maximum_fusion.8.refs_0_), channel_id=1, source_target_pairs={{0,2},{1,3},{2,0},{3,1},{4,6},{5,7},{6,4},{7,5},{8,10},{9,11},{10,... | collective-permute-start | bytes 589832 | tf_op jit(solution)/shard_map/ppermute | solution.py:954
  437.0 9.9 %collective-permute-start.51 = (bf16[2,128,384]{2,1,0:T(8,128)(2,1)S(1)}, bf16[2,128,384]{2,1,0:T(8,128)(2,1)S(1)}, u32[]{:S(2)}, u32[]{:S(2)}) collective-permute-start(bf16[2,128,384]{2,1,0:T(8,128)(2,1)S(1)} %pad_maximum_fusion.8.refs_0_), channel_id=1, source_target_pairs={{0,1},{1,0},{2,3},{3,2},{4,5},{5,4},{6,7},{7,6},{8,9},{9,8},{10,11... | collective-permute-start | bytes 589832 | tf_op jit(solution)/shard_map/ppermute | solution.py:954
  (48 other events, 385.6 us)
Sparse Core Ops, SparseCore 0:
  210.2 96.2 reduce-scatter.1

commit v6 on v5

--- a/solution.py
+++ b/solution.py
@@ -1132,8 +1132,11 @@
         if c < clips - 1:
             far_ones[-1], crossed[-1] = after(far_ones[-1], crossed[-1])
         saved.append((out[4], out[5], gone, out[7], out[8]))
+        if c == clips - 1:
+            far_ones[-1], mine_mixed = after(far_ones[-1], mine_mixed)
         back = list(proj_back_call(meta, gone, far_ones[c], proj_weight, zs))
-        back[0], mine_mixed = after(back[0], mine_mixed)
+        if c < clips - 1:
+            back[0], mine_mixed = after(back[0], mine_mixed)
         mixed.append([mine_mixed, swap(mine_mixed)])
         grads.append(spread(back, seq_size))
     row = width // seq_size
@@ -1209,7 +1212,12 @@
             "qkv_weight_grad",
         )
         pairs_qkv = [shares[:2], shares[2:]]
-        pairs_qkv = step_in(pairs_qkv, step_out(pairs_qkv, turns[0], clip_size))
+        arrived = step_out(pairs_qkv, turns[0], clip_size)
+        if len(blocks) > 1:
+            landed = z_out(blocks, seq_size)
+            arrived, landed = after(arrived, landed)
+            blocks = z_in(blocks, landed)
+        pairs_qkv = step_in(pairs_qkv, arrived)
         for bits in turns[1:]:
             pairs_qkv = step_in(pairs_qkv, step_out(pairs_qkv, bits, clip_size))
     own_sums = jnp.sum(
@@ -1222,7 +1230,12 @@
     late = double(message[None], "clip", clip_size)
     piece = sum_z(blocks, seq_size)
     if aligned:
-        pairs_qkv, piece, late = after(pairs_qkv, piece, late)
+        pairs_qkv, late = after(pairs_qkv, late)
+        blocks = [*pairs_qkv[0][0], *pairs_qkv[1][0]]
+        if len(blocks) > 1:
+            landed = z_out(blocks, seq_size)
+            landed, late = after(landed, late)
+            blocks = z_in(blocks, landed)
     own_sums = jnp.sum(late[:, seq_size * stop :].astype(F32), axis=0).reshape(2, -1)
     late = late[:, : seq_size * stop].reshape(clip_size * seq_size, stop, width)
     devices = clip_size * seq_size
@@ -1271,11 +1284,14 @@
     proj_bgrad = own_part(bias_sums[hidden + width : hidden + 2 * width])
     if aligned:
         pieces = gather_pieces(piece, clip_size)
-        piece = sum_z([*pairs_qkv[0][0], *pairs_qkv[1][0]], seq_size)
-        piece = piece.reshape(2, row, 3 * LANES)
+        if len(blocks) > 1:
+            landed = z_out(blocks, seq_size)
+            landed, mod_wgrad, table_grad = after(landed, mod_wgrad, table_grad)
+            blocks = z_in(blocks, landed)
+        piece = sum_z(blocks, seq_size).reshape(2, row, 3 * LANES)
         own_rows = lax.dynamic_index_in_dim(piece, parity, 0, keepdims=False)
         far_rows = swap(lax.dynamic_index_in_dim(piece, 1 - parity, 0, keepdims=False))
-        far_rows, pieces, mod_wgrad, table_grad = after(far_rows, pieces, mod_wgrad, table_grad)
+        far_rows, pieces = after(far_rows, pieces)
         pieces_qkv = gather_pieces(jnp.stack([own_rows, far_rows]), clip_size)
     else:
         pieces = gather_pieces(piece, clip_size)

time: 464 us -> 453 us (0.976)
  waiting for transfers between devices: 111 us -> 101 us
    ppermute x54, waiting for transfers between devices: 89.2 us -> 82 us  [exchange(): return lax.ppermute(array, axis, [(k, k ^ distance) for k in range(size)])]
  transfers between devices with their start and end apart: 55 -> 55, of which waited for: 16 -> 18; matrix products, arithmetic and copies ran while one was open for 10% -> 10% of each run, Pallas kernels for 36% -> 38%
where the time goes in v6:
time: 453 us; the launch traced here: 446 us
  Pallas kernels  203 us (45%)
  waiting for transfers between devices  101 us (22%)
  starting transfers between devices  78.4 us (17%)
  local copies, waits for them, and re-layouts  18.3 us (4%)
  other arithmetic  18.2 us (4%)
  between operations  15.3 us (3%)
  matrix products  12.1 us (3%)
    ppermute x54, waiting for transfers between devices, exchange(): return lax.ppermute(array, axis, [(k, k ^ distance) for k in range(size)])  82 us
    ppermute x54, starting transfers between devices, exchange(): return lax.ppermute(array, axis, [(k, k ^ distance) for k in range(size)])  78.3 us
    pallas_call x2, Pallas kernels, attend_grad_call(): pl.pallas_call(functools.partial(attend_grad_kernel, slots, head, clip),...  52.7 us
    pallas_call x2, Pallas kernels, forward_back_call(): pl.pallas_call(functools.partial(forward_back_kernel, slots, clip), grid=...  38.2 us
    pallas_call x2, Pallas kernels, attend_call(): pl.pallas_call(functools.partial(attend_kernel, slots, head, clip), out_s...  33.4 us
    pallas_call x2, Pallas kernels, weight_grad_call(): pl.pallas_call(functools.partial(weight_grad_kernel, tuple(jobs), clip_si...  24.8 us
    reduce_scatter x1, waiting for transfers between devices, on_device(): lax.psum_scatter(shares.reshape(-1, shares.shape[-1]), 'clip', scatter_di...  18.8 us
    pallas_call x2, Pallas kernels, qkv_grad_call(): pl.pallas_call(functools.partial(qkv_grad_kernel, zs, head, clip), out_sh...  13.1 us
  transfers between devices with their start and end apart: 55, of which 18 were waited for; matrix products, arithmetic and copies ran while one was open for 10% of the time, Pallas kernels for 38%

profile of v6, /device:TPU:0, one launch (start us, length us, event | category | flops | bytes accessed | tf_op | source)
XLA Modules:
  0.0 445.8 jit_solution(15701917918984359079)
XLA Ops:
  11.0 1.3 broadcast_in_dim.47.bias
  15.5 4.0 modulation.2
  21.3 10.1 %norm_qkv.1 = (bf16[2,3,256,128]{3,2,1,0:T(8,128)(2,1)}, bf16[2,3,256,128]{3,2,1,0:T(8,128)(2,1)}, bf16[2,3,256,128]{3,2,1,0:T(8,128)(2,1)}, bf16[2,3,256,128]{3...) custom-call(s32[4]{0:T(128)} %pad_add_fusion.1.meta, ...), custom_call_target="tpu_custom_call" | custom-call | flops 3221225472 | bytes 11534336 | tf_op jit(solution)/shard_map/norm_qkv/pallas_call | solution.py:226
  31.3 3.1 collective-permute-start.2
  34.4 2.6 collective-permute-start.3
  38.8 6.4 %modulation.3 = (f32[4,2,1024]{2,1,0:T(2,128)}, f32[2,1024]{1,0:T(2,128)}) custom-call(s32[2]{0:T(128)} %copy-done.31, bf16[1024,1024]{1,0:T(8,128)(2,1)} %table.3, bf16[1024,6144]{1,0:T(8,128)(2,1)} %weight.3, bf16[1,6144]{1,0:T(2,128)(2,1)} %broadcast_in_dim.47.bias), custom_call_target="tpu_custom_call" | custom-call | bytes 10485760 | tf_op jit(solution)/shard_map/modulation/pallas_call | solution.py:128
  46.1 3.5 collective-permute-start.6
  49.6 2.7 collective-permute-done.2.refs_1_
  52.3 4.1 collective-permute-start.7
  56.5 8.1 %collective-permute-done.3.refs_2_ = bf16[2,3,256,128]{3,2,1,0:T(8,128)(2,1)} collective-permute-done((bf16[2,3,256,128]{3,2,1,0:T(8,128)(2,1)}, bf16[2,3,256,128]{3,2,1,0:T(8,128)(2,1)}, u32[]{:S(2)}, u32[]{:S(2)}) %collective-permute-start.3) | collective-permute-done | bytes 393248 | tf_op jit(solution)/shard_map/ppermute | solution.py:954
  64.5 18.4 %attend.2 = (bf16[2,256,128]{2,1,0:T(8,128)(2,1)}, bf16[2,256,128]{2,1,0:T(8,128)(2,1)}, bf16[2,256,128]{2,1,0:T(8,128)(2,1)}, bf16[2,256,128]{2,1,0:T(8,128)(2,...) custom-call(s32[4]{0:T(128)} %pad_add_fusion.1.meta, bf16[2,3,256,128]{3,2,1,0:T(8,128)(2,1)} %get-tuple-element.197.refs_0_, ...), custom_call_target="tpu_custom_call" | custom-call | flops 8589934592 | bytes 3145728 | tf_op jit(solution)/shard_map/attend/pallas_call | solution.py:325
  83.0 15.2 %collective-permute-done.6.refs_2_ = bf16[2,3,256,128]{3,2,1,0:T(8,128)(2,1)S(1)} collective-permute-done((bf16[2,3,256,128]{3,2,1,0:T(8,128)(2,1)}, bf16[2,3,256,128]{3,2,1,0:T(8,128)(2,1)S(1)}, u32[]{:S(2)}, u32[]{:S(2)}) %collective-permute-start.6) | collective-permute-done | bytes 393248 | tf_op jit(solution)/shard_map/ppermute | solution.py:954
  98.2 10.8 %collective-permute-start.8 = (bf16[2,256,128]{2,1,0:T(8,128)(2,1)}, bf16[2,256,128]{2,1,0:T(8,128)(2,1)S(1)}, u32[]{:S(2)}, u32[]{:S(2)}) collective-permute-start(bf16[2,256,128]{2,1,0:T(8,128)(2,1)} %get-tuple-element.218), channel_id=1, source_target_pairs={{0,8},{4,12},{8,0},{12,4},{16,24},{20,28},{24,16},{28,20},{1,9},{5... | collective-permute-start | bytes 393224 | tf_op jit(solution)/shard_map/ppermute | solution.py:954
  110.0 1.4 collective-permute-start.10
  111.4 15.0 %attend.3 = (bf16[2,256,128]{2,1,0:T(8,128)(2,1)}, bf16[2,256,128]{2,1,0:T(8,128)(2,1)}, bf16[2,256,128]{2,1,0:T(8,128)(2,1)}, bf16[2,256,128]{2,1,0:T(8,128)(2,...) custom-call(s32[4]{0:T(128)} %pad_add_fusion.1.meta, bf16[2,3,256,128]{3,2,1,0:T(8,128)(2,1)} %get-tuple-element.209.refs_0_, ...), custom_call_target="tpu_custom_call" | custom-call | flops 8589934592 | bytes 3145728 | tf_op jit(solution)/shard_map/attend/pallas_call | solution.py:325
  127.8 2.0 collective-permute-start.13
  129.8 1.4 collective-permute-start.14
  131.9 19.0 %feed_forward.2 = (bf16[256,1024]{1,0:T(8,128)(2,1)}, f32[256,1024]{1,0:T(8,128)}, f32[8,1024]{1,0:T(8,128)}, f32[1,4096]{1,0:T(1,128)}, bf16[256,512]{1,0:T(8,1...) custom-call(s32[4]{0:T(128)} %pad_add_fusion.1.meta, ...), custom_call_target="tpu_custom_call" | custom-call | flops 9663676416 | bytes 37748736 | tf_op jit(solution)/shard_map/feed_forward/pallas_call | solution.py:607
  151.7 1.6 collective-permute-done.16.refs_4_
  154.2 3.5 proj_back.2
  158.0 2.9 collective-permute-start.18
  160.9 1.4 collective-permute-start.19
  162.3 19.2 %feed_forward.3 = (bf16[256,1024]{1,0:T(8,128)(2,1)}, f32[256,1024]{1,0:T(8,128)}, f32[8,1024]{1,0:T(8,128)}, f32[1,4096]{1,0:T(1,128)}, bf16[256,512]{1,0:T(8,1...) custom-call(s32[4]{0:T(128)} %pad_add_fusion.1.meta, ...), custom_call_target="tpu_custom_call" | custom-call | flops 9663676416 | bytes 37748736 | tf_op jit(solution)/shard_map/feed_forward/pallas_call | solution.py:607
  181.7 2.1 collective-permute-done.21.far.refs_7_
  184.6 3.5 proj_back.3
  188.1 2.8 collective-permute-done.22.refs_11_.refs_15_.refs_19_.refs_23_
  190.9 16.1 %weight_grads.1 = bf16[4,4,1152,256]{3,2,1,0:T(8,128)(2,1)} custom-call(s32[4]{0:T(128)} %pad_add_fusion.1.meta, bf16[256,512]{1,0:T(8,128)(2,1)} %get-tuple-element.256.refs_0_, bf16[256,512]{1,0:T(8,128)(2,1)} %get-tuple-element.257.refs_1_, bf16[256,512]{1,0:T(8,128)(2,1)} %get-tuple-element.258.refs_2_, bf16[256,512]{1,0:T(8,128)(2,1)} %get-tuple-element.259.refs_3_, ...), custom_call_target="tpu_custom_call" | custom-call | flops 9663676416 | bytes 18874368 | tf_op jit(solution)/shard_map/weight_grads/pallas_call | solution.py:882
  208.5 3.0 collective-permute-start.24
  211.5 1.4 collective-permute-start.25
  212.8 28.7 %attend_grad.2 = (bf16[2,3,256,128]{3,2,1,0:T(8,128)(2,1)}, bf16[2,3,256,128]{3,2,1,0:T(8,128)(2,1)}, bf16[2,3,256,128]{3,2,1,0:T(8,128)(2,1)}, bf16[2,3,256,128]{3,2,1,0:T(8,128)(2,1)}) custom-call(s32[4]{0:T(128)} %pad_add_fusion.1.meta, bf16[2,3,256,128]{3,2,1,0:T(8,128)(2,1)} %get-tuple-element.197.refs_0_, bf16[2,3,256,128]{3,2,1,0:T(8,128)(2,1)} %copy-done.40, ...), custom_call_target="tpu_custom_call" | custom-call | flops 2147483648 | bytes 524288 | tf_op jit(solution)/shard_map/attend_grad/pallas_call | solution.py:436
  241.7 3.3 collective-permute-start.27
  246.9 24.0 %attend_grad.3 = (bf16[2,3,256,128]{3,2,1,0:T(8,128)(2,1)}, bf16[2,3,256,128]{3,2,1,0:T(8,128)(2,1)}, bf16[2,3,256,128]{3,2,1,0:T(8,128)(2,1)}, bf16[2,3,256,128]{3,2,1,0:T(8,128)(2,1)}) custom-call(s32[4]{0:T(128)} %pad_add_fusion.1.meta, bf16[2,3,256,128]{3,2,1,0:T(8,128)(2,1)} %get-tuple-element.209.refs_0_, bf16[2,3,256,128]{3,2,1,0:T(8,128)(2,1)} %copy-done.37, ...), custom_call_target="tpu_custom_call" | custom-call | flops 2147483648 | bytes 524288 | tf_op jit(solution)/shard_map/attend_grad/pallas_call | solution.py:436
  272.1 7.1 %collective-permute-start.29 = (bf16[2,3,256,128]{3,2,1,0:T(8,128)(2,1)}, bf16[2,3,256,128]{3,2,1,0:T(8,128)(2,1)}, u32[]{:S(2)}, u32[]{:S(2)}) collective-permute-start(bf16[2,3,256,128]{3,2,1,0:T(8,128)(2,1)} %get-tuple-element.306), channel_id=1, source_target_pairs={{0,8},{4,12},{8,0},{12,4},{16,24},{20,28},{24,16},{28,20},{1,9},{5... | collective-permute-start | bytes 1179656 | tf_op jit(solution)/shard_map/ppermute | solution.py:954
  280.2 1.5 collective-permute-start.31
  281.7 18.8 %reduce-scatter.2.cloned.1.call-done = bf16[4608,256]{1,0:T(8,128)(2,1)} async-done(((bf16[18432,256]{1,0:T(8,128)(2,1)}), bf16[4608,256]{1,0:T(8,128)(2,1)}) %reduce-scatter.2.cloned.1.call-update) | async-done | bytes 2359312 | tf_op jit(solution)/shard_map/reduce_scatter | solution.py:1158
  300.5 1.3 slice_bitcast_fusion.2
  303.0 1.5 collective-permute-start.36
  304.5 6.5 %qkv_grad.2 = (bf16[256,1536]{1,0:T(8,128)(2,1)}, bf16[256,1536]{1,0:T(8,128)(2,1)}, f32[256,1024]{1,0:T(8,128)}, f32[256,1024]{1,0:T(8,128)}, f32[8,512]{1,0:T(8,128)}) custom-call(s32[4]{0:T(128)} %pad_add_fusion.1.meta, f32[4,128]{1,0:T(4,128)} %get-tuple-element.430.refs_0_, f32[4,128]{1,0:T(4,128)} %get-tuple-element.429.refs_1_, ...), custom_call_target="tpu_custom_call" | custom-call | flops 161061280 | bytes 1048576 | tf_op jit(solution)/shard_map/qkv_grad/pallas_call | solution.py:709
  311.2 6.6 %qkv_grad.3 = (bf16[256,1536]{1,0:T(8,128)(2,1)}, bf16[256,1536]{1,0:T(8,128)(2,1)}, f32[256,1024]{1,0:T(8,128)}, f32[256,1024]{1,0:T(8,128)}, f32[8,512]{1,0:T(8,128)}) custom-call(s32[4]{0:T(128)} %pad_add_fusion.1.meta, f32[4,128]{1,0:T(4,128)} %get-tuple-element.430.refs_0_, f32[4,128]{1,0:T(4,128)} %get-tuple-element.429.refs_1_, ...), custom_call_target="tpu_custom_call" | custom-call | flops 161061280 | bytes 1048576 | tf_op jit(solution)/shard_map/qkv_grad/pallas_call | solution.py:709
  320.4 8.8 %qkv_weight_grad.1 = (bf16[2,2,256,384]{3,2,1,0:T(8,128)(2,1)}, bf16[2,2,256,384]{3,2,1,0:T(8,128)(2,1)}, bf16[2,2,256,384]{3,2,1,0:T(8,128)(2,1)}, bf16[2,2,256,384]{3,2,1,0:T(8,128)(2,1)}) custom-call(s32[4]{0:T(128)} %pad_add_fusion.1.meta, bf16[256,1024]{1,0:T(8,128)(2,1)} %get-tuple-element.315.refs_0_, bf16[256,1024]{1,0:T(8,128)(2,1)} %get-tuple-element.316.refs_1_, ...), custom_call_target="tpu_custom_call" | custom-call | flops 3221225472 | bytes 6291456 | tf_op jit(solution)/shard_map/qkv_weight_grad/pallas_call | solution.py:882
  329.2 1.4 collective-permute-start.34
  331.3 6.2 %norm_grad.1 = (f32[2,1,256,1024]{3,2,1,0:T(8,128)}, f32[2,8,1024]{2,1,0:T(8,128)}) custom-call(bf16[2,1,256,1024]{3,2,1,0:T(8,128)(2,1)} %tokens.7, f32[2,4,1024]{2,1,0:T(4,128)} %get-tuple-element.187.mod, f32[256,1024]{1,0:T(8,128)} %get-tuple-element.304.refs_0_, f32[256,1024]{1,0:T(8,128)} %get-tuple-element.309.refs_1_, ...), custom_call_target="tpu_custom_call" | custom-call | flops 1572864 | bytes 1048576 | tf_op jit(solution)/shard_map/norm_grad/pallas_call | solution.py:743
  339.9 2.1 collective-permute-start.40
  342.0 3.3 collective-permute-done.40
  345.3 2.7 collective-permute-start.41
  348.6 2.3 maximum_bitcast_fusion
  350.8 6.3 %collective-permute-done.41 = bf16[4,24,1024]{2,1,0:T(8,128)(2,1)S(1)} collective-permute-done((bf16[4,24,1024]{2,1,0:T(8,128)(2,1)S(1)}, bf16[4,24,1024]{2,1,0:T(8,128)(2,1)S(1)}, u32[]{:S(2)}, u32[]{:S(2)}) %collective-permute-start.41) | collective-permute-done | bytes 196640 | tf_op jit(solution)/shard_map/ppermute | solution.py:954
  357.3 1.6 collective-permute-start.42
  359.0 1.4 add_convert_fusion.1
  361.0 1.7 collective-permute-start.37
  362.7 4.7 %collective-permute-done.42 = bf16[1,144,1024]{2,1,0:T(8,128)(2,1)S(1)} collective-permute-done((bf16[1,144,1024]{2,1,0:T(8,128)(2,1)S(1)}, bf16[1,144,1024]{2,1,0:T(8,128)(2,1)S(1)}, u32[]{:S(2)}, u32[]{:S(2)}) %collective-permute-start.42) | collective-permute-done | bytes 294944 | tf_op jit(solution)/shard_map/ppermute | solution.py:954
  367.4 1.7 collective-permute-start.43
  369.4 4.4 collective-permute-done.38
  375.2 8.1 %collective-permute-done.43 = bf16[2,144,1024]{2,1,0:T(8,128)(2,1)S(1)} collective-permute-done((bf16[2,144,1024]{2,1,0:T(8,128)(2,1)S(1)}, bf16[2,144,1024]{2,1,0:T(8,128)(2,1)S(1)}, u32[]{:S(2)}, u32[]{:S(2)}) %collective-permute-start.43) | collective-permute-done | bytes 589856 | tf_op jit(solution)/shard_map/ppermute | solution.py:954
  383.6 10.6 %collective-permute-done.47 = bf16[1,1152,256]{2,1,0:T(8,128)(2,1)S(1)} collective-permute-done((bf16[1,1152,256]{2,1,0:T(8,128)(2,1)S(1)}, bf16[1,1152,256]{2,1,0:T(8,128)(2,1)S(1)}, u32[]{:S(2)}, u32[]{:S(2)}) %collective-permute-start.47) | collective-permute-done | bytes 589856 | tf_op jit(solution)/shard_map/ppermute | solution.py:954
  394.5 1.5 collective-permute-start.50
  395.9 1.7 collective-permute-start.49
  398.0 4.5 %collective-permute-done.44 = bf16[2,256,384]{2,1,0:T(8,128)(2,1)S(1)} collective-permute-done((bf16[2,256,384]{2,1,0:T(8,128)(2,1)S(1)}, bf16[2,256,384]{2,1,0:T(8,128)(2,1)S(1)}, u32[]{:S(2)}, u32[]{:S(2)}) %collective-permute-start.44) | collective-permute-done | bytes 393248 | tf_op jit(solution)/shard_map/ppermute | solution.py:954
  405.7 8.5 %fusion.36 = f32[64,1024]{1,0:T(8,128)S(1)} fusion(bf16[64,6144]{1,0:T(8,128)(2,1)S(1)} %reshape.274, bf16[1024,6144]{1,0:T(8,128)(2,1)} %weight.3), kind=kOutput, calls=%fused_computation.107 | convolution fusion | flops 805306368 | bytes 13631488 | tf_op jit(solution)/shard_map/dot_general | solution.py:1259
  414.3 2.3 fusion.15
  419.2 4.2 collective-permute-done.49.refs_2_
  423.4 1.8 collective-permute-start.53
  430.3 4.1 place_grads.1
  436.2 2.6 place_qkv_grad.1
  (267 shorter events, 46.1 us)
Async XLA Ops:
  7.2 293.3 %reduce-scatter.2.cloned.1.call-start = ((), (), s32[]{:S(2)}) async-start(), calls=%async_computation.1 | async-start | bytes 11796480 | tf_op jit(solution)/shard_map/reduce_scatter | solution.py:1158
  7.9 5.7 %collective-permute-start.1 = (s32[2,2]{1,0:T(2,128)S(1)}, s32[2,2]{1,0:T(2,128)S(1)}, u32[]{:S(2)}, u32[]{:S(2)}) collective-permute-start(s32[2,2]{1,0:T(2,128)S(1)} %pad_add_fusion), channel_id=1, source_target_pairs={{0,4},{4,0},{8,12},{12,8},{16,20},{20,16},{24,28},{28,24},{1,5},{5... | collective-permute-start | bytes 56 | tf_op jit(solution)/shard_map/ppermute | solution.py:954
  8.4 11.9 %collective-permute-start = (bf16[2,1,256,1024]{3,2,1,0:T(8,128)(2,1)}, bf16[2,1,256,1024]{3,2,1,0:T(8,128)(2,1)S(1)}, u32[]{:S(2)}, u32[]{:S(2)}) collective-permute-start(bf16[2,1,256,1024]{3,2,1,0:T(8,128)(2,1)} %tokens.7), channel_id=1, source_target_pairs={{0,4},{4,0},{8,12},{12,8},{16,20},{20,16},{24,28},{28,24},{1,5},{5... | collective-permute-start | bytes 3145736 | tf_op jit(solution)/shard_map/ppermute | solution.py:954
  31.3 21.0 %collective-permute-start.2 = (bf16[2,3,256,128]{3,2,1,0:T(8,128)(2,1)}, bf16[2,3,256,128]{3,2,1,0:T(8,128)(2,1)S(1)}, u32[]{:S(2)}, u32[]{:S(2)}) collective-permute-start(bf16[2,3,256,128]{3,2,1,0:T(8,128)(2,1)} %get-tuple-element.189), channel_id=1, source_target_pairs={{0,8},{4,12},{8,0},{12,4},{16,24},{20,28},{24,16},{28,20},{1,9},{5... | collective-permute-start | bytes 1179656 | tf_op jit(solution)/shard_map/ppermute | solution.py:954
  34.4 30.1 %collective-permute-start.3 = (bf16[2,3,256,128]{3,2,1,0:T(8,128)(2,1)}, bf16[2,3,256,128]{3,2,1,0:T(8,128)(2,1)}, u32[]{:S(2)}, u32[]{:S(2)}) collective-permute-start(bf16[2,3,256,128]{3,2,1,0:T(8,128)(2,1)} %get-tuple-element.190), channel_id=1, source_target_pairs={{0,16},{4,20},{8,24},{12,28},{16,0},{20,4},{24,8},{28,12},{1,17},{... | collective-permute-start | bytes 1179656 | tf_op jit(solution)/shard_map/ppermute | solution.py:954
  37.0 27.5 %collective-permute-start.4 = (bf16[2,3,256,128]{3,2,1,0:T(8,128)(2,1)}, bf16[2,3,256,128]{3,2,1,0:T(8,128)(2,1)}, u32[]{:S(2)}, u32[]{:S(2)}) collective-permute-start(bf16[2,3,256,128]{3,2,1,0:T(8,128)(2,1)} %get-tuple-element.191), channel_id=1, source_target_pairs={{0,24},{4,28},{8,16},{12,20},{16,8},{20,12},{24,0},{28,4},{1,25},{... | collective-permute-start | bytes 1179656 | tf_op jit(solution)/shard_map/ppermute | solution.py:954
  45.3 37.7 %collective-permute-start.5 = (bf16[2,3,256,128]{3,2,1,0:T(8,128)(2,1)}, bf16[2,3,256,128]{3,2,1,0:T(8,128)(2,1)S(1)}, u32[]{:S(2)}, u32[]{:S(2)}) collective-permute-start(bf16[2,3,256,128]{3,2,1,0:T(8,128)(2,1)} %get-tuple-element.206), channel_id=1, source_target_pairs={{0,8},{4,12},{8,0},{12,4},{16,24},{20,28},{24,16},{28,20},{1,9},{5... | collective-permute-start | bytes 1179656 | tf_op jit(solution)/shard_map/ppermute | solution.py:954
  46.1 52.0 %collective-permute-start.6 = (bf16[2,3,256,128]{3,2,1,0:T(8,128)(2,1)}, bf16[2,3,256,128]{3,2,1,0:T(8,128)(2,1)S(1)}, u32[]{:S(2)}, u32[]{:S(2)}) collective-permute-start(bf16[2,3,256,128]{3,2,1,0:T(8,128)(2,1)} %get-tuple-element.207), channel_id=1, source_target_pairs={{0,16},{4,20},{8,24},{12,28},{16,0},{20,4},{24,8},{28,12},{1,17},{... | collective-permute-start | bytes 1179656 | tf_op jit(solution)/shard_map/ppermute | solution.py:954
  52.3 45.8 %collective-permute-start.7 = (bf16[2,3,256,128]{3,2,1,0:T(8,128)(2,1)}, bf16[2,3,256,128]{3,2,1,0:T(8,128)(2,1)S(1)}, u32[]{:S(2)}, u32[]{:S(2)}) collective-permute-start(bf16[2,3,256,128]{3,2,1,0:T(8,128)(2,1)} %get-tuple-element.208), channel_id=1, source_target_pairs={{0,24},{4,28},{8,16},{12,20},{16,8},{20,12},{24,0},{28,4},{1,25},{... | collective-permute-start | bytes 1179656 | tf_op jit(solution)/shard_map/ppermute | solution.py:954
  83.0 28.4 %copy-start.37 = (bf16[2,3,256,128]{3,2,1,0:T(8,128)(2,1)}, bf16[2,3,256,128]{3,2,1,0:T(8,128)(2,1)S(1)}, u32[]{:S(2)}) copy-start(bf16[2,3,256,128]{3,2,1,0:T(8,128)(2,1)S(1)} %collective-permute-done.5.refs_1_) | copy-start | bytes 1179652
  98.1 28.4 %copy-start.23 = (bf16[2,256,128]{2,1,0:T(8,128)(2,1)S(1)}, bf16[2,256,128]{2,1,0:T(8,128)(2,1)}, u32[]{:S(2)}) copy-start(bf16[2,256,128]{2,1,0:T(8,128)(2,1)} %get-tuple-element.221.refs_0_) | copy-start | bytes 393220
  98.2 28.3 %collective-permute-start.8 = (bf16[2,256,128]{2,1,0:T(8,128)(2,1)}, bf16[2,256,128]{2,1,0:T(8,128)(2,1)S(1)}, u32[]{:S(2)}, u32[]{:S(2)}) collective-permute-start(bf16[2,256,128]{2,1,0:T(8,128)(2,1)} %get-tuple-element.218), channel_id=1, source_target_pairs={{0,8},{4,12},{8,0},{12,4},{16,24},{20,28},{24,16},{28,20},{1,9},{5... | collective-permute-start | bytes 393224 | tf_op jit(solution)/shard_map/ppermute | solution.py:954
  108.9 17.5 %collective-permute-start.9 = (bf16[2,256,128]{2,1,0:T(8,128)(2,1)}, bf16[2,256,128]{2,1,0:T(8,128)(2,1)S(1)}, u32[]{:S(2)}, u32[]{:S(2)}) collective-permute-start(bf16[2,256,128]{2,1,0:T(8,128)(2,1)} %get-tuple-element.219), channel_id=1, source_target_pairs={{0,16},{4,20},{8,24},{12,28},{16,0},{20,4},{24,8},{28,12},{1,17},{... | collective-permute-start | bytes 393224 | tf_op jit(solution)/shard_map/ppermute | solution.py:954
  110.0 16.5 %collective-permute-start.10 = (bf16[2,256,128]{2,1,0:T(8,128)(2,1)}, bf16[2,256,128]{2,1,0:T(8,128)(2,1)S(1)}, u32[]{:S(2)}, u32[]{:S(2)}) collective-permute-start(bf16[2,256,128]{2,1,0:T(8,128)(2,1)} %get-tuple-element.220), channel_id=1, source_target_pairs={{0,24},{4,28},{8,16},{12,20},{16,8},{20,12},{24,0},{28,4},{1,25},{... | collective-permute-start | bytes 393224 | tf_op jit(solution)/shard_map/ppermute | solution.py:954
  126.6 4.5 %collective-permute-start.11 = (bf16[4,256,128]{2,1,0:T(8,128)(2,1)S(1)}, bf16[4,256,128]{2,1,0:T(8,128)(2,1)S(1)}, u32[]{:S(2)}, u32[]{:S(2)}) collective-permute-start(bf16[4,256,128]{2,1,0:T(8,128)(2,1)S(1)} %pad_maximum_fusion.5), channel_id=1, source_target_pairs={{0,4},{4,0},{8,12},{12,8},{16,20},{20,16},{24,28},{28,24},{1,5},{5... | collective-permute-start | bytes 786440 | tf_op jit(solution)/shard_map/ppermute | solution.py:954
  126.7 24.2 %collective-permute-start.12 = (bf16[2,256,128]{2,1,0:T(8,128)(2,1)}, bf16[2,256,128]{2,1,0:T(8,128)(2,1)S(1)}, u32[]{:S(2)}, u32[]{:S(2)}) collective-permute-start(bf16[2,256,128]{2,1,0:T(8,128)(2,1)} %get-tuple-element.229), channel_id=1, source_target_pairs={{0,8},{4,12},{8,0},{12,4},{16,24},{20,28},{24,16},{28,20},{1,9},{5... | collective-permute-start | bytes 393224 | tf_op jit(solution)/shard_map/ppermute | solution.py:954
  127.8 23.1 %collective-permute-start.13 = (bf16[2,256,128]{2,1,0:T(8,128)(2,1)}, bf16[2,256,128]{2,1,0:T(8,128)(2,1)S(1)}, u32[]{:S(2)}, u32[]{:S(2)}) collective-permute-start(bf16[2,256,128]{2,1,0:T(8,128)(2,1)} %get-tuple-element.230), channel_id=1, source_target_pairs={{0,16},{4,20},{8,24},{12,28},{16,0},{20,4},{24,8},{28,12},{1,17},{... | collective-permute-start | bytes 393224 | tf_op jit(solution)/shard_map/ppermute | solution.py:954
  129.8 21.2 %collective-permute-start.14 = (bf16[2,256,128]{2,1,0:T(8,128)(2,1)}, bf16[2,256,128]{2,1,0:T(8,128)(2,1)S(1)}, u32[]{:S(2)}, u32[]{:S(2)}) collective-permute-start(bf16[2,256,128]{2,1,0:T(8,128)(2,1)} %get-tuple-element.231), channel_id=1, source_target_pairs={{0,24},{4,28},{8,16},{12,20},{16,8},{20,12},{24,0},{28,4},{1,25},{... | collective-permute-start | bytes 393224 | tf_op jit(solution)/shard_map/ppermute | solution.py:954
  151.0 2.4 collective-permute-start.15
  151.2 2.2 collective-permute-start.16
  157.7 23.9 %collective-permute-start.20 = (bf16[256,7680]{1,0:T(8,128)(2,1)}, bf16[256,7680]{1,0:T(8,128)(2,1)}, u32[]{:S(2)}, u32[]{:S(2)}) collective-permute-start(bf16[256,7680]{1,0:T(8,128)(2,1)} %get-tuple-element.264.refs_12_.refs_20_), channel_id=1, source_target_pairs={{0,4},{4,0},{8,12},{12,8},{16,20},{20,16},{24,28},{28,24},{1,5},{5... | collective-permute-start | bytes 11796488 | tf_op jit(solution)/shard_map/ppermute | solution.py:954
  157.9 23.6 %collective-permute-start.17 = (bf16[2,256,128]{2,1,0:T(8,128)(2,1)}, bf16[2,256,128]{2,1,0:T(8,128)(2,1)S(1)}, u32[]{:S(2)}, u32[]{:S(2)}) collective-permute-start(bf16[2,256,128]{2,1,0:T(8,128)(2,1)} %get-tuple-element.247), channel_id=1, source_target_pairs={{0,8},{4,12},{8,0},{12,4},{16,24},{20,28},{24,16},{28,20},{1,9},{5... | collective-permute-start | bytes 393224 | tf_op jit(solution)/shard_map/ppermute | solution.py:954
  158.0 23.5 %collective-permute-start.18 = (bf16[2,256,128]{2,1,0:T(8,128)(2,1)}, bf16[2,256,128]{2,1,0:T(8,128)(2,1)S(1)}, u32[]{:S(2)}, u32[]{:S(2)}) collective-permute-start(bf16[2,256,128]{2,1,0:T(8,128)(2,1)} %get-tuple-element.248), channel_id=1, source_target_pairs={{0,16},{4,20},{8,24},{12,28},{16,0},{20,4},{24,8},{28,12},{1,17},{... | collective-permute-start | bytes 393224 | tf_op jit(solution)/shard_map/ppermute | solution.py:954
  160.9 20.7 %collective-permute-start.19 = (bf16[2,256,128]{2,1,0:T(8,128)(2,1)}, bf16[2,256,128]{2,1,0:T(8,128)(2,1)S(1)}, u32[]{:S(2)}, u32[]{:S(2)}) collective-permute-start(bf16[2,256,128]{2,1,0:T(8,128)(2,1)} %get-tuple-element.249), channel_id=1, source_target_pairs={{0,24},{4,28},{8,16},{12,20},{16,8},{20,12},{24,0},{28,4},{1,25},{... | collective-permute-start | bytes 393224 | tf_op jit(solution)/shard_map/ppermute | solution.py:954
  181.5 25.5 %copy-start.43 = (bf16[2,256,128]{2,1,0:T(8,128)(2,1)}, bf16[2,256,128]{2,1,0:T(8,128)(2,1)S(1)}, u32[]{:S(2)}) copy-start(bf16[2,256,128]{2,1,0:T(8,128)(2,1)S(1)} %collective-permute-done.17.refs_5_) | copy-start | bytes 393220
  181.6 25.5 %copy-start.44 = (bf16[2,256,128]{2,1,0:T(8,128)(2,1)}, bf16[2,256,128]{2,1,0:T(8,128)(2,1)S(1)}, u32[]{:S(2)}) copy-start(bf16[2,256,128]{2,1,0:T(8,128)(2,1)S(1)} %collective-permute-done.18.refs_6_) | copy-start | bytes 393220
  181.6 2.2 collective-permute-start.21
  183.8 7.1 %collective-permute-start.22 = (bf16[256,7680]{1,0:T(8,128)(2,1)}, bf16[256,7680]{1,0:T(8,128)(2,1)}, u32[]{:S(2)}, u32[]{:S(2)}) collective-permute-start(bf16[256,7680]{1,0:T(8,128)(2,1)} %get-tuple-element.263.refs_14_.refs_22_), channel_id=1, source_target_pairs={{0,4},{4,0},{8,12},{12,8},{16,20},{20,16},{24,28},{28,24},{1,5},{5... | collective-permute-start | bytes 11796488 | tf_op jit(solution)/shard_map/ppermute | solution.py:954
  208.4 33.1 %collective-permute-start.23 = (bf16[2,256,128]{2,1,0:T(8,128)(2,1)S(1)}, bf16[2,256,128]{2,1,0:T(8,128)(2,1)S(1)}, u32[]{:S(2)}, u32[]{:S(2)}) collective-permute-start(bf16[2,256,128]{2,1,0:T(8,128)(2,1)S(1)} %copy-done.48), channel_id=1, source_target_pairs={{0,8},{4,12},{8,0},{12,4},{16,24},{20,28},{24,16},{28,20},{1,9},{5... | collective-permute-start | bytes 393224 | tf_op jit(solution)/shard_map/ppermute | solution.py:954
  208.5 33.1 %collective-permute-start.24 = (bf16[2,256,128]{2,1,0:T(8,128)(2,1)S(1)}, bf16[2,256,128]{2,1,0:T(8,128)(2,1)S(1)}, u32[]{:S(2)}, u32[]{:S(2)}) collective-permute-start(bf16[2,256,128]{2,1,0:T(8,128)(2,1)S(1)} %copy-done.47), channel_id=1, source_target_pairs={{0,16},{4,20},{8,24},{12,28},{16,0},{20,4},{24,8},{28,12},{1,17},{... | collective-permute-start | bytes 393224 | tf_op jit(solution)/shard_map/ppermute | solution.py:954
  211.5 30.1 %collective-permute-start.25 = (bf16[2,256,128]{2,1,0:T(8,128)(2,1)S(1)}, bf16[2,256,128]{2,1,0:T(8,128)(2,1)S(1)}, u32[]{:S(2)}, u32[]{:S(2)}) collective-permute-start(bf16[2,256,128]{2,1,0:T(8,128)(2,1)S(1)} %copy-done.46), channel_id=1, source_target_pairs={{0,24},{4,28},{8,16},{12,20},{16,8},{20,12},{24,0},{28,4},{1,25},{... | collective-permute-start | bytes 393224 | tf_op jit(solution)/shard_map/ppermute | solution.py:954
  212.8 33.2 %copy-start.30 = (f32[8,1024]{1,0:T(8,128)S(1)}, f32[8,1024]{1,0:T(8,128)}, u32[]{:S(2)}) copy-start(f32[8,1024]{1,0:T(8,128)} %get-tuple-element.333) | copy-start | bytes 98308
  241.6 29.4 %collective-permute-start.26 = (bf16[2,3,256,128]{3,2,1,0:T(8,128)(2,1)}, bf16[2,3,256,128]{3,2,1,0:T(8,128)(2,1)S(1)}, u32[]{:S(2)}, u32[]{:S(2)}) collective-permute-start(bf16[2,3,256,128]{3,2,1,0:T(8,128)(2,1)} %get-tuple-element.295), channel_id=1, source_target_pairs={{0,8},{4,12},{8,0},{12,4},{16,24},{20,28},{24,16},{28,20},{1,9},{5... | collective-permute-start | bytes 1179656 | tf_op jit(solution)/shard_map/ppermute | solution.py:954
  241.7 30.4 %collective-permute-start.27 = (bf16[2,3,256,128]{3,2,1,0:T(8,128)(2,1)}, bf16[2,3,256,128]{3,2,1,0:T(8,128)(2,1)S(1)}, u32[]{:S(2)}, u32[]{:S(2)}) collective-permute-start(bf16[2,3,256,128]{3,2,1,0:T(8,128)(2,1)} %get-tuple-element.296), channel_id=1, source_target_pairs={{0,16},{4,20},{8,24},{12,28},{16,0},{20,4},{24,8},{28,12},{1,17},{... | collective-permute-start | bytes 1179656 | tf_op jit(solution)/shard_map/ppermute | solution.py:954
  245.0 27.1 %collective-permute-start.28 = (bf16[2,3,256,128]{3,2,1,0:T(8,128)(2,1)}, bf16[2,3,256,128]{3,2,1,0:T(8,128)(2,1)S(1)}, u32[]{:S(2)}, u32[]{:S(2)}) collective-permute-start(bf16[2,3,256,128]{3,2,1,0:T(8,128)(2,1)} %get-tuple-element.297), channel_id=1, source_target_pairs={{0,24},{4,28},{8,16},{12,20},{16,8},{20,12},{24,0},{28,4},{1,25},{... | collective-permute-start | bytes 1179656 | tf_op jit(solution)/shard_map/ppermute | solution.py:954
  271.0 32.0 %copy-start.13 = (bf16[2,3,256,128]{3,2,1,0:T(8,128)(2,1)}, bf16[2,3,256,128]{3,2,1,0:T(8,128)(2,1)S(1)}, u32[]{:S(2)}) copy-start(bf16[2,3,256,128]{3,2,1,0:T(8,128)(2,1)S(1)} %collective-permute-done.26.refs_5_) | copy-start | bytes 1179652
  272.1 30.9 %copy-start.14 = (bf16[2,3,256,128]{3,2,1,0:T(8,128)(2,1)}, bf16[2,3,256,128]{3,2,1,0:T(8,128)(2,1)S(1)}, u32[]{:S(2)}) copy-start(bf16[2,3,256,128]{3,2,1,0:T(8,128)(2,1)S(1)} %collective-permute-done.27.refs_6_) | copy-start | bytes 1179652
  272.1 29.8 %copy-start.15 = (bf16[2,3,256,128]{3,2,1,0:T(8,128)(2,1)}, bf16[2,3,256,128]{3,2,1,0:T(8,128)(2,1)S(1)}, u32[]{:S(2)}) copy-start(bf16[2,3,256,128]{3,2,1,0:T(8,128)(2,1)S(1)} %collective-permute-done.28.refs_7_) | copy-start | bytes 1179652
  272.1 39.1 %collective-permute-start.29 = (bf16[2,3,256,128]{3,2,1,0:T(8,128)(2,1)}, bf16[2,3,256,128]{3,2,1,0:T(8,128)(2,1)}, u32[]{:S(2)}, u32[]{:S(2)}) collective-permute-start(bf16[2,3,256,128]{3,2,1,0:T(8,128)(2,1)} %get-tuple-element.306), channel_id=1, source_target_pairs={{0,8},{4,12},{8,0},{12,4},{16,24},{20,28},{24,16},{28,20},{1,9},{5... | collective-permute-start | bytes 1179656 | tf_op jit(solution)/shard_map/ppermute | solution.py:954
  279.2 31.9 %collective-permute-start.30 = (bf16[2,3,256,128]{3,2,1,0:T(8,128)(2,1)}, bf16[2,3,256,128]{3,2,1,0:T(8,128)(2,1)}, u32[]{:S(2)}, u32[]{:S(2)}) collective-permute-start(bf16[2,3,256,128]{3,2,1,0:T(8,128)(2,1)} %get-tuple-element.307), channel_id=1, source_target_pairs={{0,16},{4,20},{8,24},{12,28},{16,0},{20,4},{24,8},{28,12},{1,17},{... | collective-permute-start | bytes 1179656 | tf_op jit(solution)/shard_map/ppermute | solution.py:954
  280.2 31.0 %collective-permute-start.31 = (bf16[2,3,256,128]{3,2,1,0:T(8,128)(2,1)}, bf16[2,3,256,128]{3,2,1,0:T(8,128)(2,1)}, u32[]{:S(2)}, u32[]{:S(2)}) collective-permute-start(bf16[2,3,256,128]{3,2,1,0:T(8,128)(2,1)} %get-tuple-element.308), channel_id=1, source_target_pairs={{0,24},{4,28},{8,16},{12,20},{16,8},{20,12},{24,0},{28,4},{1,25},{... | collective-permute-start | bytes 1179656 | tf_op jit(solution)/shard_map/ppermute | solution.py:954
  303.0 34.5 %collective-permute-start.36 = (bf16[2,1152,256]{2,1,0:T(8,128)(2,1)}, bf16[2,1152,256]{2,1,0:T(8,128)(2,1)S(1)}, u32[]{:S(2)}, u32[]{:S(2)}) collective-permute-start(bf16[2,1152,256]{2,1,0:T(8,128)(2,1)} %pad_maximum_fusion), channel_id=1, source_target_pairs={{0,8},{4,12},{8,0},{12,4},{16,24},{20,28},{24,16},{28,20},{1,9},{5... | collective-permute-start | bytes 3538952 | tf_op jit(solution)/shard_map/ppermute | solution.py:954
  311.1 20.2 %collective-permute-start.32 = (f32[256,1024]{1,0:T(8,128)}, f32[256,1024]{1,0:T(8,128)}, u32[]{:S(2)}, u32[]{:S(2)}) collective-permute-start(f32[256,1024]{1,0:T(8,128)} %get-tuple-element.310), channel_id=1, source_target_pairs={{0,4},{4,0},{8,12},{12,8},{16,20},{20,16},{24,28},{28,24},{1,5},{5... | collective-permute-start | bytes 3145736 | tf_op jit(solution)/shard_map/ppermute | solution.py:954
  317.7 13.6 %collective-permute-start.33 = (f32[256,1024]{1,0:T(8,128)}, f32[256,1024]{1,0:T(8,128)}, u32[]{:S(2)}, u32[]{:S(2)}) collective-permute-start(f32[256,1024]{1,0:T(8,128)} %get-tuple-element.311), channel_id=1, source_target_pairs={{0,4},{4,0},{8,12},{12,8},{16,20},{20,16},{24,28},{28,24},{1,5},{5... | collective-permute-start | bytes 3145736 | tf_op jit(solution)/shard_map/ppermute | solution.py:954
  329.2 21.6 %collective-permute-start.34 = (bf16[2,2,256,384]{3,2,1,0:T(8,128)(2,1)}, bf16[2,2,256,384]{3,2,1,0:T(8,128)(2,1)S(1)}, u32[]{:S(2)}, u32[]{:S(2)}) collective-permute-start(bf16[2,2,256,384]{3,2,1,0:T(8,128)(2,1)} %get-tuple-element.324), channel_id=1, source_target_pairs={{0,1},{1,0},{2,3},{3,2},{4,5},{5,4},{6,7},{7,6},{8,9},{9,8},{10,11... | collective-permute-start | bytes 2359304 | tf_op jit(solution)/shard_map/ppermute | solution.py:954
  330.6 20.2 %collective-permute-start.35 = (bf16[2,2,256,384]{3,2,1,0:T(8,128)(2,1)}, bf16[2,2,256,384]{3,2,1,0:T(8,128)(2,1)}, u32[]{:S(2)}, u32[]{:S(2)}) collective-permute-start(bf16[2,2,256,384]{3,2,1,0:T(8,128)(2,1)} %get-tuple-element.325), channel_id=1, source_target_pairs={{0,2},{1,3},{2,0},{3,1},{4,6},{5,7},{6,4},{7,5},{8,10},{9,11},{10,... | collective-permute-start | bytes 2359304 | tf_op jit(solution)/shard_map/ppermute | solution.py:954
  337.5 31.7 %copy-start.4 = (bf16[2,1152,256]{2,1,0:T(8,128)(2,1)}, bf16[2,1152,256]{2,1,0:T(8,128)(2,1)S(1)}, u32[]{:S(2)}) copy-start(bf16[2,1152,256]{2,1,0:T(8,128)(2,1)S(1)} %collective-permute-done.36) | copy-start | bytes 3538948
  338.6 1.3 collective-permute-start.39
  339.9 5.4 %collective-permute-start.40 = (bf16[2,24,1024]{2,1,0:T(8,128)(2,1)S(1)}, bf16[2,24,1024]{2,1,0:T(8,128)(2,1)S(1)}, u32[]{:S(2)}, u32[]{:S(2)}) collective-permute-start(bf16[2,24,1024]{2,1,0:T(8,128)(2,1)S(1)} %pad_maximum_fusion.10), channel_id=1, source_target_pairs={{0,8},{4,12},{8,0},{12,4},{16,24},{20,28},{24,16},{28,20},{1,9},{5... | collective-permute-start | bytes 294920 | tf_op jit(solution)/shard_map/ppermute | solution.py:954
  345.3 11.9 %collective-permute-start.41 = (bf16[4,24,1024]{2,1,0:T(8,128)(2,1)S(1)}, bf16[4,24,1024]{2,1,0:T(8,128)(2,1)S(1)}, u32[]{:S(2)}, u32[]{:S(2)}) collective-permute-start(bf16[4,24,1024]{2,1,0:T(8,128)(2,1)S(1)} %pad_maximum_fusion.7), channel_id=1, source_target_pairs={{0,16},{4,20},{8,24},{12,28},{16,0},{20,4},{24,8},{28,12},{1,17},{... | collective-permute-start | bytes 589832 | tf_op jit(solution)/shard_map/ppermute | solution.py:954
  357.3 10.0 %collective-permute-start.42 = (bf16[1,144,1024]{2,1,0:T(8,128)(2,1)S(1)}, bf16[1,144,1024]{2,1,0:T(8,128)(2,1)S(1)}, u32[]{:S(2)}, u32[]{:S(2)}) collective-permute-start(bf16[1,144,1024]{2,1,0:T(8,128)(2,1)S(1)} %maximum_bitcast_fusion.1), channel_id=1, source_target_pairs={{0,1},{1,0},{2,3},{3,2},{4,5},{5,4},{6,7},{7,6},{8,9},{9,8},{10,11... | collective-permute-start | bytes 884744 | tf_op jit(solution)/shard_map/ppermute | solution.py:954
  360.4 13.4 %collective-permute-start.38 = (bf16[1,2,256,384]{3,2,1,0:T(8,128)(2,1)S(1)}, bf16[1,2,256,384]{3,2,1,0:T(8,128)(2,1)S(1)}, u32[]{:S(2)}, u32[]{:S(2)}) collective-permute-start(bf16[1,2,256,384]{3,2,1,0:T(8,128)(2,1)S(1)} %add_convert_fusion.1), channel_id=1, source_target_pairs={{0,1},{1,0},{2,3},{3,2},{4,5},{5,4},{6,7},{7,6},{8,9},{9,8},{10,11... | collective-permute-start | bytes 1179656 | tf_op jit(solution)/shard_map/ppermute | solution.py:954
  361.0 14.0 %collective-permute-start.37 = (bf16[1,2,256,384]{3,2,1,0:T(8,128)(2,1)S(1)}, bf16[1,2,256,384]{3,2,1,0:T(8,128)(2,1)S(1)}, u32[]{:S(2)}, u32[]{:S(2)}) collective-permute-start(bf16[1,2,256,384]{3,2,1,0:T(8,128)(2,1)S(1)} %add_convert_fusion.4), channel_id=1, source_target_pairs={{0,2},{1,3},{2,0},{3,1},{4,6},{5,7},{6,4},{7,5},{8,10},{9,11},{10,... | collective-permute-start | bytes 1179656 | tf_op jit(solution)/shard_map/ppermute | solution.py:954
  367.4 15.9 %collective-permute-start.43 = (bf16[2,144,1024]{2,1,0:T(8,128)(2,1)S(1)}, bf16[2,144,1024]{2,1,0:T(8,128)(2,1)S(1)}, u32[]{:S(2)}, u32[]{:S(2)}) collective-permute-start(bf16[2,144,1024]{2,1,0:T(8,128)(2,1)S(1)} %pad_maximum_fusion.2), channel_id=1, source_target_pairs={{0,2},{1,3},{2,0},{3,1},{4,6},{5,7},{6,4},{7,5},{8,10},{9,11},{10,... | collective-permute-start | bytes 1769480 | tf_op jit(solution)/shard_map/ppermute | solution.py:954
  369.3 24.9 %collective-permute-start.47 = (bf16[1,1152,256]{2,1,0:T(8,128)(2,1)S(1)}, bf16[1,1152,256]{2,1,0:T(8,128)(2,1)S(1)}, u32[]{:S(2)}, u32[]{:S(2)}) collective-permute-start(bf16[1,1152,256]{2,1,0:T(8,128)(2,1)S(1)} %fusion.1), channel_id=1, source_target_pairs={{0,16},{4,20},{8,24},{12,28},{16,0},{20,4},{24,8},{28,12},{1,17},{... | collective-permute-start | bytes 1769480 | tf_op jit(solution)/shard_map/ppermute | solution.py:954
  383.5 19.0 %collective-permute-start.44 = (bf16[2,256,384]{2,1,0:T(8,128)(2,1)S(1)}, bf16[2,256,384]{2,1,0:T(8,128)(2,1)S(1)}, u32[]{:S(2)}, u32[]{:S(2)}) collective-permute-start(bf16[2,256,384]{2,1,0:T(8,128)(2,1)S(1)} %pad_maximum_fusion.4), channel_id=1, source_target_pairs={{0,8},{4,12},{8,0},{12,4},{16,24},{20,28},{24,16},{28,20},{1,9},{5... | collective-permute-start | bytes 1179656 | tf_op jit(solution)/shard_map/ppermute | solution.py:954
  394.5 24.7 %collective-permute-start.50 = (bf16[1152,256]{1,0:T(8,128)(2,1)S(1)}, bf16[1152,256]{1,0:T(8,128)(2,1)}, u32[]{:S(2)}, u32[]{:S(2)}) collective-permute-start(bf16[1152,256]{1,0:T(8,128)(2,1)S(1)} %fusion.refs_0_), channel_id=1, source_target_pairs={{0,3},{1,2},{2,1},{3,0},{4,7},{5,6},{6,5},{7,4},{8,11},{9,10},{10,... | collective-permute-start | bytes 1769480 | tf_op jit(solution)/shard_map/ppermute | solution.py:954
  395.9 27.4 %collective-permute-start.49 = (bf16[1152,256]{1,0:T(8,128)(2,1)S(1)}, bf16[1152,256]{1,0:T(8,128)(2,1)}, u32[]{:S(2)}, u32[]{:S(2)}) collective-permute-start(bf16[1152,256]{1,0:T(8,128)(2,1)S(1)} %fusion.refs_0_), channel_id=1, source_target_pairs={{0,2},{1,3},{2,0},{3,1},{4,6},{5,7},{6,4},{7,5},{8,10},{9,11},{10,... | collective-permute-start | bytes 1769480 | tf_op jit(solution)/shard_map/ppermute | solution.py:954
  397.6 25.7 %collective-permute-start.48 = (bf16[1152,256]{1,0:T(8,128)(2,1)S(1)}, bf16[1152,256]{1,0:T(8,128)(2,1)}, u32[]{:S(2)}, u32[]{:S(2)}) collective-permute-start(bf16[1152,256]{1,0:T(8,128)(2,1)S(1)} %fusion.refs_0_), channel_id=1, source_target_pairs={{0,1},{1,0},{2,3},{3,2},{4,5},{5,4},{6,7},{7,6},{8,9},{9,8},{10,11... | collective-permute-start | bytes 1769480 | tf_op jit(solution)/shard_map/ppermute | solution.py:954
  404.6 13.3 %collective-permute-start.45 = (bf16[1,256,384]{2,1,0:T(8,128)(2,1)}, bf16[1,256,384]{2,1,0:T(8,128)(2,1)}, u32[]{:S(2)}, u32[]{:S(2)}) collective-permute-start(bf16[1,256,384]{2,1,0:T(8,128)(2,1)} %add_convert_fusion.8), channel_id=1, source_target_pairs={{0,16},{4,20},{8,24},{12,28},{16,0},{20,4},{24,8},{28,12},{1,17},{... | collective-permute-start | bytes 589832 | tf_op jit(solution)/shard_map/ppermute | solution.py:954
  419.0 4.4 collective-permute-start.46
  423.4 11.0 %collective-permute-start.53 = (bf16[2,128,384]{2,1,0:T(8,128)(2,1)S(1)}, bf16[2,128,384]{2,1,0:T(8,128)(2,1)S(1)}, u32[]{:S(2)}, u32[]{:S(2)}) collective-permute-start(bf16[2,128,384]{2,1,0:T(8,128)(2,1)S(1)} %pad_maximum_fusion.8.refs_0_), channel_id=1, source_target_pairs={{0,3},{1,2},{2,1},{3,0},{4,7},{5,6},{6,5},{7,4},{8,11},{9,10},{10,... | collective-permute-start | bytes 589832 | tf_op jit(solution)/shard_map/ppermute | solution.py:954
  425.2 10.2 %collective-permute-start.52 = (bf16[2,128,384]{2,1,0:T(8,128)(2,1)S(1)}, bf16[2,128,384]{2,1,0:T(8,128)(2,1)S(1)}, u32[]{:S(2)}, u32[]{:S(2)}) collective-permute-start(bf16[2,128,384]{2,1,0:T(8,128)(2,1)S(1)} %pad_maximum_fusion.8.refs_0_), channel_id=1, source_target_pairs={{0,2},{1,3},{2,0},{3,1},{4,6},{5,7},{6,4},{7,5},{8,10},{9,11},{10,... | collective-permute-start | bytes 589832 | tf_op jit(solution)/shard_map/ppermute | solution.py:954
  425.8 9.6 %collective-permute-start.51 = (bf16[2,128,384]{2,1,0:T(8,128)(2,1)S(1)}, bf16[2,128,384]{2,1,0:T(8,128)(2,1)S(1)}, u32[]{:S(2)}, u32[]{:S(2)}) collective-permute-start(bf16[2,128,384]{2,1,0:T(8,128)(2,1)S(1)} %pad_maximum_fusion.8.refs_0_), channel_id=1, source_target_pairs={{0,1},{1,0},{2,3},{3,2},{4,5},{5,4},{6,7},{7,6},{8,9},{9,8},{10,11... | collective-permute-start | bytes 589832 | tf_op jit(solution)/shard_map/ppermute | solution.py:954
  (44 other events, 316.7 us)
Sparse Core Ops, SparseCore 0:
  207.2 93.2 reduce-scatter.1

commit v7 on v6

--- a/solution.py
+++ b/solution.py
@@ -19,6 +19,7 @@
 BLOCK = 256
 FF_BLOCK = 1024
 IN_FLIGHT = 3
+JOBS_AHEAD = 2
 GROUPS = (8, 4, 2, 1)
 GELU_A = 0.7978845608028654
 GELU_B = 0.044715
@@ -808,7 +809,10 @@
                 )
             )
         at += 2 * count
-    for copy in copies:
+    ends = [0]
+    for job in jobs:
+        ends.append(ends[-1] + 2 * job[0])
+    for copy in copies[: ends[min(JOBS_AHEAD, len(jobs))]]:
         copy.start()
 
     at = number = 0
@@ -818,6 +822,9 @@
         for n in range(2 * count):
             copies[at + n].wait()
         at += 2 * count
+        if job + JOBS_AHEAD < len(jobs):
+            for copy in copies[ends[job + JOBS_AHEAD] : ends[job + JOBS_AHEAD + 1]]:
+                copy.start()
         wide = right.shape[1] // (tiles * lane_parts if not tall else 1)
         part = wide // clip_size
         for repeat in range(tiles):

time: 453 us -> 455 us (level)
  waiting for transfers between devices: 101 us -> 112 us
  starting transfers between devices: 78.4 us -> 72.6 us
    reduce_scatter x1, waiting for transfers between devices: 18.8 us -> 28.1 us  [on_device(): lax.psum_scatter(shares.reshape(-1, shares.shape[-1]), 'clip', scatter_di...]
    ppermute x54, starting transfers between devices: 78.3 us -> 72.5 us  [exchange(): return lax.ppermute(array, axis, [(k, k ^ distance) for k in range(size)])]
where the time goes in v7:
time: 455 us; the launch traced here: 449 us
  Pallas kernels  201 us (44%)
  waiting for transfers between devices  112 us (25%)
  starting transfers between devices  72.6 us (16%)
  other arithmetic  18.2 us (4%)
  local copies, waits for them, and re-layouts  18.2 us (4%)
  between operations  15.4 us (3%)
  matrix products  12.1 us (3%)
    ppermute x54, waiting for transfers between devices, exchange(): return lax.ppermute(array, axis, [(k, k ^ distance) for k in range(size)])  83.5 us
    ppermute x54, starting transfers between devices, exchange(): return lax.ppermute(array, axis, [(k, k ^ distance) for k in range(size)])  72.5 us
    pallas_call x2, Pallas kernels, attend_grad_call(): pl.pallas_call(functools.partial(attend_grad_kernel, slots, head, clip),...  51.9 us
    pallas_call x2, Pallas kernels, forward_back_call(): pl.pallas_call(functools.partial(forward_back_kernel, slots, clip), grid=...  38.2 us
    pallas_call x2, Pallas kernels, attend_call(): pl.pallas_call(functools.partial(attend_kernel, slots, head, clip), out_s...  32.3 us
    reduce_scatter x1, waiting for transfers between devices, on_device(): lax.psum_scatter(shares.reshape(-1, shares.shape[-1]), 'clip', scatter_di...  28.1 us
    pallas_call x2, Pallas kernels, weight_grad_call(): pl.pallas_call(functools.partial(weight_grad_kernel, tuple(jobs), clip_si...  24.8 us
    pallas_call x2, Pallas kernels, qkv_grad_call(): pl.pallas_call(functools.partial(qkv_grad_kernel, zs, head, clip), out_sh...  13.1 us
  transfers between devices with their start and end apart: 55, of which 18 were waited for; matrix products, arithmetic and copies ran while one was open for 10% of the time, Pallas kernels for 38%

profile of v7, /device:TPU:0, one launch (start us, length us, event | category | flops | bytes accessed | tf_op | source)
XLA Modules:
  0.0 448.7 jit_solution(14139482814957153141)
XLA Ops:
  11.0 1.3 broadcast_in_dim.47.bias
  15.5 4.0 modulation.2
  21.3 10.1 %norm_qkv.1 = (bf16[2,3,256,128]{3,2,1,0:T(8,128)(2,1)}, bf16[2,3,256,128]{3,2,1,0:T(8,128)(2,1)}, bf16[2,3,256,128]{3,2,1,0:T(8,128)(2,1)}, bf16[2,3,256,128]{3...) custom-call(s32[4]{0:T(128)} %pad_add_fusion.1.meta, ...), custom_call_target="tpu_custom_call" | custom-call | flops 3221225472 | bytes 11534336 | tf_op jit(solution)/shard_map/norm_qkv/pallas_call | solution.py:227
  31.3 3.1 collective-permute-start.2
  34.4 2.6 collective-permute-start.3
  38.8 6.4 %modulation.3 = (f32[4,2,1024]{2,1,0:T(2,128)}, f32[2,1024]{1,0:T(2,128)}) custom-call(s32[2]{0:T(128)} %copy-done.31, bf16[1024,1024]{1,0:T(8,128)(2,1)} %table.3, bf16[1024,6144]{1,0:T(8,128)(2,1)} %weight.3, bf16[1,6144]{1,0:T(2,128)(2,1)} %broadcast_in_dim.47.bias), custom_call_target="tpu_custom_call" | custom-call | bytes 10485760 | tf_op jit(solution)/shard_map/modulation/pallas_call | solution.py:129
  46.1 3.5 collective-permute-start.6
  49.6 2.7 collective-permute-done.2.refs_1_
  52.3 4.1 collective-permute-start.7
  56.5 8.1 %collective-permute-done.3.refs_2_ = bf16[2,3,256,128]{3,2,1,0:T(8,128)(2,1)} collective-permute-done((bf16[2,3,256,128]{3,2,1,0:T(8,128)(2,1)}, bf16[2,3,256,128]{3,2,1,0:T(8,128)(2,1)}, u32[]{:S(2)}, u32[]{:S(2)}) %collective-permute-start.3) | collective-permute-done | bytes 393248 | tf_op jit(solution)/shard_map/ppermute | solution.py:961
  64.5 14.2 %attend.2 = (bf16[2,256,128]{2,1,0:T(8,128)(2,1)}, bf16[2,256,128]{2,1,0:T(8,128)(2,1)}, bf16[2,256,128]{2,1,0:T(8,128)(2,1)}, bf16[2,256,128]{2,1,0:T(8,128)(2,...) custom-call(s32[4]{0:T(128)} %pad_add_fusion.1.meta, bf16[2,3,256,128]{3,2,1,0:T(8,128)(2,1)} %get-tuple-element.197.refs_0_, ...), custom_call_target="tpu_custom_call" | custom-call | flops 8589934592 | bytes 3145728 | tf_op jit(solution)/shard_map/attend/pallas_call | solution.py:326
  78.7 19.4 %collective-permute-done.6.refs_2_ = bf16[2,3,256,128]{3,2,1,0:T(8,128)(2,1)S(1)} collective-permute-done((bf16[2,3,256,128]{3,2,1,0:T(8,128)(2,1)}, bf16[2,3,256,128]{3,2,1,0:T(8,128)(2,1)S(1)}, u32[]{:S(2)}, u32[]{:S(2)}) %collective-permute-start.6) | collective-permute-done | bytes 393248 | tf_op jit(solution)/shard_map/ppermute | solution.py:961
  98.2 7.8 %collective-permute-start.8 = (bf16[2,256,128]{2,1,0:T(8,128)(2,1)}, bf16[2,256,128]{2,1,0:T(8,128)(2,1)S(1)}, u32[]{:S(2)}, u32[]{:S(2)}) collective-permute-start(bf16[2,256,128]{2,1,0:T(8,128)(2,1)} %get-tuple-element.218), channel_id=1, source_target_pairs={{0,8},{4,12},{8,0},{12,4},{16,24},{20,28},{24,16},{28,20},{1,9},{5... | collective-permute-start | bytes 393224 | tf_op jit(solution)/shard_map/ppermute | solution.py:961
  107.1 1.4 collective-permute-start.10
  108.5 18.1 %attend.3 = (bf16[2,256,128]{2,1,0:T(8,128)(2,1)}, bf16[2,256,128]{2,1,0:T(8,128)(2,1)}, bf16[2,256,128]{2,1,0:T(8,128)(2,1)}, bf16[2,256,128]{2,1,0:T(8,128)(2,...) custom-call(s32[4]{0:T(128)} %pad_add_fusion.1.meta, bf16[2,3,256,128]{3,2,1,0:T(8,128)(2,1)} %get-tuple-element.209.refs_0_, ...), custom_call_target="tpu_custom_call" | custom-call | flops 8589934592 | bytes 3145728 | tf_op jit(solution)/shard_map/attend/pallas_call | solution.py:326
  127.9 2.0 collective-permute-start.13
  129.9 1.4 collective-permute-start.14
  132.0 19.0 %feed_forward.2 = (bf16[256,1024]{1,0:T(8,128)(2,1)}, f32[256,1024]{1,0:T(8,128)}, f32[8,1024]{1,0:T(8,128)}, f32[1,4096]{1,0:T(1,128)}, bf16[256,512]{1,0:T(8,1...) custom-call(s32[4]{0:T(128)} %pad_add_fusion.1.meta, ...), custom_call_target="tpu_custom_call" | custom-call | flops 9663676416 | bytes 37748736 | tf_op jit(solution)/shard_map/feed_forward/pallas_call | solution.py:608
  151.8 1.6 collective-permute-done.16.refs_4_
  154.3 3.5 proj_back.2
  158.1 2.9 collective-permute-start.18
  161.0 1.4 collective-permute-start.19
  162.4 19.2 %feed_forward.3 = (bf16[256,1024]{1,0:T(8,128)(2,1)}, f32[256,1024]{1,0:T(8,128)}, f32[8,1024]{1,0:T(8,128)}, f32[1,4096]{1,0:T(1,128)}, bf16[256,512]{1,0:T(8,1...) custom-call(s32[4]{0:T(128)} %pad_add_fusion.1.meta, ...), custom_call_target="tpu_custom_call" | custom-call | flops 9663676416 | bytes 37748736 | tf_op jit(solution)/shard_map/feed_forward/pallas_call | solution.py:608
  181.8 2.1 collective-permute-done.21.far.refs_7_
  184.7 3.5 proj_back.3
  188.2 2.8 collective-permute-done.22.refs_11_.refs_15_.refs_19_.refs_23_
  191.0 16.1 %weight_grads.1 = bf16[4,4,1152,256]{3,2,1,0:T(8,128)(2,1)} custom-call(s32[4]{0:T(128)} %pad_add_fusion.1.meta, bf16[256,512]{1,0:T(8,128)(2,1)} %get-tuple-element.256.refs_0_, bf16[256,512]{1,0:T(8,128)(2,1)} %get-tuple-element.257.refs_1_, bf16[256,512]{1,0:T(8,128)(2,1)} %get-tuple-element.258.refs_2_, bf16[256,512]{1,0:T(8,128)(2,1)} %get-tuple-element.259.refs_3_, ...), custom_call_target="tpu_custom_call" | custom-call | flops 9663676416 | bytes 18874368 | tf_op jit(solution)/shard_map/weight_grads/pallas_call | solution.py:889
  208.6 3.0 collective-permute-start.24
  211.6 1.4 collective-permute-start.25
  213.0 22.8 %attend_grad.2 = (bf16[2,3,256,128]{3,2,1,0:T(8,128)(2,1)}, bf16[2,3,256,128]{3,2,1,0:T(8,128)(2,1)}, bf16[2,3,256,128]{3,2,1,0:T(8,128)(2,1)}, bf16[2,3,256,128]{3,2,1,0:T(8,128)(2,1)}) custom-call(s32[4]{0:T(128)} %pad_add_fusion.1.meta, bf16[2,3,256,128]{3,2,1,0:T(8,128)(2,1)} %get-tuple-element.197.refs_0_, bf16[2,3,256,128]{3,2,1,0:T(8,128)(2,1)} %copy-done.40, ...), custom_call_target="tpu_custom_call" | custom-call | flops 2147483648 | bytes 524288 | tf_op jit(solution)/shard_map/attend_grad/pallas_call | solution.py:437
  235.9 2.5 collective-permute-start.27
  238.4 1.9 collective-permute-start.28
  241.2 29.1 %attend_grad.3 = (bf16[2,3,256,128]{3,2,1,0:T(8,128)(2,1)}, bf16[2,3,256,128]{3,2,1,0:T(8,128)(2,1)}, bf16[2,3,256,128]{3,2,1,0:T(8,128)(2,1)}, bf16[2,3,256,128]{3,2,1,0:T(8,128)(2,1)}) custom-call(s32[4]{0:T(128)} %pad_add_fusion.1.meta, bf16[2,3,256,128]{3,2,1,0:T(8,128)(2,1)} %get-tuple-element.209.refs_0_, bf16[2,3,256,128]{3,2,1,0:T(8,128)(2,1)} %copy-done.37, ...), custom_call_target="tpu_custom_call" | custom-call | flops 2147483648 | bytes 524288 | tf_op jit(solution)/shard_map/attend_grad/pallas_call | solution.py:437
  270.4 2.4 collective-permute-start.29
  273.7 1.5 collective-permute-start.31
  275.2 28.1 %reduce-scatter.2.cloned.1.call-done = bf16[4608,256]{1,0:T(8,128)(2,1)} async-done(((bf16[18432,256]{1,0:T(8,128)(2,1)}), bf16[4608,256]{1,0:T(8,128)(2,1)}) %reduce-scatter.2.cloned.1.call-update) | async-done | bytes 2359312 | tf_op jit(solution)/shard_map/reduce_scatter | solution.py:1165
  305.8 1.5 collective-permute-start.36
  307.3 6.5 %qkv_grad.2 = (bf16[256,1536]{1,0:T(8,128)(2,1)}, bf16[256,1536]{1,0:T(8,128)(2,1)}, f32[256,1024]{1,0:T(8,128)}, f32[256,1024]{1,0:T(8,128)}, f32[8,512]{1,0:T(8,128)}) custom-call(s32[4]{0:T(128)} %pad_add_fusion.1.meta, f32[4,128]{1,0:T(4,128)} %get-tuple-element.430.refs_0_, f32[4,128]{1,0:T(4,128)} %get-tuple-element.429.refs_1_, ...), custom_call_target="tpu_custom_call" | custom-call | flops 161061280 | bytes 1048576 | tf_op jit(solution)/shard_map/qkv_grad/pallas_call | solution.py:710
  314.0 6.6 %qkv_grad.3 = (bf16[256,1536]{1,0:T(8,128)(2,1)}, bf16[256,1536]{1,0:T(8,128)(2,1)}, f32[256,1024]{1,0:T(8,128)}, f32[256,1024]{1,0:T(8,128)}, f32[8,512]{1,0:T(8,128)}) custom-call(s32[4]{0:T(128)} %pad_add_fusion.1.meta, f32[4,128]{1,0:T(4,128)} %get-tuple-element.430.refs_0_, f32[4,128]{1,0:T(4,128)} %get-tuple-element.429.refs_1_, ...), custom_call_target="tpu_custom_call" | custom-call | flops 161061280 | bytes 1048576 | tf_op jit(solution)/shard_map/qkv_grad/pallas_call | solution.py:710
  323.3 8.8 %qkv_weight_grad.1 = (bf16[2,2,256,384]{3,2,1,0:T(8,128)(2,1)}, bf16[2,2,256,384]{3,2,1,0:T(8,128)(2,1)}, bf16[2,2,256,384]{3,2,1,0:T(8,128)(2,1)}, bf16[2,2,256,384]{3,2,1,0:T(8,128)(2,1)}) custom-call(s32[4]{0:T(128)} %pad_add_fusion.1.meta, bf16[256,1024]{1,0:T(8,128)(2,1)} %get-tuple-element.315.refs_0_, bf16[256,1024]{1,0:T(8,128)(2,1)} %get-tuple-element.316.refs_1_, ...), custom_call_target="tpu_custom_call" | custom-call | flops 3221225472 | bytes 6291456 | tf_op jit(solution)/shard_map/qkv_weight_grad/pallas_call | solution.py:889
  332.0 1.4 collective-permute-start.34
  334.2 6.2 %norm_grad.1 = (f32[2,1,256,1024]{3,2,1,0:T(8,128)}, f32[2,8,1024]{2,1,0:T(8,128)}) custom-call(bf16[2,1,256,1024]{3,2,1,0:T(8,128)(2,1)} %tokens.7, f32[2,4,1024]{2,1,0:T(4,128)} %get-tuple-element.187.mod, f32[256,1024]{1,0:T(8,128)} %get-tuple-element.304.refs_0_, f32[256,1024]{1,0:T(8,128)} %get-tuple-element.309.refs_1_, ...), custom_call_target="tpu_custom_call" | custom-call | flops 1572864 | bytes 1048576 | tf_op jit(solution)/shard_map/norm_grad/pallas_call | solution.py:744
  342.7 3.3 collective-permute-start.40
  346.0 3.2 collective-permute-done.40
  349.2 3.0 collective-permute-start.41
  352.7 2.3 maximum_bitcast_fusion
  354.9 6.1 %collective-permute-done.41 = bf16[4,24,1024]{2,1,0:T(8,128)(2,1)S(1)} collective-permute-done((bf16[4,24,1024]{2,1,0:T(8,128)(2,1)S(1)}, bf16[4,24,1024]{2,1,0:T(8,128)(2,1)S(1)}, u32[]{:S(2)}, u32[]{:S(2)}) %collective-permute-start.41) | collective-permute-done | bytes 196640 | tf_op jit(solution)/shard_map/ppermute | solution.py:961
  361.7 1.4 add_convert_fusion.1
  363.1 1.6 collective-permute-start.38
  364.8 1.9 collective-permute-start.37
  366.8 4.4 collective-permute-done.42
  371.3 1.9 collective-permute-start.43
  373.5 4.3 collective-permute-done.38
  379.1 8.2 %collective-permute-done.43 = bf16[2,144,1024]{2,1,0:T(8,128)(2,1)S(1)} collective-permute-done((bf16[2,144,1024]{2,1,0:T(8,128)(2,1)S(1)}, bf16[2,144,1024]{2,1,0:T(8,128)(2,1)S(1)}, u32[]{:S(2)}, u32[]{:S(2)}) %collective-permute-start.43) | collective-permute-done | bytes 589856 | tf_op jit(solution)/shard_map/ppermute | solution.py:961
  387.6 10.7 %collective-permute-done.47 = bf16[1,1152,256]{2,1,0:T(8,128)(2,1)S(1)} collective-permute-done((bf16[1,1152,256]{2,1,0:T(8,128)(2,1)S(1)}, bf16[1,1152,256]{2,1,0:T(8,128)(2,1)S(1)}, u32[]{:S(2)}, u32[]{:S(2)}) %collective-permute-start.47) | collective-permute-done | bytes 589856 | tf_op jit(solution)/shard_map/ppermute | solution.py:961
  398.7 1.7 collective-permute-start.49
  400.5 1.7 collective-permute-start.48
  402.1 4.5 %collective-permute-done.44 = bf16[2,256,384]{2,1,0:T(8,128)(2,1)S(1)} collective-permute-done((bf16[2,256,384]{2,1,0:T(8,128)(2,1)S(1)}, bf16[2,256,384]{2,1,0:T(8,128)(2,1)S(1)}, u32[]{:S(2)}, u32[]{:S(2)}) %collective-permute-start.44) | collective-permute-done | bytes 393248 | tf_op jit(solution)/shard_map/ppermute | solution.py:961
  409.8 8.5 %fusion.36 = f32[64,1024]{1,0:T(8,128)S(1)} fusion(bf16[64,6144]{1,0:T(8,128)(2,1)S(1)} %reshape.274, bf16[1024,6144]{1,0:T(8,128)(2,1)} %weight.3), kind=kOutput, calls=%fused_computation.107 | convolution fusion | flops 805306368 | bytes 13631488 | tf_op jit(solution)/shard_map/dot_general | solution.py:1266
  418.4 2.3 fusion.15
  423.3 3.4 collective-permute-done.49.refs_2_
  428.0 1.4 collective-permute-start.52
  433.6 4.1 place_grads.1
  439.1 2.6 place_qkv_grad.1
  (267 shorter events, 45.1 us)
Async XLA Ops:
  7.2 296.1 %reduce-scatter.2.cloned.1.call-start = ((), (), s32[]{:S(2)}) async-start(), calls=%async_computation.1 | async-start | bytes 11796480 | tf_op jit(solution)/shard_map/reduce_scatter | solution.py:1165
  7.9 5.7 %collective-permute-start.1 = (s32[2,2]{1,0:T(2,128)S(1)}, s32[2,2]{1,0:T(2,128)S(1)}, u32[]{:S(2)}, u32[]{:S(2)}) collective-permute-start(s32[2,2]{1,0:T(2,128)S(1)} %pad_add_fusion), channel_id=1, source_target_pairs={{0,4},{4,0},{8,12},{12,8},{16,20},{20,16},{24,28},{28,24},{1,5},{5... | collective-permute-start | bytes 56 | tf_op jit(solution)/shard_map/ppermute | solution.py:961
  8.4 11.9 %collective-permute-start = (bf16[2,1,256,1024]{3,2,1,0:T(8,128)(2,1)}, bf16[2,1,256,1024]{3,2,1,0:T(8,128)(2,1)S(1)}, u32[]{:S(2)}, u32[]{:S(2)}) collective-permute-start(bf16[2,1,256,1024]{3,2,1,0:T(8,128)(2,1)} %tokens.7), channel_id=1, source_target_pairs={{0,4},{4,0},{8,12},{12,8},{16,20},{20,16},{24,28},{28,24},{1,5},{5... | collective-permute-start | bytes 3145736 | tf_op jit(solution)/shard_map/ppermute | solution.py:961
  31.3 21.0 %collective-permute-start.2 = (bf16[2,3,256,128]{3,2,1,0:T(8,128)(2,1)}, bf16[2,3,256,128]{3,2,1,0:T(8,128)(2,1)S(1)}, u32[]{:S(2)}, u32[]{:S(2)}) collective-permute-start(bf16[2,3,256,128]{3,2,1,0:T(8,128)(2,1)} %get-tuple-element.189), channel_id=1, source_target_pairs={{0,8},{4,12},{8,0},{12,4},{16,24},{20,28},{24,16},{28,20},{1,9},{5... | collective-permute-start | bytes 1179656 | tf_op jit(solution)/shard_map/ppermute | solution.py:961
  34.4 30.1 %collective-permute-start.3 = (bf16[2,3,256,128]{3,2,1,0:T(8,128)(2,1)}, bf16[2,3,256,128]{3,2,1,0:T(8,128)(2,1)}, u32[]{:S(2)}, u32[]{:S(2)}) collective-permute-start(bf16[2,3,256,128]{3,2,1,0:T(8,128)(2,1)} %get-tuple-element.190), channel_id=1, source_target_pairs={{0,16},{4,20},{8,24},{12,28},{16,0},{20,4},{24,8},{28,12},{1,17},{... | collective-permute-start | bytes 1179656 | tf_op jit(solution)/shard_map/ppermute | solution.py:961
  37.0 27.5 %collective-permute-start.4 = (bf16[2,3,256,128]{3,2,1,0:T(8,128)(2,1)}, bf16[2,3,256,128]{3,2,1,0:T(8,128)(2,1)}, u32[]{:S(2)}, u32[]{:S(2)}) collective-permute-start(bf16[2,3,256,128]{3,2,1,0:T(8,128)(2,1)} %get-tuple-element.191), channel_id=1, source_target_pairs={{0,24},{4,28},{8,16},{12,20},{16,8},{20,12},{24,0},{28,4},{1,25},{... | collective-permute-start | bytes 1179656 | tf_op jit(solution)/shard_map/ppermute | solution.py:961
  45.3 33.5 %collective-permute-start.5 = (bf16[2,3,256,128]{3,2,1,0:T(8,128)(2,1)}, bf16[2,3,256,128]{3,2,1,0:T(8,128)(2,1)S(1)}, u32[]{:S(2)}, u32[]{:S(2)}) collective-permute-start(bf16[2,3,256,128]{3,2,1,0:T(8,128)(2,1)} %get-tuple-element.206), channel_id=1, source_target_pairs={{0,8},{4,12},{8,0},{12,4},{16,24},{20,28},{24,16},{28,20},{1,9},{5... | collective-permute-start | bytes 1179656 | tf_op jit(solution)/shard_map/ppermute | solution.py:961
  46.1 52.0 %collective-permute-start.6 = (bf16[2,3,256,128]{3,2,1,0:T(8,128)(2,1)}, bf16[2,3,256,128]{3,2,1,0:T(8,128)(2,1)S(1)}, u32[]{:S(2)}, u32[]{:S(2)}) collective-permute-start(bf16[2,3,256,128]{3,2,1,0:T(8,128)(2,1)} %get-tuple-element.207), channel_id=1, source_target_pairs={{0,16},{4,20},{8,24},{12,28},{16,0},{20,4},{24,8},{28,12},{1,17},{... | collective-permute-start | bytes 1179656 | tf_op jit(solution)/shard_map/ppermute | solution.py:961
  52.3 45.8 %collective-permute-start.7 = (bf16[2,3,256,128]{3,2,1,0:T(8,128)(2,1)}, bf16[2,3,256,128]{3,2,1,0:T(8,128)(2,1)S(1)}, u32[]{:S(2)}, u32[]{:S(2)}) collective-permute-start(bf16[2,3,256,128]{3,2,1,0:T(8,128)(2,1)} %get-tuple-element.208), channel_id=1, source_target_pairs={{0,24},{4,28},{8,16},{12,20},{16,8},{20,12},{24,0},{28,4},{1,25},{... | collective-permute-start | bytes 1179656 | tf_op jit(solution)/shard_map/ppermute | solution.py:961
  78.7 29.7 %copy-start.37 = (bf16[2,3,256,128]{3,2,1,0:T(8,128)(2,1)}, bf16[2,3,256,128]{3,2,1,0:T(8,128)(2,1)S(1)}, u32[]{:S(2)}) copy-start(bf16[2,3,256,128]{3,2,1,0:T(8,128)(2,1)S(1)} %collective-permute-done.5.refs_1_) | copy-start | bytes 1179652
  98.1 28.5 %copy-start.23 = (bf16[2,256,128]{2,1,0:T(8,128)(2,1)S(1)}, bf16[2,256,128]{2,1,0:T(8,128)(2,1)}, u32[]{:S(2)}) copy-start(bf16[2,256,128]{2,1,0:T(8,128)(2,1)} %get-tuple-element.221.refs_0_) | copy-start | bytes 393220
  98.2 28.4 %collective-permute-start.8 = (bf16[2,256,128]{2,1,0:T(8,128)(2,1)}, bf16[2,256,128]{2,1,0:T(8,128)(2,1)S(1)}, u32[]{:S(2)}, u32[]{:S(2)}) collective-permute-start(bf16[2,256,128]{2,1,0:T(8,128)(2,1)} %get-tuple-element.218), channel_id=1, source_target_pairs={{0,8},{4,12},{8,0},{12,4},{16,24},{20,28},{24,16},{28,20},{1,9},{5... | collective-permute-start | bytes 393224 | tf_op jit(solution)/shard_map/ppermute | solution.py:961
  106.0 20.6 %collective-permute-start.9 = (bf16[2,256,128]{2,1,0:T(8,128)(2,1)}, bf16[2,256,128]{2,1,0:T(8,128)(2,1)S(1)}, u32[]{:S(2)}, u32[]{:S(2)}) collective-permute-start(bf16[2,256,128]{2,1,0:T(8,128)(2,1)} %get-tuple-element.219), channel_id=1, source_target_pairs={{0,16},{4,20},{8,24},{12,28},{16,0},{20,4},{24,8},{28,12},{1,17},{... | collective-permute-start | bytes 393224 | tf_op jit(solution)/shard_map/ppermute | solution.py:961
  107.1 19.6 %collective-permute-start.10 = (bf16[2,256,128]{2,1,0:T(8,128)(2,1)}, bf16[2,256,128]{2,1,0:T(8,128)(2,1)S(1)}, u32[]{:S(2)}, u32[]{:S(2)}) collective-permute-start(bf16[2,256,128]{2,1,0:T(8,128)(2,1)} %get-tuple-element.220), channel_id=1, source_target_pairs={{0,24},{4,28},{8,16},{12,20},{16,8},{20,12},{24,0},{28,4},{1,25},{... | collective-permute-start | bytes 393224 | tf_op jit(solution)/shard_map/ppermute | solution.py:961
  126.8 4.5 %collective-permute-start.11 = (bf16[4,256,128]{2,1,0:T(8,128)(2,1)S(1)}, bf16[4,256,128]{2,1,0:T(8,128)(2,1)S(1)}, u32[]{:S(2)}, u32[]{:S(2)}) collective-permute-start(bf16[4,256,128]{2,1,0:T(8,128)(2,1)S(1)} %pad_maximum_fusion.5), channel_id=1, source_target_pairs={{0,4},{4,0},{8,12},{12,8},{16,20},{20,16},{24,28},{28,24},{1,5},{5... | collective-permute-start | bytes 786440 | tf_op jit(solution)/shard_map/ppermute | solution.py:961
  126.8 24.2 %collective-permute-start.12 = (bf16[2,256,128]{2,1,0:T(8,128)(2,1)}, bf16[2,256,128]{2,1,0:T(8,128)(2,1)S(1)}, u32[]{:S(2)}, u32[]{:S(2)}) collective-permute-start(bf16[2,256,128]{2,1,0:T(8,128)(2,1)} %get-tuple-element.229), channel_id=1, source_target_pairs={{0,8},{4,12},{8,0},{12,4},{16,24},{20,28},{24,16},{28,20},{1,9},{5... | collective-permute-start | bytes 393224 | tf_op jit(solution)/shard_map/ppermute | solution.py:961
  127.9 23.2 %collective-permute-start.13 = (bf16[2,256,128]{2,1,0:T(8,128)(2,1)}, bf16[2,256,128]{2,1,0:T(8,128)(2,1)S(1)}, u32[]{:S(2)}, u32[]{:S(2)}) collective-permute-start(bf16[2,256,128]{2,1,0:T(8,128)(2,1)} %get-tuple-element.230), channel_id=1, source_target_pairs={{0,16},{4,20},{8,24},{12,28},{16,0},{20,4},{24,8},{28,12},{1,17},{... | collective-permute-start | bytes 393224 | tf_op jit(solution)/shard_map/ppermute | solution.py:961
  129.9 21.2 %collective-permute-start.14 = (bf16[2,256,128]{2,1,0:T(8,128)(2,1)}, bf16[2,256,128]{2,1,0:T(8,128)(2,1)S(1)}, u32[]{:S(2)}, u32[]{:S(2)}) collective-permute-start(bf16[2,256,128]{2,1,0:T(8,128)(2,1)} %get-tuple-element.231), channel_id=1, source_target_pairs={{0,24},{4,28},{8,16},{12,20},{16,8},{20,12},{24,0},{28,4},{1,25},{... | collective-permute-start | bytes 393224 | tf_op jit(solution)/shard_map/ppermute | solution.py:961
  151.1 2.4 collective-permute-start.15
  151.3 2.2 collective-permute-start.16
  157.8 23.9 %collective-permute-start.20 = (bf16[256,7680]{1,0:T(8,128)(2,1)}, bf16[256,7680]{1,0:T(8,128)(2,1)}, u32[]{:S(2)}, u32[]{:S(2)}) collective-permute-start(bf16[256,7680]{1,0:T(8,128)(2,1)} %get-tuple-element.264.refs_12_.refs_20_), channel_id=1, source_target_pairs={{0,4},{4,0},{8,12},{12,8},{16,20},{20,16},{24,28},{28,24},{1,5},{5... | collective-permute-start | bytes 11796488 | tf_op jit(solution)/shard_map/ppermute | solution.py:961
  158.0 23.6 %collective-permute-start.17 = (bf16[2,256,128]{2,1,0:T(8,128)(2,1)}, bf16[2,256,128]{2,1,0:T(8,128)(2,1)S(1)}, u32[]{:S(2)}, u32[]{:S(2)}) collective-permute-start(bf16[2,256,128]{2,1,0:T(8,128)(2,1)} %get-tuple-element.247), channel_id=1, source_target_pairs={{0,8},{4,12},{8,0},{12,4},{16,24},{20,28},{24,16},{28,20},{1,9},{5... | collective-permute-start | bytes 393224 | tf_op jit(solution)/shard_map/ppermute | solution.py:961
  158.1 23.5 %collective-permute-start.18 = (bf16[2,256,128]{2,1,0:T(8,128)(2,1)}, bf16[2,256,128]{2,1,0:T(8,128)(2,1)S(1)}, u32[]{:S(2)}, u32[]{:S(2)}) collective-permute-start(bf16[2,256,128]{2,1,0:T(8,128)(2,1)} %get-tuple-element.248), channel_id=1, source_target_pairs={{0,16},{4,20},{8,24},{12,28},{16,0},{20,4},{24,8},{28,12},{1,17},{... | collective-permute-start | bytes 393224 | tf_op jit(solution)/shard_map/ppermute | solution.py:961
  161.0 20.7 %collective-permute-start.19 = (bf16[2,256,128]{2,1,0:T(8,128)(2,1)}, bf16[2,256,128]{2,1,0:T(8,128)(2,1)S(1)}, u32[]{:S(2)}, u32[]{:S(2)}) collective-permute-start(bf16[2,256,128]{2,1,0:T(8,128)(2,1)} %get-tuple-element.249), channel_id=1, source_target_pairs={{0,24},{4,28},{8,16},{12,20},{16,8},{20,12},{24,0},{28,4},{1,25},{... | collective-permute-start | bytes 393224 | tf_op jit(solution)/shard_map/ppermute | solution.py:961
  181.7 25.5 %copy-start.43 = (bf16[2,256,128]{2,1,0:T(8,128)(2,1)}, bf16[2,256,128]{2,1,0:T(8,128)(2,1)S(1)}, u32[]{:S(2)}) copy-start(bf16[2,256,128]{2,1,0:T(8,128)(2,1)S(1)} %collective-permute-done.17.refs_5_) | copy-start | bytes 393220
  181.7 25.5 %copy-start.44 = (bf16[2,256,128]{2,1,0:T(8,128)(2,1)}, bf16[2,256,128]{2,1,0:T(8,128)(2,1)S(1)}, u32[]{:S(2)}) copy-start(bf16[2,256,128]{2,1,0:T(8,128)(2,1)S(1)} %collective-permute-done.18.refs_6_) | copy-start | bytes 393220
  181.7 2.2 collective-permute-start.21
  183.9 7.1 %collective-permute-start.22 = (bf16[256,7680]{1,0:T(8,128)(2,1)}, bf16[256,7680]{1,0:T(8,128)(2,1)}, u32[]{:S(2)}, u32[]{:S(2)}) collective-permute-start(bf16[256,7680]{1,0:T(8,128)(2,1)} %get-tuple-element.263.refs_14_.refs_22_), channel_id=1, source_target_pairs={{0,4},{4,0},{8,12},{12,8},{16,20},{20,16},{24,28},{28,24},{1,5},{5... | collective-permute-start | bytes 11796488 | tf_op jit(solution)/shard_map/ppermute | solution.py:961
  208.6 27.2 %collective-permute-start.23 = (bf16[2,256,128]{2,1,0:T(8,128)(2,1)S(1)}, bf16[2,256,128]{2,1,0:T(8,128)(2,1)S(1)}, u32[]{:S(2)}, u32[]{:S(2)}) collective-permute-start(bf16[2,256,128]{2,1,0:T(8,128)(2,1)S(1)} %copy-done.48), channel_id=1, source_target_pairs={{0,8},{4,12},{8,0},{12,4},{16,24},{20,28},{24,16},{28,20},{1,9},{5... | collective-permute-start | bytes 393224 | tf_op jit(solution)/shard_map/ppermute | solution.py:961
  208.6 27.2 %collective-permute-start.24 = (bf16[2,256,128]{2,1,0:T(8,128)(2,1)S(1)}, bf16[2,256,128]{2,1,0:T(8,128)(2,1)S(1)}, u32[]{:S(2)}, u32[]{:S(2)}) collective-permute-start(bf16[2,256,128]{2,1,0:T(8,128)(2,1)S(1)} %copy-done.47), channel_id=1, source_target_pairs={{0,16},{4,20},{8,24},{12,28},{16,0},{20,4},{24,8},{28,12},{1,17},{... | collective-permute-start | bytes 393224 | tf_op jit(solution)/shard_map/ppermute | solution.py:961
  211.6 24.2 %collective-permute-start.25 = (bf16[2,256,128]{2,1,0:T(8,128)(2,1)S(1)}, bf16[2,256,128]{2,1,0:T(8,128)(2,1)S(1)}, u32[]{:S(2)}, u32[]{:S(2)}) collective-permute-start(bf16[2,256,128]{2,1,0:T(8,128)(2,1)S(1)} %copy-done.46), channel_id=1, source_target_pairs={{0,24},{4,28},{8,16},{12,20},{16,8},{20,12},{24,0},{28,4},{1,25},{... | collective-permute-start | bytes 393224 | tf_op jit(solution)/shard_map/ppermute | solution.py:961
  213.0 27.3 %copy-start.30 = (f32[8,1024]{1,0:T(8,128)S(1)}, f32[8,1024]{1,0:T(8,128)}, u32[]{:S(2)}) copy-start(f32[8,1024]{1,0:T(8,128)} %get-tuple-element.333) | copy-start | bytes 98308
  235.8 34.5 %collective-permute-start.26 = (bf16[2,3,256,128]{3,2,1,0:T(8,128)(2,1)}, bf16[2,3,256,128]{3,2,1,0:T(8,128)(2,1)S(1)}, u32[]{:S(2)}, u32[]{:S(2)}) collective-permute-start(bf16[2,3,256,128]{3,2,1,0:T(8,128)(2,1)} %get-tuple-element.295), channel_id=1, source_target_pairs={{0,8},{4,12},{8,0},{12,4},{16,24},{20,28},{24,16},{28,20},{1,9},{5... | collective-permute-start | bytes 1179656 | tf_op jit(solution)/shard_map/ppermute | solution.py:961
  235.9 34.5 %collective-permute-start.27 = (bf16[2,3,256,128]{3,2,1,0:T(8,128)(2,1)}, bf16[2,3,256,128]{3,2,1,0:T(8,128)(2,1)S(1)}, u32[]{:S(2)}, u32[]{:S(2)}) collective-permute-start(bf16[2,3,256,128]{3,2,1,0:T(8,128)(2,1)} %get-tuple-element.296), channel_id=1, source_target_pairs={{0,16},{4,20},{8,24},{12,28},{16,0},{20,4},{24,8},{28,12},{1,17},{... | collective-permute-start | bytes 1179656 | tf_op jit(solution)/shard_map/ppermute | solution.py:961
  238.4 32.0 %collective-permute-start.28 = (bf16[2,3,256,128]{3,2,1,0:T(8,128)(2,1)}, bf16[2,3,256,128]{3,2,1,0:T(8,128)(2,1)S(1)}, u32[]{:S(2)}, u32[]{:S(2)}) collective-permute-start(bf16[2,3,256,128]{3,2,1,0:T(8,128)(2,1)} %get-tuple-element.297), channel_id=1, source_target_pairs={{0,24},{4,28},{8,16},{12,20},{16,8},{20,12},{24,0},{28,4},{1,25},{... | collective-permute-start | bytes 1179656 | tf_op jit(solution)/shard_map/ppermute | solution.py:961
  270.4 35.4 %copy-start.13 = (bf16[2,3,256,128]{3,2,1,0:T(8,128)(2,1)}, bf16[2,3,256,128]{3,2,1,0:T(8,128)(2,1)S(1)}, u32[]{:S(2)}) copy-start(bf16[2,3,256,128]{3,2,1,0:T(8,128)(2,1)S(1)} %collective-permute-done.26.refs_5_) | copy-start | bytes 1179652
  270.4 35.4 %copy-start.14 = (bf16[2,3,256,128]{3,2,1,0:T(8,128)(2,1)}, bf16[2,3,256,128]{3,2,1,0:T(8,128)(2,1)S(1)}, u32[]{:S(2)}) copy-start(bf16[2,3,256,128]{3,2,1,0:T(8,128)(2,1)S(1)} %collective-permute-done.27.refs_6_) | copy-start | bytes 1179652
  270.4 34.2 %copy-start.15 = (bf16[2,3,256,128]{3,2,1,0:T(8,128)(2,1)}, bf16[2,3,256,128]{3,2,1,0:T(8,128)(2,1)S(1)}, u32[]{:S(2)}) copy-start(bf16[2,3,256,128]{3,2,1,0:T(8,128)(2,1)S(1)} %collective-permute-done.28.refs_7_) | copy-start | bytes 1179652
  270.4 43.5 %collective-permute-start.29 = (bf16[2,3,256,128]{3,2,1,0:T(8,128)(2,1)}, bf16[2,3,256,128]{3,2,1,0:T(8,128)(2,1)}, u32[]{:S(2)}, u32[]{:S(2)}) collective-permute-start(bf16[2,3,256,128]{3,2,1,0:T(8,128)(2,1)} %get-tuple-element.306), channel_id=1, source_target_pairs={{0,8},{4,12},{8,0},{12,4},{16,24},{20,28},{24,16},{28,20},{1,9},{5... | collective-permute-start | bytes 1179656 | tf_op jit(solution)/shard_map/ppermute | solution.py:961
  272.8 41.1 %collective-permute-start.30 = (bf16[2,3,256,128]{3,2,1,0:T(8,128)(2,1)}, bf16[2,3,256,128]{3,2,1,0:T(8,128)(2,1)}, u32[]{:S(2)}, u32[]{:S(2)}) collective-permute-start(bf16[2,3,256,128]{3,2,1,0:T(8,128)(2,1)} %get-tuple-element.307), channel_id=1, source_target_pairs={{0,16},{4,20},{8,24},{12,28},{16,0},{20,4},{24,8},{28,12},{1,17},{... | collective-permute-start | bytes 1179656 | tf_op jit(solution)/shard_map/ppermute | solution.py:961
  273.7 40.2 %collective-permute-start.31 = (bf16[2,3,256,128]{3,2,1,0:T(8,128)(2,1)}, bf16[2,3,256,128]{3,2,1,0:T(8,128)(2,1)}, u32[]{:S(2)}, u32[]{:S(2)}) collective-permute-start(bf16[2,3,256,128]{3,2,1,0:T(8,128)(2,1)} %get-tuple-element.308), channel_id=1, source_target_pairs={{0,24},{4,28},{8,16},{12,20},{16,8},{20,12},{24,0},{28,4},{1,25},{... | collective-permute-start | bytes 1179656 | tf_op jit(solution)/shard_map/ppermute | solution.py:961
  305.8 34.5 %collective-permute-start.36 = (bf16[2,1152,256]{2,1,0:T(8,128)(2,1)}, bf16[2,1152,256]{2,1,0:T(8,128)(2,1)S(1)}, u32[]{:S(2)}, u32[]{:S(2)}) collective-permute-start(bf16[2,1152,256]{2,1,0:T(8,128)(2,1)} %pad_maximum_fusion), channel_id=1, source_target_pairs={{0,8},{4,12},{8,0},{12,4},{16,24},{20,28},{24,16},{28,20},{1,9},{5... | collective-permute-start | bytes 3538952 | tf_op jit(solution)/shard_map/ppermute | solution.py:961
  313.9 20.3 %collective-permute-start.32 = (f32[256,1024]{1,0:T(8,128)}, f32[256,1024]{1,0:T(8,128)}, u32[]{:S(2)}, u32[]{:S(2)}) collective-permute-start(f32[256,1024]{1,0:T(8,128)} %get-tuple-element.310), channel_id=1, source_target_pairs={{0,4},{4,0},{8,12},{12,8},{16,20},{20,16},{24,28},{28,24},{1,5},{5... | collective-permute-start | bytes 3145736 | tf_op jit(solution)/shard_map/ppermute | solution.py:961
  320.5 13.6 %collective-permute-start.33 = (f32[256,1024]{1,0:T(8,128)}, f32[256,1024]{1,0:T(8,128)}, u32[]{:S(2)}, u32[]{:S(2)}) collective-permute-start(f32[256,1024]{1,0:T(8,128)} %get-tuple-element.311), channel_id=1, source_target_pairs={{0,4},{4,0},{8,12},{12,8},{16,20},{20,16},{24,28},{28,24},{1,5},{5... | collective-permute-start | bytes 3145736 | tf_op jit(solution)/shard_map/ppermute | solution.py:961
  332.0 22.9 %collective-permute-start.34 = (bf16[2,2,256,384]{3,2,1,0:T(8,128)(2,1)}, bf16[2,2,256,384]{3,2,1,0:T(8,128)(2,1)S(1)}, u32[]{:S(2)}, u32[]{:S(2)}) collective-permute-start(bf16[2,2,256,384]{3,2,1,0:T(8,128)(2,1)} %get-tuple-element.324), channel_id=1, source_target_pairs={{0,1},{1,0},{2,3},{3,2},{4,5},{5,4},{6,7},{7,6},{8,9},{9,8},{10,11... | collective-permute-start | bytes 2359304 | tf_op jit(solution)/shard_map/ppermute | solution.py:961
  333.5 21.5 %collective-permute-start.35 = (bf16[2,2,256,384]{3,2,1,0:T(8,128)(2,1)}, bf16[2,2,256,384]{3,2,1,0:T(8,128)(2,1)}, u32[]{:S(2)}, u32[]{:S(2)}) collective-permute-start(bf16[2,2,256,384]{3,2,1,0:T(8,128)(2,1)} %get-tuple-element.325), channel_id=1, source_target_pairs={{0,2},{1,3},{2,0},{3,1},{4,6},{5,7},{6,4},{7,5},{8,10},{9,11},{10,... | collective-permute-start | bytes 2359304 | tf_op jit(solution)/shard_map/ppermute | solution.py:961
  340.3 32.9 %copy-start.4 = (bf16[2,1152,256]{2,1,0:T(8,128)(2,1)}, bf16[2,1152,256]{2,1,0:T(8,128)(2,1)S(1)}, u32[]{:S(2)}) copy-start(bf16[2,1152,256]{2,1,0:T(8,128)(2,1)S(1)} %collective-permute-done.36) | copy-start | bytes 3538948
  341.4 1.3 collective-permute-start.39
  342.7 6.5 %collective-permute-start.40 = (bf16[2,24,1024]{2,1,0:T(8,128)(2,1)S(1)}, bf16[2,24,1024]{2,1,0:T(8,128)(2,1)S(1)}, u32[]{:S(2)}, u32[]{:S(2)}) collective-permute-start(bf16[2,24,1024]{2,1,0:T(8,128)(2,1)S(1)} %pad_maximum_fusion.10), channel_id=1, source_target_pairs={{0,8},{4,12},{8,0},{12,4},{16,24},{20,28},{24,16},{28,20},{1,9},{5... | collective-permute-start | bytes 294920 | tf_op jit(solution)/shard_map/ppermute | solution.py:961
  349.2 11.8 %collective-permute-start.41 = (bf16[4,24,1024]{2,1,0:T(8,128)(2,1)S(1)}, bf16[4,24,1024]{2,1,0:T(8,128)(2,1)S(1)}, u32[]{:S(2)}, u32[]{:S(2)}) collective-permute-start(bf16[4,24,1024]{2,1,0:T(8,128)(2,1)S(1)} %pad_maximum_fusion.7), channel_id=1, source_target_pairs={{0,16},{4,20},{8,24},{12,28},{16,0},{20,4},{24,8},{28,12},{1,17},{... | collective-permute-start | bytes 589832 | tf_op jit(solution)/shard_map/ppermute | solution.py:961
  361.2 10.0 %collective-permute-start.42 = (bf16[1,144,1024]{2,1,0:T(8,128)(2,1)S(1)}, bf16[1,144,1024]{2,1,0:T(8,128)(2,1)S(1)}, u32[]{:S(2)}, u32[]{:S(2)}) collective-permute-start(bf16[1,144,1024]{2,1,0:T(8,128)(2,1)S(1)} %maximum_bitcast_fusion.1), channel_id=1, source_target_pairs={{0,1},{1,0},{2,3},{3,2},{4,5},{5,4},{6,7},{7,6},{8,9},{9,8},{10,11... | collective-permute-start | bytes 884744 | tf_op jit(solution)/shard_map/ppermute | solution.py:961
  363.1 14.7 %collective-permute-start.38 = (bf16[1,2,256,384]{3,2,1,0:T(8,128)(2,1)S(1)}, bf16[1,2,256,384]{3,2,1,0:T(8,128)(2,1)S(1)}, u32[]{:S(2)}, u32[]{:S(2)}) collective-permute-start(bf16[1,2,256,384]{3,2,1,0:T(8,128)(2,1)S(1)} %add_convert_fusion.1), channel_id=1, source_target_pairs={{0,1},{1,0},{2,3},{3,2},{4,5},{5,4},{6,7},{7,6},{8,9},{9,8},{10,11... | collective-permute-start | bytes 1179656 | tf_op jit(solution)/shard_map/ppermute | solution.py:961
  364.8 14.1 %collective-permute-start.37 = (bf16[1,2,256,384]{3,2,1,0:T(8,128)(2,1)S(1)}, bf16[1,2,256,384]{3,2,1,0:T(8,128)(2,1)S(1)}, u32[]{:S(2)}, u32[]{:S(2)}) collective-permute-start(bf16[1,2,256,384]{3,2,1,0:T(8,128)(2,1)S(1)} %add_convert_fusion.4), channel_id=1, source_target_pairs={{0,2},{1,3},{2,0},{3,1},{4,6},{5,7},{6,4},{7,5},{8,10},{9,11},{10,... | collective-permute-start | bytes 1179656 | tf_op jit(solution)/shard_map/ppermute | solution.py:961
  371.3 16.0 %collective-permute-start.43 = (bf16[2,144,1024]{2,1,0:T(8,128)(2,1)S(1)}, bf16[2,144,1024]{2,1,0:T(8,128)(2,1)S(1)}, u32[]{:S(2)}, u32[]{:S(2)}) collective-permute-start(bf16[2,144,1024]{2,1,0:T(8,128)(2,1)S(1)} %pad_maximum_fusion.2), channel_id=1, source_target_pairs={{0,2},{1,3},{2,0},{3,1},{4,6},{5,7},{6,4},{7,5},{8,10},{9,11},{10,... | collective-permute-start | bytes 1769480 | tf_op jit(solution)/shard_map/ppermute | solution.py:961
  373.4 24.9 %collective-permute-start.47 = (bf16[1,1152,256]{2,1,0:T(8,128)(2,1)S(1)}, bf16[1,1152,256]{2,1,0:T(8,128)(2,1)S(1)}, u32[]{:S(2)}, u32[]{:S(2)}) collective-permute-start(bf16[1,1152,256]{2,1,0:T(8,128)(2,1)S(1)} %fusion.1), channel_id=1, source_target_pairs={{0,16},{4,20},{8,24},{12,28},{16,0},{20,4},{24,8},{28,12},{1,17},{... | collective-permute-start | bytes 1769480 | tf_op jit(solution)/shard_map/ppermute | solution.py:961
  387.5 19.1 %collective-permute-start.44 = (bf16[2,256,384]{2,1,0:T(8,128)(2,1)S(1)}, bf16[2,256,384]{2,1,0:T(8,128)(2,1)S(1)}, u32[]{:S(2)}, u32[]{:S(2)}) collective-permute-start(bf16[2,256,384]{2,1,0:T(8,128)(2,1)S(1)} %pad_maximum_fusion.4), channel_id=1, source_target_pairs={{0,8},{4,12},{8,0},{12,4},{16,24},{20,28},{24,16},{28,20},{1,9},{5... | collective-permute-start | bytes 1179656 | tf_op jit(solution)/shard_map/ppermute | solution.py:961
  398.6 24.7 %collective-permute-start.50 = (bf16[1152,256]{1,0:T(8,128)(2,1)S(1)}, bf16[1152,256]{1,0:T(8,128)(2,1)}, u32[]{:S(2)}, u32[]{:S(2)}) collective-permute-start(bf16[1152,256]{1,0:T(8,128)(2,1)S(1)} %fusion.refs_0_), channel_id=1, source_target_pairs={{0,3},{1,2},{2,1},{3,0},{4,7},{5,6},{6,5},{7,4},{8,11},{9,10},{10,... | collective-permute-start | bytes 1769480 | tf_op jit(solution)/shard_map/ppermute | solution.py:961
  398.7 27.9 %collective-permute-start.49 = (bf16[1152,256]{1,0:T(8,128)(2,1)S(1)}, bf16[1152,256]{1,0:T(8,128)(2,1)}, u32[]{:S(2)}, u32[]{:S(2)}) collective-permute-start(bf16[1152,256]{1,0:T(8,128)(2,1)S(1)} %fusion.refs_0_), channel_id=1, source_target_pairs={{0,2},{1,3},{2,0},{3,1},{4,6},{5,7},{6,4},{7,5},{8,10},{9,11},{10,... | collective-permute-start | bytes 1769480 | tf_op jit(solution)/shard_map/ppermute | solution.py:961
  400.5 26.2 %collective-permute-start.48 = (bf16[1152,256]{1,0:T(8,128)(2,1)S(1)}, bf16[1152,256]{1,0:T(8,128)(2,1)}, u32[]{:S(2)}, u32[]{:S(2)}) collective-permute-start(bf16[1152,256]{1,0:T(8,128)(2,1)S(1)} %fusion.refs_0_), channel_id=1, source_target_pairs={{0,1},{1,0},{2,3},{3,2},{4,5},{5,4},{6,7},{7,6},{8,9},{9,8},{10,11... | collective-permute-start | bytes 1769480 | tf_op jit(solution)/shard_map/ppermute | solution.py:961
  408.7 13.3 %collective-permute-start.45 = (bf16[1,256,384]{2,1,0:T(8,128)(2,1)}, bf16[1,256,384]{2,1,0:T(8,128)(2,1)}, u32[]{:S(2)}, u32[]{:S(2)}) collective-permute-start(bf16[1,256,384]{2,1,0:T(8,128)(2,1)} %add_convert_fusion.8), channel_id=1, source_target_pairs={{0,16},{4,20},{8,24},{12,28},{16,0},{20,4},{24,8},{28,12},{1,17},{... | collective-permute-start | bytes 589832 | tf_op jit(solution)/shard_map/ppermute | solution.py:961
  423.1 3.6 collective-permute-start.46
  426.7 11.0 %collective-permute-start.53 = (bf16[2,128,384]{2,1,0:T(8,128)(2,1)S(1)}, bf16[2,128,384]{2,1,0:T(8,128)(2,1)S(1)}, u32[]{:S(2)}, u32[]{:S(2)}) collective-permute-start(bf16[2,128,384]{2,1,0:T(8,128)(2,1)S(1)} %pad_maximum_fusion.8.refs_0_), channel_id=1, source_target_pairs={{0,3},{1,2},{2,1},{3,0},{4,7},{5,6},{6,5},{7,4},{8,11},{9,10},{10,... | collective-permute-start | bytes 589832 | tf_op jit(solution)/shard_map/ppermute | solution.py:961
  428.0 9.9 %collective-permute-start.52 = (bf16[2,128,384]{2,1,0:T(8,128)(2,1)S(1)}, bf16[2,128,384]{2,1,0:T(8,128)(2,1)S(1)}, u32[]{:S(2)}, u32[]{:S(2)}) collective-permute-start(bf16[2,128,384]{2,1,0:T(8,128)(2,1)S(1)} %pad_maximum_fusion.8.refs_0_), channel_id=1, source_target_pairs={{0,2},{1,3},{2,0},{3,1},{4,6},{5,7},{6,4},{7,5},{8,10},{9,11},{10,... | collective-permute-start | bytes 589832 | tf_op jit(solution)/shard_map/ppermute | solution.py:961
  429.4 9.0 %collective-permute-start.51 = (bf16[2,128,384]{2,1,0:T(8,128)(2,1)S(1)}, bf16[2,128,384]{2,1,0:T(8,128)(2,1)S(1)}, u32[]{:S(2)}, u32[]{:S(2)}) collective-permute-start(bf16[2,128,384]{2,1,0:T(8,128)(2,1)S(1)} %pad_maximum_fusion.8.refs_0_), channel_id=1, source_target_pairs={{0,1},{1,0},{2,3},{3,2},{4,5},{5,4},{6,7},{7,6},{8,9},{9,8},{10,11... | collective-permute-start | bytes 589832 | tf_op jit(solution)/shard_map/ppermute | solution.py:961
  (44 other events, 311.9 us)
Sparse Core Ops, SparseCore 0:
  207.3 95.8 reduce-scatter.1
